TPU v7x, 32 devices: a whole 2x2x4 slice. The times are simulated.
32 devices in a mesh: grp: 2 (over y), gene: 4 (over z), row: 4 (over x, core).
Axes of the slice: x: 2, y: 2, z: 4, core: 2. Of those that a mesh axis runs over, the one named last changes fastest.
Arguments:
- x_slab: bfloat16 [24576, 2560], P(('grp', 'row'), 'gene'), parts along dimension 0, may hold values from -6 to 6
- cell_factor: bfloat16 [4096, 128], P(('grp', 'row')), parts along dimension 0, may hold values from -1.5 to 1.5
- row_index: int32 [24576], P(('grp', 'row')), parts along dimension 0, may hold values from 0 to 2047, as said below
- gene_scale: float32 [5120], P(('grp', 'gene')), parts along dimension 0, may hold values from 0.3 to 3
- gene_factor: float32 [5120, 128], P(('grp', 'gene', 'row')), parts along dimension 0, may hold values from -1.5 to 1.5
- first_moment: float32 [5120, 128], P(('grp', 'gene', 'row')), parts along dimension 0, may hold values from -1.2 to 1.2
- second_moment: float32 [5120, 128], P(('grp', 'gene', 'row')), parts along dimension 0, may hold values from 0.05 to 1
Outputs:
- grad_cells: float32 [24576, 128], P(('grp', 'row', 'gene')), parts along dimension 0
- new_factor: float32 [5120, 128], P(('grp', 'gene', 'row')), parts along dimension 0
- new_first: float32 [5120, 128], P(('grp', 'gene', 'row')), parts along dimension 0
- new_second: float32 [5120, 128], P(('grp', 'gene', 'row')), parts along dimension 0
There are 2 independent parts, one for each index of `grp`. A program takes and returns all parts, laid end to end along the dimension named above; each array names one. Nothing has to cross between parts.
Inputs may be any that keep to these rules, and one draw needn't show every extreme that they name: `row_index`: rows r * 3072 to (r + 1) * 3072 - 1 name cells r * 512 to (r + 1) * 512 - 1; cells may repeat.
All inputs are finite; a program needn't handle non-finite values.
Results may differ from a plain program's by a relative error of at most 0.008.
Values may be sent and summed in bfloat16 or wider, within the bound.
No kernel may reach another device: no remote copies, remote signals or barrier semaphores. Data moves between devices by JAX's collectives and lax.ppermute only.
A program may use at most 64 MiB of HBM per device.

v0:
```python
import math

import jax
import jax.numpy as jnp
from jax import lax
from jax.sharding import PartitionSpec as P

tukey_c = 4.685
beta_one = 0.9
beta_two = 0.999
learn_rate = 0.02
adam_eps = 1e-08


def influence(factors, x_slab, gene_scale, piece):
    pred = lax.dot_general(
        factors, piece, (((1,), (1,)), ((), ())), preferred_element_type=jnp.float32
    )
    x_part = x_slab.astype(jnp.float32)
    scaled = (x_part - pred) / gene_scale[None, :]
    ratio = scaled / tukey_c
    inside = 1.0 - ratio * ratio
    weight = jnp.where(jnp.abs(ratio) < 1.0, inside * inside, 0.0)
    return (scaled * weight / gene_scale[None, :]).astype(jnp.bfloat16)


def local(x_slab, cell_factor, row_index, gene_scale, gene_factor, first_moment, second_moment):
    rows_dev, genes_dev = x_slab.shape
    cells_dev = cell_factor.shape[0]
    n_gene = lax.axis_size("gene")
    local_index = row_index - lax.axis_index("row") * cells_dev
    factors = jnp.take(cell_factor, local_index, axis=0)
    factor_bf = gene_factor.astype(jnp.bfloat16)
    scale_k = 4.0 / math.sqrt(genes_dev * n_gene)
    gathered = lax.all_gather(factor_bf, "row", axis=0, tiled=True)
    infl = influence(factors, x_slab, gene_scale, gathered)
    grad_rows = jnp.dot(infl, gathered, preferred_element_type=jnp.float32)
    grad_cols = lax.dot_general(
        infl, factors, (((0,), (0,)), ((), ())), preferred_element_type=jnp.float32
    )
    grad_genes = lax.psum_scatter(
        (-scale_k * grad_cols).astype(jnp.bfloat16), "row", scatter_dimension=0, tiled=True
    ).astype(jnp.float32)
    grad_cells = lax.psum_scatter(-scale_k * grad_rows, "gene", scatter_dimension=0, tiled=True)
    new_first = beta_one * first_moment + (1.0 - beta_one) * grad_genes
    new_second = beta_two * second_moment + (1.0 - beta_two) * grad_genes * grad_genes
    first_hat = new_first / (1.0 - beta_one**10)
    second_hat = new_second / (1.0 - beta_two**10)
    new_factor = gene_factor - learn_rate * first_hat / (jnp.sqrt(second_hat) + adam_eps)
    return (grad_cells, new_factor, new_first, new_second)


def solution(mesh):
    in_specs = (
        P(("grp", "row"), "gene"),
        P(("grp", "row"), None),
        P(("grp", "row")),
        P(("grp", "gene")),
        P(("grp", "gene", "row"), None),
        P(("grp", "gene", "row"), None),
        P(("grp", "gene", "row"), None),
    )
    out_specs = (
        P(("grp", "row", "gene"), None),
        P(("grp", "gene", "row"), None),
        P(("grp", "gene", "row"), None),
        P(("grp", "gene", "row"), None),
    )
    return jax.shard_map(local, mesh=mesh, in_specs=in_specs, out_specs=out_specs, check_vma=False)
```

profile of v0, /device:TPU:0, one launch (start us, length us, event | category | flops | bytes accessed | tf_op | source)
XLA Modules:
  0.0 102.1 jit_solution(13833262780194311443)
XLA Ops:
  7.2 0.0 copy-start
  7.2 0.0 copy-start.5
  7.2 0.0 reduce-scatter.5.cloned.1.call-start
  7.2 0.7 compare_and_fusion
  8.0 0.7 fusion.3
  8.7 0.9 convert_element_type.16
  9.6 6.6 %all_gather.3 = bf16[640,128]{1,0:T(8,128)(2,1)S(1)} all-gather(bf16[160,128]{1,0:T(8,128)(2,1)S(1)} %convert_element_type.16), channel_id=1, replica_groups=mesh['grp'=2,'gene'=4,'row'=4] {'row'}, dimensions={0}, use_global_device_ids=true | all-gather | bytes 204800 | tf_op jit(solution)/shard_map/all_gather | solution.py:35
  16.2 0.0 copy-done
  16.2 9.2 %gather_fusion = bf16[3072,128]{1,0:T(8,128)(2,1)S(1)} fusion(bf16[512,128]{1,0:T(8,128)(2,1)S(1)} %copy-done, s32[3072]{0:T(1024)S(1)} %fusion.3), kind=kCustom, calls=%fused_computation | custom fusion | bytes 1585152 | tf_op jit(solution)/shard_map/jit(_take)/gather | solution.py:32
  25.4 0.0 copy-done.5
  25.4 6.0 %divide_convert_fusion = bf16[3072,640]{1,0:T(8,128)(2,1)S(1)} fusion(bf16[3072,640]{1,0:T(8,128)(2,1)} %param.7, bf16[640,128]{1,0:T(8,128)(2,1)S(1)} %all_gather.3, f32[640]{0:T(1024)S(1)} %copy-done.5, bf16[3072,128]{1,0:T(8,128)(2,1)S(1)} %gather_fusion, pred[3072]{0:T(1024)(128)(4,1)S(1)} %compare_and_fusion), kind=kOutput, calls=%fused_computation.1 | convolution fusion | flops 529268736 | bytes 8820224 | tf_op jit(solution)/shard_map/dot_general | solution.py:16
  31.4 0.0 copy-start.1
  31.4 1.9 %copy-done.1 = bf16[3072,640]{1,0:T(8,128)(2,1)} copy-done((bf16[3072,640]{1,0:T(8,128)(2,1)}, bf16[3072,640]{1,0:T(8,128)(2,1)S(1)}, u32[]{:S(2)}) %copy-start.1) | copy-done | bytes 3932184
  33.2 2.4 %fusion = bf16[640,128]{1,0:T(8,128)(2,1)} fusion(bf16[3072,640]{1,0:T(8,128)(2,1)S(1)} %divide_convert_fusion, bf16[3072,128]{1,0:T(8,128)(2,1)S(1)} %gather_fusion, pred[3072]{0:T(1024)(128)(4,1)S(1)} %compare_and_fusion), kind=kOutput, calls=%fused_computation.5 | convolution fusion | flops 503873536 | bytes 4885504 | tf_op jit(solution)/shard_map/dot_general | solution.py:38
  35.6 0.0 reduce-scatter.5.cloned.1.call-update
  35.7 0.0 copy-start.2
  35.7 0.0 copy-start.3
  35.7 0.0 copy-start.4
  35.7 0.0 reduce-scatter.3.cloned.1.call-start
  35.8 4.5 %convolution_multiply_fusion = f32[3072,128]{1,0:T(8,128)} fusion(bf16[3072,640]{1,0:T(8,128)(2,1)} %copy-done.1, bf16[640,128]{1,0:T(8,128)(2,1)S(1)} %all_gather.3), kind=kOutput, calls=%fused_computation.3 | convolution fusion | flops 503709696 | bytes 5668864 | tf_op jit(solution)/shard_map/dot_general | solution.py:37
  40.2 0.0 reduce-scatter.3.cloned.1.call-update
  40.3 16.8 %reduce-scatter.5.cloned.1.call-done = bf16[160,128]{1,0:T(8,128)(2,1)} async-done(((bf16[640,128]{1,0:T(8,128)(2,1)}), bf16[160,128]{1,0:T(8,128)(2,1)}) %reduce-scatter.5.cloned.1.call-update) | async-done | bytes 40976 | tf_op jit(solution)/shard_map/reduce_scatter | solution.py:41
  57.1 1.5 %divide_subtract_fusion = (f32[160,128]{1,0:T(8,128)}, f32[160,128]{1,0:T(8,128)}, f32[160,128]{1,0:T(8,128)}) fusion(f32[160,128]{1,0:T(8,128)S(1)} %copy-done.2, bf16[160,128]{1,0:T(8,128)(2,1)} %reduce-scatter.5.cloned.1.call-done, f32[160,128]{1,0:T(8,128)S(1)} %copy-done.3, f32[160,128]{1,0:T(8,128)S(1)} %copy-done.4), kind=kLoop, calls=%fused_computation.11 | loop fusion | flops 266240 | bytes 532480 | tf_op jit(solution)/shard_map/sub | solution.py:49
  58.5 36.7 %reduce-scatter.3.cloned.1.call-done = f32[768,128]{1,0:T(8,128)} async-done(((f32[3072,128]{1,0:T(8,128)}), f32[768,128]{1,0:T(8,128)}) %reduce-scatter.3.cloned.1.call-update) | async-done | bytes 393232 | tf_op jit(solution)/shard_map/reduce_scatter | solution.py:44
  (3 shorter events, 0.0 us)
Async XLA Ops:
  7.2 9.1 %copy-start = (bf16[512,128]{1,0:T(8,128)(2,1)S(1)}, bf16[512,128]{1,0:T(8,128)(2,1)}, u32[]{:S(2)}) copy-start(bf16[512,128]{1,0:T(8,128)(2,1)} %param.8) | copy-start | bytes 393220
  7.2 18.2 %copy-start.5 = (f32[640]{0:T(1024)S(1)}, f32[640]{0:T(1024)}, u32[]{:S(2)}) copy-start(f32[640]{0:T(1024)} %param.10) | copy-start | bytes 7684
  7.2 49.9 %reduce-scatter.5.cloned.1.call-start = ((), (), s32[]{:S(2)}) async-start(), calls=%async_computation.3 | async-start | bytes 204800 | tf_op jit(solution)/shard_map/reduce_scatter | solution.py:41
  31.4 1.9 %copy-start.1 = (bf16[3072,640]{1,0:T(8,128)(2,1)}, bf16[3072,640]{1,0:T(8,128)(2,1)S(1)}, u32[]{:S(2)}) copy-start(bf16[3072,640]{1,0:T(8,128)(2,1)S(1)} %divide_convert_fusion) | copy-start | bytes 11796484
  35.7 21.4 %copy-start.2 = (f32[160,128]{1,0:T(8,128)S(1)}, f32[160,128]{1,0:T(8,128)}, u32[]{:S(2)}) copy-start(f32[160,128]{1,0:T(8,128)} %param.11) | copy-start | bytes 245764
  35.7 21.4 %copy-start.3 = (f32[160,128]{1,0:T(8,128)S(1)}, f32[160,128]{1,0:T(8,128)}, u32[]{:S(2)}) copy-start(f32[160,128]{1,0:T(8,128)} %param.12) | copy-start | bytes 245764
  35.7 21.4 %copy-start.4 = (f32[160,128]{1,0:T(8,128)S(1)}, f32[160,128]{1,0:T(8,128)}, u32[]{:S(2)}) copy-start(f32[160,128]{1,0:T(8,128)} %param.13) | copy-start | bytes 245764
  35.7 59.6 %reduce-scatter.3.cloned.1.call-start = ((), (), s32[]{:S(2)}) async-start(), calls=%async_computation.2 | async-start | bytes 1966080 | tf_op jit(solution)/shard_map/reduce_scatter | solution.py:44
Sparse Core Ops, SparseCore 0:
  35.8 21.2 reduce-scatter.4
  59.9 35.3 reduce-scatter.2
where the time goes:
time: 102 us
  waiting for transfers between devices  53.5 us (52%)
  between operations  14.1 us (14%)
  matrix products  12.9 us (13%)
  local copies, waits for them, and re-layouts  11 us (11%)
  blocking collectives  6.64 us (7%)
  other arithmetic  3.82 us (4%)
    reduce_scatter x1, waiting for transfers between devices, local(): lax.psum_scatter(-scale_k * grad_rows, 'gene', scatter_dimension=0, tiled...  36.7 us
    reduce_scatter x1, waiting for transfers between devices, local(): lax.psum_scatter((-scale_k * grad_cols).astype(jnp.bfloat16), 'row', scat...  16.8 us
    gather x1, local copies, waits for them, and re-layouts, local(): factors = jnp.take(cell_factor, local_index, axis=0)  9.15 us
    all_gather x1, blocking collectives, local(): gathered = lax.all_gather(factor_bf, 'row', axis=0, tiled=True)  6.64 us
    dot_general x1, matrix products, influence(): lax.dot_general(factors, piece, (((1,), (1,)), ((), ())), preferred_eleme...  5.96 us
    dot_general x1, matrix products, local(): grad_rows = jnp.dot(infl, gathered, preferred_element_type=jnp.float32)  4.49 us
    dot_general x1, matrix products, local(): lax.dot_general(infl, factors, (((0,), (0,)), ((), ())), preferred_elemen...  2.43 us
  transfers between devices with their start and end apart: 2, of which 2 were waited for; matrix products, arithmetic and copies ran while one was open for 6% of the time, Pallas kernels for 0%

commit v1 on v0

v1 whole, which is shorter than its diff:
```python
import functools
import math

import jax
import jax.numpy as jnp
from jax import lax
from jax.experimental import pallas as pl
from jax.experimental.pallas import tpu as pltpu
from jax.sharding import PartitionSpec as P

tukey_c = 4.685
beta_one = 0.9
beta_two = 0.999
learn_rate = 0.02
adam_eps = 1e-08

DIRECT_MOST = 8
VMEM = pltpu.VMEM
IN_VMEM = pl.BlockSpec(memory_space=VMEM)
IN_ANY = pl.BlockSpec(memory_space=pl.ANY)


def tile_of(rows, most):
    best = [t for t in range(128, most + 1, 128) if rows % t == 0]
    return best[-1] if best else rows


def params():
    return pltpu.CompilerParams(vmem_limit_bytes=24 * 1024 * 1024)


def cost(flops, moved):
    return pl.CostEstimate(flops=int(flops), bytes_accessed=int(moved), transcendentals=0)


def pinned(*arrays):
    return [pltpu.with_memory_space_constraint(a, VMEM) for a in arrays]


def prepare_kernel(scale_k, x_ref, index_ref, cell_ref, scale_ref, x_out, f_out, ft_out, bend_out, shrink_out, sem):
    load = pltpu.make_async_copy(x_ref, x_out, sem)
    load.start()
    cells, rank = cell_ref.shape
    rows = index_ref.shape[1]
    genes = scale_ref.shape[1]
    inverse = 1.0 / scale_ref[...]
    bend_out[...] = (inverse * inverse) * (1.0 / (tukey_c * tukey_c))
    shrink_out[...] = jnp.transpose(jnp.broadcast_to(-scale_k * (inverse * inverse), (rank, genes)))
    table = jnp.transpose(cell_ref[...].astype(jnp.float32)).astype(jnp.bfloat16)
    base = lax.axis_index("row") * cells
    step = tile_of(rows, 512)
    for at in range(0, rows, step):
        local = index_ref[:, at : at + step] - base
        hot = lax.broadcasted_iota(jnp.int32, (cells, step), 0) == local
        hot = jnp.where(hot, 1.0, 0.0).astype(jnp.bfloat16)
        picked = jnp.dot(table, hot, preferred_element_type=jnp.float32)
        ft_out[:, at : at + step] = picked.astype(jnp.bfloat16)
        f_out[at : at + step, :] = jnp.transpose(picked).astype(jnp.bfloat16)
    load.wait()


def prepare(x_slab, row_index, cell_factor, gene_scale, scale_k):
    rows, genes = x_slab.shape
    cells, rank = cell_factor.shape
    return pl.pallas_call(
        functools.partial(prepare_kernel, scale_k),
        out_shape=(
            VMEM((rows, genes), jnp.bfloat16),
            VMEM((rows, rank), jnp.bfloat16),
            VMEM((rank, rows), jnp.bfloat16),
            VMEM((1, genes), jnp.float32),
            VMEM((genes, rank), jnp.float32),
        ),
        in_specs=[IN_ANY, IN_VMEM, IN_VMEM, IN_VMEM],
        out_specs=(IN_VMEM,) * 5,
        scratch_shapes=[pltpu.SemaphoreType.DMA],
        compiler_params=params(),
        cost_estimate=cost(2 * rows * cells * rank, 2 * rows * genes * 2),
        name="prepare",
    )(
        pltpu.with_memory_space_constraint(x_slab, pltpu.HBM),
        row_index.reshape(1, rows),
        cell_factor,
        gene_scale.reshape(1, genes),
    )


def pick(axis, table):
    me = lax.axis_index(axis)
    value = jnp.int32(table[0])
    for place, entry in enumerate(table[1:], 1):
        value = jnp.where(me == place, entry, value)
    return value


def partner(me, hop, size):
    return me ^ hop if size & (size - 1) == 0 else (me + hop) % size


def source(me, hop, size):
    return me ^ hop if size & (size - 1) == 0 else (me + size - hop) % size


def rows_kernel(table, block, first, last, n_row, *refs):
    refs = list(refs)
    take = lambda count: [refs.pop(0) for _ in range(count)]
    x_ref, f_ref, ft_ref, bend_ref, shrink_ref = take(5)
    shares = take(n_row) if first else None
    if not first:
        wide_in, scaled_in, total_in = take(3)
    (rows_out,) = take(1)
    if first and not last:
        wide_out, scaled_out = take(2)
    if last:
        parts_out = take(n_row)
    else:
        (total_out,) = take(1)
    if first:
        (piece,) = take(1)
    if last:
        (turned,) = take(1)

    if first:
        me = lax.axis_index("row")
        depth = shares[0].shape[0]
        for hop in range(n_row):
            start = pl.multiple_of(source(me, hop, n_row) * depth, depth)
            piece[pl.ds(start, depth), :] = shares[hop][...]
        whole = piece[...].astype(jnp.float32)
        wide = jnp.transpose(whole).astype(jnp.bfloat16)
        scaled = (whole * shrink_ref[...]).astype(jnp.bfloat16)
        if not last:
            wide_out[...] = wide
            scaled_out[...] = scaled
        total = None
    else:
        wide = wide_in[...]
        scaled = scaled_in[...]
        total = total_in[...]

    bend = bend_ref[...]
    origin = pick("gene", table) * block if len(table) > 1 else 0
    step = tile_of(block, 256)
    for at in range(0, block, step):
        start = origin + at
        if len(table) > 1:
            start = pl.multiple_of(start, math.gcd(block, step))
        factors = f_ref[pl.ds(start, step), :]
        pred = jnp.dot(factors, wide, preferred_element_type=jnp.float32)
        resid = x_ref[pl.ds(start, step), :].astype(jnp.float32) - pred
        inside = jnp.maximum(1.0 - resid * resid * bend, 0.0)
        infl = (resid * (inside * inside)).astype(jnp.bfloat16)
        rows_out[at : at + step, :] = jnp.dot(infl, scaled, preferred_element_type=jnp.float32).astype(rows_out.dtype)
        cols = jnp.dot(ft_ref[:, pl.ds(start, step)], infl, preferred_element_type=jnp.float32)
        total = cols if total is None else total + cols
    if not last:
        total_out[...] = total
        return
    turned[...] = jnp.transpose(total) * shrink_ref[...]
    me = lax.axis_index("row")
    depth = parts_out[0].shape[0]
    for hop in range(n_row):
        start = pl.multiple_of(partner(me, hop, n_row) * depth, depth)
        parts_out[hop][...] = turned[pl.ds(start, depth), :].astype(parts_out[hop].dtype)


def block_rows(table, block, first, last, n_row, kind, fixed, carried):
    genes, rank = fixed[4].shape
    out = [jax.ShapeDtypeStruct((block, rank), kind)]
    if first and not last:
        out += [VMEM((rank, genes), jnp.bfloat16), VMEM((genes, rank), jnp.bfloat16)]
    if last:
        depth = genes // n_row
        out += [jax.ShapeDtypeStruct((depth, rank), jnp.float32 if hop == 0 else jnp.bfloat16) for hop in range(n_row)]
    else:
        out += [VMEM((rank, genes), jnp.float32)]
    scratch = []
    if first:
        scratch.append(VMEM((genes, rank), jnp.bfloat16))
    if last:
        scratch.append(VMEM((genes, rank), jnp.float32))
    ins = pinned(*fixed) + (list(carried) if first else pinned(*carried))
    return pl.pallas_call(
        functools.partial(rows_kernel, table, block, first, last, n_row),
        out_shape=tuple(out),
        in_specs=[IN_VMEM] * len(ins),
        out_specs=(IN_VMEM,) * len(out),
        scratch_shapes=scratch,
        compiler_params=params(),
        cost_estimate=cost(6 * block * genes * rank * 2, block * genes * 4),
        name="block_rows",
    )(*ins)


def swap_row(value, hop, size):
    return lax.ppermute(value, "row", [(me, partner(me, hop, size)) for me in range(size)])


def add_bf(a, b):
    return (a.astype(jnp.float32) + b.astype(jnp.float32)).astype(jnp.bfloat16)


def cell_gradients(n_gene, rows, make):
    block = rows // n_gene
    me = lax.axis_index("gene")
    if n_gene == 1:
        return make((0,), rows, jnp.float32, True, True)
    if n_gene > DIRECT_MOST or block % 128:
        mine = make((0,), rows, jnp.float32, True, True)
        return lax.psum_scatter(mine, "gene", scatter_dimension=0, tiled=True)
    if n_gene == 4:
        is_end = (me == 0) | (me == 3)
        near = make((3, 0, 3, 0), block, jnp.bfloat16, True, False)
        got_a = lax.ppermute(near, "gene", [(0, 1), (1, 0), (2, 3), (3, 2)])
        middle = make((2, 2, 1, 1), block, jnp.bfloat16, False, False)
        got_b = lax.ppermute(middle, "gene", [(1, 2), (2, 1)])
        got_c = lax.ppermute(middle, "gene", [(0, 2), (3, 1)])
        far = make((1, 3, 0, 2), block, jnp.bfloat16, False, False)
        mine = make((0, 1, 2, 3), block, jnp.float32, False, True)
        passed = jnp.where(is_end, far, add_bf(far, got_a))
        got_d = lax.ppermute(passed, "gene", [(0, 1), (3, 2), (1, 3), (2, 0)])
        total = mine + got_b.astype(jnp.float32) + got_c.astype(jnp.float32)
        total = total + jnp.where(is_end, got_a, jnp.zeros_like(got_a)).astype(jnp.float32)
        return total + got_d.astype(jnp.float32)
    got = []
    for hop in [*range(1, n_gene), 0]:
        table = tuple((place + hop) % n_gene for place in range(n_gene))
        mine = make(table, block, jnp.bfloat16 if hop else jnp.float32, hop == 1, hop == 0)
        if hop:
            got.append(lax.ppermute(mine, "gene", [(place, (place + hop) % n_gene) for place in range(n_gene)]))
    for part in got:
        mine = mine + part.astype(jnp.float32)
    return mine


def local(x_slab, cell_factor, row_index, gene_scale, gene_factor, first_moment, second_moment):
    rows_dev, genes_dev = x_slab.shape
    n_gene = lax.axis_size("gene")
    n_row = lax.axis_size("row")
    scale_k = 4.0 / math.sqrt(genes_dev * n_gene)
    factor_bf = gene_factor.astype(jnp.bfloat16)
    shares = [factor_bf] + [swap_row(factor_bf, hop, n_row) for hop in range(1, n_row)]
    fixed = prepare(x_slab, row_index, cell_factor, gene_scale, scale_k)

    state = {"carried": shares, "parts": None}

    def make(table, block, kind, first, last):
        out = block_rows(table, block, first, last, n_row, kind, fixed, state["carried"])
        if last:
            state["parts"] = out[1:]
        elif first:
            state["carried"] = out[1:]
        else:
            state["carried"] = [*state["carried"][:2], out[1]]
        return out[0]

    grad_cells = cell_gradients(n_gene, rows_dev, make)
    parts = state["parts"]
    grad_genes = parts[0]
    for hop in range(1, n_row):
        grad_genes = grad_genes + swap_row(parts[hop], hop, n_row).astype(jnp.float32)
    new_first = beta_one * first_moment + (1.0 - beta_one) * grad_genes
    new_second = beta_two * second_moment + (1.0 - beta_two) * grad_genes * grad_genes
    first_hat = new_first / (1.0 - beta_one**10)
    second_hat = new_second / (1.0 - beta_two**10)
    new_factor = gene_factor - learn_rate * first_hat / (jnp.sqrt(second_hat) + adam_eps)
    return (grad_cells, new_factor, new_first, new_second)


def solution(mesh):
    in_specs = (
        P(("grp", "row"), "gene"),
        P(("grp", "row"), None),
        P(("grp", "row")),
        P(("grp", "gene")),
        P(("grp", "gene", "row"), None),
        P(("grp", "gene", "row"), None),
        P(("grp", "gene", "row"), None),
    )
    out_specs = (
        P(("grp", "row", "gene"), None),
        P(("grp", "gene", "row"), None),
        P(("grp", "gene", "row"), None),
        P(("grp", "gene", "row"), None),
    )
    return jax.shard_map(local, mesh=mesh, in_specs=in_specs, out_specs=out_specs, check_vma=False)
```

time: 102 us -> 33.9 us (0.33)
  waiting for transfers between devices: 53.5 us -> 7.3 us
  between operations: 14.1 us -> 0.76 us
  starting transfers between devices: 0.08 us -> 13.4 us
  matrix products: 12.9 us -> 0 us
  local copies, waits for them, and re-layouts: 11 us -> 2.32 us
  Pallas kernels: 0 us -> 7.25 us
  blocking collectives: 6.64 us -> 0 us
  other arithmetic: 3.82 us -> 2.56 us
    reduce_scatter x2 -> x0, waiting for transfers between devices: 53.5 us -> none  [the longest x1 36.7 us: local(): lax.psum_scatter(-scale_k * grad_rows, 'gene', scatter_dimension=0, tiled...]
    ppermute x0 -> x10, starting transfers between devices: none -> 13.4 us  [the longest x1 5.75 us: cell_gradients(): got_c = lax.ppermute(middle, 'gene', [(0, 2), (3, 1)])]
    dot_general x3 -> x0, matrix products: 12.9 us -> none  [the longest x1 5.96 us: influence(): lax.dot_general(factors, piece, (((1,), (1,)), ((), ())), preferred_eleme...]
    gather x1 -> x0, local copies, waits for them, and re-layouts: 9.15 us -> none  [local(): factors = jnp.take(cell_factor, local_index, axis=0)]
    ppermute x0 -> x10, waiting for transfers between devices: none -> 7.3 us  [the longest x1 4.22 us: cell_gradients(): got_d = lax.ppermute(passed, 'gene', [(0, 1), (3, 2), (1, 3), (2, 0)])]
    pallas_call x0 -> x5, Pallas kernels: none -> 7.25 us  [the longest x4 5.12 us: block_rows(): pl.pallas_call(functools.partial(rows_kernel, table, block, first, last,...]
    all_gather x1 -> x0, blocking collectives: 6.64 us -> none  [local(): gathered = lax.all_gather(factor_bf, 'row', axis=0, tiled=True)]
  transfers between devices with their start and end apart: 2 -> 10, of which waited for: 2 -> 3; matrix products, arithmetic and copies ran while one was open for 6% -> 4% of each run, Pallas kernels for 0% -> 18%
where the time goes in v1:
time: 33.9 us; the launch traced here: 33.6 us
  starting transfers between devices  13.4 us (40%)
  waiting for transfers between devices  7.3 us (22%)
  Pallas kernels  7.25 us (21%)
  other arithmetic  2.56 us (8%)
  local copies, waits for them, and re-layouts  2.32 us (7%)
  between operations  0.76 us (2%)
    ppermute x1, starting transfers between devices, cell_gradients(): got_c = lax.ppermute(middle, 'gene', [(0, 2), (3, 1)])  5.75 us
    pallas_call x4, Pallas kernels, block_rows(): pl.pallas_call(functools.partial(rows_kernel, table, block, first, last,...  5.12 us
    ppermute x6, starting transfers between devices, swap_row(): lax.ppermute(value, 'row', [(me, partner(me, hop, size)) for me in range(...  5.02 us
    ppermute x1, waiting for transfers between devices, cell_gradients(): got_d = lax.ppermute(passed, 'gene', [(0, 1), (3, 2), (1, 3), (2, 0)])  4.22 us
    ppermute x6, waiting for transfers between devices, swap_row(): lax.ppermute(value, 'row', [(me, partner(me, hop, size)) for me in range(...  3.07 us
    pallas_call x1, Pallas kernels, prepare(): pl.pallas_call(functools.partial(prepare_kernel, scale_k), out_shape=(VME...  2.12 us
    ppermute x1, starting transfers between devices, cell_gradients(): got_a = lax.ppermute(near, 'gene', [(0, 1), (1, 0), (2, 3), (3, 2)])  1.86 us
    unnamed x10, local copies, waits for them, and re-layouts  1.63 us
  transfers between devices with their start and end apart: 10, of which 3 were waited for; matrix products, arithmetic and copies ran while one was open for 4% of the time, Pallas kernels for 18%

profile of v1, /device:TPU:0, one launch (start us, length us, event | category | flops | bytes accessed | tf_op | source)
XLA Modules:
  0.0 33.6 jit_solution(14529849337350573013)
XLA Ops:
  0.6 0.9 %convert_element_type.33.refs_5_ = bf16[160,128]{1,0:T(8,128)(2,1)S(1)} convert(f32[160,128]{1,0:T(8,128)} %param.11) | non-fusion elementwise | flops 20480 | bytes 122880 | tf_op jit(solution)/shard_map/convert_element_type | solution.py:241
  1.5 0.5 %collective-permute-start = (bf16[160,128]{1,0:T(8,128)(2,1)S(1)}, bf16[160,128]{1,0:T(8,128)(2,1)S(1)}, u32[]{:S(2)}, u32[]{:S(2)}) collective-permute-start(bf16[160,128]{1,0:T(8,128)(2,1)S(1)} %convert_element_type.33.refs_5_), channel_id=1, source_target_pairs={{0,1},{1,0},{2,3},{3,2},{4,5},{5,4},{6,7},{7,6},{8,9},{9,8},{10,11... | collective-permute-start | bytes 122888 | tf_op jit(solution)/shard_map/ppermute | solution.py:196
  2.0 2.6 %collective-permute-start.1 = (bf16[160,128]{1,0:T(8,128)(2,1)S(1)}, bf16[160,128]{1,0:T(8,128)(2,1)S(1)}, u32[]{:S(2)}, u32[]{:S(2)}) collective-permute-start(bf16[160,128]{1,0:T(8,128)(2,1)S(1)} %convert_element_type.33.refs_5_), channel_id=1, source_target_pairs={{0,2},{1,3},{2,0},{3,1},{4,6},{5,7},{6,4},{7,5},{8,10},{9,11},{10,... | collective-permute-start | bytes 122888 | tf_op jit(solution)/shard_map/ppermute | solution.py:196
  4.5 0.1 collective-permute-start.2
  4.6 0.7 %reshape.15.scale_ref = f32[1,640]{1,0:T(1,128)S(1)} reshape(f32[640]{0:T(1024)} %param.10) | data formatting | bytes 5120 | tf_op jit(solution)/shard_map/reshape | solution.py:84
  5.3 0.9 %copy-done = bf16[512,128]{1,0:T(8,128)(2,1)S(1)} copy-done((bf16[512,128]{1,0:T(8,128)(2,1)S(1)}, bf16[512,128]{1,0:T(8,128)(2,1)}, u32[]{:S(2)}) %copy-start) | copy-done | bytes 131096
  6.2 0.7 %copy-done.1 = s32[3072]{0:T(1024)S(1)} copy-done((s32[3072]{0:T(1024)S(1)}, s32[3072]{0:T(1024)}, u32[]{:S(2)}) %copy-start.1) | copy-done | bytes 12312
  6.9 2.1 %prepare.1 = (bf16[3072,640]{1,0:T(8,128)(2,1)S(1)}, bf16[3072,128]{1,0:T(8,128)(2,1)S(1)}, bf16[128,3072]{1,0:T(8,128)(2,1)S(1)}, f32[1,640]{1,0:T(1,128)S(1)}, f32[640,128]{1,0:T(8,128)S(1)}) custom-call(bf16[3072,640]{1,0:T(8,128)(2,1)} %x_ref.1, s32[1,3072]{1,0:T(1,128)S(1)} %bitcast.1, bf16[512,128]{1,0:T(8,128)(2,1)S(1)} %copy-done, ...), custom_call_target="tpu_custom_call" | custom-call | flops 402653184 | bytes 7864320 | tf_op jit(solution)/shard_map/prepare/pallas_call | solution.py:65
  9.1 1.3 %block_rows.4 = (bf16[768,128]{1,0:T(8,128)(2,1)S(1)}, bf16[128,640]{1,0:T(8,128)(2,1)S(1)}, bf16[640,128]{1,0:T(8,128)(2,1)S(1)}, f32[128,640]{1,0:T(8,128)S(1)}) custom-call(bf16[3072,640]{1,0:T(8,128)(2,1)S(1)} %get-tuple-element.22.refs_0_, bf16[3072,128]{1,0:T(8,128)(2,1)S(1)} %get-tuple-element.23.refs_1_, ...), custom_call_target="tpu_custom_call" | custom-call | flops 754974720 | bytes 1966080 | tf_op jit(solution)/shard_map/block_rows/pallas_call | solution.py:183
  10.4 1.9 %collective-permute-start.5 = (bf16[768,128]{1,0:T(8,128)(2,1)S(1)}, bf16[768,128]{1,0:T(8,128)(2,1)S(1)}, u32[]{:S(2)}, u32[]{:S(2)}) collective-permute-start(bf16[768,128]{1,0:T(8,128)(2,1)S(1)} %get-tuple-element.34), channel_id=1, source_target_pairs={{0,4},{4,0},{8,12},{12,8},{1,5},{5,1},{9,13},{13,9},{2,6},{6,2},{1... | collective-permute-start | bytes 589832 | tf_op jit(solution)/shard_map/ppermute | solution.py:214
  12.3 1.2 %block_rows.5 = (bf16[768,128]{1,0:T(8,128)(2,1)S(1)}, f32[128,640]{1,0:T(8,128)S(1)}) custom-call(bf16[3072,640]{1,0:T(8,128)(2,1)S(1)} %get-tuple-element.22.refs_0_, bf16[3072,128]{1,0:T(8,128)(2,1)S(1)} %get-tuple-element.23.refs_1_, bf16[128,3072]{1,0:T(8,128)(2,1)S(1)} %get-tuple-element.24.refs_2_, f32[1,640]{1,0:T(1,128)S(1)} %get-tuple-element.25.refs_3_, ...), custom_call_target="tpu_custom_call" | custom-call | flops 754974720 | bytes 1966080 | tf_op jit(solution)/shard_map/block_rows/pallas_call | solution.py:183
  13.5 0.7 %collective-permute-start.3 = (bf16[768,128]{1,0:T(8,128)(2,1)S(1)}, bf16[768,128]{1,0:T(8,128)(2,1)S(1)}, u32[]{:S(2)}, u32[]{:S(2)}) collective-permute-start(bf16[768,128]{1,0:T(8,128)(2,1)S(1)} %get-tuple-element.33), channel_id=1, source_target_pairs={{4,8},{8,4},{5,9},{9,5},{6,10},{10,6},{7,11},{11,7},{20,24},{24,20... | collective-permute-start | bytes 589832 | tf_op jit(solution)/shard_map/ppermute | solution.py:216
  14.2 5.8 %collective-permute-start.4 = (bf16[768,128]{1,0:T(8,128)(2,1)S(1)}, bf16[768,128]{1,0:T(8,128)(2,1)S(1)}, u32[]{:S(2)}, u32[]{:S(2)}) collective-permute-start(bf16[768,128]{1,0:T(8,128)(2,1)S(1)} %get-tuple-element.33), channel_id=1, source_target_pairs={{0,8},{12,4},{1,9},{13,5},{2,10},{14,6},{3,11},{15,7},{16,24},{28,... | collective-permute-start | bytes 589832 | tf_op jit(solution)/shard_map/ppermute | solution.py:217
  19.9 1.2 %block_rows.6 = (bf16[768,128]{1,0:T(8,128)(2,1)S(1)}, f32[128,640]{1,0:T(8,128)S(1)}) custom-call(bf16[3072,640]{1,0:T(8,128)(2,1)S(1)} %get-tuple-element.22.refs_0_, bf16[3072,128]{1,0:T(8,128)(2,1)S(1)} %get-tuple-element.23.refs_1_, bf16[128,3072]{1,0:T(8,128)(2,1)S(1)} %get-tuple-element.24.refs_2_, f32[1,640]{1,0:T(1,128)S(1)} %get-tuple-element.25.refs_3_, ...), custom_call_target="tpu_custom_call" | custom-call | flops 754974720 | bytes 1966080 | tf_op jit(solution)/shard_map/block_rows/pallas_call | solution.py:183
  21.2 1.4 %block_rows.7 = (f32[768,128]{1,0:T(8,128)S(1)}, f32[160,128]{1,0:T(8,128)S(1)}, bf16[160,128]{1,0:T(8,128)(2,1)S(1)}, bf16[160,128]{1,0:T(8,128)(2,1)S(1)}, bf16[160,128]{1,0:T(8,128)(2,1)S(1)}) custom-call(bf16[3072,640]{1,0:T(8,128)(2,1)S(1)} %get-tuple-element.22.refs_0_, bf16[3072,128]{1,0:T(8,128)(2,1)S(1)} %get-tuple-element.23.refs_1_, ...), custom_call_target="tpu_custom_call" | custom-call | flops 754974720 | bytes 1966080 | tf_op jit(solution)/shard_map/block_rows/pallas_call | solution.py:183
  22.6 0.1 collective-permute-start.7
  22.6 1.6 %collective-permute-start.8 = (bf16[160,128]{1,0:T(8,128)(2,1)S(1)}, bf16[160,128]{1,0:T(8,128)(2,1)S(1)}, u32[]{:S(2)}, u32[]{:S(2)}) collective-permute-start(bf16[160,128]{1,0:T(8,128)(2,1)S(1)} %get-tuple-element.38), channel_id=1, source_target_pairs={{0,2},{1,3},{2,0},{3,1},{4,6},{5,7},{6,4},{7,5},{8,10},{9,11},{10,... | collective-permute-start | bytes 122888 | tf_op jit(solution)/shard_map/ppermute | solution.py:196
  24.2 0.3 collective-permute-start.9
  24.5 0.1 fusion
  24.7 2.1 %collective-permute-done.8 = bf16[160,128]{1,0:T(8,128)(2,1)S(1)} collective-permute-done((bf16[160,128]{1,0:T(8,128)(2,1)S(1)}, bf16[160,128]{1,0:T(8,128)(2,1)S(1)}, u32[]{:S(2)}, u32[]{:S(2)}) %collective-permute-start.8) | collective-permute-done | bytes 40992 | tf_op jit(solution)/shard_map/ppermute | solution.py:196
  26.7 1.0 %collective-permute-done.9 = bf16[160,128]{1,0:T(8,128)(2,1)S(1)} collective-permute-done((bf16[160,128]{1,0:T(8,128)(2,1)S(1)}, bf16[160,128]{1,0:T(8,128)(2,1)S(1)}, u32[]{:S(2)}, u32[]{:S(2)}) %collective-permute-start.9) | collective-permute-done | bytes 40992 | tf_op jit(solution)/shard_map/ppermute | solution.py:196
  27.7 0.7 %divide_subtract_fusion = (f32[160,128]{1,0:T(8,128)}, f32[160,128]{1,0:T(8,128)}, f32[160,128]{1,0:T(8,128)}) fusion(f32[160,128]{1,0:T(8,128)S(1)} %copy-done.2, bf16[160,128]{1,0:T(8,128)(2,1)S(1)} %collective-permute-done.9, bf16[160,128]{1,0:T(8,128)(2,1)S(1)} %collective-permute-done.8, f32[160,128]{1,0:T(8,128)S(1)} %get-tuple-element.36, ...), kind=kLoop, calls=%fused_computation.5 | loop fusion | flops 368640 | bytes 696320 | tf_op jit(solution)/shard_map/sub | solution.py:266
  28.5 4.2 %collective-permute-done.6 = bf16[768,128]{1,0:T(8,128)(2,1)S(1)} collective-permute-done((bf16[768,128]{1,0:T(8,128)(2,1)S(1)}, bf16[768,128]{1,0:T(8,128)(2,1)S(1)}, u32[]{:S(2)}, u32[]{:S(2)}) %collective-permute-start.6) | collective-permute-done | bytes 196640 | tf_op jit(solution)/shard_map/ppermute | solution.py:221
  32.7 0.9 %convert_add_fusion = f32[768,128]{1,0:T(8,128)} fusion(bf16[768,128]{1,0:T(8,128)(2,1)S(1)} %collective-permute-done.6, bf16[768,128]{1,0:T(8,128)(2,1)S(1)} %collective-permute-done.4, f32[768,128]{1,0:T(8,128)S(1)} %get-tuple-element.32, bf16[768,128]{1,0:T(8,128)(2,1)S(1)} %collective-permute-done.3, bf16[768,128]{1,0:T(8,128)(2,1)S(1)} %collective-permute-done.5, ...), kind=kLoop, calls=%fused_computation | loop fusion | flops 884736 | bytes 1572865 | tf_op jit(solution)/shard_map/add | solution.py:224
  (16 shorter events, 0.1 us)
Async XLA Ops:
  1.5 7.5 %collective-permute-start = (bf16[160,128]{1,0:T(8,128)(2,1)S(1)}, bf16[160,128]{1,0:T(8,128)(2,1)S(1)}, u32[]{:S(2)}, u32[]{:S(2)}) collective-permute-start(bf16[160,128]{1,0:T(8,128)(2,1)S(1)} %convert_element_type.33.refs_5_), channel_id=1, source_target_pairs={{0,1},{1,0},{2,3},{3,2},{4,5},{5,4},{6,7},{7,6},{8,9},{9,8},{10,11... | collective-permute-start | bytes 122888 | tf_op jit(solution)/shard_map/ppermute | solution.py:196
  2.0 7.1 %collective-permute-start.1 = (bf16[160,128]{1,0:T(8,128)(2,1)S(1)}, bf16[160,128]{1,0:T(8,128)(2,1)S(1)}, u32[]{:S(2)}, u32[]{:S(2)}) collective-permute-start(bf16[160,128]{1,0:T(8,128)(2,1)S(1)} %convert_element_type.33.refs_5_), channel_id=1, source_target_pairs={{0,2},{1,3},{2,0},{3,1},{4,6},{5,7},{6,4},{7,5},{8,10},{9,11},{10,... | collective-permute-start | bytes 122888 | tf_op jit(solution)/shard_map/ppermute | solution.py:196
  4.5 4.5 %collective-permute-start.2 = (bf16[160,128]{1,0:T(8,128)(2,1)S(1)}, bf16[160,128]{1,0:T(8,128)(2,1)S(1)}, u32[]{:S(2)}, u32[]{:S(2)}) collective-permute-start(bf16[160,128]{1,0:T(8,128)(2,1)S(1)} %convert_element_type.33.refs_5_), channel_id=1, source_target_pairs={{0,3},{1,2},{2,1},{3,0},{4,7},{5,6},{6,5},{7,4},{8,11},{9,10},{10,... | collective-permute-start | bytes 122888 | tf_op jit(solution)/shard_map/ppermute | solution.py:196
  5.3 0.9 %copy-start = (bf16[512,128]{1,0:T(8,128)(2,1)S(1)}, bf16[512,128]{1,0:T(8,128)(2,1)}, u32[]{:S(2)}) copy-start(bf16[512,128]{1,0:T(8,128)(2,1)} %cell_ref.1) | copy-start | bytes 393220
  6.2 0.7 %copy-start.1 = (s32[3072]{0:T(1024)S(1)}, s32[3072]{0:T(1024)}, u32[]{:S(2)}) copy-start(s32[3072]{0:T(1024)} %param.9) | copy-start | bytes 36868
  10.4 13.8 %collective-permute-start.5 = (bf16[768,128]{1,0:T(8,128)(2,1)S(1)}, bf16[768,128]{1,0:T(8,128)(2,1)S(1)}, u32[]{:S(2)}, u32[]{:S(2)}) collective-permute-start(bf16[768,128]{1,0:T(8,128)(2,1)S(1)} %get-tuple-element.34), channel_id=1, source_target_pairs={{0,4},{4,0},{8,12},{12,8},{1,5},{5,1},{9,13},{13,9},{2,6},{6,2},{1... | collective-permute-start | bytes 589832 | tf_op jit(solution)/shard_map/ppermute | solution.py:214
  13.5 15.0 %collective-permute-start.3 = (bf16[768,128]{1,0:T(8,128)(2,1)S(1)}, bf16[768,128]{1,0:T(8,128)(2,1)S(1)}, u32[]{:S(2)}, u32[]{:S(2)}) collective-permute-start(bf16[768,128]{1,0:T(8,128)(2,1)S(1)} %get-tuple-element.33), channel_id=1, source_target_pairs={{4,8},{8,4},{5,9},{9,5},{6,10},{10,6},{7,11},{11,7},{20,24},{24,20... | collective-permute-start | bytes 589832 | tf_op jit(solution)/shard_map/ppermute | solution.py:216
  14.2 14.3 %collective-permute-start.4 = (bf16[768,128]{1,0:T(8,128)(2,1)S(1)}, bf16[768,128]{1,0:T(8,128)(2,1)S(1)}, u32[]{:S(2)}, u32[]{:S(2)}) collective-permute-start(bf16[768,128]{1,0:T(8,128)(2,1)S(1)} %get-tuple-element.33), channel_id=1, source_target_pairs={{0,8},{12,4},{1,9},{13,5},{2,10},{14,6},{3,11},{15,7},{16,24},{28,... | collective-permute-start | bytes 589832 | tf_op jit(solution)/shard_map/ppermute | solution.py:217
  21.2 6.6 %copy-start.2 = (f32[160,128]{1,0:T(8,128)S(1)}, f32[160,128]{1,0:T(8,128)}, u32[]{:S(2)}) copy-start(f32[160,128]{1,0:T(8,128)} %param.11) | copy-start | bytes 245764
  21.2 6.6 %copy-start.3 = (f32[160,128]{1,0:T(8,128)S(1)}, f32[160,128]{1,0:T(8,128)}, u32[]{:S(2)}) copy-start(f32[160,128]{1,0:T(8,128)} %param.12) | copy-start | bytes 245764
  21.2 6.5 %copy-start.4 = (f32[160,128]{1,0:T(8,128)S(1)}, f32[160,128]{1,0:T(8,128)}, u32[]{:S(2)}) copy-start(f32[160,128]{1,0:T(8,128)} %param.13) | copy-start | bytes 245764
  22.6 2.0 %collective-permute-start.7 = (bf16[160,128]{1,0:T(8,128)(2,1)S(1)}, bf16[160,128]{1,0:T(8,128)(2,1)S(1)}, u32[]{:S(2)}, u32[]{:S(2)}) collective-permute-start(bf16[160,128]{1,0:T(8,128)(2,1)S(1)} %get-tuple-element.37), channel_id=1, source_target_pairs={{0,1},{1,0},{2,3},{3,2},{4,5},{5,4},{6,7},{7,6},{8,9},{9,8},{10,11... | collective-permute-start | bytes 122888 | tf_op jit(solution)/shard_map/ppermute | solution.py:196
  22.6 4.1 %collective-permute-start.8 = (bf16[160,128]{1,0:T(8,128)(2,1)S(1)}, bf16[160,128]{1,0:T(8,128)(2,1)S(1)}, u32[]{:S(2)}, u32[]{:S(2)}) collective-permute-start(bf16[160,128]{1,0:T(8,128)(2,1)S(1)} %get-tuple-element.38), channel_id=1, source_target_pairs={{0,2},{1,3},{2,0},{3,1},{4,6},{5,7},{6,4},{7,5},{8,10},{9,11},{10,... | collective-permute-start | bytes 122888 | tf_op jit(solution)/shard_map/ppermute | solution.py:196
  24.2 3.5 %collective-permute-start.9 = (bf16[160,128]{1,0:T(8,128)(2,1)S(1)}, bf16[160,128]{1,0:T(8,128)(2,1)S(1)}, u32[]{:S(2)}, u32[]{:S(2)}) collective-permute-start(bf16[160,128]{1,0:T(8,128)(2,1)S(1)} %get-tuple-element.39), channel_id=1, source_target_pairs={{0,3},{1,2},{2,1},{3,0},{4,7},{5,6},{6,5},{7,4},{8,11},{9,10},{10,... | collective-permute-start | bytes 122888 | tf_op jit(solution)/shard_map/ppermute | solution.py:196
  24.6 8.1 %collective-permute-start.6 = (bf16[768,128]{1,0:T(8,128)(2,1)S(1)}, bf16[768,128]{1,0:T(8,128)(2,1)S(1)}, u32[]{:S(2)}, u32[]{:S(2)}) collective-permute-start(bf16[768,128]{1,0:T(8,128)(2,1)S(1)} %fusion), channel_id=1, source_target_pairs={{0,4},{12,8},{4,12},{8,0},{1,5},{13,9},{5,13},{9,1},{2,6},{14,10},... | collective-permute-start | bytes 589832 | tf_op jit(solution)/shard_map/ppermute | solution.py:221

commit v2 on v0

v2 whole, which is shorter than its diff:
```python
import functools
import math

import jax
import jax.numpy as jnp
from jax import lax
from jax.experimental import pallas as pl
from jax.experimental.pallas import tpu as pltpu
from jax.sharding import PartitionSpec as P

tukey_c = 4.685
beta_one = 0.9
beta_two = 0.999
learn_rate = 0.02
adam_eps = 1e-08

VMEM = pltpu.VMEM
IN_VMEM = pl.BlockSpec(memory_space=VMEM)
IN_ANY = pl.BlockSpec(memory_space=pl.ANY)


def tile_of(rows, most):
    best = [t for t in range(128, most + 1, 128) if rows % t == 0]
    return best[-1] if best else rows


def params():
    return pltpu.CompilerParams(vmem_limit_bytes=24 * 1024 * 1024)


def cost(flops, moved):
    return pl.CostEstimate(flops=int(flops), bytes_accessed=int(moved), transcendentals=0)


def pinned(*arrays):
    return [pltpu.with_memory_space_constraint(a, VMEM) for a in arrays]


def prepare_kernel(scale_k, x_in, index_in, cell_in, scale_in, x_out, f_out, ft_out, bend_out, shrink_out, index, cell, scale, sems):
    loads = [
        pltpu.make_async_copy(src, dst, sems.at[at])
        for at, (src, dst) in enumerate(((scale_in, scale), (cell_in, cell), (index_in, index), (x_in, x_out)))
    ]
    for load in loads:
        load.start()
    cells, rank = cell.shape
    rows = index.shape[0]
    genes = scale.shape[0]
    loads[0].wait()
    inverse = 1.0 / scale[...].reshape(1, genes)
    bend_out[...] = (inverse * inverse) * (1.0 / (tukey_c * tukey_c))
    shrink_out[...] = jnp.transpose(jnp.broadcast_to(-scale_k * (inverse * inverse), (rank, genes)))
    loads[1].wait()
    table = jnp.transpose(cell[...].astype(jnp.float32)).astype(jnp.bfloat16)
    base = lax.axis_index("row") * cells
    loads[2].wait()
    step = tile_of(rows, 512)
    for at in range(0, rows, step):
        local = index[at : at + step].reshape(1, step) - base
        hot = lax.broadcasted_iota(jnp.int32, (cells, step), 0) == local
        hot = jnp.where(hot, 1.0, 0.0).astype(jnp.bfloat16)
        picked = jnp.dot(table, hot, preferred_element_type=jnp.float32)
        ft_out[:, at : at + step] = picked.astype(jnp.bfloat16)
        f_out[at : at + step, :] = jnp.transpose(picked).astype(jnp.bfloat16)
    loads[3].wait()


def prepare(x_slab, row_index, cell_factor, gene_scale, scale_k):
    rows, genes = x_slab.shape
    cells, rank = cell_factor.shape
    ins = (x_slab, row_index, cell_factor, gene_scale)
    return pl.pallas_call(
        functools.partial(prepare_kernel, scale_k),
        out_shape=(
            VMEM((rows, genes), jnp.bfloat16),
            VMEM((rows, rank), jnp.bfloat16),
            VMEM((rank, rows), jnp.bfloat16),
            VMEM((1, genes), jnp.float32),
            VMEM((genes, rank), jnp.float32),
        ),
        in_specs=[IN_ANY] * 4,
        out_specs=(IN_VMEM,) * 5,
        scratch_shapes=[
            VMEM((rows,), jnp.int32),
            VMEM((cells, rank), jnp.bfloat16),
            VMEM((genes,), jnp.float32),
            pltpu.SemaphoreType.DMA((4,)),
        ],
        compiler_params=params(),
        cost_estimate=cost(2 * rows * cells * rank, 2 * rows * genes * 2),
        name="prepare",
    )(*(pltpu.with_memory_space_constraint(a, pltpu.HBM) for a in ins))


def partner(me, hop, size):
    return me ^ hop if size & (size - 1) == 0 else (me + hop) % size


def source(me, hop, size):
    return me ^ hop if size & (size - 1) == 0 else (me + size - hop) % size


def rows_kernel(n_row, x_ref, f_ref, ft_ref, bend_ref, shrink_ref, *refs):
    shares, rows_out, parts_out = refs[:n_row], refs[n_row], refs[n_row + 1 : 2 * n_row + 1]
    piece, turned = refs[2 * n_row + 1 :]
    me = lax.axis_index("row")
    depth = shares[0].shape[0]
    for hop in range(n_row):
        start = pl.multiple_of(source(me, hop, n_row) * depth, depth)
        piece[pl.ds(start, depth), :] = shares[hop][...]
    whole = piece[...].astype(jnp.float32)
    wide = jnp.transpose(whole).astype(jnp.bfloat16)
    scaled = (whole * shrink_ref[...]).astype(jnp.bfloat16)
    bend = bend_ref[...]
    rows = x_ref.shape[0]
    step = tile_of(rows, 256)
    total = None
    for at in range(0, rows, step):
        here = slice(at, at + step)
        pred = jnp.dot(f_ref[here, :], wide, preferred_element_type=jnp.float32)
        resid = x_ref[here, :].astype(jnp.float32) - pred
        inside = jnp.maximum(1.0 - resid * resid * bend, 0.0)
        infl = (resid * (inside * inside)).astype(jnp.bfloat16)
        rows_out[here, :] = jnp.dot(infl, scaled, preferred_element_type=jnp.float32).astype(rows_out.dtype)
        cols = jnp.dot(ft_ref[:, here], infl, preferred_element_type=jnp.float32)
        total = cols if total is None else total + cols
    turned[...] = jnp.transpose(total) * shrink_ref[...]
    for hop in range(n_row):
        start = pl.multiple_of(partner(me, hop, n_row) * depth, depth)
        parts_out[hop][...] = turned[pl.ds(start, depth), :].astype(parts_out[hop].dtype)


def all_rows(n_row, fixed, shares):
    rows, genes = fixed[0].shape
    depth, rank = shares[0].shape
    out = [jax.ShapeDtypeStruct((rows, rank), jnp.bfloat16)]
    out += [jax.ShapeDtypeStruct((depth, rank), jnp.bfloat16 if hop else jnp.float32) for hop in range(n_row)]
    ins = pinned(*fixed) + list(shares)
    return pl.pallas_call(
        functools.partial(rows_kernel, n_row),
        out_shape=tuple(out),
        in_specs=[IN_VMEM] * len(ins),
        out_specs=(IN_VMEM,) * len(out),
        scratch_shapes=[VMEM((genes, rank), jnp.bfloat16), VMEM((genes, rank), jnp.float32)],
        compiler_params=params(),
        cost_estimate=cost(12 * rows * genes * rank, rows * genes * 4),
        name="all_rows",
    )(*ins)


def swap_row(value, hop, size):
    return lax.ppermute(value, "row", [(me, partner(me, hop, size)) for me in range(size)])


def local(x_slab, cell_factor, row_index, gene_scale, gene_factor, first_moment, second_moment):
    rows_dev, genes_dev = x_slab.shape
    n_gene = lax.axis_size("gene")
    n_row = lax.axis_size("row")
    scale_k = 4.0 / math.sqrt(genes_dev * n_gene)
    factor_bf = gene_factor.astype(jnp.bfloat16)
    shares = [factor_bf] + [swap_row(factor_bf, hop, n_row) for hop in range(1, n_row)]
    fixed = prepare(x_slab, row_index, cell_factor, gene_scale, scale_k)
    rows, *parts = all_rows(n_row, fixed, shares)

    grad_genes = parts[0]
    for hop in range(1, n_row):
        grad_genes = grad_genes + swap_row(parts[hop], hop, n_row).astype(jnp.float32)
    new_first = beta_one * first_moment + (1.0 - beta_one) * grad_genes
    new_second = beta_two * second_moment + (1.0 - beta_two) * grad_genes * grad_genes
    first_hat = new_first / (1.0 - beta_one**10)
    second_hat = new_second / (1.0 - beta_two**10)
    new_factor = gene_factor - learn_rate * first_hat / (jnp.sqrt(second_hat) + adam_eps)

    rank = rows.shape[1]
    rows = rows.reshape(n_gene, rows_dev // n_gene, rank)
    got = lax.all_to_all(rows, "gene", split_axis=0, concat_axis=0)
    grad_cells = got[0].astype(jnp.float32)
    for place in range(1, n_gene):
        grad_cells = grad_cells + got[place].astype(jnp.float32)
    return (grad_cells, new_factor, new_first, new_second)


def solution(mesh):
    in_specs = (
        P(("grp", "row"), "gene"),
        P(("grp", "row"), None),
        P(("grp", "row")),
        P(("grp", "gene")),
        P(("grp", "gene", "row"), None),
        P(("grp", "gene", "row"), None),
        P(("grp", "gene", "row"), None),
    )
    out_specs = (
        P(("grp", "row", "gene"), None),
        P(("grp", "gene", "row"), None),
        P(("grp", "gene", "row"), None),
        P(("grp", "gene", "row"), None),
    )
    return jax.shard_map(local, mesh=mesh, in_specs=in_specs, out_specs=out_specs, check_vma=False)
```

time: 102 us -> 39.5 us (0.39)
  waiting for transfers between devices: 53.5 us -> 18.7 us
  between operations: 14.1 us -> 0.67 us
  matrix products: 12.9 us -> 0 us
  local copies, waits for them, and re-layouts: 11 us -> 0.01 us
  starting transfers between devices: 0.08 us -> 9.78 us
  Pallas kernels: 0 us -> 7.66 us
  blocking collectives: 6.64 us -> 0 us
  other arithmetic: 3.82 us -> 2.47 us
    reduce_scatter x2 -> x0, waiting for transfers between devices: 53.5 us -> none  [the longest x1 36.7 us: local(): lax.psum_scatter(-scale_k * grad_rows, 'gene', scatter_dimension=0, tiled...]
    all_to_all x0 -> x1, waiting for transfers between devices: none -> 14.6 us  [local(): got = lax.all_to_all(rows, 'gene', split_axis=0, concat_axis=0)]
    dot_general x3 -> x0, matrix products: 12.9 us -> none  [the longest x1 5.96 us: influence(): lax.dot_general(factors, piece, (((1,), (1,)), ((), ())), preferred_eleme...]
    gather x1 -> x0, local copies, waits for them, and re-layouts: 9.15 us -> none  [local(): factors = jnp.take(cell_factor, local_index, axis=0)]
    pallas_call x0 -> x2, Pallas kernels: none -> 7.66 us  [the longest x1 5.41 us: all_rows(): pl.pallas_call(functools.partial(rows_kernel, n_row), out_shape=tuple(out...]
    all_gather x1 -> x0, blocking collectives: 6.64 us -> none  [local(): gathered = lax.all_gather(factor_bf, 'row', axis=0, tiled=True)]
    ppermute x0 -> x6, starting transfers between devices: none -> 4.92 us  [swap_row(): lax.ppermute(value, 'row', [(me, partner(me, hop, size)) for me in range(...]
    all_to_all x0 -> x1, starting transfers between devices: none -> 4.87 us  [local(): got = lax.all_to_all(rows, 'gene', split_axis=0, concat_axis=0)]
  transfers between devices with their start and end apart: 2 -> 7, of which waited for: 2 -> 4; matrix products, arithmetic and copies ran while one was open for 6% -> 2% of each run, Pallas kernels for 0% -> 6%
where the time goes in v2:
time: 39.5 us; the launch traced here: 39.3 us
  waiting for transfers between devices  18.7 us (47%)
  starting transfers between devices  9.78 us (25%)
  Pallas kernels  7.66 us (19%)
  other arithmetic  2.47 us (6%)
  between operations  0.67 us (2%)
    all_to_all x1, waiting for transfers between devices, local(): got = lax.all_to_all(rows, 'gene', split_axis=0, concat_axis=0)  14.6 us
    pallas_call x1, Pallas kernels, all_rows(): pl.pallas_call(functools.partial(rows_kernel, n_row), out_shape=tuple(out...  5.41 us
    ppermute x6, starting transfers between devices, swap_row(): lax.ppermute(value, 'row', [(me, partner(me, hop, size)) for me in range(...  4.92 us
    all_to_all x1, starting transfers between devices, local(): got = lax.all_to_all(rows, 'gene', split_axis=0, concat_axis=0)  4.87 us
    ppermute x6, waiting for transfers between devices, swap_row(): lax.ppermute(value, 'row', [(me, partner(me, hop, size)) for me in range(...  4.04 us
    pallas_call x1, Pallas kernels, prepare(): pl.pallas_call(functools.partial(prepare_kernel, scale_k), out_shape=(VME...  2.26 us
    convert_element_type x1, other arithmetic, local(): factor_bf = gene_factor.astype(jnp.bfloat16)  0.9 us
    add x1, other arithmetic, local(): grad_cells = grad_cells + got[place].astype(jnp.float32)  0.84 us
  transfers between devices with their start and end apart: 7, of which 4 were waited for; matrix products, arithmetic and copies ran while one was open for 2% of the time, Pallas kernels for 6%

profile of v2, /device:TPU:0, one launch (start us, length us, event | category | flops | bytes accessed | tf_op | source)
XLA Modules:
  0.0 39.3 jit_solution(538262334438846342)
XLA Ops:
  0.6 0.9 %convert_element_type.28.refs_0_ = bf16[160,128]{1,0:T(8,128)(2,1)S(1)} convert(f32[160,128]{1,0:T(8,128)} %param.11) | non-fusion elementwise | flops 20480 | bytes 122880 | tf_op jit(solution)/shard_map/convert_element_type | solution.py:160
  1.5 2.4 %collective-permute-start.2 = (bf16[160,128]{1,0:T(8,128)(2,1)S(1)}, bf16[160,128]{1,0:T(8,128)(2,1)S(1)}, u32[]{:S(2)}, u32[]{:S(2)}) collective-permute-start(bf16[160,128]{1,0:T(8,128)(2,1)S(1)} %convert_element_type.28.refs_0_), channel_id=1, source_target_pairs={{0,3},{1,2},{2,1},{3,0},{4,7},{5,6},{6,5},{7,4},{8,11},{9,10},{10,... | collective-permute-start | bytes 122888 | tf_op jit(solution)/shard_map/ppermute | solution.py:152
  3.9 0.6 %collective-permute-start.1 = (bf16[160,128]{1,0:T(8,128)(2,1)S(1)}, bf16[160,128]{1,0:T(8,128)(2,1)S(1)}, u32[]{:S(2)}, u32[]{:S(2)}) collective-permute-start(bf16[160,128]{1,0:T(8,128)(2,1)S(1)} %convert_element_type.28.refs_0_), channel_id=1, source_target_pairs={{0,2},{1,3},{2,0},{3,1},{4,6},{5,7},{6,4},{7,5},{8,10},{9,11},{10,... | collective-permute-start | bytes 122888 | tf_op jit(solution)/shard_map/ppermute | solution.py:152
  4.5 0.0 collective-permute-start
  4.6 2.3 %prepare.1 = (bf16[3072,640]{1,0:T(8,128)(2,1)S(1)}, bf16[3072,128]{1,0:T(8,128)(2,1)S(1)}, bf16[128,3072]{1,0:T(8,128)(2,1)S(1)}, f32[1,640]{1,0:T(1,128)S(1)}, f32[640,128]{1,0:T(8,128)S(1)}) custom-call(bf16[3072,640]{1,0:T(8,128)(2,1)} %x_in.1, s32[3072]{0:T(1024)} %index_in.1, bf16[512,128]{1,0:T(8,128)(2,1)} %cell_in.1, f32[640]{0:T(1024)} %scale_in.1), custom_call_target="tpu_custom_call" | custom-call | flops 402653184 | bytes 7864320 | tf_op jit(solution)/shard_map/prepare/pallas_call | solution.py:72
  6.8 0.0 collective-permute-done.2.refs_3_
  6.9 1.2 %collective-permute-done.1.refs_2_ = bf16[160,128]{1,0:T(8,128)(2,1)S(1)} collective-permute-done((bf16[160,128]{1,0:T(8,128)(2,1)S(1)}, bf16[160,128]{1,0:T(8,128)(2,1)S(1)}, u32[]{:S(2)}, u32[]{:S(2)}) %collective-permute-start.1) | collective-permute-done | bytes 40992 | tf_op jit(solution)/shard_map/ppermute | solution.py:152
  8.1 0.0 collective-permute-done.refs_1_
  8.1 0.0 copy-start
  8.1 0.0 copy-start.1
  8.1 5.4 %all_rows.1 = (bf16[3072,128]{1,0:T(8,128)(2,1)}, f32[160,128]{1,0:T(8,128)S(1)}, bf16[160,128]{1,0:T(8,128)(2,1)S(1)}, bf16[160,128]{1,0:T(8,128)(2,1)S(1)}, bf16[160,128]{1,0:T(8,128)(2,1)S(1)}) custom-call(bf16[3072,640]{1,0:T(8,128)(2,1)S(1)} %get-tuple-element.14.x_ref, bf16[3072,128]{1,0:T(8,128)(2,1)S(1)} %get-tuple-element.15.f_ref, ...), custom_call_target="tpu_custom_call" | custom-call | flops 3019898880 | bytes 7864320 | tf_op jit(solution)/shard_map/all_rows/pallas_call | solution.py:139
  13.5 4.9 %all-to-all-start = ((bf16[4,768,128]{2,1,0:T(8,128)(2,1)}), bf16[4,768,128]{2,1,0:T(8,128)(2,1)S(1)}, u32[]{:S(2)}, u32[]{:S(2)}) async-start(bf16[4,768,128]{2,1,0:T(8,128)(2,1)} %bitcast), calls=%async_computation | async-start | bytes 1572864 | tf_op jit(solution)/shard_map/all_to_all | solution.py:176
  18.3 0.0 collective-permute-start.3
  18.3 1.2 %collective-permute-start.4 = (bf16[160,128]{1,0:T(8,128)(2,1)S(1)}, bf16[160,128]{1,0:T(8,128)(2,1)S(1)}, u32[]{:S(2)}, u32[]{:S(2)}) collective-permute-start(bf16[160,128]{1,0:T(8,128)(2,1)S(1)} %get-tuple-element.22), channel_id=1, source_target_pairs={{0,2},{1,3},{2,0},{3,1},{4,6},{5,7},{6,4},{7,5},{8,10},{9,11},{10,... | collective-permute-start | bytes 122888 | tf_op jit(solution)/shard_map/ppermute | solution.py:152
  19.5 0.7 %collective-permute-start.5 = (bf16[160,128]{1,0:T(8,128)(2,1)S(1)}, bf16[160,128]{1,0:T(8,128)(2,1)S(1)}, u32[]{:S(2)}, u32[]{:S(2)}) collective-permute-start(bf16[160,128]{1,0:T(8,128)(2,1)S(1)} %get-tuple-element.23), channel_id=1, source_target_pairs={{0,3},{1,2},{2,1},{3,0},{4,7},{5,6},{6,5},{7,4},{8,11},{9,10},{10,... | collective-permute-start | bytes 122888 | tf_op jit(solution)/shard_map/ppermute | solution.py:152
  20.2 0.0 collective-permute-done.3
  20.2 2.1 %collective-permute-done.4 = bf16[160,128]{1,0:T(8,128)(2,1)S(1)} collective-permute-done((bf16[160,128]{1,0:T(8,128)(2,1)S(1)}, bf16[160,128]{1,0:T(8,128)(2,1)S(1)}, u32[]{:S(2)}, u32[]{:S(2)}) %collective-permute-start.4) | collective-permute-done | bytes 40992 | tf_op jit(solution)/shard_map/ppermute | solution.py:152
  22.3 0.7 %collective-permute-done.5 = bf16[160,128]{1,0:T(8,128)(2,1)S(1)} collective-permute-done((bf16[160,128]{1,0:T(8,128)(2,1)S(1)}, bf16[160,128]{1,0:T(8,128)(2,1)S(1)}, u32[]{:S(2)}, u32[]{:S(2)}) %collective-permute-start.5) | collective-permute-done | bytes 40992 | tf_op jit(solution)/shard_map/ppermute | solution.py:152
  23.0 0.0 copy-done
  23.1 0.0 copy-done.1
  23.1 0.0 copy-done.2
  23.1 0.7 %divide_subtract_fusion = (f32[160,128]{1,0:T(8,128)}, f32[160,128]{1,0:T(8,128)}, f32[160,128]{1,0:T(8,128)}) fusion(f32[160,128]{1,0:T(8,128)S(1)} %copy-done, bf16[160,128]{1,0:T(8,128)(2,1)S(1)} %collective-permute-done.5, bf16[160,128]{1,0:T(8,128)(2,1)S(1)} %collective-permute-done.4, f32[160,128]{1,0:T(8,128)S(1)} %get-tuple-element.20, ...), kind=kLoop, calls=%fused_computation.3 | loop fusion | flops 368640 | bytes 696320 | tf_op jit(solution)/shard_map/sub | solution.py:172
  23.8 14.6 %all-to-all-done = bf16[4,768,128]{2,1,0:T(8,128)(2,1)S(1)} async-done(((bf16[4,768,128]{2,1,0:T(8,128)(2,1)}), bf16[4,768,128]{2,1,0:T(8,128)(2,1)S(1)}, u32[]{:S(2)}, u32[]{:S(2)}) %all-to-all-start) | async-done | bytes 786464 | tf_op jit(solution)/shard_map/all_to_all | solution.py:176
  38.4 0.8 %add_bitcast_fusion = f32[768,128]{1,0:T(8,128)} fusion(bf16[4,768,128]{2,1,0:T(8,128)(2,1)S(1)} %all-to-all-done), kind=kLoop, calls=%fused_computation | loop fusion | flops 688128 | bytes 1179648 | tf_op jit(solution)/shard_map/add | solution.py:179
  (1 shorter events, 0.0 us)
Async XLA Ops:
  1.5 5.3 %collective-permute-start.2 = (bf16[160,128]{1,0:T(8,128)(2,1)S(1)}, bf16[160,128]{1,0:T(8,128)(2,1)S(1)}, u32[]{:S(2)}, u32[]{:S(2)}) collective-permute-start(bf16[160,128]{1,0:T(8,128)(2,1)S(1)} %convert_element_type.28.refs_0_), channel_id=1, source_target_pairs={{0,3},{1,2},{2,1},{3,0},{4,7},{5,6},{6,5},{7,4},{8,11},{9,10},{10,... | collective-permute-start | bytes 122888 | tf_op jit(solution)/shard_map/ppermute | solution.py:152
  3.9 4.1 %collective-permute-start.1 = (bf16[160,128]{1,0:T(8,128)(2,1)S(1)}, bf16[160,128]{1,0:T(8,128)(2,1)S(1)}, u32[]{:S(2)}, u32[]{:S(2)}) collective-permute-start(bf16[160,128]{1,0:T(8,128)(2,1)S(1)} %convert_element_type.28.refs_0_), channel_id=1, source_target_pairs={{0,2},{1,3},{2,0},{3,1},{4,6},{5,7},{6,4},{7,5},{8,10},{9,11},{10,... | collective-permute-start | bytes 122888 | tf_op jit(solution)/shard_map/ppermute | solution.py:152
  4.5 3.5 %collective-permute-start = (bf16[160,128]{1,0:T(8,128)(2,1)S(1)}, bf16[160,128]{1,0:T(8,128)(2,1)S(1)}, u32[]{:S(2)}, u32[]{:S(2)}) collective-permute-start(bf16[160,128]{1,0:T(8,128)(2,1)S(1)} %convert_element_type.28.refs_0_), channel_id=1, source_target_pairs={{0,1},{1,0},{2,3},{3,2},{4,5},{5,4},{6,7},{7,6},{8,9},{9,8},{10,11... | collective-permute-start | bytes 122888 | tf_op jit(solution)/shard_map/ppermute | solution.py:152
  8.1 15.0 %copy-start = (f32[160,128]{1,0:T(8,128)S(1)}, f32[160,128]{1,0:T(8,128)}, u32[]{:S(2)}) copy-start(f32[160,128]{1,0:T(8,128)} %param.11) | copy-start | bytes 245764
  8.1 15.0 %copy-start.1 = (f32[160,128]{1,0:T(8,128)S(1)}, f32[160,128]{1,0:T(8,128)}, u32[]{:S(2)}) copy-start(f32[160,128]{1,0:T(8,128)} %param.12) | copy-start | bytes 245764
  8.1 15.0 %copy-start.2 = (f32[160,128]{1,0:T(8,128)S(1)}, f32[160,128]{1,0:T(8,128)}, u32[]{:S(2)}) copy-start(f32[160,128]{1,0:T(8,128)} %param.13) | copy-start | bytes 245764
  13.5 25.0 %all-to-all-start = ((bf16[4,768,128]{2,1,0:T(8,128)(2,1)}), bf16[4,768,128]{2,1,0:T(8,128)(2,1)S(1)}, u32[]{:S(2)}, u32[]{:S(2)}) async-start(bf16[4,768,128]{2,1,0:T(8,128)(2,1)} %bitcast), calls=%async_computation | async-start | bytes 1572864 | tf_op jit(solution)/shard_map/all_to_all | solution.py:176
  18.3 1.9 %collective-permute-start.3 = (bf16[160,128]{1,0:T(8,128)(2,1)S(1)}, bf16[160,128]{1,0:T(8,128)(2,1)S(1)}, u32[]{:S(2)}, u32[]{:S(2)}) collective-permute-start(bf16[160,128]{1,0:T(8,128)(2,1)S(1)} %get-tuple-element.21), channel_id=1, source_target_pairs={{0,1},{1,0},{2,3},{3,2},{4,5},{5,4},{6,7},{7,6},{8,9},{9,8},{10,11... | collective-permute-start | bytes 122888 | tf_op jit(solution)/shard_map/ppermute | solution.py:152
  18.3 4.0 %collective-permute-start.4 = (bf16[160,128]{1,0:T(8,128)(2,1)S(1)}, bf16[160,128]{1,0:T(8,128)(2,1)S(1)}, u32[]{:S(2)}, u32[]{:S(2)}) collective-permute-start(bf16[160,128]{1,0:T(8,128)(2,1)S(1)} %get-tuple-element.22), channel_id=1, source_target_pairs={{0,2},{1,3},{2,0},{3,1},{4,6},{5,7},{6,4},{7,5},{8,10},{9,11},{10,... | collective-permute-start | bytes 122888 | tf_op jit(solution)/shard_map/ppermute | solution.py:152
  19.5 3.5 %collective-permute-start.5 = (bf16[160,128]{1,0:T(8,128)(2,1)S(1)}, bf16[160,128]{1,0:T(8,128)(2,1)S(1)}, u32[]{:S(2)}, u32[]{:S(2)}) collective-permute-start(bf16[160,128]{1,0:T(8,128)(2,1)S(1)} %get-tuple-element.23), channel_id=1, source_target_pairs={{0,3},{1,2},{2,1},{3,0},{4,7},{5,6},{6,5},{7,4},{8,11},{9,10},{10,... | collective-permute-start | bytes 122888 | tf_op jit(solution)/shard_map/ppermute | solution.py:152

commit v3 on v2

--- a/solution.py
+++ b/solution.py
@@ -14,6 +14,7 @@
 learn_rate = 0.02
 adam_eps = 1e-08
 
+PLAN_MOST = 8
 VMEM = pltpu.VMEM
 IN_VMEM = pl.BlockSpec(memory_space=VMEM)
 IN_ANY = pl.BlockSpec(memory_space=pl.ANY)
@@ -92,6 +93,14 @@
     )(*(pltpu.with_memory_space_constraint(a, pltpu.HBM) for a in ins))
 
 
+def pick(axis, table):
+    me = lax.axis_index(axis)
+    value = jnp.int32(table[0])
+    for place, entry in enumerate(table[1:], 1):
+        value = jnp.where(me == place, jnp.int32(entry), value)
+    return value
+
+
 def partner(me, hop, size):
     return me ^ hop if size & (size - 1) == 0 else (me + hop) % size
 
@@ -100,67 +109,140 @@
     return me ^ hop if size & (size - 1) == 0 else (me + size - hop) % size
 
 
-def rows_kernel(n_row, x_ref, f_ref, ft_ref, bend_ref, shrink_ref, *refs):
-    shares, rows_out, parts_out = refs[:n_row], refs[n_row], refs[n_row + 1 : 2 * n_row + 1]
-    piece, turned = refs[2 * n_row + 1 :]
+def rows_kernel(tables, block, first, last, n_row, *refs):
+    refs = list(refs)
+    take = lambda count: [refs.pop(0) for _ in range(count)]
+    x_ref, f_ref, ft_ref, bend_ref, shrink_ref = take(5)
+    shares = take(n_row) if first else None
+    carried_in = None if first else take(3)
+    rows_out = take(len(tables))
+    carried_out = None if last else take(3)
+    parts_out = take(n_row) if last else None
     me = lax.axis_index("row")
-    depth = shares[0].shape[0]
-    for hop in range(n_row):
-        start = pl.multiple_of(source(me, hop, n_row) * depth, depth)
-        piece[pl.ds(start, depth), :] = shares[hop][...]
-    whole = piece[...].astype(jnp.float32)
-    wide = jnp.transpose(whole).astype(jnp.bfloat16)
-    scaled = (whole * shrink_ref[...]).astype(jnp.bfloat16)
+
+    if first:
+        (piece,) = take(1)
+        depth = shares[0].shape[0]
+        for hop in range(n_row):
+            start = pl.multiple_of(source(me, hop, n_row) * depth, depth)
+            piece[pl.ds(start, depth), :] = shares[hop][...]
+        whole = piece[...].astype(jnp.float32)
+        wide = jnp.transpose(whole).astype(jnp.bfloat16)
+        scaled = (whole * shrink_ref[...]).astype(jnp.bfloat16)
+        total = None
+    else:
+        wide, scaled, total = (ref[...] for ref in carried_in)
+
     bend = bend_ref[...]
-    rows = x_ref.shape[0]
-    step = tile_of(rows, 256)
-    total = None
-    for at in range(0, rows, step):
-        here = slice(at, at + step)
-        pred = jnp.dot(f_ref[here, :], wide, preferred_element_type=jnp.float32)
-        resid = x_ref[here, :].astype(jnp.float32) - pred
-        inside = jnp.maximum(1.0 - resid * resid * bend, 0.0)
-        infl = (resid * (inside * inside)).astype(jnp.bfloat16)
-        rows_out[here, :] = jnp.dot(infl, scaled, preferred_element_type=jnp.float32).astype(rows_out.dtype)
-        cols = jnp.dot(ft_ref[:, here], infl, preferred_element_type=jnp.float32)
-        total = cols if total is None else total + cols
+    step = tile_of(block, 256)
+    for table, out in zip(tables, rows_out):
+        origin = pick("gene", table) * block if len(table) > 1 else 0
+        for at in range(0, block, step):
+            start = origin + at
+            if len(table) > 1:
+                start = pl.multiple_of(start, math.gcd(block, step))
+            here = pl.ds(start, step)
+            pred = jnp.dot(f_ref[here, :], wide, preferred_element_type=jnp.float32)
+            resid = x_ref[here, :].astype(jnp.float32) - pred
+            inside = jnp.maximum(1.0 - resid * resid * bend, 0.0)
+            infl = (resid * (inside * inside)).astype(jnp.bfloat16)
+            out[at : at + step, :] = jnp.dot(infl, scaled, preferred_element_type=jnp.float32).astype(out.dtype)
+            cols = jnp.dot(ft_ref[:, here], infl, preferred_element_type=jnp.float32)
+            total = cols if total is None else total + cols
+    if not last:
+        for ref, value in zip(carried_out, (wide, scaled, total)):
+            ref[...] = value
+        return
+    (turned,) = take(1)
     turned[...] = jnp.transpose(total) * shrink_ref[...]
+    depth = parts_out[0].shape[0]
     for hop in range(n_row):
         start = pl.multiple_of(partner(me, hop, n_row) * depth, depth)
         parts_out[hop][...] = turned[pl.ds(start, depth), :].astype(parts_out[hop].dtype)
 
 
-def all_rows(n_row, fixed, shares):
-    rows, genes = fixed[0].shape
-    depth, rank = shares[0].shape
-    out = [jax.ShapeDtypeStruct((rows, rank), jnp.bfloat16)]
-    out += [jax.ShapeDtypeStruct((depth, rank), jnp.bfloat16 if hop else jnp.float32) for hop in range(n_row)]
-    ins = pinned(*fixed) + list(shares)
-    return pl.pallas_call(
-        functools.partial(rows_kernel, n_row),
+def block_rows(tables, kinds, block, first, last, n_row, fixed, carried):
+    genes, rank = fixed[4].shape
+    out = [jax.ShapeDtypeStruct((block, rank), kind) for kind in kinds]
+    if last:
+        out += [jax.ShapeDtypeStruct((genes // n_row, rank), jnp.bfloat16 if hop else jnp.float32) for hop in range(n_row)]
+    else:
+        out += [VMEM((rank, genes), jnp.bfloat16), VMEM((genes, rank), jnp.bfloat16), VMEM((rank, genes), jnp.float32)]
+    scratch = [VMEM((genes, rank), jnp.bfloat16)] if first else []
+    if last:
+        scratch.append(VMEM((genes, rank), jnp.float32))
+    ins = pinned(*fixed) + (list(carried) if first else pinned(*carried))
+    work = len(tables) * block * genes
+    out = pl.pallas_call(
+        functools.partial(rows_kernel, tables, block, first, last, n_row),
         out_shape=tuple(out),
         in_specs=[IN_VMEM] * len(ins),
         out_specs=(IN_VMEM,) * len(out),
-        scratch_shapes=[VMEM((genes, rank), jnp.bfloat16), VMEM((genes, rank), jnp.float32)],
+        scratch_shapes=scratch,
         compiler_params=params(),
-        cost_estimate=cost(12 * rows * genes * rank, rows * genes * 4),
-        name="all_rows",
+        cost_estimate=cost(12 * work * rank, work * 4),
+        name="block_rows",
     )(*ins)
+    return out[: len(tables)], out[len(tables) :]
 
 
 def swap_row(value, hop, size):
     return lax.ppermute(value, "row", [(me, partner(me, hop, size)) for me in range(size)])
+
+
+def plan_of(size):
+    if size == 4:
+        return [((1, 2, 3, 0), (3, 2, 1, 0)), ((2, 0, 3, 1), (2, 0, 3, 1)), ((1, 3, 0, 2), (1, 3, 0, 2))]
+    hops = [tuple((place + hop) % size for place in range(size)) for hop in range(1, size)]
+    return [(hop, hop) for hop in hops]
+
+
+def received(step):
+    targets, blocks = step
+    return [blocks[targets.index(place)] for place in range(len(targets))]
+
+
+def chosen(value, flags):
+    if all(flags):
+        return value
+    return jnp.where(pick("gene", flags) == 1, value, jnp.zeros_like(value))
+
+
+def exchange(steps, blocks, mine):
+    size = len(steps[0][0])
+    got = []
+    for at, (step, block) in enumerate(zip(steps, blocks)):
+        for earlier, value in zip(steps[:at], got):
+            flags = [int(came == sent and came != me) for me, (came, sent) in enumerate(zip(received(earlier), step[1]))]
+            if any(flags):
+                block = (block.astype(jnp.float32) + chosen(value, flags).astype(jnp.float32)).astype(jnp.bfloat16)
+        got.append(lax.ppermute(block, "gene", list(enumerate(step[0]))))
+    for step, value in zip(steps, got):
+        flags = [int(came == me) for me, came in enumerate(received(step))]
+        mine = mine + chosen(value, flags).astype(jnp.float32)
+    return mine
 
 
 def local(x_slab, cell_factor, row_index, gene_scale, gene_factor, first_moment, second_moment):
     rows_dev, genes_dev = x_slab.shape
     n_gene = lax.axis_size("gene")
     n_row = lax.axis_size("row")
+    block = rows_dev // n_gene
     scale_k = 4.0 / math.sqrt(genes_dev * n_gene)
     factor_bf = gene_factor.astype(jnp.bfloat16)
     shares = [factor_bf] + [swap_row(factor_bf, hop, n_row) for hop in range(1, n_row)]
     fixed = prepare(x_slab, row_index, cell_factor, gene_scale, scale_k)
-    rows, *parts = all_rows(n_row, fixed, shares)
+
+    if 1 < n_gene <= PLAN_MOST and block % 128 == 0:
+        steps = plan_of(n_gene)
+        tables = [step[1] for step in steps] + [tuple(range(n_gene))]
+        kinds = [jnp.bfloat16] * len(steps) + [jnp.float32]
+        near, carried = block_rows(tables[:1], kinds[:1], block, True, False, n_row, fixed, shares)
+        others, parts = block_rows(tables[1:], kinds[1:], block, False, True, n_row, fixed, carried)
+        grad_cells = exchange(steps, [*near, *others[:-1]], others[-1])
+    else:
+        (rows,), parts = block_rows([(0,)], [jnp.float32], rows_dev, True, True, n_row, fixed, shares)
+        grad_cells = lax.psum_scatter(rows, "gene", scatter_dimension=0, tiled=True)
 
     grad_genes = parts[0]
     for hop in range(1, n_row):
@@ -170,13 +252,6 @@
     first_hat = new_first / (1.0 - beta_one**10)
     second_hat = new_second / (1.0 - beta_two**10)
     new_factor = gene_factor - learn_rate * first_hat / (jnp.sqrt(second_hat) + adam_eps)
-
-    rank = rows.shape[1]
-    rows = rows.reshape(n_gene, rows_dev // n_gene, rank)
-    got = lax.all_to_all(rows, "gene", split_axis=0, concat_axis=0)
-    grad_cells = got[0].astype(jnp.float32)
-    for place in range(1, n_gene):
-        grad_cells = grad_cells + got[place].astype(jnp.float32)
     return (grad_cells, new_factor, new_first, new_second)
 
 

time: 39.5 us -> 30.9 us (0.78)
  waiting for transfers between devices: 18.7 us -> 11.7 us
  starting transfers between devices: 9.78 us -> 8.72 us
  Pallas kernels: 7.66 us -> 7.02 us
    all_to_all x1 -> x0, waiting for transfers between devices: 14.6 us -> none  [local(): got = lax.all_to_all(rows, 'gene', split_axis=0, concat_axis=0)]
    ppermute x0 -> x3, waiting for transfers between devices: none -> 10.5 us  [exchange(): got.append(lax.ppermute(block, 'gene', list(enumerate(step[0]))))]
    all_to_all x1 -> x0, starting transfers between devices: 4.87 us -> none  [local(): got = lax.all_to_all(rows, 'gene', split_axis=0, concat_axis=0)]
    ppermute x0 -> x3, starting transfers between devices: none -> 3.7 us  [exchange(): got.append(lax.ppermute(block, 'gene', list(enumerate(step[0]))))]
    ppermute x6, waiting for transfers between devices: 4.04 us -> 1.17 us  [swap_row(): lax.ppermute(value, 'row', [(me, partner(me, hop, size)) for me in range(...]
    pallas_call x1 -> x2, Pallas kernels: 5.41 us -> 4.76 us  [block_rows(): pl.pallas_call(functools.partial(rows_kernel, tables, block, first, last,...]
  transfers between devices with their start and end apart: 7 -> 9, of which waited for: 4 -> 4; matrix products, arithmetic and copies ran while one was open for 2% -> 3% of each run, Pallas kernels for 6% -> 19%
where the time goes in v3:
time: 30.9 us; the launch traced here: 30.7 us
  waiting for transfers between devices  11.7 us (38%)
  starting transfers between devices  8.72 us (28%)
  Pallas kernels  7.02 us (23%)
  other arithmetic  2.59 us (8%)
  between operations  0.71 us (2%)
    ppermute x3, waiting for transfers between devices, exchange(): got.append(lax.ppermute(block, 'gene', list(enumerate(step[0]))))  10.5 us
    ppermute x6, starting transfers between devices, swap_row(): lax.ppermute(value, 'row', [(me, partner(me, hop, size)) for me in range(...  5.02 us
    pallas_call x2, Pallas kernels, block_rows(): pl.pallas_call(functools.partial(rows_kernel, tables, block, first, last,...  4.76 us
    ppermute x3, starting transfers between devices, exchange(): got.append(lax.ppermute(block, 'gene', list(enumerate(step[0]))))  3.7 us
    pallas_call x1, Pallas kernels, prepare(): pl.pallas_call(functools.partial(prepare_kernel, scale_k), out_shape=(VME...  2.26 us
    ppermute x6, waiting for transfers between devices, swap_row(): lax.ppermute(value, 'row', [(me, partner(me, hop, size)) for me in range(...  1.17 us
    convert_element_type x1, other arithmetic, local(): factor_bf = gene_factor.astype(jnp.bfloat16)  0.9 us
    add x1, other arithmetic, exchange(): mine = mine + chosen(value, flags).astype(jnp.float32)  0.84 us
  transfers between devices with their start and end apart: 9, of which 4 were waited for; matrix products, arithmetic and copies ran while one was open for 3% of the time, Pallas kernels for 19%

profile of v3, /device:TPU:0, one launch (start us, length us, event | category | flops | bytes accessed | tf_op | source)
XLA Modules:
  0.0 30.7 jit_solution(5522757629032689436)
XLA Ops:
  0.6 0.9 %convert_element_type.39.refs_5_ = bf16[160,128]{1,0:T(8,128)(2,1)S(1)} convert(f32[160,128]{1,0:T(8,128)} %param.11) | non-fusion elementwise | flops 20480 | bytes 122880 | tf_op jit(solution)/shard_map/convert_element_type | solution.py:232
  1.5 0.5 %collective-permute-start = (bf16[160,128]{1,0:T(8,128)(2,1)S(1)}, bf16[160,128]{1,0:T(8,128)(2,1)S(1)}, u32[]{:S(2)}, u32[]{:S(2)}) collective-permute-start(bf16[160,128]{1,0:T(8,128)(2,1)S(1)} %convert_element_type.39.refs_5_), channel_id=1, source_target_pairs={{0,1},{1,0},{2,3},{3,2},{4,5},{5,4},{6,7},{7,6},{8,9},{9,8},{10,11... | collective-permute-start | bytes 122888 | tf_op jit(solution)/shard_map/ppermute | solution.py:190
  2.0 2.6 %collective-permute-start.1 = (bf16[160,128]{1,0:T(8,128)(2,1)S(1)}, bf16[160,128]{1,0:T(8,128)(2,1)S(1)}, u32[]{:S(2)}, u32[]{:S(2)}) collective-permute-start(bf16[160,128]{1,0:T(8,128)(2,1)S(1)} %convert_element_type.39.refs_5_), channel_id=1, source_target_pairs={{0,2},{1,3},{2,0},{3,1},{4,6},{5,7},{6,4},{7,5},{8,10},{9,11},{10,... | collective-permute-start | bytes 122888 | tf_op jit(solution)/shard_map/ppermute | solution.py:190
  4.5 0.1 collective-permute-start.2
  4.6 2.3 %prepare.1 = (bf16[3072,640]{1,0:T(8,128)(2,1)S(1)}, bf16[3072,128]{1,0:T(8,128)(2,1)S(1)}, bf16[128,3072]{1,0:T(8,128)(2,1)S(1)}, f32[1,640]{1,0:T(1,128)S(1)}, f32[640,128]{1,0:T(8,128)S(1)}) custom-call(bf16[3072,640]{1,0:T(8,128)(2,1)} %x_in.1, s32[3072]{0:T(1024)} %index_in.1, bf16[512,128]{1,0:T(8,128)(2,1)} %cell_in.1, f32[640]{0:T(1024)} %scale_in.1), custom_call_target="tpu_custom_call" | custom-call | flops 402653184 | bytes 7864320 | tf_op jit(solution)/shard_map/prepare/pallas_call | solution.py:73
  6.9 0.0 collective-permute-done.refs_6_
  6.9 1.2 %collective-permute-done.2.refs_8_ = bf16[160,128]{1,0:T(8,128)(2,1)S(1)} collective-permute-done((bf16[160,128]{1,0:T(8,128)(2,1)S(1)}, bf16[160,128]{1,0:T(8,128)(2,1)S(1)}, u32[]{:S(2)}, u32[]{:S(2)}) %collective-permute-start.2) | collective-permute-done | bytes 40992 | tf_op jit(solution)/shard_map/ppermute | solution.py:190
  8.1 1.3 %block_rows.2 = (bf16[768,128]{1,0:T(8,128)(2,1)S(1)}, bf16[128,640]{1,0:T(8,128)(2,1)S(1)}, bf16[640,128]{1,0:T(8,128)(2,1)S(1)}, f32[128,640]{1,0:T(8,128)S(1)}) custom-call(bf16[3072,640]{1,0:T(8,128)(2,1)S(1)} %get-tuple-element.20.refs_0_, bf16[3072,128]{1,0:T(8,128)(2,1)S(1)} %get-tuple-element.21.refs_1_, ...), custom_call_target="tpu_custom_call" | custom-call | flops 754974720 | bytes 1966080 | tf_op jit(solution)/shard_map/block_rows/pallas_call | solution.py:176
  9.4 1.6 %collective-permute-start.3 = (bf16[768,128]{1,0:T(8,128)(2,1)S(1)}, bf16[768,128]{1,0:T(8,128)(2,1)S(1)}, u32[]{:S(2)}, u32[]{:S(2)}) collective-permute-start(bf16[768,128]{1,0:T(8,128)(2,1)S(1)} %get-tuple-element.29), channel_id=1, source_target_pairs={{0,4},{4,8},{8,12},{12,0},{1,5},{5,9},{9,13},{13,1},{2,6},{6,10},{... | collective-permute-start | bytes 589832 | tf_op jit(solution)/shard_map/ppermute | solution.py:219
  11.0 3.4 %block_rows.3 = (bf16[768,128]{1,0:T(8,128)(2,1)S(1)}, bf16[768,128]{1,0:T(8,128)(2,1)S(1)}, f32[768,128]{1,0:T(8,128)S(1)}, f32[160,128]{1,0:T(8,128)S(1)}, bf1...) custom-call(bf16[3072,640]{1,0:T(8,128)(2,1)S(1)} %get-tuple-element.20.refs_0_, ...), custom_call_target="tpu_custom_call" | custom-call | flops 2264924160 | bytes 5898240 | tf_op jit(solution)/shard_map/block_rows/pallas_call | solution.py:176
  14.5 0.1 collective-permute-start.6
  14.5 0.9 %collective-permute-start.7 = (bf16[160,128]{1,0:T(8,128)(2,1)S(1)}, bf16[160,128]{1,0:T(8,128)(2,1)S(1)}, u32[]{:S(2)}, u32[]{:S(2)}) collective-permute-start(bf16[160,128]{1,0:T(8,128)(2,1)S(1)} %get-tuple-element.34), channel_id=1, source_target_pairs={{0,2},{1,3},{2,0},{3,1},{4,6},{5,7},{6,4},{7,5},{8,10},{9,11},{10,... | collective-permute-start | bytes 122888 | tf_op jit(solution)/shard_map/ppermute | solution.py:190
  15.5 0.9 %collective-permute-start.8 = (bf16[160,128]{1,0:T(8,128)(2,1)S(1)}, bf16[160,128]{1,0:T(8,128)(2,1)S(1)}, u32[]{:S(2)}, u32[]{:S(2)}) collective-permute-start(bf16[160,128]{1,0:T(8,128)(2,1)S(1)} %get-tuple-element.35), channel_id=1, source_target_pairs={{0,3},{1,2},{2,1},{3,0},{4,7},{5,6},{6,5},{7,4},{8,11},{9,10},{10,... | collective-permute-start | bytes 122888 | tf_op jit(solution)/shard_map/ppermute | solution.py:190
  16.4 1.9 %collective-permute-done.3 = bf16[768,128]{1,0:T(8,128)(2,1)S(1)} collective-permute-done((bf16[768,128]{1,0:T(8,128)(2,1)S(1)}, bf16[768,128]{1,0:T(8,128)(2,1)S(1)}, u32[]{:S(2)}, u32[]{:S(2)}) %collective-permute-start.3) | collective-permute-done | bytes 196640 | tf_op jit(solution)/shard_map/ppermute | solution.py:219
  18.3 0.1 add_convert_fusion.1
  18.4 0.8 %collective-permute-start.4 = (bf16[768,128]{1,0:T(8,128)(2,1)S(1)}, bf16[768,128]{1,0:T(8,128)(2,1)S(1)}, u32[]{:S(2)}, u32[]{:S(2)}) collective-permute-start(bf16[768,128]{1,0:T(8,128)(2,1)S(1)} %get-tuple-element.39), channel_id=1, source_target_pairs={{0,8},{4,0},{8,12},{12,4},{1,9},{5,1},{9,13},{13,5},{2,10},{6,2},{... | collective-permute-start | bytes 589832 | tf_op jit(solution)/shard_map/ppermute | solution.py:219
  19.2 1.3 %collective-permute-start.5 = (bf16[768,128]{1,0:T(8,128)(2,1)S(1)}, bf16[768,128]{1,0:T(8,128)(2,1)S(1)}, u32[]{:S(2)}, u32[]{:S(2)}) collective-permute-start(bf16[768,128]{1,0:T(8,128)(2,1)S(1)} %get-tuple-element.40), channel_id=1, source_target_pairs={{0,4},{4,12},{8,0},{12,8},{1,5},{5,13},{9,1},{13,9},{2,6},{6,14},{... | collective-permute-start | bytes 589832 | tf_op jit(solution)/shard_map/ppermute | solution.py:219
  20.5 0.0 collective-permute-done.6
  20.5 0.0 collective-permute-done.7
  20.5 0.0 collective-permute-done.8
  20.5 0.7 %divide_subtract_fusion = (f32[160,128]{1,0:T(8,128)}, f32[160,128]{1,0:T(8,128)}, f32[160,128]{1,0:T(8,128)}) fusion(f32[160,128]{1,0:T(8,128)S(1)} %copy-done, bf16[160,128]{1,0:T(8,128)(2,1)S(1)} %collective-permute-done.8, bf16[160,128]{1,0:T(8,128)(2,1)S(1)} %collective-permute-done.7, f32[160,128]{1,0:T(8,128)S(1)} %get-tuple-element.32, ...), kind=kLoop, calls=%fused_computation.5 | loop fusion | flops 368640 | bytes 696320 | tf_op jit(solution)/shard_map/sub | solution.py:254
  21.2 3.5 %collective-permute-done.4 = bf16[768,128]{1,0:T(8,128)(2,1)S(1)} collective-permute-done((bf16[768,128]{1,0:T(8,128)(2,1)S(1)}, bf16[768,128]{1,0:T(8,128)(2,1)S(1)}, u32[]{:S(2)}, u32[]{:S(2)}) %collective-permute-start.4) | collective-permute-done | bytes 196640 | tf_op jit(solution)/shard_map/ppermute | solution.py:219
  24.7 5.1 %collective-permute-done.5 = bf16[768,128]{1,0:T(8,128)(2,1)S(1)} collective-permute-done((bf16[768,128]{1,0:T(8,128)(2,1)S(1)}, bf16[768,128]{1,0:T(8,128)(2,1)S(1)}, u32[]{:S(2)}, u32[]{:S(2)}) %collective-permute-start.5) | collective-permute-done | bytes 196640 | tf_op jit(solution)/shard_map/ppermute | solution.py:219
  29.9 0.8 %convert_add_fusion = f32[768,128]{1,0:T(8,128)} fusion(bf16[768,128]{1,0:T(8,128)(2,1)S(1)} %collective-permute-done.5, bf16[768,128]{1,0:T(8,128)(2,1)S(1)} %collective-permute-done.4, f32[768,128]{1,0:T(8,128)S(1)} %get-tuple-element.28, bf16[768,128]{1,0:T(8,128)(2,1)S(1)} %collective-permute-done.3, pred[]{:T(512)S(6)} %eq.27), kind=kLoop, calls=%fused_computation | loop fusion | flops 688128 | bytes 1376257 | tf_op jit(solution)/shard_map/add | solution.py:222
  (7 shorter events, 0.0 us)
Async XLA Ops:
  1.5 5.4 %collective-permute-start = (bf16[160,128]{1,0:T(8,128)(2,1)S(1)}, bf16[160,128]{1,0:T(8,128)(2,1)S(1)}, u32[]{:S(2)}, u32[]{:S(2)}) collective-permute-start(bf16[160,128]{1,0:T(8,128)(2,1)S(1)} %convert_element_type.39.refs_5_), channel_id=1, source_target_pairs={{0,1},{1,0},{2,3},{3,2},{4,5},{5,4},{6,7},{7,6},{8,9},{9,8},{10,11... | collective-permute-start | bytes 122888 | tf_op jit(solution)/shard_map/ppermute | solution.py:190
  2.0 4.9 %collective-permute-start.1 = (bf16[160,128]{1,0:T(8,128)(2,1)S(1)}, bf16[160,128]{1,0:T(8,128)(2,1)S(1)}, u32[]{:S(2)}, u32[]{:S(2)}) collective-permute-start(bf16[160,128]{1,0:T(8,128)(2,1)S(1)} %convert_element_type.39.refs_5_), channel_id=1, source_target_pairs={{0,2},{1,3},{2,0},{3,1},{4,6},{5,7},{6,4},{7,5},{8,10},{9,11},{10,... | collective-permute-start | bytes 122888 | tf_op jit(solution)/shard_map/ppermute | solution.py:190
  4.5 3.5 %collective-permute-start.2 = (bf16[160,128]{1,0:T(8,128)(2,1)S(1)}, bf16[160,128]{1,0:T(8,128)(2,1)S(1)}, u32[]{:S(2)}, u32[]{:S(2)}) collective-permute-start(bf16[160,128]{1,0:T(8,128)(2,1)S(1)} %convert_element_type.39.refs_5_), channel_id=1, source_target_pairs={{0,3},{1,2},{2,1},{3,0},{4,7},{5,6},{6,5},{7,4},{8,11},{9,10},{10,... | collective-permute-start | bytes 122888 | tf_op jit(solution)/shard_map/ppermute | solution.py:190
  9.4 8.9 %collective-permute-start.3 = (bf16[768,128]{1,0:T(8,128)(2,1)S(1)}, bf16[768,128]{1,0:T(8,128)(2,1)S(1)}, u32[]{:S(2)}, u32[]{:S(2)}) collective-permute-start(bf16[768,128]{1,0:T(8,128)(2,1)S(1)} %get-tuple-element.29), channel_id=1, source_target_pairs={{0,4},{4,8},{8,12},{12,0},{1,5},{5,9},{9,13},{13,1},{2,6},{6,10},{... | collective-permute-start | bytes 589832 | tf_op jit(solution)/shard_map/ppermute | solution.py:219
  11.0 9.5 %copy-start = (f32[160,128]{1,0:T(8,128)S(1)}, f32[160,128]{1,0:T(8,128)}, u32[]{:S(2)}) copy-start(f32[160,128]{1,0:T(8,128)} %param.11) | copy-start | bytes 245764
  11.0 9.5 %copy-start.1 = (f32[160,128]{1,0:T(8,128)S(1)}, f32[160,128]{1,0:T(8,128)}, u32[]{:S(2)}) copy-start(f32[160,128]{1,0:T(8,128)} %param.12) | copy-start | bytes 245764
  11.0 9.5 %copy-start.2 = (f32[160,128]{1,0:T(8,128)S(1)}, f32[160,128]{1,0:T(8,128)}, u32[]{:S(2)}) copy-start(f32[160,128]{1,0:T(8,128)} %param.13) | copy-start | bytes 245764
  14.5 6.0 %collective-permute-start.6 = (bf16[160,128]{1,0:T(8,128)(2,1)S(1)}, bf16[160,128]{1,0:T(8,128)(2,1)S(1)}, u32[]{:S(2)}, u32[]{:S(2)}) collective-permute-start(bf16[160,128]{1,0:T(8,128)(2,1)S(1)} %get-tuple-element.33), channel_id=1, source_target_pairs={{0,1},{1,0},{2,3},{3,2},{4,5},{5,4},{6,7},{7,6},{8,9},{9,8},{10,11... | collective-permute-start | bytes 122888 | tf_op jit(solution)/shard_map/ppermute | solution.py:190
  14.5 5.9 %collective-permute-start.7 = (bf16[160,128]{1,0:T(8,128)(2,1)S(1)}, bf16[160,128]{1,0:T(8,128)(2,1)S(1)}, u32[]{:S(2)}, u32[]{:S(2)}) collective-permute-start(bf16[160,128]{1,0:T(8,128)(2,1)S(1)} %get-tuple-element.34), channel_id=1, source_target_pairs={{0,2},{1,3},{2,0},{3,1},{4,6},{5,7},{6,4},{7,5},{8,10},{9,11},{10,... | collective-permute-start | bytes 122888 | tf_op jit(solution)/shard_map/ppermute | solution.py:190
  15.5 5.0 %collective-permute-start.8 = (bf16[160,128]{1,0:T(8,128)(2,1)S(1)}, bf16[160,128]{1,0:T(8,128)(2,1)S(1)}, u32[]{:S(2)}, u32[]{:S(2)}) collective-permute-start(bf16[160,128]{1,0:T(8,128)(2,1)S(1)} %get-tuple-element.35), channel_id=1, source_target_pairs={{0,3},{1,2},{2,1},{3,0},{4,7},{5,6},{6,5},{7,4},{8,11},{9,10},{10,... | collective-permute-start | bytes 122888 | tf_op jit(solution)/shard_map/ppermute | solution.py:190
  18.4 6.4 %collective-permute-start.4 = (bf16[768,128]{1,0:T(8,128)(2,1)S(1)}, bf16[768,128]{1,0:T(8,128)(2,1)S(1)}, u32[]{:S(2)}, u32[]{:S(2)}) collective-permute-start(bf16[768,128]{1,0:T(8,128)(2,1)S(1)} %get-tuple-element.39), channel_id=1, source_target_pairs={{0,8},{4,0},{8,12},{12,4},{1,9},{5,1},{9,13},{13,5},{2,10},{6,2},{... | collective-permute-start | bytes 589832 | tf_op jit(solution)/shard_map/ppermute | solution.py:219
  19.2 10.7 %collective-permute-start.5 = (bf16[768,128]{1,0:T(8,128)(2,1)S(1)}, bf16[768,128]{1,0:T(8,128)(2,1)S(1)}, u32[]{:S(2)}, u32[]{:S(2)}) collective-permute-start(bf16[768,128]{1,0:T(8,128)(2,1)S(1)} %get-tuple-element.40), channel_id=1, source_target_pairs={{0,4},{4,12},{8,0},{12,8},{1,5},{5,13},{9,1},{13,9},{2,6},{6,14},{... | collective-permute-start | bytes 589832 | tf_op jit(solution)/shard_map/ppermute | solution.py:219

commit v4 on v3

--- a/solution.py
+++ b/solution.py
@@ -1,4 +1,5 @@
 import functools
+import itertools
 import math
 
 import jax
@@ -14,7 +15,7 @@
 learn_rate = 0.02
 adam_eps = 1e-08
 
-PLAN_MOST = 8
+RING_MOST = 8
 VMEM = pltpu.VMEM
 IN_VMEM = pl.BlockSpec(memory_space=VMEM)
 IN_ANY = pl.BlockSpec(memory_space=pl.ANY)
@@ -116,7 +117,7 @@
     shares = take(n_row) if first else None
     carried_in = None if first else take(3)
     rows_out = take(len(tables))
-    carried_out = None if last else take(3)
+    carried_out = None if last else take(3 if first else 1)
     parts_out = take(n_row) if last else None
     me = lax.axis_index("row")
 
@@ -131,7 +132,7 @@
         scaled = (whole * shrink_ref[...]).astype(jnp.bfloat16)
         total = None
     else:
-        wide, scaled, total = (ref[...] for ref in carried_in)
+        total, wide, scaled = (ref[...] for ref in carried_in)
 
     bend = bend_ref[...]
     step = tile_of(block, 256)
@@ -149,9 +150,11 @@
             out[at : at + step, :] = jnp.dot(infl, scaled, preferred_element_type=jnp.float32).astype(out.dtype)
             cols = jnp.dot(ft_ref[:, here], infl, preferred_element_type=jnp.float32)
             total = cols if total is None else total + cols
+    if first and not last:
+        carried_out[1][...] = wide
+        carried_out[2][...] = scaled
     if not last:
-        for ref, value in zip(carried_out, (wide, scaled, total)):
-            ref[...] = value
+        carried_out[0][...] = total
         return
     (turned,) = take(1)
     turned[...] = jnp.transpose(total) * shrink_ref[...]
@@ -167,7 +170,9 @@
     if last:
         out += [jax.ShapeDtypeStruct((genes // n_row, rank), jnp.bfloat16 if hop else jnp.float32) for hop in range(n_row)]
     else:
-        out += [VMEM((rank, genes), jnp.bfloat16), VMEM((genes, rank), jnp.bfloat16), VMEM((rank, genes), jnp.float32)]
+        out += [VMEM((rank, genes), jnp.float32)]
+    if first and not last:
+        out += [VMEM((rank, genes), jnp.bfloat16), VMEM((genes, rank), jnp.bfloat16)]
     scratch = [VMEM((genes, rank), jnp.bfloat16)] if first else []
     if last:
         scratch.append(VMEM((genes, rank), jnp.float32))
@@ -183,43 +188,41 @@
         cost_estimate=cost(12 * work * rank, work * 4),
         name="block_rows",
     )(*ins)
-    return out[: len(tables)], out[len(tables) :]
+    done, rest = list(out[: len(tables)]), list(out[len(tables) :])
+    return done, rest if first or last else rest + list(carried[1:])
 
 
 def swap_row(value, hop, size):
     return lax.ppermute(value, "row", [(me, partner(me, hop, size)) for me in range(size)])
 
 
-def plan_of(size):
-    if size == 4:
-        return [((1, 2, 3, 0), (3, 2, 1, 0)), ((2, 0, 3, 1), (2, 0, 3, 1)), ((1, 3, 0, 2), (1, 3, 0, 2))]
-    hops = [tuple((place + hop) % size for place in range(size)) for hop in range(1, size)]
-    return [(hop, hop) for hop in hops]
-
-
-def received(step):
-    targets, blocks = step
-    return [blocks[targets.index(place)] for place in range(len(targets))]
-
-
-def chosen(value, flags):
-    if all(flags):
-        return value
-    return jnp.where(pick("gene", flags) == 1, value, jnp.zeros_like(value))
-
-
-def exchange(steps, blocks, mine):
-    size = len(steps[0][0])
-    got = []
-    for at, (step, block) in enumerate(zip(steps, blocks)):
-        for earlier, value in zip(steps[:at], got):
-            flags = [int(came == sent and came != me) for me, (came, sent) in enumerate(zip(received(earlier), step[1]))]
-            if any(flags):
-                block = (block.astype(jnp.float32) + chosen(value, flags).astype(jnp.float32)).astype(jnp.bfloat16)
-        got.append(lax.ppermute(block, "gene", list(enumerate(step[0]))))
-    for step, value in zip(steps, got):
-        flags = [int(came == me) for me, came in enumerate(received(step))]
-        mine = mine + chosen(value, flags).astype(jnp.float32)
+def ring_of(size):
+    return [*range(0, size, 2), *reversed(range(1, size, 2))]
+
+
+def steps_of(size):
+    ahead = [(1, distance) for distance in range(size // 2, 0, -1)]
+    back = [(-1, distance) for distance in range((size - 1) // 2, 0, -1)]
+    return [step for pair in itertools.zip_longest(ahead, back) for step in pair if step]
+
+
+def around(size, hops):
+    ring = ring_of(size)
+    return tuple(ring[(ring.index(place) + hops) % size] for place in range(size))
+
+
+def plus(wide, narrow):
+    return wide.astype(jnp.float32) + narrow.astype(jnp.float32)
+
+
+def reduce_scatter(size, steps, blocks, mine):
+    came = {}
+    for (way, _), block in zip(steps, blocks):
+        if way in came:
+            block = plus(block, came[way]).astype(jnp.bfloat16)
+        came[way] = lax.ppermute(block, "gene", list(enumerate(around(size, way))))
+    for value in came.values():
+        mine = plus(mine, value)
     return mine
 
 
@@ -233,13 +236,18 @@
     shares = [factor_bf] + [swap_row(factor_bf, hop, n_row) for hop in range(1, n_row)]
     fixed = prepare(x_slab, row_index, cell_factor, gene_scale, scale_k)
 
-    if 1 < n_gene <= PLAN_MOST and block % 128 == 0:
-        steps = plan_of(n_gene)
-        tables = [step[1] for step in steps] + [tuple(range(n_gene))]
+    if 1 < n_gene <= RING_MOST and block % 128 == 0:
+        steps = steps_of(n_gene)
+        tables = [around(n_gene, way * distance) for way, distance in steps] + [tuple(range(n_gene))]
         kinds = [jnp.bfloat16] * len(steps) + [jnp.float32]
-        near, carried = block_rows(tables[:1], kinds[:1], block, True, False, n_row, fixed, shares)
-        others, parts = block_rows(tables[1:], kinds[1:], block, False, True, n_row, fixed, carried)
-        grad_cells = exchange(steps, [*near, *others[:-1]], others[-1])
+        cuts = [0, 1, 2, len(tables)] if len(steps) > 2 else [0, 1, len(tables)]
+        carried, blocks = shares, []
+        for low, high in zip(cuts, cuts[1:]):
+            last = high == len(tables)
+            done, carried = block_rows(tables[low:high], kinds[low:high], block, low == 0, last, n_row, fixed, carried)
+            blocks += done
+        parts = carried
+        grad_cells = reduce_scatter(n_gene, steps, blocks[:-1], blocks[-1])
     else:
         (rows,), parts = block_rows([(0,)], [jnp.float32], rows_dev, True, True, n_row, fixed, shares)
         grad_cells = lax.psum_scatter(rows, "gene", scatter_dimension=0, tiled=True)

time: 30.9 us -> 30.1 us (0.974)
  waiting for transfers between devices: 11.7 us -> 8.87 us
  starting transfers between devices: 8.72 us -> 10.6 us
    ppermute x3, waiting for transfers between devices: 10.5 us -> 7.67 us  [reduce_scatter(): came[way] = lax.ppermute(block, 'gene', list(enumerate(around(size, way))))]
    ppermute x3, starting transfers between devices: 3.7 us -> 5.61 us  [reduce_scatter(): came[way] = lax.ppermute(block, 'gene', list(enumerate(around(size, way))))]
    pallas_call x2 -> x3, Pallas kernels: 4.76 us -> 4.98 us  [block_rows(): pl.pallas_call(functools.partial(rows_kernel, tables, block, first, last,...]
  transfers between devices with their start and end apart: 9 -> 9, of which waited for: 4 -> 3; matrix products, arithmetic and copies ran while one was open for 3% -> 3% of each run, Pallas kernels for 19% -> 20%
where the time goes in v4:
time: 30.1 us; the launch traced here: 30 us
  starting transfers between devices  10.6 us (35%)
  waiting for transfers between devices  8.87 us (29%)
  Pallas kernels  7.24 us (24%)
  other arithmetic  2.5 us (8%)
  between operations  0.74 us (2%)
    ppermute x3, waiting for transfers between devices, reduce_scatter(): came[way] = lax.ppermute(block, 'gene', list(enumerate(around(size, way))))  7.67 us
    ppermute x3, starting transfers between devices, reduce_scatter(): came[way] = lax.ppermute(block, 'gene', list(enumerate(around(size, way))))  5.61 us
    ppermute x6, starting transfers between devices, swap_row(): lax.ppermute(value, 'row', [(me, partner(me, hop, size)) for me in range(...  4.99 us
    pallas_call x3, Pallas kernels, block_rows(): pl.pallas_call(functools.partial(rows_kernel, tables, block, first, last,...  4.98 us
    pallas_call x1, Pallas kernels, prepare(): pl.pallas_call(functools.partial(prepare_kernel, scale_k), out_shape=(VME...  2.26 us
    ppermute x6, waiting for transfers between devices, swap_row(): lax.ppermute(value, 'row', [(me, partner(me, hop, size)) for me in range(...  1.2 us
    convert_element_type x1, other arithmetic, local(): factor_bf = gene_factor.astype(jnp.bfloat16)  0.9 us
    add x1, other arithmetic, plus(): return wide.astype(jnp.float32) + narrow.astype(jnp.float32)  0.82 us
  transfers between devices with their start and end apart: 9, of which 3 were waited for; matrix products, arithmetic and copies ran while one was open for 3% of the time, Pallas kernels for 20%

profile of v4, /device:TPU:0, one launch (start us, length us, event | category | flops | bytes accessed | tf_op | source)
XLA Modules:
  0.0 30.0 jit_solution(1350656832358604831)
XLA Ops:
  0.6 0.9 %convert_element_type.27.refs_5_ = bf16[160,128]{1,0:T(8,128)(2,1)S(1)} convert(f32[160,128]{1,0:T(8,128)} %param.11) | non-fusion elementwise | flops 20480 | bytes 122880 | tf_op jit(solution)/shard_map/convert_element_type | solution.py:235
  1.5 2.4 %collective-permute-start.2 = (bf16[160,128]{1,0:T(8,128)(2,1)S(1)}, bf16[160,128]{1,0:T(8,128)(2,1)S(1)}, u32[]{:S(2)}, u32[]{:S(2)}) collective-permute-start(bf16[160,128]{1,0:T(8,128)(2,1)S(1)} %convert_element_type.27.refs_5_), channel_id=1, source_target_pairs={{0,3},{1,2},{2,1},{3,0},{4,7},{5,6},{6,5},{7,4},{8,11},{9,10},{10,... | collective-permute-start | bytes 122888 | tf_op jit(solution)/shard_map/ppermute | solution.py:196
  3.9 0.6 %collective-permute-start.1 = (bf16[160,128]{1,0:T(8,128)(2,1)S(1)}, bf16[160,128]{1,0:T(8,128)(2,1)S(1)}, u32[]{:S(2)}, u32[]{:S(2)}) collective-permute-start(bf16[160,128]{1,0:T(8,128)(2,1)S(1)} %convert_element_type.27.refs_5_), channel_id=1, source_target_pairs={{0,2},{1,3},{2,0},{3,1},{4,6},{5,7},{6,4},{7,5},{8,10},{9,11},{10,... | collective-permute-start | bytes 122888 | tf_op jit(solution)/shard_map/ppermute | solution.py:196
  4.5 0.0 collective-permute-start
  4.6 2.3 %prepare.1 = (bf16[3072,640]{1,0:T(8,128)(2,1)S(1)}, bf16[3072,128]{1,0:T(8,128)(2,1)S(1)}, bf16[128,3072]{1,0:T(8,128)(2,1)S(1)}, f32[1,640]{1,0:T(1,128)S(1)}, f32[640,128]{1,0:T(8,128)S(1)}) custom-call(bf16[3072,640]{1,0:T(8,128)(2,1)} %x_in.1, s32[3072]{0:T(1024)} %index_in.1, bf16[512,128]{1,0:T(8,128)(2,1)} %cell_in.1, f32[640]{0:T(1024)} %scale_in.1), custom_call_target="tpu_custom_call" | custom-call | flops 402653184 | bytes 7864320 | tf_op jit(solution)/shard_map/prepare/pallas_call | solution.py:74
  6.8 0.0 collective-permute-done.2.refs_8_
  6.9 1.2 %collective-permute-done.1.refs_7_ = bf16[160,128]{1,0:T(8,128)(2,1)S(1)} collective-permute-done((bf16[160,128]{1,0:T(8,128)(2,1)S(1)}, bf16[160,128]{1,0:T(8,128)(2,1)S(1)}, u32[]{:S(2)}, u32[]{:S(2)}) %collective-permute-start.1) | collective-permute-done | bytes 40992 | tf_op jit(solution)/shard_map/ppermute | solution.py:196
  8.1 1.3 %block_rows.3 = (bf16[768,128]{1,0:T(8,128)(2,1)S(1)}, f32[128,640]{1,0:T(8,128)S(1)}, bf16[128,640]{1,0:T(8,128)(2,1)S(1)}, bf16[640,128]{1,0:T(8,128)(2,1)S(1)}) custom-call(bf16[3072,640]{1,0:T(8,128)(2,1)S(1)} %get-tuple-element.21.refs_0_, bf16[3072,128]{1,0:T(8,128)(2,1)S(1)} %get-tuple-element.22.refs_1_, ...), custom_call_target="tpu_custom_call" | custom-call | flops 754974720 | bytes 1966080 | tf_op jit(solution)/shard_map/block_rows/pallas_call | solution.py:181
  9.4 2.6 %collective-permute-start.3 = (bf16[768,128]{1,0:T(8,128)(2,1)S(1)}, bf16[768,128]{1,0:T(8,128)(2,1)S(1)}, u32[]{:S(2)}, u32[]{:S(2)}) collective-permute-start(bf16[768,128]{1,0:T(8,128)(2,1)S(1)} %get-tuple-element.32), channel_id=1, source_target_pairs={{0,8},{4,0},{8,12},{12,4},{1,9},{5,1},{9,13},{13,5},{2,10},{6,2},{... | collective-permute-start | bytes 589832 | tf_op jit(solution)/shard_map/ppermute | solution.py:223
  12.0 1.2 %block_rows.4 = (bf16[768,128]{1,0:T(8,128)(2,1)S(1)}, f32[128,640]{1,0:T(8,128)S(1)}) custom-call(bf16[3072,640]{1,0:T(8,128)(2,1)S(1)} %get-tuple-element.21.refs_0_, bf16[3072,128]{1,0:T(8,128)(2,1)S(1)} %get-tuple-element.22.refs_1_, bf16[128,3072]{1,0:T(8,128)(2,1)S(1)} %get-tuple-element.23.refs_2_, f32[1,640]{1,0:T(1,128)S(1)} %get-tuple-element.24.refs_3_, ...), custom_call_target="tpu_custom_call" | custom-call | flops 754974720 | bytes 1966080 | tf_op jit(solution)/shard_map/block_rows/pallas_call | solution.py:181
  13.2 0.0 copy-start
  13.3 0.0 copy-start.1
  13.3 0.0 copy-start.2
  13.3 2.4 %block_rows.5 = (bf16[768,128]{1,0:T(8,128)(2,1)S(1)}, f32[768,128]{1,0:T(8,128)S(1)}, f32[160,128]{1,0:T(8,128)S(1)}, bf16[160,128]{1,0:T(8,128)(2,1)S(1)}, bf1...) custom-call(bf16[3072,640]{1,0:T(8,128)(2,1)S(1)} %get-tuple-element.21.refs_0_, ...), custom_call_target="tpu_custom_call" | custom-call | flops 1509949440 | bytes 3932160 | tf_op jit(solution)/shard_map/block_rows/pallas_call | solution.py:181
  15.7 0.1 collective-permute-start.6
  15.8 1.2 %collective-permute-start.7 = (bf16[160,128]{1,0:T(8,128)(2,1)S(1)}, bf16[160,128]{1,0:T(8,128)(2,1)S(1)}, u32[]{:S(2)}, u32[]{:S(2)}) collective-permute-start(bf16[160,128]{1,0:T(8,128)(2,1)S(1)} %get-tuple-element.36), channel_id=1, source_target_pairs={{0,2},{1,3},{2,0},{3,1},{4,6},{5,7},{6,4},{7,5},{8,10},{9,11},{10,... | collective-permute-start | bytes 122888 | tf_op jit(solution)/shard_map/ppermute | solution.py:196
  17.0 0.6 %collective-permute-start.8 = (bf16[160,128]{1,0:T(8,128)(2,1)S(1)}, bf16[160,128]{1,0:T(8,128)(2,1)S(1)}, u32[]{:S(2)}, u32[]{:S(2)}) collective-permute-start(bf16[160,128]{1,0:T(8,128)(2,1)S(1)} %get-tuple-element.37), channel_id=1, source_target_pairs={{0,3},{1,2},{2,1},{3,0},{4,7},{5,6},{6,5},{7,4},{8,11},{9,10},{10,... | collective-permute-start | bytes 122888 | tf_op jit(solution)/shard_map/ppermute | solution.py:196
  17.7 0.1 add_convert_fusion
  17.7 3.0 %collective-permute-start.4 = (bf16[768,128]{1,0:T(8,128)(2,1)S(1)}, bf16[768,128]{1,0:T(8,128)(2,1)S(1)}, u32[]{:S(2)}, u32[]{:S(2)}) collective-permute-start(bf16[768,128]{1,0:T(8,128)(2,1)S(1)} %add_convert_fusion), channel_id=1, source_target_pairs={{0,8},{4,0},{8,12},{12,4},{1,9},{5,1},{9,13},{13,5},{2,10},{6,2},{... | collective-permute-start | bytes 589832 | tf_op jit(solution)/shard_map/ppermute | solution.py:223
  20.7 0.0 collective-permute-done.8
  20.7 0.7 %divide_subtract_fusion = (f32[160,128]{1,0:T(8,128)}, f32[160,128]{1,0:T(8,128)}, f32[160,128]{1,0:T(8,128)}) fusion(f32[160,128]{1,0:T(8,128)S(1)} %copy-done, bf16[160,128]{1,0:T(8,128)(2,1)S(1)} %collective-permute-done.8, bf16[160,128]{1,0:T(8,128)(2,1)S(1)} %collective-permute-done.7, f32[160,128]{1,0:T(8,128)S(1)} %get-tuple-element.34, ...), kind=kLoop, calls=%fused_computation.4 | loop fusion | flops 368640 | bytes 696320 | tf_op jit(solution)/shard_map/sub | solution.py:262
  21.5 4.8 %collective-permute-done.5 = bf16[768,128]{1,0:T(8,128)(2,1)S(1)} collective-permute-done((bf16[768,128]{1,0:T(8,128)(2,1)S(1)}, bf16[768,128]{1,0:T(8,128)(2,1)S(1)}, u32[]{:S(2)}, u32[]{:S(2)}) %collective-permute-start.5) | collective-permute-done | bytes 196640 | tf_op jit(solution)/shard_map/ppermute | solution.py:223
  26.3 2.9 %collective-permute-done.4 = bf16[768,128]{1,0:T(8,128)(2,1)S(1)} collective-permute-done((bf16[768,128]{1,0:T(8,128)(2,1)S(1)}, bf16[768,128]{1,0:T(8,128)(2,1)S(1)}, u32[]{:S(2)}, u32[]{:S(2)}) %collective-permute-start.4) | collective-permute-done | bytes 196640 | tf_op jit(solution)/shard_map/ppermute | solution.py:223
  29.2 0.8 %convert_add_fusion = f32[768,128]{1,0:T(8,128)} fusion(bf16[768,128]{1,0:T(8,128)(2,1)S(1)} %collective-permute-done.5, f32[768,128]{1,0:T(8,128)S(1)} %get-tuple-element.30, bf16[768,128]{1,0:T(8,128)(2,1)S(1)} %collective-permute-done.4), kind=kLoop, calls=%fused_computation | loop fusion | flops 393216 | bytes 1179648 | tf_op jit(solution)/shard_map/add | solution.py:215
  (8 shorter events, 0.0 us)
Async XLA Ops:
  1.5 5.3 %collective-permute-start.2 = (bf16[160,128]{1,0:T(8,128)(2,1)S(1)}, bf16[160,128]{1,0:T(8,128)(2,1)S(1)}, u32[]{:S(2)}, u32[]{:S(2)}) collective-permute-start(bf16[160,128]{1,0:T(8,128)(2,1)S(1)} %convert_element_type.27.refs_5_), channel_id=1, source_target_pairs={{0,3},{1,2},{2,1},{3,0},{4,7},{5,6},{6,5},{7,4},{8,11},{9,10},{10,... | collective-permute-start | bytes 122888 | tf_op jit(solution)/shard_map/ppermute | solution.py:196
  3.9 4.1 %collective-permute-start.1 = (bf16[160,128]{1,0:T(8,128)(2,1)S(1)}, bf16[160,128]{1,0:T(8,128)(2,1)S(1)}, u32[]{:S(2)}, u32[]{:S(2)}) collective-permute-start(bf16[160,128]{1,0:T(8,128)(2,1)S(1)} %convert_element_type.27.refs_5_), channel_id=1, source_target_pairs={{0,2},{1,3},{2,0},{3,1},{4,6},{5,7},{6,4},{7,5},{8,10},{9,11},{10,... | collective-permute-start | bytes 122888 | tf_op jit(solution)/shard_map/ppermute | solution.py:196
  4.5 3.5 %collective-permute-start = (bf16[160,128]{1,0:T(8,128)(2,1)S(1)}, bf16[160,128]{1,0:T(8,128)(2,1)S(1)}, u32[]{:S(2)}, u32[]{:S(2)}) collective-permute-start(bf16[160,128]{1,0:T(8,128)(2,1)S(1)} %convert_element_type.27.refs_5_), channel_id=1, source_target_pairs={{0,1},{1,0},{2,3},{3,2},{4,5},{5,4},{6,7},{7,6},{8,9},{9,8},{10,11... | collective-permute-start | bytes 122888 | tf_op jit(solution)/shard_map/ppermute | solution.py:196
  9.4 8.3 %collective-permute-start.3 = (bf16[768,128]{1,0:T(8,128)(2,1)S(1)}, bf16[768,128]{1,0:T(8,128)(2,1)S(1)}, u32[]{:S(2)}, u32[]{:S(2)}) collective-permute-start(bf16[768,128]{1,0:T(8,128)(2,1)S(1)} %get-tuple-element.32), channel_id=1, source_target_pairs={{0,8},{4,0},{8,12},{12,4},{1,9},{5,1},{9,13},{13,5},{2,10},{6,2},{... | collective-permute-start | bytes 589832 | tf_op jit(solution)/shard_map/ppermute | solution.py:223
  13.2 7.5 %copy-start = (f32[160,128]{1,0:T(8,128)S(1)}, f32[160,128]{1,0:T(8,128)}, u32[]{:S(2)}) copy-start(f32[160,128]{1,0:T(8,128)} %param.11) | copy-start | bytes 245764
  13.3 7.5 %copy-start.1 = (f32[160,128]{1,0:T(8,128)S(1)}, f32[160,128]{1,0:T(8,128)}, u32[]{:S(2)}) copy-start(f32[160,128]{1,0:T(8,128)} %param.12) | copy-start | bytes 245764
  13.3 7.5 %copy-start.2 = (f32[160,128]{1,0:T(8,128)S(1)}, f32[160,128]{1,0:T(8,128)}, u32[]{:S(2)}) copy-start(f32[160,128]{1,0:T(8,128)} %param.13) | copy-start | bytes 245764
  15.7 5.0 %collective-permute-start.6 = (bf16[160,128]{1,0:T(8,128)(2,1)S(1)}, bf16[160,128]{1,0:T(8,128)(2,1)S(1)}, u32[]{:S(2)}, u32[]{:S(2)}) collective-permute-start(bf16[160,128]{1,0:T(8,128)(2,1)S(1)} %get-tuple-element.35), channel_id=1, source_target_pairs={{0,1},{1,0},{2,3},{3,2},{4,5},{5,4},{6,7},{7,6},{8,9},{9,8},{10,11... | collective-permute-start | bytes 122888 | tf_op jit(solution)/shard_map/ppermute | solution.py:196
  15.8 4.9 %collective-permute-start.7 = (bf16[160,128]{1,0:T(8,128)(2,1)S(1)}, bf16[160,128]{1,0:T(8,128)(2,1)S(1)}, u32[]{:S(2)}, u32[]{:S(2)}) collective-permute-start(bf16[160,128]{1,0:T(8,128)(2,1)S(1)} %get-tuple-element.36), channel_id=1, source_target_pairs={{0,2},{1,3},{2,0},{3,1},{4,6},{5,7},{6,4},{7,5},{8,10},{9,11},{10,... | collective-permute-start | bytes 122888 | tf_op jit(solution)/shard_map/ppermute | solution.py:196
  17.0 3.7 %collective-permute-start.8 = (bf16[160,128]{1,0:T(8,128)(2,1)S(1)}, bf16[160,128]{1,0:T(8,128)(2,1)S(1)}, u32[]{:S(2)}, u32[]{:S(2)}) collective-permute-start(bf16[160,128]{1,0:T(8,128)(2,1)S(1)} %get-tuple-element.37), channel_id=1, source_target_pairs={{0,3},{1,2},{2,1},{3,0},{4,7},{5,6},{6,5},{7,4},{8,11},{9,10},{10,... | collective-permute-start | bytes 122888 | tf_op jit(solution)/shard_map/ppermute | solution.py:196
  17.7 8.6 %collective-permute-start.5 = (bf16[768,128]{1,0:T(8,128)(2,1)S(1)}, bf16[768,128]{1,0:T(8,128)(2,1)S(1)}, u32[]{:S(2)}, u32[]{:S(2)}) collective-permute-start(bf16[768,128]{1,0:T(8,128)(2,1)S(1)} %get-tuple-element.33), channel_id=1, source_target_pairs={{0,4},{4,12},{8,0},{12,8},{1,5},{5,13},{9,1},{13,9},{2,6},{6,14},{... | collective-permute-start | bytes 589832 | tf_op jit(solution)/shard_map/ppermute | solution.py:223
  17.7 11.4 %collective-permute-start.4 = (bf16[768,128]{1,0:T(8,128)(2,1)S(1)}, bf16[768,128]{1,0:T(8,128)(2,1)S(1)}, u32[]{:S(2)}, u32[]{:S(2)}) collective-permute-start(bf16[768,128]{1,0:T(8,128)(2,1)S(1)} %add_convert_fusion), channel_id=1, source_target_pairs={{0,8},{4,0},{8,12},{12,4},{1,9},{5,1},{9,13},{13,5},{2,10},{6,2},{... | collective-permute-start | bytes 589832 | tf_op jit(solution)/shard_map/ppermute | solution.py:223

commit v5 on v4

--- a/solution.py
+++ b/solution.py
@@ -185,7 +185,7 @@
         out_specs=(IN_VMEM,) * len(out),
         scratch_shapes=scratch,
         compiler_params=params(),
-        cost_estimate=cost(12 * work * rank, work * 4),
+        cost_estimate=cost(6 * work * rank, work * 2),
         name="block_rows",
     )(*ins)
     done, rest = list(out[: len(tables)]), list(out[len(tables) :])
@@ -215,15 +215,17 @@
     return wide.astype(jnp.float32) + narrow.astype(jnp.float32)
 
 
-def reduce_scatter(size, steps, blocks, mine):
+def reduce_scatter(size, steps, blocks, mine, parts):
     came = {}
-    for (way, _), block in zip(steps, blocks):
+    for at, ((way, _), block) in enumerate(zip(steps, blocks), 1):
         if way in came:
             block = plus(block, came[way]).astype(jnp.bfloat16)
+        if at == len(steps):
+            block, *parts = lax.optimization_barrier((block, *parts))
         came[way] = lax.ppermute(block, "gene", list(enumerate(around(size, way))))
     for value in came.values():
         mine = plus(mine, value)
-    return mine
+    return mine, list(came.values()), parts
 
 
 def local(x_slab, cell_factor, row_index, gene_scale, gene_factor, first_moment, second_moment):
@@ -246,15 +248,17 @@
             last = high == len(tables)
             done, carried = block_rows(tables[low:high], kinds[low:high], block, low == 0, last, n_row, fixed, carried)
             blocks += done
-        parts = carried
-        grad_cells = reduce_scatter(n_gene, steps, blocks[:-1], blocks[-1])
+        grad_cells, ends, parts = reduce_scatter(n_gene, steps, blocks[:-1], blocks[-1], carried)
     else:
         (rows,), parts = block_rows([(0,)], [jnp.float32], rows_dev, True, True, n_row, fixed, shares)
-        grad_cells = lax.psum_scatter(rows, "gene", scatter_dimension=0, tiled=True)
+        grad_cells, ends = lax.psum_scatter(rows, "gene", scatter_dimension=0, tiled=True), []
 
     grad_genes = parts[0]
-    for hop in range(1, n_row):
-        grad_genes = grad_genes + swap_row(parts[hop], hop, n_row).astype(jnp.float32)
+    others = [swap_row(parts[hop], hop, n_row) for hop in range(1, n_row)]
+    if others and len(ends) > 1:
+        others[0], _ = lax.optimization_barrier((others[0], ends[1]))
+    for value in others:
+        grad_genes = grad_genes + value.astype(jnp.float32)
     new_first = beta_one * first_moment + (1.0 - beta_one) * grad_genes
     new_second = beta_two * second_moment + (1.0 - beta_two) * grad_genes * grad_genes
     first_hat = new_first / (1.0 - beta_one**10)

time: 30.1 us -> 28.4 us (0.944)
  waiting for transfers between devices: 8.87 us -> 6.63 us
  starting transfers between devices: 10.6 us -> 11.1 us
    ppermute x3, waiting for transfers between devices: 7.67 us -> 5.43 us  [reduce_scatter(): came[way] = lax.ppermute(block, 'gene', list(enumerate(around(size, way))))]
    ppermute x3, starting transfers between devices: 5.61 us -> 6.08 us  [reduce_scatter(): came[way] = lax.ppermute(block, 'gene', list(enumerate(around(size, way))))]
  transfers between devices with their start and end apart: 9 -> 9, of which waited for: 3 -> 3; matrix products, arithmetic and copies ran while one was open for 3% -> 3% of each run, Pallas kernels for 20% -> 21%
where the time goes in v5:
time: 28.4 us; the launch traced here: 28.2 us
  starting transfers between devices  11.1 us (39%)
  Pallas kernels  7.24 us (25%)
  waiting for transfers between devices  6.63 us (23%)
  other arithmetic  2.5 us (9%)
  between operations  0.75 us (3%)
    ppermute x3, starting transfers between devices, reduce_scatter(): came[way] = lax.ppermute(block, 'gene', list(enumerate(around(size, way))))  6.08 us
    ppermute x3, waiting for transfers between devices, reduce_scatter(): came[way] = lax.ppermute(block, 'gene', list(enumerate(around(size, way))))  5.43 us
    ppermute x6, starting transfers between devices, swap_row(): lax.ppermute(value, 'row', [(me, partner(me, hop, size)) for me in range(...  4.99 us
    pallas_call x3, Pallas kernels, block_rows(): pl.pallas_call(functools.partial(rows_kernel, tables, block, first, last,...  4.98 us
    pallas_call x1, Pallas kernels, prepare(): pl.pallas_call(functools.partial(prepare_kernel, scale_k), out_shape=(VME...  2.26 us
    ppermute x6, waiting for transfers between devices, swap_row(): lax.ppermute(value, 'row', [(me, partner(me, hop, size)) for me in range(...  1.2 us
    convert_element_type x1, other arithmetic, local(): factor_bf = gene_factor.astype(jnp.bfloat16)  0.9 us
    add x1, other arithmetic, plus(): return wide.astype(jnp.float32) + narrow.astype(jnp.float32)  0.81 us
  transfers between devices with their start and end apart: 9, of which 3 were waited for; matrix products, arithmetic and copies ran while one was open for 3% of the time, Pallas kernels for 21%

profile of v5, /device:TPU:0, one launch (start us, length us, event | category | flops | bytes accessed | tf_op | source)
XLA Modules:
  0.0 28.2 jit_solution(1940394959615169102)
XLA Ops:
  0.6 0.9 %convert_element_type.27.refs_5_ = bf16[160,128]{1,0:T(8,128)(2,1)S(1)} convert(f32[160,128]{1,0:T(8,128)} %param.11) | non-fusion elementwise | flops 20480 | bytes 122880 | tf_op jit(solution)/shard_map/convert_element_type | solution.py:237
  1.5 2.4 %collective-permute-start.2 = (bf16[160,128]{1,0:T(8,128)(2,1)S(1)}, bf16[160,128]{1,0:T(8,128)(2,1)S(1)}, u32[]{:S(2)}, u32[]{:S(2)}) collective-permute-start(bf16[160,128]{1,0:T(8,128)(2,1)S(1)} %convert_element_type.27.refs_5_), channel_id=1, source_target_pairs={{0,3},{1,2},{2,1},{3,0},{4,7},{5,6},{6,5},{7,4},{8,11},{9,10},{10,... | collective-permute-start | bytes 122888 | tf_op jit(solution)/shard_map/ppermute | solution.py:196
  3.9 0.6 %collective-permute-start.1 = (bf16[160,128]{1,0:T(8,128)(2,1)S(1)}, bf16[160,128]{1,0:T(8,128)(2,1)S(1)}, u32[]{:S(2)}, u32[]{:S(2)}) collective-permute-start(bf16[160,128]{1,0:T(8,128)(2,1)S(1)} %convert_element_type.27.refs_5_), channel_id=1, source_target_pairs={{0,2},{1,3},{2,0},{3,1},{4,6},{5,7},{6,4},{7,5},{8,10},{9,11},{10,... | collective-permute-start | bytes 122888 | tf_op jit(solution)/shard_map/ppermute | solution.py:196
  4.5 0.0 collective-permute-start
  4.6 2.3 %prepare.1 = (bf16[3072,640]{1,0:T(8,128)(2,1)S(1)}, bf16[3072,128]{1,0:T(8,128)(2,1)S(1)}, bf16[128,3072]{1,0:T(8,128)(2,1)S(1)}, f32[1,640]{1,0:T(1,128)S(1)}, f32[640,128]{1,0:T(8,128)S(1)}) custom-call(bf16[3072,640]{1,0:T(8,128)(2,1)} %x_in.1, s32[3072]{0:T(1024)} %index_in.1, bf16[512,128]{1,0:T(8,128)(2,1)} %cell_in.1, f32[640]{0:T(1024)} %scale_in.1), custom_call_target="tpu_custom_call" | custom-call | flops 402653184 | bytes 7864320 | tf_op jit(solution)/shard_map/prepare/pallas_call | solution.py:74
  6.8 0.0 collective-permute-done.2.refs_8_
  6.9 1.2 %collective-permute-done.1.refs_7_ = bf16[160,128]{1,0:T(8,128)(2,1)S(1)} collective-permute-done((bf16[160,128]{1,0:T(8,128)(2,1)S(1)}, bf16[160,128]{1,0:T(8,128)(2,1)S(1)}, u32[]{:S(2)}, u32[]{:S(2)}) %collective-permute-start.1) | collective-permute-done | bytes 40992 | tf_op jit(solution)/shard_map/ppermute | solution.py:196
  8.1 1.3 %block_rows.3 = (bf16[768,128]{1,0:T(8,128)(2,1)S(1)}, f32[128,640]{1,0:T(8,128)S(1)}, bf16[128,640]{1,0:T(8,128)(2,1)S(1)}, bf16[640,128]{1,0:T(8,128)(2,1)S(1)}) custom-call(bf16[3072,640]{1,0:T(8,128)(2,1)S(1)} %get-tuple-element.27.refs_0_, bf16[3072,128]{1,0:T(8,128)(2,1)S(1)} %get-tuple-element.28.refs_1_, ...), custom_call_target="tpu_custom_call" | custom-call | flops 377487360 | bytes 983040 | tf_op jit(solution)/shard_map/block_rows/pallas_call | solution.py:181
  9.4 2.6 %collective-permute-start.3 = (bf16[768,128]{1,0:T(8,128)(2,1)S(1)}, bf16[768,128]{1,0:T(8,128)(2,1)S(1)}, u32[]{:S(2)}, u32[]{:S(2)}) collective-permute-start(bf16[768,128]{1,0:T(8,128)(2,1)S(1)} %get-tuple-element.38), channel_id=1, source_target_pairs={{0,8},{4,0},{8,12},{12,4},{1,9},{5,1},{9,13},{13,5},{2,10},{6,2},{... | collective-permute-start | bytes 589832 | tf_op jit(solution)/shard_map/ppermute | solution.py:225
  12.0 1.2 %block_rows.4 = (bf16[768,128]{1,0:T(8,128)(2,1)S(1)}, f32[128,640]{1,0:T(8,128)S(1)}) custom-call(bf16[3072,640]{1,0:T(8,128)(2,1)S(1)} %get-tuple-element.27.refs_0_, bf16[3072,128]{1,0:T(8,128)(2,1)S(1)} %get-tuple-element.28.refs_1_, bf16[128,3072]{1,0:T(8,128)(2,1)S(1)} %get-tuple-element.29.refs_2_, f32[1,640]{1,0:T(1,128)S(1)} %get-tuple-element.30.refs_3_, ...), custom_call_target="tpu_custom_call" | custom-call | flops 377487360 | bytes 983040 | tf_op jit(solution)/shard_map/block_rows/pallas_call | solution.py:181
  13.2 0.0 copy-start
  13.3 0.0 copy-start.1
  13.3 0.0 copy-start.2
  13.3 0.1 collective-permute-start.5
  13.3 2.4 %block_rows.5 = (bf16[768,128]{1,0:T(8,128)(2,1)S(1)}, f32[768,128]{1,0:T(8,128)S(1)}, f32[160,128]{1,0:T(8,128)S(1)}, bf16[160,128]{1,0:T(8,128)(2,1)S(1)}, bf1...) custom-call(bf16[3072,640]{1,0:T(8,128)(2,1)S(1)} %get-tuple-element.27.refs_0_, ...), custom_call_target="tpu_custom_call" | custom-call | flops 754974720 | bytes 1966080 | tf_op jit(solution)/shard_map/block_rows/pallas_call | solution.py:181
  15.8 1.5 %collective-permute-done.3 = bf16[768,128]{1,0:T(8,128)(2,1)S(1)} collective-permute-done((bf16[768,128]{1,0:T(8,128)(2,1)S(1)}, bf16[768,128]{1,0:T(8,128)(2,1)S(1)}, u32[]{:S(2)}, u32[]{:S(2)}) %collective-permute-start.3) | collective-permute-done | bytes 196640 | tf_op jit(solution)/shard_map/ppermute | solution.py:225
  17.3 0.1 add_convert_fusion
  17.4 0.1 collective-permute-start.6
  17.5 1.2 %collective-permute-start.7 = (bf16[160,128]{1,0:T(8,128)(2,1)S(1)}, bf16[160,128]{1,0:T(8,128)(2,1)S(1)}, u32[]{:S(2)}, u32[]{:S(2)}) collective-permute-start(bf16[160,128]{1,0:T(8,128)(2,1)S(1)} %get-tuple-element.48), channel_id=1, source_target_pairs={{0,2},{1,3},{2,0},{3,1},{4,6},{5,7},{6,4},{7,5},{8,10},{9,11},{10,... | collective-permute-start | bytes 122888 | tf_op jit(solution)/shard_map/ppermute | solution.py:196
  18.7 0.6 %collective-permute-start.8 = (bf16[160,128]{1,0:T(8,128)(2,1)S(1)}, bf16[160,128]{1,0:T(8,128)(2,1)S(1)}, u32[]{:S(2)}, u32[]{:S(2)}) collective-permute-start(bf16[160,128]{1,0:T(8,128)(2,1)S(1)} %get-tuple-element.49), channel_id=1, source_target_pairs={{0,3},{1,2},{2,1},{3,0},{4,7},{5,6},{6,5},{7,4},{8,11},{9,10},{10,... | collective-permute-start | bytes 122888 | tf_op jit(solution)/shard_map/ppermute | solution.py:196
  19.3 3.4 %collective-permute-start.4 = (bf16[768,128]{1,0:T(8,128)(2,1)S(1)}, bf16[768,128]{1,0:T(8,128)(2,1)S(1)}, u32[]{:S(2)}, u32[]{:S(2)}) collective-permute-start(bf16[768,128]{1,0:T(8,128)(2,1)S(1)} %add_convert_fusion), channel_id=1, source_target_pairs={{0,8},{4,0},{8,12},{12,4},{1,9},{5,1},{9,13},{13,5},{2,10},{6,2},{... | collective-permute-start | bytes 589832 | tf_op jit(solution)/shard_map/ppermute | solution.py:225
  22.8 0.7 %divide_subtract_fusion = (f32[160,128]{1,0:T(8,128)}, f32[160,128]{1,0:T(8,128)}, f32[160,128]{1,0:T(8,128)}) fusion(f32[160,128]{1,0:T(8,128)S(1)} %copy-done, bf16[160,128]{1,0:T(8,128)(2,1)S(1)} %collective-permute-done.8, bf16[160,128]{1,0:T(8,128)(2,1)S(1)} %collective-permute-done.7, f32[160,128]{1,0:T(8,128)S(1)} %get-tuple-element.45, ...), kind=kLoop, calls=%fused_computation.4 | loop fusion | flops 368640 | bytes 696320 | tf_op jit(solution)/shard_map/sub | solution.py:266
  23.5 3.9 %collective-permute-done.4 = bf16[768,128]{1,0:T(8,128)(2,1)S(1)} collective-permute-done((bf16[768,128]{1,0:T(8,128)(2,1)S(1)}, bf16[768,128]{1,0:T(8,128)(2,1)S(1)}, u32[]{:S(2)}, u32[]{:S(2)}) %collective-permute-start.4) | collective-permute-done | bytes 196640 | tf_op jit(solution)/shard_map/ppermute | solution.py:225
  27.4 0.8 %convert_add_fusion = f32[768,128]{1,0:T(8,128)} fusion(bf16[768,128]{1,0:T(8,128)(2,1)S(1)} %collective-permute-done.5, f32[768,128]{1,0:T(8,128)S(1)} %get-tuple-element.36, bf16[768,128]{1,0:T(8,128)(2,1)S(1)} %collective-permute-done.4), kind=kLoop, calls=%fused_computation | loop fusion | flops 393216 | bytes 1179648 | tf_op jit(solution)/shard_map/add | solution.py:215
  (8 shorter events, 0.0 us)
Async XLA Ops:
  1.5 5.3 %collective-permute-start.2 = (bf16[160,128]{1,0:T(8,128)(2,1)S(1)}, bf16[160,128]{1,0:T(8,128)(2,1)S(1)}, u32[]{:S(2)}, u32[]{:S(2)}) collective-permute-start(bf16[160,128]{1,0:T(8,128)(2,1)S(1)} %convert_element_type.27.refs_5_), channel_id=1, source_target_pairs={{0,3},{1,2},{2,1},{3,0},{4,7},{5,6},{6,5},{7,4},{8,11},{9,10},{10,... | collective-permute-start | bytes 122888 | tf_op jit(solution)/shard_map/ppermute | solution.py:196
  3.9 4.1 %collective-permute-start.1 = (bf16[160,128]{1,0:T(8,128)(2,1)S(1)}, bf16[160,128]{1,0:T(8,128)(2,1)S(1)}, u32[]{:S(2)}, u32[]{:S(2)}) collective-permute-start(bf16[160,128]{1,0:T(8,128)(2,1)S(1)} %convert_element_type.27.refs_5_), channel_id=1, source_target_pairs={{0,2},{1,3},{2,0},{3,1},{4,6},{5,7},{6,4},{7,5},{8,10},{9,11},{10,... | collective-permute-start | bytes 122888 | tf_op jit(solution)/shard_map/ppermute | solution.py:196
  4.5 3.5 %collective-permute-start = (bf16[160,128]{1,0:T(8,128)(2,1)S(1)}, bf16[160,128]{1,0:T(8,128)(2,1)S(1)}, u32[]{:S(2)}, u32[]{:S(2)}) collective-permute-start(bf16[160,128]{1,0:T(8,128)(2,1)S(1)} %convert_element_type.27.refs_5_), channel_id=1, source_target_pairs={{0,1},{1,0},{2,3},{3,2},{4,5},{5,4},{6,7},{7,6},{8,9},{9,8},{10,11... | collective-permute-start | bytes 122888 | tf_op jit(solution)/shard_map/ppermute | solution.py:196
  9.4 8.0 %collective-permute-start.3 = (bf16[768,128]{1,0:T(8,128)(2,1)S(1)}, bf16[768,128]{1,0:T(8,128)(2,1)S(1)}, u32[]{:S(2)}, u32[]{:S(2)}) collective-permute-start(bf16[768,128]{1,0:T(8,128)(2,1)S(1)} %get-tuple-element.38), channel_id=1, source_target_pairs={{0,8},{4,0},{8,12},{12,4},{1,9},{5,1},{9,13},{13,5},{2,10},{6,2},{... | collective-permute-start | bytes 589832 | tf_op jit(solution)/shard_map/ppermute | solution.py:225
  13.2 9.5 %copy-start = (f32[160,128]{1,0:T(8,128)S(1)}, f32[160,128]{1,0:T(8,128)}, u32[]{:S(2)}) copy-start(f32[160,128]{1,0:T(8,128)} %param.11) | copy-start | bytes 245764
  13.3 9.5 %copy-start.1 = (f32[160,128]{1,0:T(8,128)S(1)}, f32[160,128]{1,0:T(8,128)}, u32[]{:S(2)}) copy-start(f32[160,128]{1,0:T(8,128)} %param.12) | copy-start | bytes 245764
  13.3 9.5 %copy-start.2 = (f32[160,128]{1,0:T(8,128)S(1)}, f32[160,128]{1,0:T(8,128)}, u32[]{:S(2)}) copy-start(f32[160,128]{1,0:T(8,128)} %param.13) | copy-start | bytes 245764
  13.3 9.4 %collective-permute-start.5 = (bf16[768,128]{1,0:T(8,128)(2,1)S(1)}, bf16[768,128]{1,0:T(8,128)(2,1)S(1)}, u32[]{:S(2)}, u32[]{:S(2)}) collective-permute-start(bf16[768,128]{1,0:T(8,128)(2,1)S(1)} %get-tuple-element.44), channel_id=1, source_target_pairs={{0,4},{4,12},{8,0},{12,8},{1,5},{5,13},{9,1},{13,9},{2,6},{6,14},{... | collective-permute-start | bytes 589832 | tf_op jit(solution)/shard_map/ppermute | solution.py:225
  17.4 5.3 %collective-permute-start.6 = (bf16[160,128]{1,0:T(8,128)(2,1)S(1)}, bf16[160,128]{1,0:T(8,128)(2,1)S(1)}, u32[]{:S(2)}, u32[]{:S(2)}) collective-permute-start(bf16[160,128]{1,0:T(8,128)(2,1)S(1)} %get-tuple-element.46), channel_id=1, source_target_pairs={{0,1},{1,0},{2,3},{3,2},{4,5},{5,4},{6,7},{7,6},{8,9},{9,8},{10,11... | collective-permute-start | bytes 122888 | tf_op jit(solution)/shard_map/ppermute | solution.py:196
  17.5 5.3 %collective-permute-start.7 = (bf16[160,128]{1,0:T(8,128)(2,1)S(1)}, bf16[160,128]{1,0:T(8,128)(2,1)S(1)}, u32[]{:S(2)}, u32[]{:S(2)}) collective-permute-start(bf16[160,128]{1,0:T(8,128)(2,1)S(1)} %get-tuple-element.48), channel_id=1, source_target_pairs={{0,2},{1,3},{2,0},{3,1},{4,6},{5,7},{6,4},{7,5},{8,10},{9,11},{10,... | collective-permute-start | bytes 122888 | tf_op jit(solution)/shard_map/ppermute | solution.py:196
  18.7 4.0 %collective-permute-start.8 = (bf16[160,128]{1,0:T(8,128)(2,1)S(1)}, bf16[160,128]{1,0:T(8,128)(2,1)S(1)}, u32[]{:S(2)}, u32[]{:S(2)}) collective-permute-start(bf16[160,128]{1,0:T(8,128)(2,1)S(1)} %get-tuple-element.49), channel_id=1, source_target_pairs={{0,3},{1,2},{2,1},{3,0},{4,7},{5,6},{6,5},{7,4},{8,11},{9,10},{10,... | collective-permute-start | bytes 122888 | tf_op jit(solution)/shard_map/ppermute | solution.py:196
  19.3 8.1 %collective-permute-start.4 = (bf16[768,128]{1,0:T(8,128)(2,1)S(1)}, bf16[768,128]{1,0:T(8,128)(2,1)S(1)}, u32[]{:S(2)}, u32[]{:S(2)}) collective-permute-start(bf16[768,128]{1,0:T(8,128)(2,1)S(1)} %add_convert_fusion), channel_id=1, source_target_pairs={{0,8},{4,0},{8,12},{12,4},{1,9},{5,1},{9,13},{13,5},{2,10},{6,2},{... | collective-permute-start | bytes 589832 | tf_op jit(solution)/shard_map/ppermute | solution.py:225

commit v6 on v4

--- a/solution.py
+++ b/solution.py
@@ -185,7 +185,7 @@
         out_specs=(IN_VMEM,) * len(out),
         scratch_shapes=scratch,
         compiler_params=params(),
-        cost_estimate=cost(12 * work * rank, work * 4),
+        cost_estimate=cost(6 * work * rank, work * 2),
         name="block_rows",
     )(*ins)
     done, rest = list(out[: len(tables)]), list(out[len(tables) :])
@@ -215,15 +215,39 @@
     return wide.astype(jnp.float32) + narrow.astype(jnp.float32)
 
 
-def reduce_scatter(size, steps, blocks, mine):
-    came = {}
-    for (way, _), block in zip(steps, blocks):
-        if way in came:
-            block = plus(block, came[way]).astype(jnp.bfloat16)
-        came[way] = lax.ppermute(block, "gene", list(enumerate(around(size, way))))
-    for value in came.values():
-        mine = plus(mine, value)
-    return mine
+def finish_kernel(n_ends, n_parts, *refs):
+    ins, outs = refs[: n_ends + n_parts + 3], refs[n_ends + n_parts + 3 :]
+    ends, parts = ins[:n_ends], ins[n_ends : n_ends + n_parts]
+    factor, first, second = ins[n_ends + n_parts :]
+    grad = parts[0][...]
+    for part in parts[1:]:
+        grad = plus(grad, part[...])
+    new_first = beta_one * first[...] + (1.0 - beta_one) * grad
+    new_second = beta_two * second[...] + (1.0 - beta_two) * grad * grad
+    first_hat = new_first / (1.0 - beta_one**10)
+    second_hat = new_second / (1.0 - beta_two**10)
+    outs[0][...] = factor[...] - learn_rate * first_hat / (jnp.sqrt(second_hat) + adam_eps)
+    outs[1][...] = new_first
+    outs[2][...] = new_second
+    if ends:
+        rows = ends[0][...]
+        for end in ends[1:]:
+            rows = plus(rows, end[...])
+        outs[3][...] = rows
+
+
+def finish(ends, parts, factor, first, second):
+    ins = [*ends, *parts, factor, first, second]
+    shapes = [factor, factor, factor] + list(ends[:1])
+    return pl.pallas_call(
+        functools.partial(finish_kernel, len(ends), len(parts)),
+        out_shape=tuple(jax.ShapeDtypeStruct(like.shape, jnp.float32) for like in shapes),
+        in_specs=[IN_VMEM] * len(ins),
+        out_specs=(IN_VMEM,) * len(shapes),
+        compiler_params=params(),
+        cost_estimate=cost(20 * factor.size, sum(4 * a.size for a in ins)),
+        name="finish",
+    )(*ins)
 
 
 def local(x_slab, cell_factor, row_index, gene_scale, gene_factor, first_moment, second_moment):
@@ -235,32 +259,33 @@
     factor_bf = gene_factor.astype(jnp.bfloat16)
     shares = [factor_bf] + [swap_row(factor_bf, hop, n_row) for hop in range(1, n_row)]
     fixed = prepare(x_slab, row_index, cell_factor, gene_scale, scale_k)
-
-    if 1 < n_gene <= RING_MOST and block % 128 == 0:
-        steps = steps_of(n_gene)
-        tables = [around(n_gene, way * distance) for way, distance in steps] + [tuple(range(n_gene))]
-        kinds = [jnp.bfloat16] * len(steps) + [jnp.float32]
-        cuts = [0, 1, 2, len(tables)] if len(steps) > 2 else [0, 1, len(tables)]
-        carried, blocks = shares, []
-        for low, high in zip(cuts, cuts[1:]):
-            last = high == len(tables)
-            done, carried = block_rows(tables[low:high], kinds[low:high], block, low == 0, last, n_row, fixed, carried)
-            blocks += done
-        parts = carried
-        grad_cells = reduce_scatter(n_gene, steps, blocks[:-1], blocks[-1])
-    else:
+    adam = (gene_factor, first_moment, second_moment)
+
+    if n_gene == 1 or n_gene > RING_MOST or block % 128:
         (rows,), parts = block_rows([(0,)], [jnp.float32], rows_dev, True, True, n_row, fixed, shares)
         grad_cells = lax.psum_scatter(rows, "gene", scatter_dimension=0, tiled=True)
-
-    grad_genes = parts[0]
-    for hop in range(1, n_row):
-        grad_genes = grad_genes + swap_row(parts[hop], hop, n_row).astype(jnp.float32)
-    new_first = beta_one * first_moment + (1.0 - beta_one) * grad_genes
-    new_second = beta_two * second_moment + (1.0 - beta_two) * grad_genes * grad_genes
-    first_hat = new_first / (1.0 - beta_one**10)
-    second_hat = new_second / (1.0 - beta_two**10)
-    new_factor = gene_factor - learn_rate * first_hat / (jnp.sqrt(second_hat) + adam_eps)
-    return (grad_cells, new_factor, new_first, new_second)
+        others = [swap_row(parts[hop], hop, n_row) for hop in range(1, n_row)]
+        return (grad_cells, *finish([], [parts[0], *others], *adam))
+
+    steps = steps_of(n_gene)
+    tables = [around(n_gene, way * distance) for way, distance in steps] + [tuple(range(n_gene))]
+    kinds = [jnp.bfloat16] * len(steps) + [jnp.float32]
+    cuts = [0, 1, 2, len(tables)] if len(steps) > 2 else [0, 1, len(tables)]
+    carried, blocks = shares, []
+    for low, high in zip(cuts, cuts[1:]):
+        last = high == len(tables)
+        done, carried = block_rows(tables[low:high], kinds[low:high], block, low == 0, last, n_row, fixed, carried)
+        blocks += done
+    parts = carried
+
+    came = {}
+    for (way, _), own in zip(steps, blocks):
+        if way in came:
+            own = plus(own, came[way]).astype(jnp.bfloat16)
+        came[way] = lax.ppermute(own, "gene", list(enumerate(around(n_gene, way))))
+    others = [swap_row(parts[hop], hop, n_row) for hop in range(1, n_row)]
+    *adam_out, grad_cells = finish([blocks[-1], *came.values()], [parts[0], *others], *adam)
+    return (grad_cells, *adam_out)
 
 
 def solution(mesh):

time: 30.1 us -> 27.1 us (0.900)
  waiting for transfers between devices: 8.87 us -> 6.09 us
  other arithmetic: 2.5 us -> 0.95 us
  Pallas kernels: 7.24 us -> 8.16 us
  starting transfers between devices: 10.6 us -> 11 us
    ppermute x3, waiting for transfers between devices: 7.67 us -> 2.06 us  [local(): came[way] = lax.ppermute(own, 'gene', list(enumerate(around(n_gene, way))))]
    ppermute x6, waiting for transfers between devices: 1.2 us -> 4.03 us  [swap_row(): lax.ppermute(value, 'row', [(me, partner(me, hop, size)) for me in range(...]
    pallas_call x0 -> x1, Pallas kernels: none -> 0.92 us  [finish(): pl.pallas_call(functools.partial(finish_kernel, len(ends), len(parts)), o...]
    add x1 -> x0, other arithmetic: 0.82 us -> none  [plus(): return wide.astype(jnp.float32) + narrow.astype(jnp.float32)]
    sub x1 -> x0, other arithmetic: 0.73 us -> none  [local(): gene_factor - learn_rate * first_hat / (jnp.sqrt(second_hat) + adam_eps)]
    ppermute x3, starting transfers between devices: 5.61 us -> 6.13 us  [local(): came[way] = lax.ppermute(own, 'gene', list(enumerate(around(n_gene, way))))]
  transfers between devices with their start and end apart: 9 -> 9, of which waited for: 3 -> 5; matrix products, arithmetic and copies ran while one was open for 3% -> 0% of each run, Pallas kernels for 20% -> 22%
where the time goes in v6:
time: 27.1 us; the launch traced here: 27 us
  starting transfers between devices  11 us (41%)
  Pallas kernels  8.16 us (30%)
  waiting for transfers between devices  6.09 us (22%)
  other arithmetic  0.95 us (4%)
  between operations  0.71 us (3%)
    ppermute x3, starting transfers between devices, local(): came[way] = lax.ppermute(own, 'gene', list(enumerate(around(n_gene, way))))  6.13 us
    pallas_call x3, Pallas kernels, block_rows(): pl.pallas_call(functools.partial(rows_kernel, tables, block, first, last,...  4.98 us
    ppermute x6, starting transfers between devices, swap_row(): lax.ppermute(value, 'row', [(me, partner(me, hop, size)) for me in range(...  4.92 us
    ppermute x6, waiting for transfers between devices, swap_row(): lax.ppermute(value, 'row', [(me, partner(me, hop, size)) for me in range(...  4.03 us
    pallas_call x1, Pallas kernels, prepare(): pl.pallas_call(functools.partial(prepare_kernel, scale_k), out_shape=(VME...  2.26 us
    ppermute x3, waiting for transfers between devices, local(): came[way] = lax.ppermute(own, 'gene', list(enumerate(around(n_gene, way))))  2.06 us
    pallas_call x1, Pallas kernels, finish(): pl.pallas_call(functools.partial(finish_kernel, len(ends), len(parts)), o...  0.92 us
    convert_element_type x1, other arithmetic, local(): factor_bf = gene_factor.astype(jnp.bfloat16)  0.9 us
  transfers between devices with their start and end apart: 9, of which 5 were waited for; matrix products, arithmetic and copies ran while one was open for 0% of the time, Pallas kernels for 22%

profile of v6, /device:TPU:0, one launch (start us, length us, event | category | flops | bytes accessed | tf_op | source)
XLA Modules:
  0.0 27.0 jit_solution(13051396959066749084)
XLA Ops:
  0.6 0.9 %convert_element_type.12.refs_5_ = bf16[160,128]{1,0:T(8,128)(2,1)S(1)} convert(f32[160,128]{1,0:T(8,128)} %refs_7_.1) | non-fusion elementwise | flops 20480 | bytes 122880 | tf_op jit(solution)/shard_map/convert_element_type | solution.py:259
  1.5 2.4 %collective-permute-start.2 = (bf16[160,128]{1,0:T(8,128)(2,1)S(1)}, bf16[160,128]{1,0:T(8,128)(2,1)S(1)}, u32[]{:S(2)}, u32[]{:S(2)}) collective-permute-start(bf16[160,128]{1,0:T(8,128)(2,1)S(1)} %convert_element_type.12.refs_5_), channel_id=1, source_target_pairs={{0,3},{1,2},{2,1},{3,0},{4,7},{5,6},{6,5},{7,4},{8,11},{9,10},{10,... | collective-permute-start | bytes 122888 | tf_op jit(solution)/shard_map/ppermute | solution.py:196
  3.9 0.6 %collective-permute-start.1 = (bf16[160,128]{1,0:T(8,128)(2,1)S(1)}, bf16[160,128]{1,0:T(8,128)(2,1)S(1)}, u32[]{:S(2)}, u32[]{:S(2)}) collective-permute-start(bf16[160,128]{1,0:T(8,128)(2,1)S(1)} %convert_element_type.12.refs_5_), channel_id=1, source_target_pairs={{0,2},{1,3},{2,0},{3,1},{4,6},{5,7},{6,4},{7,5},{8,10},{9,11},{10,... | collective-permute-start | bytes 122888 | tf_op jit(solution)/shard_map/ppermute | solution.py:196
  4.5 0.0 collective-permute-start
  4.6 2.3 %prepare.1 = (bf16[3072,640]{1,0:T(8,128)(2,1)S(1)}, bf16[3072,128]{1,0:T(8,128)(2,1)S(1)}, bf16[128,3072]{1,0:T(8,128)(2,1)S(1)}, f32[1,640]{1,0:T(1,128)S(1)}, f32[640,128]{1,0:T(8,128)S(1)}) custom-call(bf16[3072,640]{1,0:T(8,128)(2,1)} %x_in.1, s32[3072]{0:T(1024)} %index_in.1, bf16[512,128]{1,0:T(8,128)(2,1)} %cell_in.1, f32[640]{0:T(1024)} %scale_in.1), custom_call_target="tpu_custom_call" | custom-call | flops 402653184 | bytes 7864320 | tf_op jit(solution)/shard_map/prepare/pallas_call | solution.py:74
  6.9 1.2 %collective-permute-done.1.refs_7_ = bf16[160,128]{1,0:T(8,128)(2,1)S(1)} collective-permute-done((bf16[160,128]{1,0:T(8,128)(2,1)S(1)}, bf16[160,128]{1,0:T(8,128)(2,1)S(1)}, u32[]{:S(2)}, u32[]{:S(2)}) %collective-permute-start.1) | collective-permute-done | bytes 40992 | tf_op jit(solution)/shard_map/ppermute | solution.py:196
  8.1 0.0 collective-permute-done.refs_6_
  8.1 1.3 %block_rows.3 = (bf16[768,128]{1,0:T(8,128)(2,1)S(1)}, f32[128,640]{1,0:T(8,128)S(1)}, bf16[128,640]{1,0:T(8,128)(2,1)S(1)}, bf16[640,128]{1,0:T(8,128)(2,1)S(1)}) custom-call(bf16[3072,640]{1,0:T(8,128)(2,1)S(1)} %get-tuple-element.25.refs_0_, bf16[3072,128]{1,0:T(8,128)(2,1)S(1)} %get-tuple-element.26.refs_1_, ...), custom_call_target="tpu_custom_call" | custom-call | flops 377487360 | bytes 983040 | tf_op jit(solution)/shard_map/block_rows/pallas_call | solution.py:181
  9.4 2.6 %collective-permute-start.3 = (bf16[768,128]{1,0:T(8,128)(2,1)S(1)}, bf16[768,128]{1,0:T(8,128)(2,1)S(1)}, u32[]{:S(2)}, u32[]{:S(2)}) collective-permute-start(bf16[768,128]{1,0:T(8,128)(2,1)S(1)} %get-tuple-element.36), channel_id=1, source_target_pairs={{0,8},{4,0},{8,12},{12,4},{1,9},{5,1},{9,13},{13,5},{2,10},{6,2},{... | collective-permute-start | bytes 589832 | tf_op jit(solution)/shard_map/ppermute | solution.py:285
  12.0 1.2 %block_rows.4 = (bf16[768,128]{1,0:T(8,128)(2,1)S(1)}, f32[128,640]{1,0:T(8,128)S(1)}) custom-call(bf16[3072,640]{1,0:T(8,128)(2,1)S(1)} %get-tuple-element.25.refs_0_, bf16[3072,128]{1,0:T(8,128)(2,1)S(1)} %get-tuple-element.26.refs_1_, bf16[128,3072]{1,0:T(8,128)(2,1)S(1)} %get-tuple-element.27.refs_2_, f32[1,640]{1,0:T(1,128)S(1)} %get-tuple-element.28.refs_3_, ...), custom_call_target="tpu_custom_call" | custom-call | flops 377487360 | bytes 983040 | tf_op jit(solution)/shard_map/block_rows/pallas_call | solution.py:181
  13.2 0.0 copy-start
  13.3 0.0 copy-start.1
  13.3 0.0 copy-start.2
  13.3 0.1 collective-permute-start.5
  13.3 2.4 %block_rows.5 = (bf16[768,128]{1,0:T(8,128)(2,1)S(1)}, f32[768,128]{1,0:T(8,128)S(1)}, f32[160,128]{1,0:T(8,128)S(1)}, bf16[160,128]{1,0:T(8,128)(2,1)S(1)}, bf1...) custom-call(bf16[3072,640]{1,0:T(8,128)(2,1)S(1)} %get-tuple-element.25.refs_0_, ...), custom_call_target="tpu_custom_call" | custom-call | flops 754974720 | bytes 1966080 | tf_op jit(solution)/shard_map/block_rows/pallas_call | solution.py:181
  15.8 1.5 %collective-permute-done.3 = bf16[768,128]{1,0:T(8,128)(2,1)S(1)} collective-permute-done((bf16[768,128]{1,0:T(8,128)(2,1)S(1)}, bf16[768,128]{1,0:T(8,128)(2,1)S(1)}, u32[]{:S(2)}, u32[]{:S(2)}) %collective-permute-start.3) | collective-permute-done | bytes 196640 | tf_op jit(solution)/shard_map/ppermute | solution.py:285
  17.3 0.1 add_convert_fusion
  17.4 3.4 %collective-permute-start.4 = (bf16[768,128]{1,0:T(8,128)(2,1)S(1)}, bf16[768,128]{1,0:T(8,128)(2,1)S(1)}, u32[]{:S(2)}, u32[]{:S(2)}) collective-permute-start(bf16[768,128]{1,0:T(8,128)(2,1)S(1)} %add_convert_fusion), channel_id=1, source_target_pairs={{0,8},{4,0},{8,12},{12,4},{1,9},{5,1},{9,13},{13,5},{2,10},{6,2},{... | collective-permute-start | bytes 589832 | tf_op jit(solution)/shard_map/ppermute | solution.py:285
  20.8 1.2 %collective-permute-start.7 = (bf16[160,128]{1,0:T(8,128)(2,1)S(1)}, bf16[160,128]{1,0:T(8,128)(2,1)S(1)}, u32[]{:S(2)}, u32[]{:S(2)}) collective-permute-start(bf16[160,128]{1,0:T(8,128)(2,1)S(1)} %get-tuple-element.40), channel_id=1, source_target_pairs={{0,2},{1,3},{2,0},{3,1},{4,6},{5,7},{6,4},{7,5},{8,10},{9,11},{10,... | collective-permute-start | bytes 122888 | tf_op jit(solution)/shard_map/ppermute | solution.py:196
  22.0 0.7 %collective-permute-start.8 = (bf16[160,128]{1,0:T(8,128)(2,1)S(1)}, bf16[160,128]{1,0:T(8,128)(2,1)S(1)}, u32[]{:S(2)}, u32[]{:S(2)}) collective-permute-start(bf16[160,128]{1,0:T(8,128)(2,1)S(1)} %get-tuple-element.41), channel_id=1, source_target_pairs={{0,3},{1,2},{2,1},{3,0},{4,7},{5,6},{6,5},{7,4},{8,11},{9,10},{10,... | collective-permute-start | bytes 122888 | tf_op jit(solution)/shard_map/ppermute | solution.py:196
  22.7 2.1 %collective-permute-done.7.refs_5_ = bf16[160,128]{1,0:T(8,128)(2,1)S(1)} collective-permute-done((bf16[160,128]{1,0:T(8,128)(2,1)S(1)}, bf16[160,128]{1,0:T(8,128)(2,1)S(1)}, u32[]{:S(2)}, u32[]{:S(2)}) %collective-permute-start.7) | collective-permute-done | bytes 40992 | tf_op jit(solution)/shard_map/ppermute | solution.py:196
  24.8 0.7 %collective-permute-done.8.refs_6_ = bf16[160,128]{1,0:T(8,128)(2,1)S(1)} collective-permute-done((bf16[160,128]{1,0:T(8,128)(2,1)S(1)}, bf16[160,128]{1,0:T(8,128)(2,1)S(1)}, u32[]{:S(2)}, u32[]{:S(2)}) %collective-permute-start.8) | collective-permute-done | bytes 40992 | tf_op jit(solution)/shard_map/ppermute | solution.py:196
  25.5 0.5 %collective-permute-done.4.refs_1_ = bf16[768,128]{1,0:T(8,128)(2,1)S(1)} collective-permute-done((bf16[768,128]{1,0:T(8,128)(2,1)S(1)}, bf16[768,128]{1,0:T(8,128)(2,1)S(1)}, u32[]{:S(2)}, u32[]{:S(2)}) %collective-permute-start.4) | collective-permute-done | bytes 196640 | tf_op jit(solution)/shard_map/ppermute | solution.py:285
  26.1 0.9 %finish.1 = (f32[160,128]{1,0:T(8,128)}, f32[160,128]{1,0:T(8,128)}, f32[160,128]{1,0:T(8,128)}, f32[768,128]{1,0:T(8,128)}) custom-call(f32[768,128]{1,0:T(8,128)S(1)} %get-tuple-element.34.refs_0_, bf16[768,128]{1,0:T(8,128)(2,1)S(1)} %collective-permute-done.4.refs_1_, bf16[768,128]{1,0:T(8,128)(2,1)S(1)} %collective-permute-done.5.refs_2_, ...), custom_call_target="tpu_custom_call" | custom-call | flops 409600 | bytes 1753088 | tf_op jit(solution)/shard_map/finish/pallas_call | solution.py:242
  (7 shorter events, 0.0 us)
Async XLA Ops:
  1.5 5.3 %collective-permute-start.2 = (bf16[160,128]{1,0:T(8,128)(2,1)S(1)}, bf16[160,128]{1,0:T(8,128)(2,1)S(1)}, u32[]{:S(2)}, u32[]{:S(2)}) collective-permute-start(bf16[160,128]{1,0:T(8,128)(2,1)S(1)} %convert_element_type.12.refs_5_), channel_id=1, source_target_pairs={{0,3},{1,2},{2,1},{3,0},{4,7},{5,6},{6,5},{7,4},{8,11},{9,10},{10,... | collective-permute-start | bytes 122888 | tf_op jit(solution)/shard_map/ppermute | solution.py:196
  3.9 4.1 %collective-permute-start.1 = (bf16[160,128]{1,0:T(8,128)(2,1)S(1)}, bf16[160,128]{1,0:T(8,128)(2,1)S(1)}, u32[]{:S(2)}, u32[]{:S(2)}) collective-permute-start(bf16[160,128]{1,0:T(8,128)(2,1)S(1)} %convert_element_type.12.refs_5_), channel_id=1, source_target_pairs={{0,2},{1,3},{2,0},{3,1},{4,6},{5,7},{6,4},{7,5},{8,10},{9,11},{10,... | collective-permute-start | bytes 122888 | tf_op jit(solution)/shard_map/ppermute | solution.py:196
  4.5 3.5 %collective-permute-start = (bf16[160,128]{1,0:T(8,128)(2,1)S(1)}, bf16[160,128]{1,0:T(8,128)(2,1)S(1)}, u32[]{:S(2)}, u32[]{:S(2)}) collective-permute-start(bf16[160,128]{1,0:T(8,128)(2,1)S(1)} %convert_element_type.12.refs_5_), channel_id=1, source_target_pairs={{0,1},{1,0},{2,3},{3,2},{4,5},{5,4},{6,7},{7,6},{8,9},{9,8},{10,11... | collective-permute-start | bytes 122888 | tf_op jit(solution)/shard_map/ppermute | solution.py:196
  9.4 8.0 %collective-permute-start.3 = (bf16[768,128]{1,0:T(8,128)(2,1)S(1)}, bf16[768,128]{1,0:T(8,128)(2,1)S(1)}, u32[]{:S(2)}, u32[]{:S(2)}) collective-permute-start(bf16[768,128]{1,0:T(8,128)(2,1)S(1)} %get-tuple-element.36), channel_id=1, source_target_pairs={{0,8},{4,0},{8,12},{12,4},{1,9},{5,1},{9,13},{13,5},{2,10},{6,2},{... | collective-permute-start | bytes 589832 | tf_op jit(solution)/shard_map/ppermute | solution.py:285
  13.2 12.8 %copy-start = (f32[160,128]{1,0:T(8,128)S(1)}, f32[160,128]{1,0:T(8,128)}, u32[]{:S(2)}) copy-start(f32[160,128]{1,0:T(8,128)} %refs_7_.1) | copy-start | bytes 245764
  13.3 12.8 %copy-start.1 = (f32[160,128]{1,0:T(8,128)S(1)}, f32[160,128]{1,0:T(8,128)}, u32[]{:S(2)}) copy-start(f32[160,128]{1,0:T(8,128)} %refs_8_.1) | copy-start | bytes 245764
  13.3 12.8 %copy-start.2 = (f32[160,128]{1,0:T(8,128)S(1)}, f32[160,128]{1,0:T(8,128)}, u32[]{:S(2)}) copy-start(f32[160,128]{1,0:T(8,128)} %refs_9_.1) | copy-start | bytes 245764
  13.3 12.3 %collective-permute-start.5 = (bf16[768,128]{1,0:T(8,128)(2,1)S(1)}, bf16[768,128]{1,0:T(8,128)(2,1)S(1)}, u32[]{:S(2)}, u32[]{:S(2)}) collective-permute-start(bf16[768,128]{1,0:T(8,128)(2,1)S(1)} %get-tuple-element.37), channel_id=1, source_target_pairs={{0,4},{4,12},{8,0},{12,8},{1,5},{5,13},{9,1},{13,9},{2,6},{6,14},{... | collective-permute-start | bytes 589832 | tf_op jit(solution)/shard_map/ppermute | solution.py:285
  17.4 8.7 %collective-permute-start.4 = (bf16[768,128]{1,0:T(8,128)(2,1)S(1)}, bf16[768,128]{1,0:T(8,128)(2,1)S(1)}, u32[]{:S(2)}, u32[]{:S(2)}) collective-permute-start(bf16[768,128]{1,0:T(8,128)(2,1)S(1)} %add_convert_fusion), channel_id=1, source_target_pairs={{0,8},{4,0},{8,12},{12,4},{1,9},{5,1},{9,13},{13,5},{2,10},{6,2},{... | collective-permute-start | bytes 589832 | tf_op jit(solution)/shard_map/ppermute | solution.py:285
  20.8 1.9 %collective-permute-start.6 = (bf16[160,128]{1,0:T(8,128)(2,1)S(1)}, bf16[160,128]{1,0:T(8,128)(2,1)S(1)}, u32[]{:S(2)}, u32[]{:S(2)}) collective-permute-start(bf16[160,128]{1,0:T(8,128)(2,1)S(1)} %get-tuple-element.39), channel_id=1, source_target_pairs={{0,1},{1,0},{2,3},{3,2},{4,5},{5,4},{6,7},{7,6},{8,9},{9,8},{10,11... | collective-permute-start | bytes 122888 | tf_op jit(solution)/shard_map/ppermute | solution.py:196
  20.8 4.0 %collective-permute-start.7 = (bf16[160,128]{1,0:T(8,128)(2,1)S(1)}, bf16[160,128]{1,0:T(8,128)(2,1)S(1)}, u32[]{:S(2)}, u32[]{:S(2)}) collective-permute-start(bf16[160,128]{1,0:T(8,128)(2,1)S(1)} %get-tuple-element.40), channel_id=1, source_target_pairs={{0,2},{1,3},{2,0},{3,1},{4,6},{5,7},{6,4},{7,5},{8,10},{9,11},{10,... | collective-permute-start | bytes 122888 | tf_op jit(solution)/shard_map/ppermute | solution.py:196
  22.0 3.5 %collective-permute-start.8 = (bf16[160,128]{1,0:T(8,128)(2,1)S(1)}, bf16[160,128]{1,0:T(8,128)(2,1)S(1)}, u32[]{:S(2)}, u32[]{:S(2)}) collective-permute-start(bf16[160,128]{1,0:T(8,128)(2,1)S(1)} %get-tuple-element.41), channel_id=1, source_target_pairs={{0,3},{1,2},{2,1},{3,0},{4,7},{5,6},{6,5},{7,4},{8,11},{9,10},{10,... | collective-permute-start | bytes 122888 | tf_op jit(solution)/shard_map/ppermute | solution.py:196

commit v7 on v6

--- a/solution.py
+++ b/solution.py
@@ -196,10 +196,6 @@
     return lax.ppermute(value, "row", [(me, partner(me, hop, size)) for me in range(size)])
 
 
-def ring_of(size):
-    return [*range(0, size, 2), *reversed(range(1, size, 2))]
-
-
 def steps_of(size):
     ahead = [(1, distance) for distance in range(size // 2, 0, -1)]
     back = [(-1, distance) for distance in range((size - 1) // 2, 0, -1)]
@@ -207,8 +203,7 @@
 
 
 def around(size, hops):
-    ring = ring_of(size)
-    return tuple(ring[(ring.index(place) + hops) % size] for place in range(size))
+    return tuple((place + hops) % size for place in range(size))
 
 
 def plus(wide, narrow):

time: 27.1 us -> 28.1 us (1.037)
  waiting for transfers between devices: 6.09 us -> 9.14 us
  starting transfers between devices: 11 us -> 8.97 us
    ppermute x3, waiting for transfers between devices: 2.06 us -> 5.08 us  [local(): came[way] = lax.ppermute(own, 'gene', list(enumerate(around(n_gene, way))))]
    ppermute x3, starting transfers between devices: 6.13 us -> 3.98 us  [local(): came[way] = lax.ppermute(own, 'gene', list(enumerate(around(n_gene, way))))]
  transfers between devices with their start and end apart: 9 -> 9, of which waited for: 5 -> 5; matrix products, arithmetic and copies ran while one was open for 0% -> 0% of each run, Pallas kernels for 22% -> 21%
where the time goes in v7:
time: 28.1 us; the launch traced here: 28 us
  waiting for transfers between devices  9.14 us (33%)
  starting transfers between devices  8.97 us (32%)
  Pallas kernels  8.14 us (29%)
  other arithmetic  0.95 us (3%)
  between operations  0.72 us (3%)
    ppermute x3, waiting for transfers between devices, local(): came[way] = lax.ppermute(own, 'gene', list(enumerate(around(n_gene, way))))  5.08 us
    ppermute x6, starting transfers between devices, swap_row(): lax.ppermute(value, 'row', [(me, partner(me, hop, size)) for me in range(...  4.99 us
    pallas_call x3, Pallas kernels, block_rows(): pl.pallas_call(functools.partial(rows_kernel, tables, block, first, last,...  4.97 us
    ppermute x6, waiting for transfers between devices, swap_row(): lax.ppermute(value, 'row', [(me, partner(me, hop, size)) for me in range(...  4.06 us
    ppermute x3, starting transfers between devices, local(): came[way] = lax.ppermute(own, 'gene', list(enumerate(around(n_gene, way))))  3.98 us
    pallas_call x1, Pallas kernels, prepare(): pl.pallas_call(functools.partial(prepare_kernel, scale_k), out_shape=(VME...  2.26 us
    pallas_call x1, Pallas kernels, finish(): pl.pallas_call(functools.partial(finish_kernel, len(ends), len(parts)), o...  0.92 us
    convert_element_type x1, other arithmetic, local(): factor_bf = gene_factor.astype(jnp.bfloat16)  0.9 us
  transfers between devices with their start and end apart: 9, of which 5 were waited for; matrix products, arithmetic and copies ran while one was open for 0% of the time, Pallas kernels for 21%

profile of v7, /device:TPU:0, one launch (start us, length us, event | category | flops | bytes accessed | tf_op | source)
XLA Modules:
  0.0 28.0 jit_solution(10909192816996604729)
XLA Ops:
  0.6 0.9 %convert_element_type.12.refs_5_ = bf16[160,128]{1,0:T(8,128)(2,1)S(1)} convert(f32[160,128]{1,0:T(8,128)} %refs_7_.1) | non-fusion elementwise | flops 20480 | bytes 122880 | tf_op jit(solution)/shard_map/convert_element_type | solution.py:254
  1.5 2.4 %collective-permute-start.2 = (bf16[160,128]{1,0:T(8,128)(2,1)S(1)}, bf16[160,128]{1,0:T(8,128)(2,1)S(1)}, u32[]{:S(2)}, u32[]{:S(2)}) collective-permute-start(bf16[160,128]{1,0:T(8,128)(2,1)S(1)} %convert_element_type.12.refs_5_), channel_id=1, source_target_pairs={{0,3},{1,2},{2,1},{3,0},{4,7},{5,6},{6,5},{7,4},{8,11},{9,10},{10,... | collective-permute-start | bytes 122888 | tf_op jit(solution)/shard_map/ppermute | solution.py:196
  3.9 0.6 %collective-permute-start.1 = (bf16[160,128]{1,0:T(8,128)(2,1)S(1)}, bf16[160,128]{1,0:T(8,128)(2,1)S(1)}, u32[]{:S(2)}, u32[]{:S(2)}) collective-permute-start(bf16[160,128]{1,0:T(8,128)(2,1)S(1)} %convert_element_type.12.refs_5_), channel_id=1, source_target_pairs={{0,2},{1,3},{2,0},{3,1},{4,6},{5,7},{6,4},{7,5},{8,10},{9,11},{10,... | collective-permute-start | bytes 122888 | tf_op jit(solution)/shard_map/ppermute | solution.py:196
  4.5 0.0 collective-permute-start
  4.6 2.3 %prepare.1 = (bf16[3072,640]{1,0:T(8,128)(2,1)S(1)}, bf16[3072,128]{1,0:T(8,128)(2,1)S(1)}, bf16[128,3072]{1,0:T(8,128)(2,1)S(1)}, f32[1,640]{1,0:T(1,128)S(1)}, f32[640,128]{1,0:T(8,128)S(1)}) custom-call(bf16[3072,640]{1,0:T(8,128)(2,1)} %x_in.1, s32[3072]{0:T(1024)} %index_in.1, bf16[512,128]{1,0:T(8,128)(2,1)} %cell_in.1, f32[640]{0:T(1024)} %scale_in.1), custom_call_target="tpu_custom_call" | custom-call | flops 402653184 | bytes 7864320 | tf_op jit(solution)/shard_map/prepare/pallas_call | solution.py:74
  6.9 1.2 %collective-permute-done.1.refs_7_ = bf16[160,128]{1,0:T(8,128)(2,1)S(1)} collective-permute-done((bf16[160,128]{1,0:T(8,128)(2,1)S(1)}, bf16[160,128]{1,0:T(8,128)(2,1)S(1)}, u32[]{:S(2)}, u32[]{:S(2)}) %collective-permute-start.1) | collective-permute-done | bytes 40992 | tf_op jit(solution)/shard_map/ppermute | solution.py:196
  8.1 1.3 %block_rows.3 = (bf16[768,128]{1,0:T(8,128)(2,1)S(1)}, f32[128,640]{1,0:T(8,128)S(1)}, bf16[128,640]{1,0:T(8,128)(2,1)S(1)}, bf16[640,128]{1,0:T(8,128)(2,1)S(1)}) custom-call(bf16[3072,640]{1,0:T(8,128)(2,1)S(1)} %get-tuple-element.25.refs_0_, bf16[3072,128]{1,0:T(8,128)(2,1)S(1)} %get-tuple-element.26.refs_1_, ...), custom_call_target="tpu_custom_call" | custom-call | flops 377487360 | bytes 983040 | tf_op jit(solution)/shard_map/block_rows/pallas_call | solution.py:181
  9.4 1.6 %collective-permute-start.3 = (bf16[768,128]{1,0:T(8,128)(2,1)S(1)}, bf16[768,128]{1,0:T(8,128)(2,1)S(1)}, u32[]{:S(2)}, u32[]{:S(2)}) collective-permute-start(bf16[768,128]{1,0:T(8,128)(2,1)S(1)} %get-tuple-element.36), channel_id=1, source_target_pairs={{0,4},{4,8},{8,12},{12,0},{1,5},{5,9},{9,13},{13,1},{2,6},{6,10},{... | collective-permute-start | bytes 589832 | tf_op jit(solution)/shard_map/ppermute | solution.py:280
  11.0 1.2 %block_rows.4 = (bf16[768,128]{1,0:T(8,128)(2,1)S(1)}, f32[128,640]{1,0:T(8,128)S(1)}) custom-call(bf16[3072,640]{1,0:T(8,128)(2,1)S(1)} %get-tuple-element.25.refs_0_, bf16[3072,128]{1,0:T(8,128)(2,1)S(1)} %get-tuple-element.26.refs_1_, bf16[128,3072]{1,0:T(8,128)(2,1)S(1)} %get-tuple-element.27.refs_2_, f32[1,640]{1,0:T(1,128)S(1)} %get-tuple-element.28.refs_3_, ...), custom_call_target="tpu_custom_call" | custom-call | flops 377487360 | bytes 983040 | tf_op jit(solution)/shard_map/block_rows/pallas_call | solution.py:181
  12.2 0.0 copy-start
  12.2 0.0 copy-start.1
  12.3 0.0 copy-start.2
  12.3 2.3 %collective-permute-start.5 = (bf16[768,128]{1,0:T(8,128)(2,1)S(1)}, bf16[768,128]{1,0:T(8,128)(2,1)S(1)}, u32[]{:S(2)}, u32[]{:S(2)}) collective-permute-start(bf16[768,128]{1,0:T(8,128)(2,1)S(1)} %get-tuple-element.37), channel_id=1, source_target_pairs={{0,12},{4,0},{8,4},{12,8},{1,13},{5,1},{9,5},{13,9},{2,14},{6,2},{... | collective-permute-start | bytes 589832 | tf_op jit(solution)/shard_map/ppermute | solution.py:280
  14.6 2.4 %block_rows.5 = (bf16[768,128]{1,0:T(8,128)(2,1)S(1)}, f32[768,128]{1,0:T(8,128)S(1)}, f32[160,128]{1,0:T(8,128)S(1)}, bf16[160,128]{1,0:T(8,128)(2,1)S(1)}, bf1...) custom-call(bf16[3072,640]{1,0:T(8,128)(2,1)S(1)} %get-tuple-element.25.refs_0_, ...), custom_call_target="tpu_custom_call" | custom-call | flops 754974720 | bytes 1966080 | tf_op jit(solution)/shard_map/block_rows/pallas_call | solution.py:181
  17.0 2.0 %collective-permute-done.3 = bf16[768,128]{1,0:T(8,128)(2,1)S(1)} collective-permute-done((bf16[768,128]{1,0:T(8,128)(2,1)S(1)}, bf16[768,128]{1,0:T(8,128)(2,1)S(1)}, u32[]{:S(2)}, u32[]{:S(2)}) %collective-permute-start.3) | collective-permute-done | bytes 196640 | tf_op jit(solution)/shard_map/ppermute | solution.py:280
  19.0 0.1 add_convert_fusion
  19.1 0.1 collective-permute-start.4
  19.1 0.1 collective-permute-start.6
  19.2 1.2 %collective-permute-start.7 = (bf16[160,128]{1,0:T(8,128)(2,1)S(1)}, bf16[160,128]{1,0:T(8,128)(2,1)S(1)}, u32[]{:S(2)}, u32[]{:S(2)}) collective-permute-start(bf16[160,128]{1,0:T(8,128)(2,1)S(1)} %get-tuple-element.40), channel_id=1, source_target_pairs={{0,2},{1,3},{2,0},{3,1},{4,6},{5,7},{6,4},{7,5},{8,10},{9,11},{10,... | collective-permute-start | bytes 122888 | tf_op jit(solution)/shard_map/ppermute | solution.py:196
  20.4 0.7 %collective-permute-start.8 = (bf16[160,128]{1,0:T(8,128)(2,1)S(1)}, bf16[160,128]{1,0:T(8,128)(2,1)S(1)}, u32[]{:S(2)}, u32[]{:S(2)}) collective-permute-start(bf16[160,128]{1,0:T(8,128)(2,1)S(1)} %get-tuple-element.41), channel_id=1, source_target_pairs={{0,3},{1,2},{2,1},{3,0},{4,7},{5,6},{6,5},{7,4},{8,11},{9,10},{10,... | collective-permute-start | bytes 122888 | tf_op jit(solution)/shard_map/ppermute | solution.py:196
  21.1 2.2 %collective-permute-done.7.refs_5_ = bf16[160,128]{1,0:T(8,128)(2,1)S(1)} collective-permute-done((bf16[160,128]{1,0:T(8,128)(2,1)S(1)}, bf16[160,128]{1,0:T(8,128)(2,1)S(1)}, u32[]{:S(2)}, u32[]{:S(2)}) %collective-permute-start.7) | collective-permute-done | bytes 40992 | tf_op jit(solution)/shard_map/ppermute | solution.py:196
  23.3 0.7 %collective-permute-done.8.refs_6_ = bf16[160,128]{1,0:T(8,128)(2,1)S(1)} collective-permute-done((bf16[160,128]{1,0:T(8,128)(2,1)S(1)}, bf16[160,128]{1,0:T(8,128)(2,1)S(1)}, u32[]{:S(2)}, u32[]{:S(2)}) %collective-permute-start.8) | collective-permute-done | bytes 40992 | tf_op jit(solution)/shard_map/ppermute | solution.py:196
  23.9 3.1 %collective-permute-done.4.refs_1_ = bf16[768,128]{1,0:T(8,128)(2,1)S(1)} collective-permute-done((bf16[768,128]{1,0:T(8,128)(2,1)S(1)}, bf16[768,128]{1,0:T(8,128)(2,1)S(1)}, u32[]{:S(2)}, u32[]{:S(2)}) %collective-permute-start.4) | collective-permute-done | bytes 196640 | tf_op jit(solution)/shard_map/ppermute | solution.py:280
  27.0 0.9 %finish.1 = (f32[160,128]{1,0:T(8,128)}, f32[160,128]{1,0:T(8,128)}, f32[160,128]{1,0:T(8,128)}, f32[768,128]{1,0:T(8,128)}) custom-call(f32[768,128]{1,0:T(8,128)S(1)} %get-tuple-element.34.refs_0_, bf16[768,128]{1,0:T(8,128)(2,1)S(1)} %collective-permute-done.4.refs_1_, bf16[768,128]{1,0:T(8,128)(2,1)S(1)} %collective-permute-done.5.refs_2_, ...), custom_call_target="tpu_custom_call" | custom-call | flops 409600 | bytes 1753088 | tf_op jit(solution)/shard_map/finish/pallas_call | solution.py:237
  (7 shorter events, 0.0 us)
Async XLA Ops:
  1.5 5.3 %collective-permute-start.2 = (bf16[160,128]{1,0:T(8,128)(2,1)S(1)}, bf16[160,128]{1,0:T(8,128)(2,1)S(1)}, u32[]{:S(2)}, u32[]{:S(2)}) collective-permute-start(bf16[160,128]{1,0:T(8,128)(2,1)S(1)} %convert_element_type.12.refs_5_), channel_id=1, source_target_pairs={{0,3},{1,2},{2,1},{3,0},{4,7},{5,6},{6,5},{7,4},{8,11},{9,10},{10,... | collective-permute-start | bytes 122888 | tf_op jit(solution)/shard_map/ppermute | solution.py:196
  3.9 4.1 %collective-permute-start.1 = (bf16[160,128]{1,0:T(8,128)(2,1)S(1)}, bf16[160,128]{1,0:T(8,128)(2,1)S(1)}, u32[]{:S(2)}, u32[]{:S(2)}) collective-permute-start(bf16[160,128]{1,0:T(8,128)(2,1)S(1)} %convert_element_type.12.refs_5_), channel_id=1, source_target_pairs={{0,2},{1,3},{2,0},{3,1},{4,6},{5,7},{6,4},{7,5},{8,10},{9,11},{10,... | collective-permute-start | bytes 122888 | tf_op jit(solution)/shard_map/ppermute | solution.py:196
  4.5 3.5 %collective-permute-start = (bf16[160,128]{1,0:T(8,128)(2,1)S(1)}, bf16[160,128]{1,0:T(8,128)(2,1)S(1)}, u32[]{:S(2)}, u32[]{:S(2)}) collective-permute-start(bf16[160,128]{1,0:T(8,128)(2,1)S(1)} %convert_element_type.12.refs_5_), channel_id=1, source_target_pairs={{0,1},{1,0},{2,3},{3,2},{4,5},{5,4},{6,7},{7,6},{8,9},{9,8},{10,11... | collective-permute-start | bytes 122888 | tf_op jit(solution)/shard_map/ppermute | solution.py:196
  9.4 9.6 %collective-permute-start.3 = (bf16[768,128]{1,0:T(8,128)(2,1)S(1)}, bf16[768,128]{1,0:T(8,128)(2,1)S(1)}, u32[]{:S(2)}, u32[]{:S(2)}) collective-permute-start(bf16[768,128]{1,0:T(8,128)(2,1)S(1)} %get-tuple-element.36), channel_id=1, source_target_pairs={{0,4},{4,8},{8,12},{12,0},{1,5},{5,9},{9,13},{13,1},{2,6},{6,10},{... | collective-permute-start | bytes 589832 | tf_op jit(solution)/shard_map/ppermute | solution.py:280
  12.2 14.8 %copy-start = (f32[160,128]{1,0:T(8,128)S(1)}, f32[160,128]{1,0:T(8,128)}, u32[]{:S(2)}) copy-start(f32[160,128]{1,0:T(8,128)} %refs_7_.1) | copy-start | bytes 245764
  12.2 14.8 %copy-start.1 = (f32[160,128]{1,0:T(8,128)S(1)}, f32[160,128]{1,0:T(8,128)}, u32[]{:S(2)}) copy-start(f32[160,128]{1,0:T(8,128)} %refs_8_.1) | copy-start | bytes 245764
  12.3 14.8 %copy-start.2 = (f32[160,128]{1,0:T(8,128)S(1)}, f32[160,128]{1,0:T(8,128)}, u32[]{:S(2)}) copy-start(f32[160,128]{1,0:T(8,128)} %refs_9_.1) | copy-start | bytes 245764
  12.3 11.7 %collective-permute-start.5 = (bf16[768,128]{1,0:T(8,128)(2,1)S(1)}, bf16[768,128]{1,0:T(8,128)(2,1)S(1)}, u32[]{:S(2)}, u32[]{:S(2)}) collective-permute-start(bf16[768,128]{1,0:T(8,128)(2,1)S(1)} %get-tuple-element.37), channel_id=1, source_target_pairs={{0,12},{4,0},{8,4},{12,8},{1,13},{5,1},{9,5},{13,9},{2,14},{6,2},{... | collective-permute-start | bytes 589832 | tf_op jit(solution)/shard_map/ppermute | solution.py:280
  19.1 8.0 %collective-permute-start.4 = (bf16[768,128]{1,0:T(8,128)(2,1)S(1)}, bf16[768,128]{1,0:T(8,128)(2,1)S(1)}, u32[]{:S(2)}, u32[]{:S(2)}) collective-permute-start(bf16[768,128]{1,0:T(8,128)(2,1)S(1)} %add_convert_fusion), channel_id=1, source_target_pairs={{0,4},{4,8},{8,12},{12,0},{1,5},{5,9},{9,13},{13,1},{2,6},{6,10},{... | collective-permute-start | bytes 589832 | tf_op jit(solution)/shard_map/ppermute | solution.py:280
  19.1 1.9 %collective-permute-start.6 = (bf16[160,128]{1,0:T(8,128)(2,1)S(1)}, bf16[160,128]{1,0:T(8,128)(2,1)S(1)}, u32[]{:S(2)}, u32[]{:S(2)}) collective-permute-start(bf16[160,128]{1,0:T(8,128)(2,1)S(1)} %get-tuple-element.39), channel_id=1, source_target_pairs={{0,1},{1,0},{2,3},{3,2},{4,5},{5,4},{6,7},{7,6},{8,9},{9,8},{10,11... | collective-permute-start | bytes 122888 | tf_op jit(solution)/shard_map/ppermute | solution.py:196
  19.2 4.1 %collective-permute-start.7 = (bf16[160,128]{1,0:T(8,128)(2,1)S(1)}, bf16[160,128]{1,0:T(8,128)(2,1)S(1)}, u32[]{:S(2)}, u32[]{:S(2)}) collective-permute-start(bf16[160,128]{1,0:T(8,128)(2,1)S(1)} %get-tuple-element.40), channel_id=1, source_target_pairs={{0,2},{1,3},{2,0},{3,1},{4,6},{5,7},{6,4},{7,5},{8,10},{9,11},{10,... | collective-permute-start | bytes 122888 | tf_op jit(solution)/shard_map/ppermute | solution.py:196
  20.4 3.5 %collective-permute-start.8 = (bf16[160,128]{1,0:T(8,128)(2,1)S(1)}, bf16[160,128]{1,0:T(8,128)(2,1)S(1)}, u32[]{:S(2)}, u32[]{:S(2)}) collective-permute-start(bf16[160,128]{1,0:T(8,128)(2,1)S(1)} %get-tuple-element.41), channel_id=1, source_target_pairs={{0,3},{1,2},{2,1},{3,0},{4,7},{5,6},{6,5},{7,4},{8,11},{9,10},{10,... | collective-permute-start | bytes 122888 | tf_op jit(solution)/shard_map/ppermute | solution.py:196

commit v8 on v6

--- a/solution.py
+++ b/solution.py
@@ -136,20 +136,39 @@
 
     bend = bend_ref[...]
     step = tile_of(block, 256)
+    tiles = []
     for table, out in zip(tables, rows_out):
         origin = pick("gene", table) * block if len(table) > 1 else 0
         for at in range(0, block, step):
             start = origin + at
             if len(table) > 1:
                 start = pl.multiple_of(start, math.gcd(block, step))
-            here = pl.ds(start, step)
-            pred = jnp.dot(f_ref[here, :], wide, preferred_element_type=jnp.float32)
-            resid = x_ref[here, :].astype(jnp.float32) - pred
-            inside = jnp.maximum(1.0 - resid * resid * bend, 0.0)
-            infl = (resid * (inside * inside)).astype(jnp.bfloat16)
-            out[at : at + step, :] = jnp.dot(infl, scaled, preferred_element_type=jnp.float32).astype(out.dtype)
-            cols = jnp.dot(ft_ref[:, here], infl, preferred_element_type=jnp.float32)
-            total = cols if total is None else total + cols
+            tiles.append((out, at, pl.ds(start, step)))
+
+    def predict(here):
+        return jnp.dot(f_ref[here, :], wide, preferred_element_type=jnp.float32)
+
+    def influence(here, pred):
+        resid = x_ref[here, :].astype(jnp.float32) - pred
+        inside = jnp.maximum(1.0 - resid * resid * bend, 0.0)
+        return (resid * (inside * inside)).astype(jnp.bfloat16)
+
+    def gradients(tile, infl, total):
+        out, at, here = tile
+        cols = jnp.dot(ft_ref[:, here], infl, preferred_element_type=jnp.float32)
+        out[at : at + step, :] = jnp.dot(infl, scaled, preferred_element_type=jnp.float32).astype(out.dtype)
+        return cols if total is None else total + cols
+
+    pred = predict(tiles[0][2])
+    infl = None
+    for at, tile in enumerate(tiles):
+        later = predict(tiles[at + 1][2]) if at + 1 < len(tiles) else None
+        now = influence(tile[2], pred)
+        if at:
+            total = gradients(tiles[at - 1], infl, total)
+        infl, pred = now, later
+    total = gradients(tiles[-1], infl, total)
+
     if first and not last:
         carried_out[1][...] = wide
         carried_out[2][...] = scaled

time: 27.1 us -> 27.1 us (level)
  Pallas kernels: 8.16 us -> 7.73 us
  waiting for transfers between devices: 6.09 us -> 6.48 us
    pallas_call x3, Pallas kernels: 4.98 us -> 4.55 us  [block_rows(): pl.pallas_call(functools.partial(rows_kernel, tables, block, first, last,...]
    ppermute x3, waiting for transfers between devices: 2.06 us -> 2.45 us  [local(): came[way] = lax.ppermute(own, 'gene', list(enumerate(around(n_gene, way))))]
  transfers between devices with their start and end apart: 9 -> 9, of which waited for: 5 -> 5; matrix products, arithmetic and copies ran while one was open for 0% -> 0% of each run, Pallas kernels for 22% -> 21%
where the time goes in v8:
time: 27.1 us; the launch traced here: 26.9 us
  starting transfers between devices  11 us (41%)
  Pallas kernels  7.73 us (29%)
  waiting for transfers between devices  6.48 us (24%)
  other arithmetic  0.95 us (4%)
  between operations  0.71 us (3%)
    ppermute x3, starting transfers between devices, local(): came[way] = lax.ppermute(own, 'gene', list(enumerate(around(n_gene, way))))  6.13 us
    ppermute x6, starting transfers between devices, swap_row(): lax.ppermute(value, 'row', [(me, partner(me, hop, size)) for me in range(...  4.92 us
    pallas_call x3, Pallas kernels, block_rows(): pl.pallas_call(functools.partial(rows_kernel, tables, block, first, last,...  4.55 us
    ppermute x6, waiting for transfers between devices, swap_row(): lax.ppermute(value, 'row', [(me, partner(me, hop, size)) for me in range(...  4.03 us
    ppermute x3, waiting for transfers between devices, local(): came[way] = lax.ppermute(own, 'gene', list(enumerate(around(n_gene, way))))  2.45 us
    pallas_call x1, Pallas kernels, prepare(): pl.pallas_call(functools.partial(prepare_kernel, scale_k), out_shape=(VME...  2.26 us
    pallas_call x1, Pallas kernels, finish(): pl.pallas_call(functools.partial(finish_kernel, len(ends), len(parts)), o...  0.92 us
    convert_element_type x1, other arithmetic, local(): factor_bf = gene_factor.astype(jnp.bfloat16)  0.9 us
  transfers between devices with their start and end apart: 9, of which 5 were waited for; matrix products, arithmetic and copies ran while one was open for 0% of the time, Pallas kernels for 21%

profile of v8, /device:TPU:0, one launch (start us, length us, event | category | flops | bytes accessed | tf_op | source)
XLA Modules:
  0.0 26.9 jit_solution(14513956620901089550)
XLA Ops:
  0.6 0.9 %convert_element_type.12.refs_5_ = bf16[160,128]{1,0:T(8,128)(2,1)S(1)} convert(f32[160,128]{1,0:T(8,128)} %refs_7_.1) | non-fusion elementwise | flops 20480 | bytes 122880 | tf_op jit(solution)/shard_map/convert_element_type | solution.py:278
  1.5 2.4 %collective-permute-start.2 = (bf16[160,128]{1,0:T(8,128)(2,1)S(1)}, bf16[160,128]{1,0:T(8,128)(2,1)S(1)}, u32[]{:S(2)}, u32[]{:S(2)}) collective-permute-start(bf16[160,128]{1,0:T(8,128)(2,1)S(1)} %convert_element_type.12.refs_5_), channel_id=1, source_target_pairs={{0,3},{1,2},{2,1},{3,0},{4,7},{5,6},{6,5},{7,4},{8,11},{9,10},{10,... | collective-permute-start | bytes 122888 | tf_op jit(solution)/shard_map/ppermute | solution.py:215
  3.9 0.6 %collective-permute-start.1 = (bf16[160,128]{1,0:T(8,128)(2,1)S(1)}, bf16[160,128]{1,0:T(8,128)(2,1)S(1)}, u32[]{:S(2)}, u32[]{:S(2)}) collective-permute-start(bf16[160,128]{1,0:T(8,128)(2,1)S(1)} %convert_element_type.12.refs_5_), channel_id=1, source_target_pairs={{0,2},{1,3},{2,0},{3,1},{4,6},{5,7},{6,4},{7,5},{8,10},{9,11},{10,... | collective-permute-start | bytes 122888 | tf_op jit(solution)/shard_map/ppermute | solution.py:215
  4.5 0.0 collective-permute-start
  4.6 2.3 %prepare.1 = (bf16[3072,640]{1,0:T(8,128)(2,1)S(1)}, bf16[3072,128]{1,0:T(8,128)(2,1)S(1)}, bf16[128,3072]{1,0:T(8,128)(2,1)S(1)}, f32[1,640]{1,0:T(1,128)S(1)}, f32[640,128]{1,0:T(8,128)S(1)}) custom-call(bf16[3072,640]{1,0:T(8,128)(2,1)} %x_in.1, s32[3072]{0:T(1024)} %index_in.1, bf16[512,128]{1,0:T(8,128)(2,1)} %cell_in.1, f32[640]{0:T(1024)} %scale_in.1), custom_call_target="tpu_custom_call" | custom-call | flops 402653184 | bytes 7864320 | tf_op jit(solution)/shard_map/prepare/pallas_call | solution.py:74
  6.8 0.0 collective-permute-done.2.refs_8_
  6.9 1.2 %collective-permute-done.1.refs_7_ = bf16[160,128]{1,0:T(8,128)(2,1)S(1)} collective-permute-done((bf16[160,128]{1,0:T(8,128)(2,1)S(1)}, bf16[160,128]{1,0:T(8,128)(2,1)S(1)}, u32[]{:S(2)}, u32[]{:S(2)}) %collective-permute-start.1) | collective-permute-done | bytes 40992 | tf_op jit(solution)/shard_map/ppermute | solution.py:215
  8.1 1.3 %block_rows.3 = (bf16[768,128]{1,0:T(8,128)(2,1)S(1)}, f32[128,640]{1,0:T(8,128)S(1)}, bf16[128,640]{1,0:T(8,128)(2,1)S(1)}, bf16[640,128]{1,0:T(8,128)(2,1)S(1)}) custom-call(bf16[3072,640]{1,0:T(8,128)(2,1)S(1)} %get-tuple-element.25.refs_0_, bf16[3072,128]{1,0:T(8,128)(2,1)S(1)} %get-tuple-element.26.refs_1_, ...), custom_call_target="tpu_custom_call" | custom-call | flops 377487360 | bytes 983040 | tf_op jit(solution)/shard_map/block_rows/pallas_call | solution.py:200
  9.3 2.6 %collective-permute-start.3 = (bf16[768,128]{1,0:T(8,128)(2,1)S(1)}, bf16[768,128]{1,0:T(8,128)(2,1)S(1)}, u32[]{:S(2)}, u32[]{:S(2)}) collective-permute-start(bf16[768,128]{1,0:T(8,128)(2,1)S(1)} %get-tuple-element.36), channel_id=1, source_target_pairs={{0,8},{4,0},{8,12},{12,4},{1,9},{5,1},{9,13},{13,5},{2,10},{6,2},{... | collective-permute-start | bytes 589832 | tf_op jit(solution)/shard_map/ppermute | solution.py:304
  12.0 1.2 %block_rows.4 = (bf16[768,128]{1,0:T(8,128)(2,1)S(1)}, f32[128,640]{1,0:T(8,128)S(1)}) custom-call(bf16[3072,640]{1,0:T(8,128)(2,1)S(1)} %get-tuple-element.25.refs_0_, bf16[3072,128]{1,0:T(8,128)(2,1)S(1)} %get-tuple-element.26.refs_1_, bf16[128,3072]{1,0:T(8,128)(2,1)S(1)} %get-tuple-element.27.refs_2_, f32[1,640]{1,0:T(1,128)S(1)} %get-tuple-element.28.refs_3_, ...), custom_call_target="tpu_custom_call" | custom-call | flops 377487360 | bytes 983040 | tf_op jit(solution)/shard_map/block_rows/pallas_call | solution.py:200
  13.2 0.0 copy-start
  13.2 0.0 copy-start.1
  13.2 0.0 copy-start.2
  13.2 0.1 collective-permute-start.5
  13.3 2.1 %block_rows.5 = (bf16[768,128]{1,0:T(8,128)(2,1)S(1)}, f32[768,128]{1,0:T(8,128)S(1)}, f32[160,128]{1,0:T(8,128)S(1)}, bf16[160,128]{1,0:T(8,128)(2,1)S(1)}, bf1...) custom-call(bf16[3072,640]{1,0:T(8,128)(2,1)S(1)} %get-tuple-element.25.refs_0_, ...), custom_call_target="tpu_custom_call" | custom-call | flops 754974720 | bytes 1966080 | tf_op jit(solution)/shard_map/block_rows/pallas_call | solution.py:200
  15.4 1.9 %collective-permute-done.3 = bf16[768,128]{1,0:T(8,128)(2,1)S(1)} collective-permute-done((bf16[768,128]{1,0:T(8,128)(2,1)S(1)}, bf16[768,128]{1,0:T(8,128)(2,1)S(1)}, u32[]{:S(2)}, u32[]{:S(2)}) %collective-permute-start.3) | collective-permute-done | bytes 196640 | tf_op jit(solution)/shard_map/ppermute | solution.py:304
  17.3 0.1 add_convert_fusion
  17.4 3.4 %collective-permute-start.4 = (bf16[768,128]{1,0:T(8,128)(2,1)S(1)}, bf16[768,128]{1,0:T(8,128)(2,1)S(1)}, u32[]{:S(2)}, u32[]{:S(2)}) collective-permute-start(bf16[768,128]{1,0:T(8,128)(2,1)S(1)} %add_convert_fusion), channel_id=1, source_target_pairs={{0,8},{4,0},{8,12},{12,4},{1,9},{5,1},{9,13},{13,5},{2,10},{6,2},{... | collective-permute-start | bytes 589832 | tf_op jit(solution)/shard_map/ppermute | solution.py:304
  20.8 1.2 %collective-permute-start.7 = (bf16[160,128]{1,0:T(8,128)(2,1)S(1)}, bf16[160,128]{1,0:T(8,128)(2,1)S(1)}, u32[]{:S(2)}, u32[]{:S(2)}) collective-permute-start(bf16[160,128]{1,0:T(8,128)(2,1)S(1)} %get-tuple-element.40), channel_id=1, source_target_pairs={{0,2},{1,3},{2,0},{3,1},{4,6},{5,7},{6,4},{7,5},{8,10},{9,11},{10,... | collective-permute-start | bytes 122888 | tf_op jit(solution)/shard_map/ppermute | solution.py:215
  22.0 0.7 %collective-permute-start.8 = (bf16[160,128]{1,0:T(8,128)(2,1)S(1)}, bf16[160,128]{1,0:T(8,128)(2,1)S(1)}, u32[]{:S(2)}, u32[]{:S(2)}) collective-permute-start(bf16[160,128]{1,0:T(8,128)(2,1)S(1)} %get-tuple-element.41), channel_id=1, source_target_pairs={{0,3},{1,2},{2,1},{3,0},{4,7},{5,6},{6,5},{7,4},{8,11},{9,10},{10,... | collective-permute-start | bytes 122888 | tf_op jit(solution)/shard_map/ppermute | solution.py:215
  22.7 2.1 %collective-permute-done.7.refs_5_ = bf16[160,128]{1,0:T(8,128)(2,1)S(1)} collective-permute-done((bf16[160,128]{1,0:T(8,128)(2,1)S(1)}, bf16[160,128]{1,0:T(8,128)(2,1)S(1)}, u32[]{:S(2)}, u32[]{:S(2)}) %collective-permute-start.7) | collective-permute-done | bytes 40992 | tf_op jit(solution)/shard_map/ppermute | solution.py:215
  24.8 0.7 %collective-permute-done.8.refs_6_ = bf16[160,128]{1,0:T(8,128)(2,1)S(1)} collective-permute-done((bf16[160,128]{1,0:T(8,128)(2,1)S(1)}, bf16[160,128]{1,0:T(8,128)(2,1)S(1)}, u32[]{:S(2)}, u32[]{:S(2)}) %collective-permute-start.8) | collective-permute-done | bytes 40992 | tf_op jit(solution)/shard_map/ppermute | solution.py:215
  25.5 0.5 %collective-permute-done.4.refs_1_ = bf16[768,128]{1,0:T(8,128)(2,1)S(1)} collective-permute-done((bf16[768,128]{1,0:T(8,128)(2,1)S(1)}, bf16[768,128]{1,0:T(8,128)(2,1)S(1)}, u32[]{:S(2)}, u32[]{:S(2)}) %collective-permute-start.4) | collective-permute-done | bytes 196640 | tf_op jit(solution)/shard_map/ppermute | solution.py:304
  26.0 0.9 %finish.1 = (f32[160,128]{1,0:T(8,128)}, f32[160,128]{1,0:T(8,128)}, f32[160,128]{1,0:T(8,128)}, f32[768,128]{1,0:T(8,128)}) custom-call(f32[768,128]{1,0:T(8,128)S(1)} %get-tuple-element.34.refs_0_, bf16[768,128]{1,0:T(8,128)(2,1)S(1)} %collective-permute-done.4.refs_1_, bf16[768,128]{1,0:T(8,128)(2,1)S(1)} %collective-permute-done.5.refs_2_, ...), custom_call_target="tpu_custom_call" | custom-call | flops 409600 | bytes 1753088 | tf_op jit(solution)/shard_map/finish/pallas_call | solution.py:261
  (7 shorter events, 0.0 us)
Async XLA Ops:
  1.5 5.3 %collective-permute-start.2 = (bf16[160,128]{1,0:T(8,128)(2,1)S(1)}, bf16[160,128]{1,0:T(8,128)(2,1)S(1)}, u32[]{:S(2)}, u32[]{:S(2)}) collective-permute-start(bf16[160,128]{1,0:T(8,128)(2,1)S(1)} %convert_element_type.12.refs_5_), channel_id=1, source_target_pairs={{0,3},{1,2},{2,1},{3,0},{4,7},{5,6},{6,5},{7,4},{8,11},{9,10},{10,... | collective-permute-start | bytes 122888 | tf_op jit(solution)/shard_map/ppermute | solution.py:215
  3.9 4.1 %collective-permute-start.1 = (bf16[160,128]{1,0:T(8,128)(2,1)S(1)}, bf16[160,128]{1,0:T(8,128)(2,1)S(1)}, u32[]{:S(2)}, u32[]{:S(2)}) collective-permute-start(bf16[160,128]{1,0:T(8,128)(2,1)S(1)} %convert_element_type.12.refs_5_), channel_id=1, source_target_pairs={{0,2},{1,3},{2,0},{3,1},{4,6},{5,7},{6,4},{7,5},{8,10},{9,11},{10,... | collective-permute-start | bytes 122888 | tf_op jit(solution)/shard_map/ppermute | solution.py:215
  4.5 3.5 %collective-permute-start = (bf16[160,128]{1,0:T(8,128)(2,1)S(1)}, bf16[160,128]{1,0:T(8,128)(2,1)S(1)}, u32[]{:S(2)}, u32[]{:S(2)}) collective-permute-start(bf16[160,128]{1,0:T(8,128)(2,1)S(1)} %convert_element_type.12.refs_5_), channel_id=1, source_target_pairs={{0,1},{1,0},{2,3},{3,2},{4,5},{5,4},{6,7},{7,6},{8,9},{9,8},{10,11... | collective-permute-start | bytes 122888 | tf_op jit(solution)/shard_map/ppermute | solution.py:215
  9.3 8.0 %collective-permute-start.3 = (bf16[768,128]{1,0:T(8,128)(2,1)S(1)}, bf16[768,128]{1,0:T(8,128)(2,1)S(1)}, u32[]{:S(2)}, u32[]{:S(2)}) collective-permute-start(bf16[768,128]{1,0:T(8,128)(2,1)S(1)} %get-tuple-element.36), channel_id=1, source_target_pairs={{0,8},{4,0},{8,12},{12,4},{1,9},{5,1},{9,13},{13,5},{2,10},{6,2},{... | collective-permute-start | bytes 589832 | tf_op jit(solution)/shard_map/ppermute | solution.py:304
  13.2 12.9 %copy-start = (f32[160,128]{1,0:T(8,128)S(1)}, f32[160,128]{1,0:T(8,128)}, u32[]{:S(2)}) copy-start(f32[160,128]{1,0:T(8,128)} %refs_7_.1) | copy-start | bytes 245764
  13.2 12.8 %copy-start.1 = (f32[160,128]{1,0:T(8,128)S(1)}, f32[160,128]{1,0:T(8,128)}, u32[]{:S(2)}) copy-start(f32[160,128]{1,0:T(8,128)} %refs_8_.1) | copy-start | bytes 245764
  13.2 12.8 %copy-start.2 = (f32[160,128]{1,0:T(8,128)S(1)}, f32[160,128]{1,0:T(8,128)}, u32[]{:S(2)}) copy-start(f32[160,128]{1,0:T(8,128)} %refs_9_.1) | copy-start | bytes 245764
  13.2 12.3 %collective-permute-start.5 = (bf16[768,128]{1,0:T(8,128)(2,1)S(1)}, bf16[768,128]{1,0:T(8,128)(2,1)S(1)}, u32[]{:S(2)}, u32[]{:S(2)}) collective-permute-start(bf16[768,128]{1,0:T(8,128)(2,1)S(1)} %get-tuple-element.37), channel_id=1, source_target_pairs={{0,4},{4,12},{8,0},{12,8},{1,5},{5,13},{9,1},{13,9},{2,6},{6,14},{... | collective-permute-start | bytes 589832 | tf_op jit(solution)/shard_map/ppermute | solution.py:304
  17.4 8.7 %collective-permute-start.4 = (bf16[768,128]{1,0:T(8,128)(2,1)S(1)}, bf16[768,128]{1,0:T(8,128)(2,1)S(1)}, u32[]{:S(2)}, u32[]{:S(2)}) collective-permute-start(bf16[768,128]{1,0:T(8,128)(2,1)S(1)} %add_convert_fusion), channel_id=1, source_target_pairs={{0,8},{4,0},{8,12},{12,4},{1,9},{5,1},{9,13},{13,5},{2,10},{6,2},{... | collective-permute-start | bytes 589832 | tf_op jit(solution)/shard_map/ppermute | solution.py:304
  20.8 1.9 %collective-permute-start.6 = (bf16[160,128]{1,0:T(8,128)(2,1)S(1)}, bf16[160,128]{1,0:T(8,128)(2,1)S(1)}, u32[]{:S(2)}, u32[]{:S(2)}) collective-permute-start(bf16[160,128]{1,0:T(8,128)(2,1)S(1)} %get-tuple-element.39), channel_id=1, source_target_pairs={{0,1},{1,0},{2,3},{3,2},{4,5},{5,4},{6,7},{7,6},{8,9},{9,8},{10,11... | collective-permute-start | bytes 122888 | tf_op jit(solution)/shard_map/ppermute | solution.py:215
  20.8 4.0 %collective-permute-start.7 = (bf16[160,128]{1,0:T(8,128)(2,1)S(1)}, bf16[160,128]{1,0:T(8,128)(2,1)S(1)}, u32[]{:S(2)}, u32[]{:S(2)}) collective-permute-start(bf16[160,128]{1,0:T(8,128)(2,1)S(1)} %get-tuple-element.40), channel_id=1, source_target_pairs={{0,2},{1,3},{2,0},{3,1},{4,6},{5,7},{6,4},{7,5},{8,10},{9,11},{10,... | collective-permute-start | bytes 122888 | tf_op jit(solution)/shard_map/ppermute | solution.py:215
  22.0 3.5 %collective-permute-start.8 = (bf16[160,128]{1,0:T(8,128)(2,1)S(1)}, bf16[160,128]{1,0:T(8,128)(2,1)S(1)}, u32[]{:S(2)}, u32[]{:S(2)}) collective-permute-start(bf16[160,128]{1,0:T(8,128)(2,1)S(1)} %get-tuple-element.41), channel_id=1, source_target_pairs={{0,3},{1,2},{2,1},{3,0},{4,7},{5,6},{6,5},{7,4},{8,11},{9,10},{10,... | collective-permute-start | bytes 122888 | tf_op jit(solution)/shard_map/ppermute | solution.py:215

commit v9 on v8

--- a/solution.py
+++ b/solution.py
@@ -110,13 +110,13 @@
     return me ^ hop if size & (size - 1) == 0 else (me + size - hop) % size
 
 
-def rows_kernel(tables, block, first, last, n_row, *refs):
+def rows_kernel(pieces, block, first, last, n_row, *refs):
     refs = list(refs)
     take = lambda count: [refs.pop(0) for _ in range(count)]
     x_ref, f_ref, ft_ref, bend_ref, shrink_ref = take(5)
     shares = take(n_row) if first else None
     carried_in = None if first else take(3)
-    rows_out = take(len(tables))
+    rows_out = take(len(pieces))
     carried_out = None if last else take(3 if first else 1)
     parts_out = take(n_row) if last else None
     me = lax.axis_index("row")
@@ -135,15 +135,15 @@
         total, wide, scaled = (ref[...] for ref in carried_in)
 
     bend = bend_ref[...]
-    step = tile_of(block, 256)
     tiles = []
-    for table, out in zip(tables, rows_out):
+    for (table, low, high), out in zip(pieces, rows_out):
+        step = tile_of(high - low, 256)
         origin = pick("gene", table) * block if len(table) > 1 else 0
-        for at in range(0, block, step):
+        for at in range(low, high, step):
             start = origin + at
             if len(table) > 1:
-                start = pl.multiple_of(start, math.gcd(block, step))
-            tiles.append((out, at, pl.ds(start, step)))
+                start = pl.multiple_of(start, math.gcd(block, low, step))
+            tiles.append((out, at - low, pl.ds(start, step)))
 
     def predict(here):
         return jnp.dot(f_ref[here, :], wide, preferred_element_type=jnp.float32)
@@ -156,7 +156,8 @@
     def gradients(tile, infl, total):
         out, at, here = tile
         cols = jnp.dot(ft_ref[:, here], infl, preferred_element_type=jnp.float32)
-        out[at : at + step, :] = jnp.dot(infl, scaled, preferred_element_type=jnp.float32).astype(out.dtype)
+        rows = jnp.dot(infl, scaled, preferred_element_type=jnp.float32)
+        out[at : at + rows.shape[0], :] = rows.astype(out.dtype)
         return cols if total is None else total + cols
 
     pred = predict(tiles[0][2])
@@ -183,9 +184,9 @@
         parts_out[hop][...] = turned[pl.ds(start, depth), :].astype(parts_out[hop].dtype)
 
 
-def block_rows(tables, kinds, block, first, last, n_row, fixed, carried):
+def block_rows(pieces, kinds, block, first, last, n_row, fixed, carried):
     genes, rank = fixed[4].shape
-    out = [jax.ShapeDtypeStruct((block, rank), kind) for kind in kinds]
+    out = [jax.ShapeDtypeStruct((high - low, rank), kind) for (_, low, high), kind in zip(pieces, kinds)]
     if last:
         out += [jax.ShapeDtypeStruct((genes // n_row, rank), jnp.bfloat16 if hop else jnp.float32) for hop in range(n_row)]
     else:
@@ -196,9 +197,9 @@
     if last:
         scratch.append(VMEM((genes, rank), jnp.float32))
     ins = pinned(*fixed) + (list(carried) if first else pinned(*carried))
-    work = len(tables) * block * genes
+    work = sum(high - low for _, low, high in pieces) * genes
     out = pl.pallas_call(
-        functools.partial(rows_kernel, tables, block, first, last, n_row),
+        functools.partial(rows_kernel, pieces, block, first, last, n_row),
         out_shape=tuple(out),
         in_specs=[IN_VMEM] * len(ins),
         out_specs=(IN_VMEM,) * len(out),
@@ -207,7 +208,7 @@
         cost_estimate=cost(6 * work * rank, work * 2),
         name="block_rows",
     )(*ins)
-    done, rest = list(out[: len(tables)]), list(out[len(tables) :])
+    done, rest = list(out[: len(pieces)]), list(out[len(pieces) :])
     return done, rest if first or last else rest + list(carried[1:])
 
 
@@ -281,29 +282,46 @@
     adam = (gene_factor, first_moment, second_moment)
 
     if n_gene == 1 or n_gene > RING_MOST or block % 128:
-        (rows,), parts = block_rows([(0,)], [jnp.float32], rows_dev, True, True, n_row, fixed, shares)
+        (rows,), parts = block_rows([((0,), 0, rows_dev)], [jnp.float32], rows_dev, True, True, n_row, fixed, shares)
         grad_cells = lax.psum_scatter(rows, "gene", scatter_dimension=0, tiled=True)
         others = [swap_row(parts[hop], hop, n_row) for hop in range(1, n_row)]
         return (grad_cells, *finish([], [parts[0], *others], *adam))
 
     steps = steps_of(n_gene)
-    tables = [around(n_gene, way * distance) for way, distance in steps] + [tuple(range(n_gene))]
-    kinds = [jnp.bfloat16] * len(steps) + [jnp.float32]
-    cuts = [0, 1, 2, len(tables)] if len(steps) > 2 else [0, 1, len(tables)]
-    carried, blocks = shares, []
-    for low, high in zip(cuts, cuts[1:]):
-        last = high == len(tables)
-        done, carried = block_rows(tables[low:high], kinds[low:high], block, low == 0, last, n_row, fixed, carried)
+    cut = tile_of(block, 256)
+    sent = [[(0, cut), (cut, block)] if at == 0 and cut < block else [(0, block)] for at in range(len(steps))]
+    pieces = [(around(n_gene, way * far), low, high) for (way, far), part in zip(steps, sent) for low, high in part]
+    pieces.append((tuple(range(n_gene)), 0, block))
+    alone = len(pieces) - 2
+    targets = {way: list(enumerate(around(n_gene, way))) for way in (1, -1)}
+    carried, blocks, early = shares, [], None
+    for low in range(alone + 1):
+        last = low == alone
+        group = pieces[low:] if last else pieces[low : low + 1]
+        kinds = [jnp.bfloat16] * len(group)
+        if last:
+            kinds[-1] = jnp.float32
+        if last and early is not None:
+            total, _ = lax.optimization_barrier((carried[0], early))
+            carried = [total, *carried[1:]]
+        done, carried = block_rows(group, kinds, block, low == 0, last, n_row, fixed, carried)
         blocks += done
+        if low == 0 and len(sent[0]) > 1:
+            early = lax.ppermute(done[0], "gene", targets[1])
     parts = carried
 
-    came = {}
-    for (way, _), own in zip(steps, blocks):
+    came, at = {}, 0
+    for (way, _), part in zip(steps, sent):
+        values = blocks[at : at + len(part)]
+        at += len(part)
         if way in came:
-            own = plus(own, came[way]).astype(jnp.bfloat16)
-        came[way] = lax.ppermute(own, "gene", list(enumerate(around(n_gene, way))))
+            values = [plus(jnp.concatenate(values), jnp.concatenate(came[way])).astype(jnp.bfloat16)]
+        came[way] = [lax.ppermute(value, "gene", targets[way]) for value in values]
+        if len(part) > 1:
+            came[way][0] = early
+    ends = [jnp.concatenate(value) for value in came.values()]
     others = [swap_row(parts[hop], hop, n_row) for hop in range(1, n_row)]
-    *adam_out, grad_cells = finish([blocks[-1], *came.values()], [parts[0], *others], *adam)
+    *adam_out, grad_cells = finish([blocks[-1], *ends], [parts[0], *others], *adam)
     return (grad_cells, *adam_out)
 
 

time: 27.1 us -> 27.7 us (1.022)
  starting transfers between devices: 11 us -> 13.1 us
  waiting for transfers between devices: 6.48 us -> 4.77 us
    ppermute x3 -> x4, starting transfers between devices: 6.13 us -> 8.22 us  [the longest x3 5.58 us: local(): came[way] = [lax.ppermute(value, 'gene', targets[way]) for value in values]]
    ppermute x3 -> x4, waiting for transfers between devices: 2.45 us -> 0.7 us  [the longest x3 0.69 us: local(): came[way] = [lax.ppermute(value, 'gene', targets[way]) for value in values]]
    pallas_call x3 -> x4, Pallas kernels: 4.55 us -> 4.8 us  [block_rows(): pl.pallas_call(functools.partial(rows_kernel, pieces, block, first, last,...]
  transfers between devices with their start and end apart: 9 -> 10, of which waited for: 5 -> 4; matrix products, arithmetic and copies ran while one was open for 0% -> 0% of each run, Pallas kernels for 21% -> 23%
where the time goes in v9:
time: 27.7 us; the launch traced here: 27.6 us
  starting transfers between devices  13.1 us (47%)
  Pallas kernels  7.98 us (29%)
  waiting for transfers between devices  4.77 us (17%)
  other arithmetic  0.95 us (3%)
  between operations  0.73 us (3%)
    ppermute x3, starting transfers between devices, local(): came[way] = [lax.ppermute(value, 'gene', targets[way]) for value in values]  5.58 us
    ppermute x6, starting transfers between devices, swap_row(): lax.ppermute(value, 'row', [(me, partner(me, hop, size)) for me in range(...  4.92 us
    pallas_call x4, Pallas kernels, block_rows(): pl.pallas_call(functools.partial(rows_kernel, pieces, block, first, last,...  4.8 us
    ppermute x6, waiting for transfers between devices, swap_row(): lax.ppermute(value, 'row', [(me, partner(me, hop, size)) for me in range(...  4.07 us
    ppermute x1, starting transfers between devices, local(): early = lax.ppermute(done[0], 'gene', targets[1])  2.64 us
    pallas_call x1, Pallas kernels, prepare(): pl.pallas_call(functools.partial(prepare_kernel, scale_k), out_shape=(VME...  2.26 us
    pallas_call x1, Pallas kernels, finish(): pl.pallas_call(functools.partial(finish_kernel, len(ends), len(parts)), o...  0.92 us
    convert_element_type x1, other arithmetic, local(): factor_bf = gene_factor.astype(jnp.bfloat16)  0.9 us
  transfers between devices with their start and end apart: 10, of which 4 were waited for; matrix products, arithmetic and copies ran while one was open for 0% of the time, Pallas kernels for 23%

profile of v9, /device:TPU:0, one launch (start us, length us, event | category | flops | bytes accessed | tf_op | source)
XLA Modules:
  0.0 27.6 jit_solution(15273878271514572932)
XLA Ops:
  0.6 0.9 %convert_element_type.12.refs_5_ = bf16[160,128]{1,0:T(8,128)(2,1)S(1)} convert(f32[160,128]{1,0:T(8,128)} %refs_7_.1) | non-fusion elementwise | flops 20480 | bytes 122880 | tf_op jit(solution)/shard_map/convert_element_type | solution.py:279
  1.5 2.4 %collective-permute-start.2 = (bf16[160,128]{1,0:T(8,128)(2,1)S(1)}, bf16[160,128]{1,0:T(8,128)(2,1)S(1)}, u32[]{:S(2)}, u32[]{:S(2)}) collective-permute-start(bf16[160,128]{1,0:T(8,128)(2,1)S(1)} %convert_element_type.12.refs_5_), channel_id=1, source_target_pairs={{0,3},{1,2},{2,1},{3,0},{4,7},{5,6},{6,5},{7,4},{8,11},{9,10},{10,... | collective-permute-start | bytes 122888 | tf_op jit(solution)/shard_map/ppermute | solution.py:216
  3.9 0.6 %collective-permute-start.1 = (bf16[160,128]{1,0:T(8,128)(2,1)S(1)}, bf16[160,128]{1,0:T(8,128)(2,1)S(1)}, u32[]{:S(2)}, u32[]{:S(2)}) collective-permute-start(bf16[160,128]{1,0:T(8,128)(2,1)S(1)} %convert_element_type.12.refs_5_), channel_id=1, source_target_pairs={{0,2},{1,3},{2,0},{3,1},{4,6},{5,7},{6,4},{7,5},{8,10},{9,11},{10,... | collective-permute-start | bytes 122888 | tf_op jit(solution)/shard_map/ppermute | solution.py:216
  4.5 0.0 collective-permute-start
  4.6 2.3 %prepare.1 = (bf16[3072,640]{1,0:T(8,128)(2,1)S(1)}, bf16[3072,128]{1,0:T(8,128)(2,1)S(1)}, bf16[128,3072]{1,0:T(8,128)(2,1)S(1)}, f32[1,640]{1,0:T(1,128)S(1)}, f32[640,128]{1,0:T(8,128)S(1)}) custom-call(bf16[3072,640]{1,0:T(8,128)(2,1)} %x_in.1, s32[3072]{0:T(1024)} %index_in.1, bf16[512,128]{1,0:T(8,128)(2,1)} %cell_in.1, f32[640]{0:T(1024)} %scale_in.1), custom_call_target="tpu_custom_call" | custom-call | flops 402653184 | bytes 7864320 | tf_op jit(solution)/shard_map/prepare/pallas_call | solution.py:74
  6.9 1.2 %collective-permute-done.1.refs_7_ = bf16[160,128]{1,0:T(8,128)(2,1)S(1)} collective-permute-done((bf16[160,128]{1,0:T(8,128)(2,1)S(1)}, bf16[160,128]{1,0:T(8,128)(2,1)S(1)}, u32[]{:S(2)}, u32[]{:S(2)}) %collective-permute-start.1) | collective-permute-done | bytes 40992 | tf_op jit(solution)/shard_map/ppermute | solution.py:216
  8.1 0.7 %block_rows.4 = (bf16[256,128]{1,0:T(8,128)(2,1)S(1)}, f32[128,640]{1,0:T(8,128)S(1)}, bf16[128,640]{1,0:T(8,128)(2,1)S(1)}, bf16[640,128]{1,0:T(8,128)(2,1)S(1)}) custom-call(bf16[3072,640]{1,0:T(8,128)(2,1)S(1)} %get-tuple-element.28.refs_0_, bf16[3072,128]{1,0:T(8,128)(2,1)S(1)} %get-tuple-element.29.refs_1_, ...), custom_call_target="tpu_custom_call" | custom-call | flops 125829120 | bytes 327680 | tf_op jit(solution)/shard_map/block_rows/pallas_call | solution.py:201
  8.8 2.6 %collective-permute-start.3 = (bf16[256,128]{1,0:T(8,128)(2,1)S(1)}, bf16[256,128]{1,0:T(8,128)(2,1)S(1)}, u32[]{:S(2)}, u32[]{:S(2)}) collective-permute-start(bf16[256,128]{1,0:T(8,128)(2,1)S(1)} %get-tuple-element.38), channel_id=1, source_target_pairs={{0,8},{4,0},{8,12},{12,4},{1,9},{5,1},{9,13},{13,5},{2,10},{6,2},{... | collective-permute-start | bytes 196616 | tf_op jit(solution)/shard_map/ppermute | solution.py:310
  11.4 0.8 %block_rows.5 = (bf16[512,128]{1,0:T(8,128)(2,1)S(1)}, f32[128,640]{1,0:T(8,128)S(1)}) custom-call(bf16[3072,640]{1,0:T(8,128)(2,1)S(1)} %get-tuple-element.28.refs_0_, bf16[3072,128]{1,0:T(8,128)(2,1)S(1)} %get-tuple-element.29.refs_1_, bf16[128,3072]{1,0:T(8,128)(2,1)S(1)} %get-tuple-element.30.refs_2_, f32[1,640]{1,0:T(1,128)S(1)} %get-tuple-element.31.refs_3_, ...), custom_call_target="tpu_custom_call" | custom-call | flops 251658240 | bytes 655360 | tf_op jit(solution)/shard_map/block_rows/pallas_call | solution.py:201
  12.2 1.6 %collective-permute-start.4 = (bf16[512,128]{1,0:T(8,128)(2,1)S(1)}, bf16[512,128]{1,0:T(8,128)(2,1)S(1)}, u32[]{:S(2)}, u32[]{:S(2)}) collective-permute-start(bf16[512,128]{1,0:T(8,128)(2,1)S(1)} %get-tuple-element.42), channel_id=1, source_target_pairs={{0,8},{4,0},{8,12},{12,4},{1,9},{5,1},{9,13},{13,5},{2,10},{6,2},{... | collective-permute-start | bytes 393224 | tf_op jit(solution)/shard_map/ppermute | solution.py:319
  13.9 1.2 %block_rows.6 = (bf16[768,128]{1,0:T(8,128)(2,1)S(1)}, f32[128,640]{1,0:T(8,128)S(1)}) custom-call(bf16[3072,640]{1,0:T(8,128)(2,1)S(1)} %get-tuple-element.28.refs_0_, bf16[3072,128]{1,0:T(8,128)(2,1)S(1)} %get-tuple-element.29.refs_1_, bf16[128,3072]{1,0:T(8,128)(2,1)S(1)} %get-tuple-element.30.refs_2_, f32[1,640]{1,0:T(1,128)S(1)} %get-tuple-element.31.refs_3_, ...), custom_call_target="tpu_custom_call" | custom-call | flops 377487360 | bytes 983040 | tf_op jit(solution)/shard_map/block_rows/pallas_call | solution.py:201
  15.0 0.0 copy-start
  15.0 0.0 copy-start.1
  15.1 0.5 %collective-permute-start.6 = (bf16[768,128]{1,0:T(8,128)(2,1)S(1)}, bf16[768,128]{1,0:T(8,128)(2,1)S(1)}, u32[]{:S(2)}, u32[]{:S(2)}) collective-permute-start(bf16[768,128]{1,0:T(8,128)(2,1)S(1)} %get-tuple-element.43), channel_id=1, source_target_pairs={{0,4},{4,12},{8,0},{12,8},{1,5},{5,13},{9,1},{13,9},{2,6},{6,14},{... | collective-permute-start | bytes 589832 | tf_op jit(solution)/shard_map/ppermute | solution.py:319
  15.6 2.1 %block_rows.7 = (bf16[768,128]{1,0:T(8,128)(2,1)S(1)}, f32[768,128]{1,0:T(8,128)S(1)}, f32[160,128]{1,0:T(8,128)S(1)}, bf16[160,128]{1,0:T(8,128)(2,1)S(1)}, bf1...) custom-call(bf16[3072,640]{1,0:T(8,128)(2,1)S(1)} %get-tuple-element.28.refs_0_, ...), custom_call_target="tpu_custom_call" | custom-call | flops 754974720 | bytes 1966080 | tf_op jit(solution)/shard_map/block_rows/pallas_call | solution.py:201
  17.7 0.0 collective-permute-done.4
  17.7 0.1 add_convert_fusion
  17.8 3.4 %collective-permute-start.5 = (bf16[768,128]{1,0:T(8,128)(2,1)S(1)}, bf16[768,128]{1,0:T(8,128)(2,1)S(1)}, u32[]{:S(2)}, u32[]{:S(2)}) collective-permute-start(bf16[768,128]{1,0:T(8,128)(2,1)S(1)} %add_convert_fusion), channel_id=1, source_target_pairs={{0,8},{4,0},{8,12},{12,4},{1,9},{5,1},{9,13},{13,5},{2,10},{6,2},{... | collective-permute-start | bytes 589832 | tf_op jit(solution)/shard_map/ppermute | solution.py:319
  21.2 1.2 %collective-permute-start.8 = (bf16[160,128]{1,0:T(8,128)(2,1)S(1)}, bf16[160,128]{1,0:T(8,128)(2,1)S(1)}, u32[]{:S(2)}, u32[]{:S(2)}) collective-permute-start(bf16[160,128]{1,0:T(8,128)(2,1)S(1)} %get-tuple-element.46), channel_id=1, source_target_pairs={{0,2},{1,3},{2,0},{3,1},{4,6},{5,7},{6,4},{7,5},{8,10},{9,11},{10,... | collective-permute-start | bytes 122888 | tf_op jit(solution)/shard_map/ppermute | solution.py:216
  22.4 0.7 %collective-permute-start.9 = (bf16[160,128]{1,0:T(8,128)(2,1)S(1)}, bf16[160,128]{1,0:T(8,128)(2,1)S(1)}, u32[]{:S(2)}, u32[]{:S(2)}) collective-permute-start(bf16[160,128]{1,0:T(8,128)(2,1)S(1)} %get-tuple-element.47), channel_id=1, source_target_pairs={{0,3},{1,2},{2,1},{3,0},{4,7},{5,6},{6,5},{7,4},{8,11},{9,10},{10,... | collective-permute-start | bytes 122888 | tf_op jit(solution)/shard_map/ppermute | solution.py:216
  23.1 2.1 %collective-permute-done.8.refs_5_ = bf16[160,128]{1,0:T(8,128)(2,1)S(1)} collective-permute-done((bf16[160,128]{1,0:T(8,128)(2,1)S(1)}, bf16[160,128]{1,0:T(8,128)(2,1)S(1)}, u32[]{:S(2)}, u32[]{:S(2)}) %collective-permute-start.8) | collective-permute-done | bytes 40992 | tf_op jit(solution)/shard_map/ppermute | solution.py:216
  25.2 0.7 %collective-permute-done.9.refs_6_ = bf16[160,128]{1,0:T(8,128)(2,1)S(1)} collective-permute-done((bf16[160,128]{1,0:T(8,128)(2,1)S(1)}, bf16[160,128]{1,0:T(8,128)(2,1)S(1)}, u32[]{:S(2)}, u32[]{:S(2)}) %collective-permute-start.9) | collective-permute-done | bytes 40992 | tf_op jit(solution)/shard_map/ppermute | solution.py:216
  26.0 0.7 %collective-permute-done.6.refs_2_ = bf16[768,128]{1,0:T(8,128)(2,1)S(1)} collective-permute-done((bf16[768,128]{1,0:T(8,128)(2,1)S(1)}, bf16[768,128]{1,0:T(8,128)(2,1)S(1)}, u32[]{:S(2)}, u32[]{:S(2)}) %collective-permute-start.6) | collective-permute-done | bytes 196640 | tf_op jit(solution)/shard_map/ppermute | solution.py:319
  26.7 0.9 %finish.1 = (f32[160,128]{1,0:T(8,128)}, f32[160,128]{1,0:T(8,128)}, f32[160,128]{1,0:T(8,128)}, f32[768,128]{1,0:T(8,128)}) custom-call(f32[768,128]{1,0:T(8,128)S(1)} %get-tuple-element.40.refs_0_, bf16[768,128]{1,0:T(8,128)(2,1)S(1)} %collective-permute-done.5.refs_1_, bf16[768,128]{1,0:T(8,128)(2,1)S(1)} %collective-permute-done.6.refs_2_, ...), custom_call_target="tpu_custom_call" | custom-call | flops 409600 | bytes 1753088 | tf_op jit(solution)/shard_map/finish/pallas_call | solution.py:262
  (10 shorter events, 0.0 us)
Async XLA Ops:
  1.5 5.3 %collective-permute-start.2 = (bf16[160,128]{1,0:T(8,128)(2,1)S(1)}, bf16[160,128]{1,0:T(8,128)(2,1)S(1)}, u32[]{:S(2)}, u32[]{:S(2)}) collective-permute-start(bf16[160,128]{1,0:T(8,128)(2,1)S(1)} %convert_element_type.12.refs_5_), channel_id=1, source_target_pairs={{0,3},{1,2},{2,1},{3,0},{4,7},{5,6},{6,5},{7,4},{8,11},{9,10},{10,... | collective-permute-start | bytes 122888 | tf_op jit(solution)/shard_map/ppermute | solution.py:216
  3.9 4.1 %collective-permute-start.1 = (bf16[160,128]{1,0:T(8,128)(2,1)S(1)}, bf16[160,128]{1,0:T(8,128)(2,1)S(1)}, u32[]{:S(2)}, u32[]{:S(2)}) collective-permute-start(bf16[160,128]{1,0:T(8,128)(2,1)S(1)} %convert_element_type.12.refs_5_), channel_id=1, source_target_pairs={{0,2},{1,3},{2,0},{3,1},{4,6},{5,7},{6,4},{7,5},{8,10},{9,11},{10,... | collective-permute-start | bytes 122888 | tf_op jit(solution)/shard_map/ppermute | solution.py:216
  4.5 3.5 %collective-permute-start = (bf16[160,128]{1,0:T(8,128)(2,1)S(1)}, bf16[160,128]{1,0:T(8,128)(2,1)S(1)}, u32[]{:S(2)}, u32[]{:S(2)}) collective-permute-start(bf16[160,128]{1,0:T(8,128)(2,1)S(1)} %convert_element_type.12.refs_5_), channel_id=1, source_target_pairs={{0,1},{1,0},{2,3},{3,2},{4,5},{5,4},{6,7},{7,6},{8,9},{9,8},{10,11... | collective-permute-start | bytes 122888 | tf_op jit(solution)/shard_map/ppermute | solution.py:216
  8.8 6.8 %collective-permute-start.3 = (bf16[256,128]{1,0:T(8,128)(2,1)S(1)}, bf16[256,128]{1,0:T(8,128)(2,1)S(1)}, u32[]{:S(2)}, u32[]{:S(2)}) collective-permute-start(bf16[256,128]{1,0:T(8,128)(2,1)S(1)} %get-tuple-element.38), channel_id=1, source_target_pairs={{0,8},{4,0},{8,12},{12,4},{1,9},{5,1},{9,13},{13,5},{2,10},{6,2},{... | collective-permute-start | bytes 196616 | tf_op jit(solution)/shard_map/ppermute | solution.py:310
  12.2 5.5 %collective-permute-start.4 = (bf16[512,128]{1,0:T(8,128)(2,1)S(1)}, bf16[512,128]{1,0:T(8,128)(2,1)S(1)}, u32[]{:S(2)}, u32[]{:S(2)}) collective-permute-start(bf16[512,128]{1,0:T(8,128)(2,1)S(1)} %get-tuple-element.42), channel_id=1, source_target_pairs={{0,8},{4,0},{8,12},{12,4},{1,9},{5,1},{9,13},{13,5},{2,10},{6,2},{... | collective-permute-start | bytes 393224 | tf_op jit(solution)/shard_map/ppermute | solution.py:319
  15.0 11.6 %copy-start = (f32[160,128]{1,0:T(8,128)S(1)}, f32[160,128]{1,0:T(8,128)}, u32[]{:S(2)}) copy-start(f32[160,128]{1,0:T(8,128)} %refs_7_.1) | copy-start | bytes 245764
  15.0 11.6 %copy-start.1 = (f32[160,128]{1,0:T(8,128)S(1)}, f32[160,128]{1,0:T(8,128)}, u32[]{:S(2)}) copy-start(f32[160,128]{1,0:T(8,128)} %refs_8_.1) | copy-start | bytes 245764
  15.1 11.6 %copy-start.2 = (f32[160,128]{1,0:T(8,128)S(1)}, f32[160,128]{1,0:T(8,128)}, u32[]{:S(2)}) copy-start(f32[160,128]{1,0:T(8,128)} %refs_9_.1) | copy-start | bytes 245764
  15.1 11.6 %collective-permute-start.6 = (bf16[768,128]{1,0:T(8,128)(2,1)S(1)}, bf16[768,128]{1,0:T(8,128)(2,1)S(1)}, u32[]{:S(2)}, u32[]{:S(2)}) collective-permute-start(bf16[768,128]{1,0:T(8,128)(2,1)S(1)} %get-tuple-element.43), channel_id=1, source_target_pairs={{0,4},{4,12},{8,0},{12,8},{1,5},{5,13},{9,1},{13,9},{2,6},{6,14},{... | collective-permute-start | bytes 589832 | tf_op jit(solution)/shard_map/ppermute | solution.py:319
  17.8 8.9 %collective-permute-start.5 = (bf16[768,128]{1,0:T(8,128)(2,1)S(1)}, bf16[768,128]{1,0:T(8,128)(2,1)S(1)}, u32[]{:S(2)}, u32[]{:S(2)}) collective-permute-start(bf16[768,128]{1,0:T(8,128)(2,1)S(1)} %add_convert_fusion), channel_id=1, source_target_pairs={{0,8},{4,0},{8,12},{12,4},{1,9},{5,1},{9,13},{13,5},{2,10},{6,2},{... | collective-permute-start | bytes 589832 | tf_op jit(solution)/shard_map/ppermute | solution.py:319
  21.2 1.9 %collective-permute-start.7 = (bf16[160,128]{1,0:T(8,128)(2,1)S(1)}, bf16[160,128]{1,0:T(8,128)(2,1)S(1)}, u32[]{:S(2)}, u32[]{:S(2)}) collective-permute-start(bf16[160,128]{1,0:T(8,128)(2,1)S(1)} %get-tuple-element.45), channel_id=1, source_target_pairs={{0,1},{1,0},{2,3},{3,2},{4,5},{5,4},{6,7},{7,6},{8,9},{9,8},{10,11... | collective-permute-start | bytes 122888 | tf_op jit(solution)/shard_map/ppermute | solution.py:216
  21.2 4.0 %collective-permute-start.8 = (bf16[160,128]{1,0:T(8,128)(2,1)S(1)}, bf16[160,128]{1,0:T(8,128)(2,1)S(1)}, u32[]{:S(2)}, u32[]{:S(2)}) collective-permute-start(bf16[160,128]{1,0:T(8,128)(2,1)S(1)} %get-tuple-element.46), channel_id=1, source_target_pairs={{0,2},{1,3},{2,0},{3,1},{4,6},{5,7},{6,4},{7,5},{8,10},{9,11},{10,... | collective-permute-start | bytes 122888 | tf_op jit(solution)/shard_map/ppermute | solution.py:216
  22.4 3.5 %collective-permute-start.9 = (bf16[160,128]{1,0:T(8,128)(2,1)S(1)}, bf16[160,128]{1,0:T(8,128)(2,1)S(1)}, u32[]{:S(2)}, u32[]{:S(2)}) collective-permute-start(bf16[160,128]{1,0:T(8,128)(2,1)S(1)} %get-tuple-element.47), channel_id=1, source_target_pairs={{0,3},{1,2},{2,1},{3,0},{4,7},{5,6},{6,5},{7,4},{8,11},{9,10},{10,... | collective-permute-start | bytes 122888 | tf_op jit(solution)/shard_map/ppermute | solution.py:216

commit v10 on v8

--- a/solution.py
+++ b/solution.py
@@ -216,7 +216,7 @@
 
 
 def ring_of(size):
-    return [*range(0, size, 2), *reversed(range(1, size, 2))]
+    return [0, *range(1, size, 2), *reversed(range(2, size, 2))]
 
 
 def steps_of(size):

time: 27.1 us -> 28.8 us (1.063)
  the two profiles are of different devices: /device:TPU:0 before, /device:TPU:9 now
where the time goes in v10:
time: 28.8 us; the launch traced here: 28.7 us
  starting transfers between devices  15 us (52%)
  Pallas kernels  7.73 us (27%)
  waiting for transfers between devices  4.2 us (15%)
  other arithmetic  0.95 us (3%)
  between operations  0.73 us (3%)
    ppermute x6, starting transfers between devices, swap_row(): lax.ppermute(value, 'row', [(me, partner(me, hop, size)) for me in range(...  8.96 us
    ppermute x3, starting transfers between devices, local(): came[way] = lax.ppermute(own, 'gene', list(enumerate(around(n_gene, way))))  6.07 us
    pallas_call x3, Pallas kernels, block_rows(): pl.pallas_call(functools.partial(rows_kernel, tables, block, first, last,...  4.56 us
    ppermute x6, waiting for transfers between devices, swap_row(): lax.ppermute(value, 'row', [(me, partner(me, hop, size)) for me in range(...  3.4 us
    pallas_call x1, Pallas kernels, prepare(): pl.pallas_call(functools.partial(prepare_kernel, scale_k), out_shape=(VME...  2.26 us
    pallas_call x1, Pallas kernels, finish(): pl.pallas_call(functools.partial(finish_kernel, len(ends), len(parts)), o...  0.92 us
    convert_element_type x1, other arithmetic, local(): factor_bf = gene_factor.astype(jnp.bfloat16)  0.9 us
    ppermute x3, waiting for transfers between devices, local(): came[way] = lax.ppermute(own, 'gene', list(enumerate(around(n_gene, way))))  0.8 us
  transfers between devices with their start and end apart: 9, of which 4 were waited for; matrix products, arithmetic and copies ran while one was open for 0% of the time, Pallas kernels for 19%

profile of v10, /device:TPU:9, one launch (start us, length us, event | category | flops | bytes accessed | tf_op | source)
XLA Modules:
  0.0 28.7 jit_solution(2010536042143200921)
XLA Ops:
  0.6 0.9 %convert_element_type.12.refs_5_ = bf16[160,128]{1,0:T(8,128)(2,1)S(1)} convert(f32[160,128]{1,0:T(8,128)} %refs_7_.1) | non-fusion elementwise | flops 20480 | bytes 122880 | tf_op jit(solution)/shard_map/convert_element_type | solution.py:278
  1.5 1.8 %collective-permute-start.2 = (bf16[160,128]{1,0:T(8,128)(2,1)S(1)}, bf16[160,128]{1,0:T(8,128)(2,1)S(1)}, u32[]{:S(2)}, u32[]{:S(2)}) collective-permute-start(bf16[160,128]{1,0:T(8,128)(2,1)S(1)} %convert_element_type.12.refs_5_), channel_id=1, source_target_pairs={{0,3},{1,2},{2,1},{3,0},{4,7},{5,6},{6,5},{7,4},{8,11},{9,10},{10,... | collective-permute-start | bytes 122888 | tf_op jit(solution)/shard_map/ppermute | solution.py:215
  3.3 0.3 collective-permute-start.1
  3.6 0.2 collective-permute-start
  3.8 2.3 %prepare.1 = (bf16[3072,640]{1,0:T(8,128)(2,1)S(1)}, bf16[3072,128]{1,0:T(8,128)(2,1)S(1)}, bf16[128,3072]{1,0:T(8,128)(2,1)S(1)}, f32[1,640]{1,0:T(1,128)S(1)}, f32[640,128]{1,0:T(8,128)S(1)}) custom-call(bf16[3072,640]{1,0:T(8,128)(2,1)} %x_in.1, s32[3072]{0:T(1024)} %index_in.1, bf16[512,128]{1,0:T(8,128)(2,1)} %cell_in.1, f32[640]{0:T(1024)} %scale_in.1), custom_call_target="tpu_custom_call" | custom-call | flops 402653184 | bytes 7864320 | tf_op jit(solution)/shard_map/prepare/pallas_call | solution.py:74
  6.0 0.5 %collective-permute-done.1.refs_7_ = bf16[160,128]{1,0:T(8,128)(2,1)S(1)} collective-permute-done((bf16[160,128]{1,0:T(8,128)(2,1)S(1)}, bf16[160,128]{1,0:T(8,128)(2,1)S(1)}, u32[]{:S(2)}, u32[]{:S(2)}) %collective-permute-start.1) | collective-permute-done | bytes 40992 | tf_op jit(solution)/shard_map/ppermute | solution.py:215
  6.6 0.0 collective-permute-done.refs_6_
  6.6 1.3 %block_rows.3 = (bf16[768,128]{1,0:T(8,128)(2,1)S(1)}, f32[128,640]{1,0:T(8,128)S(1)}, bf16[128,640]{1,0:T(8,128)(2,1)S(1)}, bf16[640,128]{1,0:T(8,128)(2,1)S(1)}) custom-call(bf16[3072,640]{1,0:T(8,128)(2,1)S(1)} %get-tuple-element.25.refs_0_, bf16[3072,128]{1,0:T(8,128)(2,1)S(1)} %get-tuple-element.26.refs_1_, ...), custom_call_target="tpu_custom_call" | custom-call | flops 377487360 | bytes 983040 | tf_op jit(solution)/shard_map/block_rows/pallas_call | solution.py:200
  7.9 2.4 %collective-permute-start.3 = (bf16[768,128]{1,0:T(8,128)(2,1)S(1)}, bf16[768,128]{1,0:T(8,128)(2,1)S(1)}, u32[]{:S(2)}, u32[]{:S(2)}) collective-permute-start(bf16[768,128]{1,0:T(8,128)(2,1)S(1)} %get-tuple-element.36), channel_id=1, source_target_pairs={{0,4},{4,12},{8,0},{12,8},{1,5},{5,13},{9,1},{13,9},{2,6},{6,14},{... | collective-permute-start | bytes 589832 | tf_op jit(solution)/shard_map/ppermute | solution.py:304
  10.2 1.2 %block_rows.4 = (bf16[768,128]{1,0:T(8,128)(2,1)S(1)}, f32[128,640]{1,0:T(8,128)S(1)}) custom-call(bf16[3072,640]{1,0:T(8,128)(2,1)S(1)} %get-tuple-element.25.refs_0_, bf16[3072,128]{1,0:T(8,128)(2,1)S(1)} %get-tuple-element.26.refs_1_, bf16[128,3072]{1,0:T(8,128)(2,1)S(1)} %get-tuple-element.27.refs_2_, f32[1,640]{1,0:T(1,128)S(1)} %get-tuple-element.28.refs_3_, ...), custom_call_target="tpu_custom_call" | custom-call | flops 377487360 | bytes 983040 | tf_op jit(solution)/shard_map/block_rows/pallas_call | solution.py:200
  11.4 0.0 copy-start
  11.4 0.0 copy-start.1
  11.4 0.0 copy-start.2
  11.5 0.1 collective-permute-start.5
  11.5 2.1 %block_rows.5 = (bf16[768,128]{1,0:T(8,128)(2,1)S(1)}, f32[768,128]{1,0:T(8,128)S(1)}, f32[160,128]{1,0:T(8,128)S(1)}, bf16[160,128]{1,0:T(8,128)(2,1)S(1)}, bf1...) custom-call(bf16[3072,640]{1,0:T(8,128)(2,1)S(1)} %get-tuple-element.25.refs_0_, ...), custom_call_target="tpu_custom_call" | custom-call | flops 754974720 | bytes 1966080 | tf_op jit(solution)/shard_map/block_rows/pallas_call | solution.py:200
  13.6 0.8 %collective-permute-done.3 = bf16[768,128]{1,0:T(8,128)(2,1)S(1)} collective-permute-done((bf16[768,128]{1,0:T(8,128)(2,1)S(1)}, bf16[768,128]{1,0:T(8,128)(2,1)S(1)}, u32[]{:S(2)}, u32[]{:S(2)}) %collective-permute-start.3) | collective-permute-done | bytes 196640 | tf_op jit(solution)/shard_map/ppermute | solution.py:304
  14.4 0.1 add_convert_fusion
  14.5 3.6 %collective-permute-start.4 = (bf16[768,128]{1,0:T(8,128)(2,1)S(1)}, bf16[768,128]{1,0:T(8,128)(2,1)S(1)}, u32[]{:S(2)}, u32[]{:S(2)}) collective-permute-start(bf16[768,128]{1,0:T(8,128)(2,1)S(1)} %add_convert_fusion), channel_id=1, source_target_pairs={{0,4},{4,12},{8,0},{12,8},{1,5},{5,13},{9,1},{13,9},{2,6},{6,14},{... | collective-permute-start | bytes 589832 | tf_op jit(solution)/shard_map/ppermute | solution.py:304
  18.1 5.1 %collective-permute-start.6 = (bf16[160,128]{1,0:T(8,128)(2,1)S(1)}, bf16[160,128]{1,0:T(8,128)(2,1)S(1)}, u32[]{:S(2)}, u32[]{:S(2)}) collective-permute-start(bf16[160,128]{1,0:T(8,128)(2,1)S(1)} %get-tuple-element.39), channel_id=1, source_target_pairs={{0,1},{1,0},{2,3},{3,2},{4,5},{5,4},{6,7},{7,6},{8,9},{9,8},{10,11... | collective-permute-start | bytes 122888 | tf_op jit(solution)/shard_map/ppermute | solution.py:215
  23.2 1.0 %collective-permute-start.7 = (bf16[160,128]{1,0:T(8,128)(2,1)S(1)}, bf16[160,128]{1,0:T(8,128)(2,1)S(1)}, u32[]{:S(2)}, u32[]{:S(2)}) collective-permute-start(bf16[160,128]{1,0:T(8,128)(2,1)S(1)} %get-tuple-element.40), channel_id=1, source_target_pairs={{0,2},{1,3},{2,0},{3,1},{4,6},{5,7},{6,4},{7,5},{8,10},{9,11},{10,... | collective-permute-start | bytes 122888 | tf_op jit(solution)/shard_map/ppermute | solution.py:215
  24.2 0.6 %collective-permute-start.8 = (bf16[160,128]{1,0:T(8,128)(2,1)S(1)}, bf16[160,128]{1,0:T(8,128)(2,1)S(1)}, u32[]{:S(2)}, u32[]{:S(2)}) collective-permute-start(bf16[160,128]{1,0:T(8,128)(2,1)S(1)} %get-tuple-element.41), channel_id=1, source_target_pairs={{0,3},{1,2},{2,1},{3,0},{4,7},{5,6},{6,5},{7,4},{8,11},{9,10},{10,... | collective-permute-start | bytes 122888 | tf_op jit(solution)/shard_map/ppermute | solution.py:215
  24.9 1.2 %collective-permute-done.7.refs_5_ = bf16[160,128]{1,0:T(8,128)(2,1)S(1)} collective-permute-done((bf16[160,128]{1,0:T(8,128)(2,1)S(1)}, bf16[160,128]{1,0:T(8,128)(2,1)S(1)}, u32[]{:S(2)}, u32[]{:S(2)}) %collective-permute-start.7) | collective-permute-done | bytes 40992 | tf_op jit(solution)/shard_map/ppermute | solution.py:215
  26.1 1.6 %collective-permute-done.8.refs_6_ = bf16[160,128]{1,0:T(8,128)(2,1)S(1)} collective-permute-done((bf16[160,128]{1,0:T(8,128)(2,1)S(1)}, bf16[160,128]{1,0:T(8,128)(2,1)S(1)}, u32[]{:S(2)}, u32[]{:S(2)}) %collective-permute-start.8) | collective-permute-done | bytes 40992 | tf_op jit(solution)/shard_map/ppermute | solution.py:215
  27.7 0.9 %finish.1 = (f32[160,128]{1,0:T(8,128)}, f32[160,128]{1,0:T(8,128)}, f32[160,128]{1,0:T(8,128)}, f32[768,128]{1,0:T(8,128)}) custom-call(f32[768,128]{1,0:T(8,128)S(1)} %get-tuple-element.34.refs_0_, bf16[768,128]{1,0:T(8,128)(2,1)S(1)} %collective-permute-done.4.refs_1_, bf16[768,128]{1,0:T(8,128)(2,1)S(1)} %collective-permute-done.5.refs_2_, ...), custom_call_target="tpu_custom_call" | custom-call | flops 409600 | bytes 1753088 | tf_op jit(solution)/shard_map/finish/pallas_call | solution.py:261
  (7 shorter events, 0.0 us)
Async XLA Ops:
  1.5 4.5 %collective-permute-start.2 = (bf16[160,128]{1,0:T(8,128)(2,1)S(1)}, bf16[160,128]{1,0:T(8,128)(2,1)S(1)}, u32[]{:S(2)}, u32[]{:S(2)}) collective-permute-start(bf16[160,128]{1,0:T(8,128)(2,1)S(1)} %convert_element_type.12.refs_5_), channel_id=1, source_target_pairs={{0,3},{1,2},{2,1},{3,0},{4,7},{5,6},{6,5},{7,4},{8,11},{9,10},{10,... | collective-permute-start | bytes 122888 | tf_op jit(solution)/shard_map/ppermute | solution.py:215
  3.3 3.3 %collective-permute-start.1 = (bf16[160,128]{1,0:T(8,128)(2,1)S(1)}, bf16[160,128]{1,0:T(8,128)(2,1)S(1)}, u32[]{:S(2)}, u32[]{:S(2)}) collective-permute-start(bf16[160,128]{1,0:T(8,128)(2,1)S(1)} %convert_element_type.12.refs_5_), channel_id=1, source_target_pairs={{0,2},{1,3},{2,0},{3,1},{4,6},{5,7},{6,4},{7,5},{8,10},{9,11},{10,... | collective-permute-start | bytes 122888 | tf_op jit(solution)/shard_map/ppermute | solution.py:215
  3.6 3.0 %collective-permute-start = (bf16[160,128]{1,0:T(8,128)(2,1)S(1)}, bf16[160,128]{1,0:T(8,128)(2,1)S(1)}, u32[]{:S(2)}, u32[]{:S(2)}) collective-permute-start(bf16[160,128]{1,0:T(8,128)(2,1)S(1)} %convert_element_type.12.refs_5_), channel_id=1, source_target_pairs={{0,1},{1,0},{2,3},{3,2},{4,5},{5,4},{6,7},{7,6},{8,9},{9,8},{10,11... | collective-permute-start | bytes 122888 | tf_op jit(solution)/shard_map/ppermute | solution.py:215
  7.9 6.6 %collective-permute-start.3 = (bf16[768,128]{1,0:T(8,128)(2,1)S(1)}, bf16[768,128]{1,0:T(8,128)(2,1)S(1)}, u32[]{:S(2)}, u32[]{:S(2)}) collective-permute-start(bf16[768,128]{1,0:T(8,128)(2,1)S(1)} %get-tuple-element.36), channel_id=1, source_target_pairs={{0,4},{4,12},{8,0},{12,8},{1,5},{5,13},{9,1},{13,9},{2,6},{6,14},{... | collective-permute-start | bytes 589832 | tf_op jit(solution)/shard_map/ppermute | solution.py:304
  11.4 16.3 %copy-start = (f32[160,128]{1,0:T(8,128)S(1)}, f32[160,128]{1,0:T(8,128)}, u32[]{:S(2)}) copy-start(f32[160,128]{1,0:T(8,128)} %refs_7_.1) | copy-start | bytes 245764
  11.4 16.3 %copy-start.1 = (f32[160,128]{1,0:T(8,128)S(1)}, f32[160,128]{1,0:T(8,128)}, u32[]{:S(2)}) copy-start(f32[160,128]{1,0:T(8,128)} %refs_8_.1) | copy-start | bytes 245764
  11.4 16.3 %copy-start.2 = (f32[160,128]{1,0:T(8,128)S(1)}, f32[160,128]{1,0:T(8,128)}, u32[]{:S(2)}) copy-start(f32[160,128]{1,0:T(8,128)} %refs_9_.1) | copy-start | bytes 245764
  11.5 16.2 %collective-permute-start.5 = (bf16[768,128]{1,0:T(8,128)(2,1)S(1)}, bf16[768,128]{1,0:T(8,128)(2,1)S(1)}, u32[]{:S(2)}, u32[]{:S(2)}) collective-permute-start(bf16[768,128]{1,0:T(8,128)(2,1)S(1)} %get-tuple-element.37), channel_id=1, source_target_pairs={{0,8},{4,0},{8,12},{12,4},{1,9},{5,1},{9,13},{13,5},{2,10},{6,2},{... | collective-permute-start | bytes 589832 | tf_op jit(solution)/shard_map/ppermute | solution.py:304
  14.5 13.2 %collective-permute-start.4 = (bf16[768,128]{1,0:T(8,128)(2,1)S(1)}, bf16[768,128]{1,0:T(8,128)(2,1)S(1)}, u32[]{:S(2)}, u32[]{:S(2)}) collective-permute-start(bf16[768,128]{1,0:T(8,128)(2,1)S(1)} %add_convert_fusion), channel_id=1, source_target_pairs={{0,4},{4,12},{8,0},{12,8},{1,5},{5,13},{9,1},{13,9},{2,6},{6,14},{... | collective-permute-start | bytes 589832 | tf_op jit(solution)/shard_map/ppermute | solution.py:304
  18.1 6.7 %collective-permute-start.6 = (bf16[160,128]{1,0:T(8,128)(2,1)S(1)}, bf16[160,128]{1,0:T(8,128)(2,1)S(1)}, u32[]{:S(2)}, u32[]{:S(2)}) collective-permute-start(bf16[160,128]{1,0:T(8,128)(2,1)S(1)} %get-tuple-element.39), channel_id=1, source_target_pairs={{0,1},{1,0},{2,3},{3,2},{4,5},{5,4},{6,7},{7,6},{8,9},{9,8},{10,11... | collective-permute-start | bytes 122888 | tf_op jit(solution)/shard_map/ppermute | solution.py:215
  23.2 2.9 %collective-permute-start.7 = (bf16[160,128]{1,0:T(8,128)(2,1)S(1)}, bf16[160,128]{1,0:T(8,128)(2,1)S(1)}, u32[]{:S(2)}, u32[]{:S(2)}) collective-permute-start(bf16[160,128]{1,0:T(8,128)(2,1)S(1)} %get-tuple-element.40), channel_id=1, source_target_pairs={{0,2},{1,3},{2,0},{3,1},{4,6},{5,7},{6,4},{7,5},{8,10},{9,11},{10,... | collective-permute-start | bytes 122888 | tf_op jit(solution)/shard_map/ppermute | solution.py:215
  24.2 3.5 %collective-permute-start.8 = (bf16[160,128]{1,0:T(8,128)(2,1)S(1)}, bf16[160,128]{1,0:T(8,128)(2,1)S(1)}, u32[]{:S(2)}, u32[]{:S(2)}) collective-permute-start(bf16[160,128]{1,0:T(8,128)(2,1)S(1)} %get-tuple-element.41), channel_id=1, source_target_pairs={{0,3},{1,2},{2,1},{3,0},{4,7},{5,6},{6,5},{7,4},{8,11},{9,10},{10,... | collective-permute-start | bytes 122888 | tf_op jit(solution)/shard_map/ppermute | solution.py:215

commit v11 on v10

--- a/solution.py
+++ b/solution.py
@@ -215,10 +215,6 @@
     return lax.ppermute(value, "row", [(me, partner(me, hop, size)) for me in range(size)])
 
 
-def ring_of(size):
-    return [0, *range(1, size, 2), *reversed(range(2, size, 2))]
-
-
 def steps_of(size):
     ahead = [(1, distance) for distance in range(size // 2, 0, -1)]
     back = [(-1, distance) for distance in range((size - 1) // 2, 0, -1)]
@@ -226,8 +222,7 @@
 
 
 def around(size, hops):
-    ring = ring_of(size)
-    return tuple(ring[(ring.index(place) + hops) % size] for place in range(size))
+    return tuple((place + hops) % size for place in range(size))
 
 
 def plus(wide, narrow):
@@ -289,7 +284,7 @@
     steps = steps_of(n_gene)
     tables = [around(n_gene, way * distance) for way, distance in steps] + [tuple(range(n_gene))]
     kinds = [jnp.bfloat16] * len(steps) + [jnp.float32]
-    cuts = [0, 1, 2, len(tables)] if len(steps) > 2 else [0, 1, len(tables)]
+    cuts = [0, 1, len(tables)]
     carried, blocks = shares, []
     for low, high in zip(cuts, cuts[1:]):
         last = high == len(tables)

time: 28.8 us -> 27.7 us (0.962)
  the two profiles are of different devices: /device:TPU:9 before, /device:TPU:0 now
where the time goes in v11:
time: 27.7 us; the launch traced here: 27.5 us
  waiting for transfers between devices  9.47 us (34%)
  starting transfers between devices  8.96 us (32%)
  Pallas kernels  7.4 us (27%)
  other arithmetic  0.95 us (3%)
  between operations  0.71 us (3%)
    ppermute x3, waiting for transfers between devices, local(): came[way] = lax.ppermute(own, 'gene', list(enumerate(around(n_gene, way))))  5.11 us
    ppermute x6, starting transfers between devices, swap_row(): lax.ppermute(value, 'row', [(me, partner(me, hop, size)) for me in range(...  4.99 us
    ppermute x6, waiting for transfers between devices, swap_row(): lax.ppermute(value, 'row', [(me, partner(me, hop, size)) for me in range(...  4.36 us
    pallas_call x2, Pallas kernels, block_rows(): pl.pallas_call(functools.partial(rows_kernel, tables, block, first, last,...  4.22 us
    ppermute x3, starting transfers between devices, local(): came[way] = lax.ppermute(own, 'gene', list(enumerate(around(n_gene, way))))  3.97 us
    pallas_call x1, Pallas kernels, prepare(): pl.pallas_call(functools.partial(prepare_kernel, scale_k), out_shape=(VME...  2.26 us
    pallas_call x1, Pallas kernels, finish(): pl.pallas_call(functools.partial(finish_kernel, len(ends), len(parts)), o...  0.92 us
    convert_element_type x1, other arithmetic, local(): factor_bf = gene_factor.astype(jnp.bfloat16)  0.9 us
  transfers between devices with their start and end apart: 9, of which 5 were waited for; matrix products, arithmetic and copies ran while one was open for 0% of the time, Pallas kernels for 19%

profile of v11, /device:TPU:0, one launch (start us, length us, event | category | flops | bytes accessed | tf_op | source)
XLA Modules:
  0.0 27.5 jit_solution(6147446929047459537)
XLA Ops:
  0.6 0.9 %convert_element_type.12.refs_5_ = bf16[160,128]{1,0:T(8,128)(2,1)S(1)} convert(f32[160,128]{1,0:T(8,128)} %refs_7_.1) | non-fusion elementwise | flops 20480 | bytes 122880 | tf_op jit(solution)/shard_map/convert_element_type | solution.py:273
  1.5 2.4 %collective-permute-start.2 = (bf16[160,128]{1,0:T(8,128)(2,1)S(1)}, bf16[160,128]{1,0:T(8,128)(2,1)S(1)}, u32[]{:S(2)}, u32[]{:S(2)}) collective-permute-start(bf16[160,128]{1,0:T(8,128)(2,1)S(1)} %convert_element_type.12.refs_5_), channel_id=1, source_target_pairs={{0,3},{1,2},{2,1},{3,0},{4,7},{5,6},{6,5},{7,4},{8,11},{9,10},{10,... | collective-permute-start | bytes 122888 | tf_op jit(solution)/shard_map/ppermute | solution.py:215
  3.9 0.6 %collective-permute-start.1 = (bf16[160,128]{1,0:T(8,128)(2,1)S(1)}, bf16[160,128]{1,0:T(8,128)(2,1)S(1)}, u32[]{:S(2)}, u32[]{:S(2)}) collective-permute-start(bf16[160,128]{1,0:T(8,128)(2,1)S(1)} %convert_element_type.12.refs_5_), channel_id=1, source_target_pairs={{0,2},{1,3},{2,0},{3,1},{4,6},{5,7},{6,4},{7,5},{8,10},{9,11},{10,... | collective-permute-start | bytes 122888 | tf_op jit(solution)/shard_map/ppermute | solution.py:215
  4.5 0.0 collective-permute-start
  4.6 2.3 %prepare.1 = (bf16[3072,640]{1,0:T(8,128)(2,1)S(1)}, bf16[3072,128]{1,0:T(8,128)(2,1)S(1)}, bf16[128,3072]{1,0:T(8,128)(2,1)S(1)}, f32[1,640]{1,0:T(1,128)S(1)}, f32[640,128]{1,0:T(8,128)S(1)}) custom-call(bf16[3072,640]{1,0:T(8,128)(2,1)} %x_in.1, s32[3072]{0:T(1024)} %index_in.1, bf16[512,128]{1,0:T(8,128)(2,1)} %cell_in.1, f32[640]{0:T(1024)} %scale_in.1), custom_call_target="tpu_custom_call" | custom-call | flops 402653184 | bytes 7864320 | tf_op jit(solution)/shard_map/prepare/pallas_call | solution.py:74
  6.9 1.2 %collective-permute-done.1.refs_7_ = bf16[160,128]{1,0:T(8,128)(2,1)S(1)} collective-permute-done((bf16[160,128]{1,0:T(8,128)(2,1)S(1)}, bf16[160,128]{1,0:T(8,128)(2,1)S(1)}, u32[]{:S(2)}, u32[]{:S(2)}) %collective-permute-start.1) | collective-permute-done | bytes 40992 | tf_op jit(solution)/shard_map/ppermute | solution.py:215
  8.1 0.0 collective-permute-done.refs_6_
  8.1 1.3 %block_rows.2 = (bf16[768,128]{1,0:T(8,128)(2,1)S(1)}, f32[128,640]{1,0:T(8,128)S(1)}, bf16[128,640]{1,0:T(8,128)(2,1)S(1)}, bf16[640,128]{1,0:T(8,128)(2,1)S(1)}) custom-call(bf16[3072,640]{1,0:T(8,128)(2,1)S(1)} %get-tuple-element.24.refs_0_, bf16[3072,128]{1,0:T(8,128)(2,1)S(1)} %get-tuple-element.25.refs_1_, ...), custom_call_target="tpu_custom_call" | custom-call | flops 377487360 | bytes 983040 | tf_op jit(solution)/shard_map/block_rows/pallas_call | solution.py:200
  9.3 0.0 copy-start
  9.4 0.0 copy-start.1
  9.4 0.0 copy-start.2
  9.4 1.6 %collective-permute-start.3 = (bf16[768,128]{1,0:T(8,128)(2,1)S(1)}, bf16[768,128]{1,0:T(8,128)(2,1)S(1)}, u32[]{:S(2)}, u32[]{:S(2)}) collective-permute-start(bf16[768,128]{1,0:T(8,128)(2,1)S(1)} %get-tuple-element.34), channel_id=1, source_target_pairs={{0,4},{4,8},{8,12},{12,0},{1,5},{5,9},{9,13},{13,1},{2,6},{6,10},{... | collective-permute-start | bytes 589832 | tf_op jit(solution)/shard_map/ppermute | solution.py:299
  11.0 2.9 %block_rows.3 = (bf16[768,128]{1,0:T(8,128)(2,1)S(1)}, bf16[768,128]{1,0:T(8,128)(2,1)S(1)}, f32[768,128]{1,0:T(8,128)S(1)}, f32[160,128]{1,0:T(8,128)S(1)}, bf1...) custom-call(bf16[3072,640]{1,0:T(8,128)(2,1)S(1)} %get-tuple-element.24.refs_0_, ...), custom_call_target="tpu_custom_call" | custom-call | flops 1132462080 | bytes 2949120 | tf_op jit(solution)/shard_map/block_rows/pallas_call | solution.py:200
  14.0 2.3 %collective-permute-start.5 = (bf16[768,128]{1,0:T(8,128)(2,1)S(1)}, bf16[768,128]{1,0:T(8,128)(2,1)S(1)}, u32[]{:S(2)}, u32[]{:S(2)}) collective-permute-start(bf16[768,128]{1,0:T(8,128)(2,1)S(1)} %get-tuple-element.35), channel_id=1, source_target_pairs={{0,12},{4,0},{8,4},{12,8},{1,13},{5,1},{9,5},{13,9},{2,14},{6,2},{... | collective-permute-start | bytes 589832 | tf_op jit(solution)/shard_map/ppermute | solution.py:299
  16.2 1.8 %collective-permute-done.3 = bf16[768,128]{1,0:T(8,128)(2,1)S(1)} collective-permute-done((bf16[768,128]{1,0:T(8,128)(2,1)S(1)}, bf16[768,128]{1,0:T(8,128)(2,1)S(1)}, u32[]{:S(2)}, u32[]{:S(2)}) %collective-permute-start.3) | collective-permute-done | bytes 196640 | tf_op jit(solution)/shard_map/ppermute | solution.py:299
  18.1 0.1 add_convert_fusion
  18.1 0.1 collective-permute-start.4
  18.2 0.1 collective-permute-start.6
  18.3 1.5 %collective-permute-start.7 = (bf16[160,128]{1,0:T(8,128)(2,1)S(1)}, bf16[160,128]{1,0:T(8,128)(2,1)S(1)}, u32[]{:S(2)}, u32[]{:S(2)}) collective-permute-start(bf16[160,128]{1,0:T(8,128)(2,1)S(1)} %get-tuple-element.38), channel_id=1, source_target_pairs={{0,2},{1,3},{2,0},{3,1},{4,6},{5,7},{6,4},{7,5},{8,10},{9,11},{10,... | collective-permute-start | bytes 122888 | tf_op jit(solution)/shard_map/ppermute | solution.py:215
  19.8 0.4 %collective-permute-start.8 = (bf16[160,128]{1,0:T(8,128)(2,1)S(1)}, bf16[160,128]{1,0:T(8,128)(2,1)S(1)}, u32[]{:S(2)}, u32[]{:S(2)}) collective-permute-start(bf16[160,128]{1,0:T(8,128)(2,1)S(1)} %get-tuple-element.39), channel_id=1, source_target_pairs={{0,3},{1,2},{2,1},{3,0},{4,7},{5,6},{6,5},{7,4},{8,11},{9,10},{10,... | collective-permute-start | bytes 122888 | tf_op jit(solution)/shard_map/ppermute | solution.py:215
  20.1 2.2 %collective-permute-done.7.refs_5_ = bf16[160,128]{1,0:T(8,128)(2,1)S(1)} collective-permute-done((bf16[160,128]{1,0:T(8,128)(2,1)S(1)}, bf16[160,128]{1,0:T(8,128)(2,1)S(1)}, u32[]{:S(2)}, u32[]{:S(2)}) %collective-permute-start.7) | collective-permute-done | bytes 40992 | tf_op jit(solution)/shard_map/ppermute | solution.py:215
  22.3 1.0 %collective-permute-done.8.refs_6_ = bf16[160,128]{1,0:T(8,128)(2,1)S(1)} collective-permute-done((bf16[160,128]{1,0:T(8,128)(2,1)S(1)}, bf16[160,128]{1,0:T(8,128)(2,1)S(1)}, u32[]{:S(2)}, u32[]{:S(2)}) %collective-permute-start.8) | collective-permute-done | bytes 40992 | tf_op jit(solution)/shard_map/ppermute | solution.py:215
  23.3 3.3 %collective-permute-done.4.refs_1_ = bf16[768,128]{1,0:T(8,128)(2,1)S(1)} collective-permute-done((bf16[768,128]{1,0:T(8,128)(2,1)S(1)}, bf16[768,128]{1,0:T(8,128)(2,1)S(1)}, u32[]{:S(2)}, u32[]{:S(2)}) %collective-permute-start.4) | collective-permute-done | bytes 196640 | tf_op jit(solution)/shard_map/ppermute | solution.py:299
  26.6 0.9 %finish.1 = (f32[160,128]{1,0:T(8,128)}, f32[160,128]{1,0:T(8,128)}, f32[160,128]{1,0:T(8,128)}, f32[768,128]{1,0:T(8,128)}) custom-call(f32[768,128]{1,0:T(8,128)S(1)} %get-tuple-element.32.refs_0_, bf16[768,128]{1,0:T(8,128)(2,1)S(1)} %collective-permute-done.4.refs_1_, bf16[768,128]{1,0:T(8,128)(2,1)S(1)} %collective-permute-done.5.refs_2_, ...), custom_call_target="tpu_custom_call" | custom-call | flops 409600 | bytes 1753088 | tf_op jit(solution)/shard_map/finish/pallas_call | solution.py:256
  (6 shorter events, 0.0 us)
Async XLA Ops:
  1.5 5.3 %collective-permute-start.2 = (bf16[160,128]{1,0:T(8,128)(2,1)S(1)}, bf16[160,128]{1,0:T(8,128)(2,1)S(1)}, u32[]{:S(2)}, u32[]{:S(2)}) collective-permute-start(bf16[160,128]{1,0:T(8,128)(2,1)S(1)} %convert_element_type.12.refs_5_), channel_id=1, source_target_pairs={{0,3},{1,2},{2,1},{3,0},{4,7},{5,6},{6,5},{7,4},{8,11},{9,10},{10,... | collective-permute-start | bytes 122888 | tf_op jit(solution)/shard_map/ppermute | solution.py:215
  3.9 4.1 %collective-permute-start.1 = (bf16[160,128]{1,0:T(8,128)(2,1)S(1)}, bf16[160,128]{1,0:T(8,128)(2,1)S(1)}, u32[]{:S(2)}, u32[]{:S(2)}) collective-permute-start(bf16[160,128]{1,0:T(8,128)(2,1)S(1)} %convert_element_type.12.refs_5_), channel_id=1, source_target_pairs={{0,2},{1,3},{2,0},{3,1},{4,6},{5,7},{6,4},{7,5},{8,10},{9,11},{10,... | collective-permute-start | bytes 122888 | tf_op jit(solution)/shard_map/ppermute | solution.py:215
  4.5 3.5 %collective-permute-start = (bf16[160,128]{1,0:T(8,128)(2,1)S(1)}, bf16[160,128]{1,0:T(8,128)(2,1)S(1)}, u32[]{:S(2)}, u32[]{:S(2)}) collective-permute-start(bf16[160,128]{1,0:T(8,128)(2,1)S(1)} %convert_element_type.12.refs_5_), channel_id=1, source_target_pairs={{0,1},{1,0},{2,3},{3,2},{4,5},{5,4},{6,7},{7,6},{8,9},{9,8},{10,11... | collective-permute-start | bytes 122888 | tf_op jit(solution)/shard_map/ppermute | solution.py:215
  9.3 17.2 %copy-start = (f32[160,128]{1,0:T(8,128)S(1)}, f32[160,128]{1,0:T(8,128)}, u32[]{:S(2)}) copy-start(f32[160,128]{1,0:T(8,128)} %refs_7_.1) | copy-start | bytes 245764
  9.4 17.2 %copy-start.1 = (f32[160,128]{1,0:T(8,128)S(1)}, f32[160,128]{1,0:T(8,128)}, u32[]{:S(2)}) copy-start(f32[160,128]{1,0:T(8,128)} %refs_8_.1) | copy-start | bytes 245764
  9.4 17.2 %copy-start.2 = (f32[160,128]{1,0:T(8,128)S(1)}, f32[160,128]{1,0:T(8,128)}, u32[]{:S(2)}) copy-start(f32[160,128]{1,0:T(8,128)} %refs_9_.1) | copy-start | bytes 245764
  9.4 8.7 %collective-permute-start.3 = (bf16[768,128]{1,0:T(8,128)(2,1)S(1)}, bf16[768,128]{1,0:T(8,128)(2,1)S(1)}, u32[]{:S(2)}, u32[]{:S(2)}) collective-permute-start(bf16[768,128]{1,0:T(8,128)(2,1)S(1)} %get-tuple-element.34), channel_id=1, source_target_pairs={{0,4},{4,8},{8,12},{12,0},{1,5},{5,9},{9,13},{13,1},{2,6},{6,10},{... | collective-permute-start | bytes 589832 | tf_op jit(solution)/shard_map/ppermute | solution.py:299
  14.0 9.3 %collective-permute-start.5 = (bf16[768,128]{1,0:T(8,128)(2,1)S(1)}, bf16[768,128]{1,0:T(8,128)(2,1)S(1)}, u32[]{:S(2)}, u32[]{:S(2)}) collective-permute-start(bf16[768,128]{1,0:T(8,128)(2,1)S(1)} %get-tuple-element.35), channel_id=1, source_target_pairs={{0,12},{4,0},{8,4},{12,8},{1,13},{5,1},{9,5},{13,9},{2,14},{6,2},{... | collective-permute-start | bytes 589832 | tf_op jit(solution)/shard_map/ppermute | solution.py:299
  18.1 8.5 %collective-permute-start.4 = (bf16[768,128]{1,0:T(8,128)(2,1)S(1)}, bf16[768,128]{1,0:T(8,128)(2,1)S(1)}, u32[]{:S(2)}, u32[]{:S(2)}) collective-permute-start(bf16[768,128]{1,0:T(8,128)(2,1)S(1)} %add_convert_fusion), channel_id=1, source_target_pairs={{0,4},{4,8},{8,12},{12,0},{1,5},{5,9},{9,13},{13,1},{2,6},{6,10},{... | collective-permute-start | bytes 589832 | tf_op jit(solution)/shard_map/ppermute | solution.py:299
  18.2 1.9 %collective-permute-start.6 = (bf16[160,128]{1,0:T(8,128)(2,1)S(1)}, bf16[160,128]{1,0:T(8,128)(2,1)S(1)}, u32[]{:S(2)}, u32[]{:S(2)}) collective-permute-start(bf16[160,128]{1,0:T(8,128)(2,1)S(1)} %get-tuple-element.37), channel_id=1, source_target_pairs={{0,1},{1,0},{2,3},{3,2},{4,5},{5,4},{6,7},{7,6},{8,9},{9,8},{10,11... | collective-permute-start | bytes 122888 | tf_op jit(solution)/shard_map/ppermute | solution.py:215
  18.3 4.1 %collective-permute-start.7 = (bf16[160,128]{1,0:T(8,128)(2,1)S(1)}, bf16[160,128]{1,0:T(8,128)(2,1)S(1)}, u32[]{:S(2)}, u32[]{:S(2)}) collective-permute-start(bf16[160,128]{1,0:T(8,128)(2,1)S(1)} %get-tuple-element.38), channel_id=1, source_target_pairs={{0,2},{1,3},{2,0},{3,1},{4,6},{5,7},{6,4},{7,5},{8,10},{9,11},{10,... | collective-permute-start | bytes 122888 | tf_op jit(solution)/shard_map/ppermute | solution.py:215
  19.8 3.5 %collective-permute-start.8 = (bf16[160,128]{1,0:T(8,128)(2,1)S(1)}, bf16[160,128]{1,0:T(8,128)(2,1)S(1)}, u32[]{:S(2)}, u32[]{:S(2)}) collective-permute-start(bf16[160,128]{1,0:T(8,128)(2,1)S(1)} %get-tuple-element.39), channel_id=1, source_target_pairs={{0,3},{1,2},{2,1},{3,0},{4,7},{5,6},{6,5},{7,4},{8,11},{9,10},{10,... | collective-permute-start | bytes 122888 | tf_op jit(solution)/shard_map/ppermute | solution.py:215

commit v12 on v8

--- a/solution.py
+++ b/solution.py
@@ -289,7 +289,7 @@
     steps = steps_of(n_gene)
     tables = [around(n_gene, way * distance) for way, distance in steps] + [tuple(range(n_gene))]
     kinds = [jnp.bfloat16] * len(steps) + [jnp.float32]
-    cuts = [0, 1, 2, len(tables)] if len(steps) > 2 else [0, 1, len(tables)]
+    cuts = [0, 1, len(tables)]
     carried, blocks = shares, []
     for low, high in zip(cuts, cuts[1:]):
         last = high == len(tables)

time: 27.1 us -> 27.6 us (1.018)
  waiting for transfers between devices: 6.48 us -> 7.3 us
  Pallas kernels: 7.73 us -> 7.37 us
    ppermute x3, waiting for transfers between devices: 2.45 us -> 3.3 us  [local(): came[way] = lax.ppermute(own, 'gene', list(enumerate(around(n_gene, way))))]
    pallas_call x3 -> x2, Pallas kernels: 4.55 us -> 4.2 us  [block_rows(): pl.pallas_call(functools.partial(rows_kernel, tables, block, first, last,...]
  transfers between devices with their start and end apart: 9 -> 9, of which waited for: 5 -> 5; matrix products, arithmetic and copies ran while one was open for 0% -> 0% of each run, Pallas kernels for 21% -> 19%
where the time goes in v12:
time: 27.6 us; the launch traced here: 27.4 us
  starting transfers between devices  11.1 us (40%)
  Pallas kernels  7.37 us (27%)
  waiting for transfers between devices  7.3 us (26%)
  other arithmetic  0.95 us (3%)
  between operations  0.71 us (3%)
    ppermute x3, starting transfers between devices, local(): came[way] = lax.ppermute(own, 'gene', list(enumerate(around(n_gene, way))))  6.13 us
    ppermute x6, starting transfers between devices, swap_row(): lax.ppermute(value, 'row', [(me, partner(me, hop, size)) for me in range(...  4.92 us
    pallas_call x2, Pallas kernels, block_rows(): pl.pallas_call(functools.partial(rows_kernel, tables, block, first, last,...  4.2 us
    ppermute x6, waiting for transfers between devices, swap_row(): lax.ppermute(value, 'row', [(me, partner(me, hop, size)) for me in range(...  4.01 us
    ppermute x3, waiting for transfers between devices, local(): came[way] = lax.ppermute(own, 'gene', list(enumerate(around(n_gene, way))))  3.3 us
    pallas_call x1, Pallas kernels, prepare(): pl.pallas_call(functools.partial(prepare_kernel, scale_k), out_shape=(VME...  2.26 us
    pallas_call x1, Pallas kernels, finish(): pl.pallas_call(functools.partial(finish_kernel, len(ends), len(parts)), o...  0.92 us
    convert_element_type x1, other arithmetic, local(): factor_bf = gene_factor.astype(jnp.bfloat16)  0.9 us
  transfers between devices with their start and end apart: 9, of which 5 were waited for; matrix products, arithmetic and copies ran while one was open for 0% of the time, Pallas kernels for 19%

profile of v12, /device:TPU:0, one launch (start us, length us, event | category | flops | bytes accessed | tf_op | source)
XLA Modules:
  0.0 27.4 jit_solution(17872132450175508114)
XLA Ops:
  0.6 0.9 %convert_element_type.12.refs_5_ = bf16[160,128]{1,0:T(8,128)(2,1)S(1)} convert(f32[160,128]{1,0:T(8,128)} %refs_7_.1) | non-fusion elementwise | flops 20480 | bytes 122880 | tf_op jit(solution)/shard_map/convert_element_type | solution.py:278
  1.5 2.4 %collective-permute-start.2 = (bf16[160,128]{1,0:T(8,128)(2,1)S(1)}, bf16[160,128]{1,0:T(8,128)(2,1)S(1)}, u32[]{:S(2)}, u32[]{:S(2)}) collective-permute-start(bf16[160,128]{1,0:T(8,128)(2,1)S(1)} %convert_element_type.12.refs_5_), channel_id=1, source_target_pairs={{0,3},{1,2},{2,1},{3,0},{4,7},{5,6},{6,5},{7,4},{8,11},{9,10},{10,... | collective-permute-start | bytes 122888 | tf_op jit(solution)/shard_map/ppermute | solution.py:215
  3.9 0.6 %collective-permute-start.1 = (bf16[160,128]{1,0:T(8,128)(2,1)S(1)}, bf16[160,128]{1,0:T(8,128)(2,1)S(1)}, u32[]{:S(2)}, u32[]{:S(2)}) collective-permute-start(bf16[160,128]{1,0:T(8,128)(2,1)S(1)} %convert_element_type.12.refs_5_), channel_id=1, source_target_pairs={{0,2},{1,3},{2,0},{3,1},{4,6},{5,7},{6,4},{7,5},{8,10},{9,11},{10,... | collective-permute-start | bytes 122888 | tf_op jit(solution)/shard_map/ppermute | solution.py:215
  4.5 0.0 collective-permute-start
  4.6 2.3 %prepare.1 = (bf16[3072,640]{1,0:T(8,128)(2,1)S(1)}, bf16[3072,128]{1,0:T(8,128)(2,1)S(1)}, bf16[128,3072]{1,0:T(8,128)(2,1)S(1)}, f32[1,640]{1,0:T(1,128)S(1)}, f32[640,128]{1,0:T(8,128)S(1)}) custom-call(bf16[3072,640]{1,0:T(8,128)(2,1)} %x_in.1, s32[3072]{0:T(1024)} %index_in.1, bf16[512,128]{1,0:T(8,128)(2,1)} %cell_in.1, f32[640]{0:T(1024)} %scale_in.1), custom_call_target="tpu_custom_call" | custom-call | flops 402653184 | bytes 7864320 | tf_op jit(solution)/shard_map/prepare/pallas_call | solution.py:74
  6.9 1.2 %collective-permute-done.1.refs_7_ = bf16[160,128]{1,0:T(8,128)(2,1)S(1)} collective-permute-done((bf16[160,128]{1,0:T(8,128)(2,1)S(1)}, bf16[160,128]{1,0:T(8,128)(2,1)S(1)}, u32[]{:S(2)}, u32[]{:S(2)}) %collective-permute-start.1) | collective-permute-done | bytes 40992 | tf_op jit(solution)/shard_map/ppermute | solution.py:215
  8.1 0.0 collective-permute-done.refs_6_
  8.1 1.3 %block_rows.2 = (bf16[768,128]{1,0:T(8,128)(2,1)S(1)}, f32[128,640]{1,0:T(8,128)S(1)}, bf16[128,640]{1,0:T(8,128)(2,1)S(1)}, bf16[640,128]{1,0:T(8,128)(2,1)S(1)}) custom-call(bf16[3072,640]{1,0:T(8,128)(2,1)S(1)} %get-tuple-element.24.refs_0_, bf16[3072,128]{1,0:T(8,128)(2,1)S(1)} %get-tuple-element.25.refs_1_, ...), custom_call_target="tpu_custom_call" | custom-call | flops 377487360 | bytes 983040 | tf_op jit(solution)/shard_map/block_rows/pallas_call | solution.py:200
  9.3 0.0 copy-start
  9.4 0.0 copy-start.1
  9.4 0.0 copy-start.2
  9.4 2.6 %collective-permute-start.3 = (bf16[768,128]{1,0:T(8,128)(2,1)S(1)}, bf16[768,128]{1,0:T(8,128)(2,1)S(1)}, u32[]{:S(2)}, u32[]{:S(2)}) collective-permute-start(bf16[768,128]{1,0:T(8,128)(2,1)S(1)} %get-tuple-element.34), channel_id=1, source_target_pairs={{0,8},{4,0},{8,12},{12,4},{1,9},{5,1},{9,13},{13,5},{2,10},{6,2},{... | collective-permute-start | bytes 589832 | tf_op jit(solution)/shard_map/ppermute | solution.py:304
  12.0 2.9 %block_rows.3 = (bf16[768,128]{1,0:T(8,128)(2,1)S(1)}, bf16[768,128]{1,0:T(8,128)(2,1)S(1)}, f32[768,128]{1,0:T(8,128)S(1)}, f32[160,128]{1,0:T(8,128)S(1)}, bf1...) custom-call(bf16[3072,640]{1,0:T(8,128)(2,1)S(1)} %get-tuple-element.24.refs_0_, ...), custom_call_target="tpu_custom_call" | custom-call | flops 1132462080 | bytes 2949120 | tf_op jit(solution)/shard_map/block_rows/pallas_call | solution.py:200
  14.9 0.1 collective-permute-start.5
  15.0 2.3 %collective-permute-done.3 = bf16[768,128]{1,0:T(8,128)(2,1)S(1)} collective-permute-done((bf16[768,128]{1,0:T(8,128)(2,1)S(1)}, bf16[768,128]{1,0:T(8,128)(2,1)S(1)}, u32[]{:S(2)}, u32[]{:S(2)}) %collective-permute-start.3) | collective-permute-done | bytes 196640 | tf_op jit(solution)/shard_map/ppermute | solution.py:304
  17.3 0.1 add_convert_fusion
  17.4 3.4 %collective-permute-start.4 = (bf16[768,128]{1,0:T(8,128)(2,1)S(1)}, bf16[768,128]{1,0:T(8,128)(2,1)S(1)}, u32[]{:S(2)}, u32[]{:S(2)}) collective-permute-start(bf16[768,128]{1,0:T(8,128)(2,1)S(1)} %add_convert_fusion), channel_id=1, source_target_pairs={{0,8},{4,0},{8,12},{12,4},{1,9},{5,1},{9,13},{13,5},{2,10},{6,2},{... | collective-permute-start | bytes 589832 | tf_op jit(solution)/shard_map/ppermute | solution.py:304
  20.8 0.0 collective-permute-start.6
  20.8 1.1 %collective-permute-start.7 = (bf16[160,128]{1,0:T(8,128)(2,1)S(1)}, bf16[160,128]{1,0:T(8,128)(2,1)S(1)}, u32[]{:S(2)}, u32[]{:S(2)}) collective-permute-start(bf16[160,128]{1,0:T(8,128)(2,1)S(1)} %get-tuple-element.38), channel_id=1, source_target_pairs={{0,2},{1,3},{2,0},{3,1},{4,6},{5,7},{6,4},{7,5},{8,10},{9,11},{10,... | collective-permute-start | bytes 122888 | tf_op jit(solution)/shard_map/ppermute | solution.py:215
  21.9 0.7 %collective-permute-start.8 = (bf16[160,128]{1,0:T(8,128)(2,1)S(1)}, bf16[160,128]{1,0:T(8,128)(2,1)S(1)}, u32[]{:S(2)}, u32[]{:S(2)}) collective-permute-start(bf16[160,128]{1,0:T(8,128)(2,1)S(1)} %get-tuple-element.39), channel_id=1, source_target_pairs={{0,3},{1,2},{2,1},{3,0},{4,7},{5,6},{6,5},{7,4},{8,11},{9,10},{10,... | collective-permute-start | bytes 122888 | tf_op jit(solution)/shard_map/ppermute | solution.py:215
  22.7 2.1 %collective-permute-done.7.refs_5_ = bf16[160,128]{1,0:T(8,128)(2,1)S(1)} collective-permute-done((bf16[160,128]{1,0:T(8,128)(2,1)S(1)}, bf16[160,128]{1,0:T(8,128)(2,1)S(1)}, u32[]{:S(2)}, u32[]{:S(2)}) %collective-permute-start.7) | collective-permute-done | bytes 40992 | tf_op jit(solution)/shard_map/ppermute | solution.py:215
  24.8 0.7 %collective-permute-done.8.refs_6_ = bf16[160,128]{1,0:T(8,128)(2,1)S(1)} collective-permute-done((bf16[160,128]{1,0:T(8,128)(2,1)S(1)}, bf16[160,128]{1,0:T(8,128)(2,1)S(1)}, u32[]{:S(2)}, u32[]{:S(2)}) %collective-permute-start.8) | collective-permute-done | bytes 40992 | tf_op jit(solution)/shard_map/ppermute | solution.py:215
  25.5 1.0 %collective-permute-done.4.refs_1_ = bf16[768,128]{1,0:T(8,128)(2,1)S(1)} collective-permute-done((bf16[768,128]{1,0:T(8,128)(2,1)S(1)}, bf16[768,128]{1,0:T(8,128)(2,1)S(1)}, u32[]{:S(2)}, u32[]{:S(2)}) %collective-permute-start.4) | collective-permute-done | bytes 196640 | tf_op jit(solution)/shard_map/ppermute | solution.py:304
  26.5 0.9 %finish.1 = (f32[160,128]{1,0:T(8,128)}, f32[160,128]{1,0:T(8,128)}, f32[160,128]{1,0:T(8,128)}, f32[768,128]{1,0:T(8,128)}) custom-call(f32[768,128]{1,0:T(8,128)S(1)} %get-tuple-element.32.refs_0_, bf16[768,128]{1,0:T(8,128)(2,1)S(1)} %collective-permute-done.4.refs_1_, bf16[768,128]{1,0:T(8,128)(2,1)S(1)} %collective-permute-done.5.refs_2_, ...), custom_call_target="tpu_custom_call" | custom-call | flops 409600 | bytes 1753088 | tf_op jit(solution)/shard_map/finish/pallas_call | solution.py:261
  (6 shorter events, 0.0 us)
Async XLA Ops:
  1.5 5.3 %collective-permute-start.2 = (bf16[160,128]{1,0:T(8,128)(2,1)S(1)}, bf16[160,128]{1,0:T(8,128)(2,1)S(1)}, u32[]{:S(2)}, u32[]{:S(2)}) collective-permute-start(bf16[160,128]{1,0:T(8,128)(2,1)S(1)} %convert_element_type.12.refs_5_), channel_id=1, source_target_pairs={{0,3},{1,2},{2,1},{3,0},{4,7},{5,6},{6,5},{7,4},{8,11},{9,10},{10,... | collective-permute-start | bytes 122888 | tf_op jit(solution)/shard_map/ppermute | solution.py:215
  3.9 4.1 %collective-permute-start.1 = (bf16[160,128]{1,0:T(8,128)(2,1)S(1)}, bf16[160,128]{1,0:T(8,128)(2,1)S(1)}, u32[]{:S(2)}, u32[]{:S(2)}) collective-permute-start(bf16[160,128]{1,0:T(8,128)(2,1)S(1)} %convert_element_type.12.refs_5_), channel_id=1, source_target_pairs={{0,2},{1,3},{2,0},{3,1},{4,6},{5,7},{6,4},{7,5},{8,10},{9,11},{10,... | collective-permute-start | bytes 122888 | tf_op jit(solution)/shard_map/ppermute | solution.py:215
  4.5 3.5 %collective-permute-start = (bf16[160,128]{1,0:T(8,128)(2,1)S(1)}, bf16[160,128]{1,0:T(8,128)(2,1)S(1)}, u32[]{:S(2)}, u32[]{:S(2)}) collective-permute-start(bf16[160,128]{1,0:T(8,128)(2,1)S(1)} %convert_element_type.12.refs_5_), channel_id=1, source_target_pairs={{0,1},{1,0},{2,3},{3,2},{4,5},{5,4},{6,7},{7,6},{8,9},{9,8},{10,11... | collective-permute-start | bytes 122888 | tf_op jit(solution)/shard_map/ppermute | solution.py:215
  9.3 17.1 %copy-start = (f32[160,128]{1,0:T(8,128)S(1)}, f32[160,128]{1,0:T(8,128)}, u32[]{:S(2)}) copy-start(f32[160,128]{1,0:T(8,128)} %refs_7_.1) | copy-start | bytes 245764
  9.4 17.1 %copy-start.1 = (f32[160,128]{1,0:T(8,128)S(1)}, f32[160,128]{1,0:T(8,128)}, u32[]{:S(2)}) copy-start(f32[160,128]{1,0:T(8,128)} %refs_8_.1) | copy-start | bytes 245764
  9.4 17.1 %copy-start.2 = (f32[160,128]{1,0:T(8,128)S(1)}, f32[160,128]{1,0:T(8,128)}, u32[]{:S(2)}) copy-start(f32[160,128]{1,0:T(8,128)} %refs_9_.1) | copy-start | bytes 245764
  9.4 8.0 %collective-permute-start.3 = (bf16[768,128]{1,0:T(8,128)(2,1)S(1)}, bf16[768,128]{1,0:T(8,128)(2,1)S(1)}, u32[]{:S(2)}, u32[]{:S(2)}) collective-permute-start(bf16[768,128]{1,0:T(8,128)(2,1)S(1)} %get-tuple-element.34), channel_id=1, source_target_pairs={{0,8},{4,0},{8,12},{12,4},{1,9},{5,1},{9,13},{13,5},{2,10},{6,2},{... | collective-permute-start | bytes 589832 | tf_op jit(solution)/shard_map/ppermute | solution.py:304
  14.9 10.6 %collective-permute-start.5 = (bf16[768,128]{1,0:T(8,128)(2,1)S(1)}, bf16[768,128]{1,0:T(8,128)(2,1)S(1)}, u32[]{:S(2)}, u32[]{:S(2)}) collective-permute-start(bf16[768,128]{1,0:T(8,128)(2,1)S(1)} %get-tuple-element.35), channel_id=1, source_target_pairs={{0,4},{4,12},{8,0},{12,8},{1,5},{5,13},{9,1},{13,9},{2,6},{6,14},{... | collective-permute-start | bytes 589832 | tf_op jit(solution)/shard_map/ppermute | solution.py:304
  17.4 9.1 %collective-permute-start.4 = (bf16[768,128]{1,0:T(8,128)(2,1)S(1)}, bf16[768,128]{1,0:T(8,128)(2,1)S(1)}, u32[]{:S(2)}, u32[]{:S(2)}) collective-permute-start(bf16[768,128]{1,0:T(8,128)(2,1)S(1)} %add_convert_fusion), channel_id=1, source_target_pairs={{0,8},{4,0},{8,12},{12,4},{1,9},{5,1},{9,13},{13,5},{2,10},{6,2},{... | collective-permute-start | bytes 589832 | tf_op jit(solution)/shard_map/ppermute | solution.py:304
  20.8 1.9 %collective-permute-start.6 = (bf16[160,128]{1,0:T(8,128)(2,1)S(1)}, bf16[160,128]{1,0:T(8,128)(2,1)S(1)}, u32[]{:S(2)}, u32[]{:S(2)}) collective-permute-start(bf16[160,128]{1,0:T(8,128)(2,1)S(1)} %get-tuple-element.37), channel_id=1, source_target_pairs={{0,1},{1,0},{2,3},{3,2},{4,5},{5,4},{6,7},{7,6},{8,9},{9,8},{10,11... | collective-permute-start | bytes 122888 | tf_op jit(solution)/shard_map/ppermute | solution.py:215
  20.8 4.0 %collective-permute-start.7 = (bf16[160,128]{1,0:T(8,128)(2,1)S(1)}, bf16[160,128]{1,0:T(8,128)(2,1)S(1)}, u32[]{:S(2)}, u32[]{:S(2)}) collective-permute-start(bf16[160,128]{1,0:T(8,128)(2,1)S(1)} %get-tuple-element.38), channel_id=1, source_target_pairs={{0,2},{1,3},{2,0},{3,1},{4,6},{5,7},{6,4},{7,5},{8,10},{9,11},{10,... | collective-permute-start | bytes 122888 | tf_op jit(solution)/shard_map/ppermute | solution.py:215
  21.9 3.5 %collective-permute-start.8 = (bf16[160,128]{1,0:T(8,128)(2,1)S(1)}, bf16[160,128]{1,0:T(8,128)(2,1)S(1)}, u32[]{:S(2)}, u32[]{:S(2)}) collective-permute-start(bf16[160,128]{1,0:T(8,128)(2,1)S(1)} %get-tuple-element.39), channel_id=1, source_target_pairs={{0,3},{1,2},{2,1},{3,0},{4,7},{5,6},{6,5},{7,4},{8,11},{9,10},{10,... | collective-permute-start | bytes 122888 | tf_op jit(solution)/shard_map/ppermute | solution.py:215

commit v13 on v8

--- a/solution.py
+++ b/solution.py
@@ -148,11 +148,6 @@
     def predict(here):
         return jnp.dot(f_ref[here, :], wide, preferred_element_type=jnp.float32)
 
-    def influence(here, pred):
-        resid = x_ref[here, :].astype(jnp.float32) - pred
-        inside = jnp.maximum(1.0 - resid * resid * bend, 0.0)
-        return (resid * (inside * inside)).astype(jnp.bfloat16)
-
     def gradients(tile, infl, total):
         out, at, here = tile
         cols = jnp.dot(ft_ref[:, here], infl, preferred_element_type=jnp.float32)
@@ -163,7 +158,7 @@
     infl = None
     for at, tile in enumerate(tiles):
         later = predict(tiles[at + 1][2]) if at + 1 < len(tiles) else None
-        now = influence(tile[2], pred)
+        now = influence(x_ref[tile[2], :], pred, bend)
         if at:
             total = gradients(tiles[at - 1], infl, total)
         infl, pred = now, later
@@ -211,6 +206,126 @@
     return done, rest if first or last else rest + list(carried[1:])
 
 
+def lane_parts(genes, depth, n_row):
+    if n_row != 4:
+        return None
+    pairs = [(2 * depth * (place // 2), 2 * depth * (place // 2 + 1)) for place in range(n_row)]
+    low = [-(-begin // 128) * 128 for begin, _ in pairs]
+    width = min(end // 128 * 128 - begin for begin, (_, end) in zip(low, pairs))
+    if width <= 0 or any(begin not in (0, genes - width) for begin in low):
+        return None
+    return low, width, [width if begin == 0 else 0 for begin in low]
+
+
+def lanes(table, width):
+    return pl.ds(pl.multiple_of(pick("row", table), 128), width)
+
+
+def influence(x, pred, bend):
+    resid = x.astype(jnp.float32) - pred
+    inside = jnp.maximum(1.0 - resid * resid * bend, 0.0)
+    return (resid * (inside * inside)).astype(jnp.bfloat16)
+
+
+def part_of_block(table, block, here, x_ref, f_ref, ft_ref, bend_ref, wide, scaled):
+    step = tile_of(block, 256)
+    origin = pick("gene", table) * block
+    tiles = [pl.ds(pl.multiple_of(origin + at, math.gcd(block, step)), step) for at in range(0, block, step)]
+    bend = bend_ref[:, here]
+    preds = [jnp.dot(f_ref[tile, :], wide, preferred_element_type=jnp.float32) for tile in tiles]
+    infls = [influence(x_ref[tile, here], pred, bend) for tile, pred in zip(tiles, preds)]
+    rows, total = [], None
+    for tile, infl in zip(tiles, infls):
+        cols = jnp.dot(ft_ref[:, tile], infl, preferred_element_type=jnp.float32)
+        rows.append(jnp.dot(infl, scaled, preferred_element_type=jnp.float32))
+        total = cols if total is None else total + cols
+    return rows, total
+
+
+def early_kernel(table, block, parts, x_ref, f_ref, ft_ref, bend_ref, shrink_ref, own, other, *refs):
+    rows_out, total_out, wide_out, scaled_out, pair = refs
+    low, width, _ = parts
+    depth = own.shape[0]
+    odd = lax.axis_index("row") % 2
+    pair[pl.ds(pl.multiple_of(odd * depth, depth), depth), :] = own[...]
+    pair[pl.ds(pl.multiple_of((1 - odd) * depth, depth), depth), :] = other[...]
+    inset = [begin - 2 * depth * (place // 2) for place, begin in enumerate(low)]
+    whole = pair[pl.ds(pl.multiple_of(pick("row", inset), math.gcd(*inset, 128)), width), :].astype(jnp.float32)
+    here = lanes(low, width)
+    wide = jnp.transpose(whole).astype(jnp.bfloat16)
+    scaled = (whole * shrink_ref[here, :]).astype(jnp.bfloat16)
+    wide_out[...] = wide
+    scaled_out[...] = scaled
+    rows, total = part_of_block(table, block, here, x_ref, f_ref, ft_ref, bend_ref, wide, scaled)
+    for at, value in enumerate(rows):
+        rows_out[at * value.shape[0] : (at + 1) * value.shape[0], :] = value
+    total_out[...] = total
+
+
+def rest_kernel(table, block, parts, n_row, x_ref, f_ref, ft_ref, bend_ref, shrink_ref, *refs):
+    shares, (rows_in, total_in, wide_in, scaled_in) = refs[:n_row], refs[n_row : n_row + 4]
+    rows_out, total_out, wide_out, scaled_out, piece = refs[n_row + 4 :]
+    low, width, rest = parts
+    me = lax.axis_index("row")
+    depth = shares[0].shape[0]
+    for hop in range(n_row):
+        start = pl.multiple_of(source(me, hop, n_row) * depth, depth)
+        piece[pl.ds(start, depth), :] = shares[hop][...]
+    here = lanes(rest, n_row * depth - width)
+    whole = piece[here, :].astype(jnp.float32)
+    wide = jnp.transpose(whole).astype(jnp.bfloat16)
+    scaled = (whole * shrink_ref[here, :]).astype(jnp.bfloat16)
+    rows, total = part_of_block(table, block, here, x_ref, f_ref, ft_ref, bend_ref, wide, scaled)
+    for at, value in enumerate(rows):
+        span = slice(at * value.shape[0], (at + 1) * value.shape[0])
+        rows_out[span, :] = (rows_in[span, :] + value).astype(rows_out.dtype)
+    done = lanes(low, width)
+    total_out[:, here] = total
+    total_out[:, done] = total_in[...]
+    wide_out[:, here] = wide
+    wide_out[:, done] = wide_in[...]
+    scaled_out[here, :] = scaled
+    scaled_out[done, :] = scaled_in[...]
+
+
+def first_block(table, block, parts, n_row, fixed, shares):
+    genes, rank = fixed[4].shape
+    depth = genes // n_row
+    width = parts[1]
+    ins = pinned(*fixed)
+    early = pl.pallas_call(
+        functools.partial(early_kernel, table, block, parts),
+        out_shape=(
+            VMEM((block, rank), jnp.float32),
+            VMEM((rank, width), jnp.float32),
+            VMEM((rank, width), jnp.bfloat16),
+            VMEM((width, rank), jnp.bfloat16),
+        ),
+        in_specs=[IN_VMEM] * 7,
+        out_specs=(IN_VMEM,) * 4,
+        scratch_shapes=[VMEM((2 * depth, rank), jnp.bfloat16)],
+        compiler_params=params(),
+        cost_estimate=cost(12 * block * width * rank, block * width * 4),
+        name="early_part",
+    )(*ins, *shares[:2])
+    done, *carried = pl.pallas_call(
+        functools.partial(rest_kernel, table, block, parts, n_row),
+        out_shape=(
+            jax.ShapeDtypeStruct((block, rank), jnp.bfloat16),
+            VMEM((rank, genes), jnp.float32),
+            VMEM((rank, genes), jnp.bfloat16),
+            VMEM((genes, rank), jnp.bfloat16),
+        ),
+        in_specs=[IN_VMEM] * (9 + n_row),
+        out_specs=(IN_VMEM,) * 4,
+        scratch_shapes=[VMEM((genes, rank), jnp.bfloat16)],
+        compiler_params=params(),
+        cost_estimate=cost(12 * block * (genes - width) * rank, block * (genes - width) * 4),
+        name="rest_part",
+    )(*ins, *shares, *pinned(*early))
+    return [done], carried
+
+
 def swap_row(value, hop, size):
     return lax.ppermute(value, "row", [(me, partner(me, hop, size)) for me in range(size)])
 
@@ -235,34 +350,51 @@
 
 
 def finish_kernel(n_ends, n_parts, *refs):
-    ins, outs = refs[: n_ends + n_parts + 3], refs[n_ends + n_parts + 3 :]
+    n_ins = n_ends + n_parts + 3
+    ins, outs = refs[:n_ins], refs[n_ins : n_ins + 3 + bool(n_ends)]
+    *held, sems = refs[n_ins + len(outs) :]
     ends, parts = ins[:n_ends], ins[n_ends : n_ends + n_parts]
     factor, first, second = ins[n_ends + n_parts :]
+    copies = []
+
+    def send(at, span, value):
+        held[at][span, :] = value
+        copies.append(pltpu.make_async_copy(held[at].at[span, :], outs[at].at[span, :], sems.at[len(copies)]))
+        copies[-1].start()
+
+    if ends:
+        step = tile_of(ends[0].shape[0], 256)
+        for low in range(0, ends[0].shape[0], step):
+            span = pl.ds(low, step)
+            rows = ends[0][span, :]
+            for end in ends[1:]:
+                rows = plus(rows, end[span, :])
+            send(3, span, rows)
     grad = parts[0][...]
     for part in parts[1:]:
         grad = plus(grad, part[...])
+    span = pl.ds(0, grad.shape[0])
     new_first = beta_one * first[...] + (1.0 - beta_one) * grad
     new_second = beta_two * second[...] + (1.0 - beta_two) * grad * grad
+    send(1, span, new_first)
+    send(2, span, new_second)
     first_hat = new_first / (1.0 - beta_one**10)
     second_hat = new_second / (1.0 - beta_two**10)
-    outs[0][...] = factor[...] - learn_rate * first_hat / (jnp.sqrt(second_hat) + adam_eps)
-    outs[1][...] = new_first
-    outs[2][...] = new_second
-    if ends:
-        rows = ends[0][...]
-        for end in ends[1:]:
-            rows = plus(rows, end[...])
-        outs[3][...] = rows
+    send(0, span, factor[...] - learn_rate * first_hat / (jnp.sqrt(second_hat) + adam_eps))
+    for copy in copies:
+        copy.wait()
 
 
 def finish(ends, parts, factor, first, second):
     ins = [*ends, *parts, factor, first, second]
     shapes = [factor, factor, factor] + list(ends[:1])
+    n_copies = 3 + (ends[0].shape[0] // tile_of(ends[0].shape[0], 256) if ends else 0)
     return pl.pallas_call(
         functools.partial(finish_kernel, len(ends), len(parts)),
         out_shape=tuple(jax.ShapeDtypeStruct(like.shape, jnp.float32) for like in shapes),
         in_specs=[IN_VMEM] * len(ins),
-        out_specs=(IN_VMEM,) * len(shapes),
+        out_specs=(IN_ANY,) * len(shapes),
+        scratch_shapes=[VMEM(like.shape, jnp.float32) for like in shapes] + [pltpu.SemaphoreType.DMA((n_copies,))],
         compiler_params=params(),
         cost_estimate=cost(20 * factor.size, sum(4 * a.size for a in ins)),
         name="finish",
@@ -290,9 +422,14 @@
     tables = [around(n_gene, way * distance) for way, distance in steps] + [tuple(range(n_gene))]
     kinds = [jnp.bfloat16] * len(steps) + [jnp.float32]
     cuts = [0, 1, 2, len(tables)] if len(steps) > 2 else [0, 1, len(tables)]
+    parted = lane_parts(genes_dev, genes_dev // n_row, n_row)
     carried, blocks = shares, []
     for low, high in zip(cuts, cuts[1:]):
         last = high == len(tables)
+        if low == 0 and parted:
+            done, carried = first_block(tables[0], block, parted, n_row, fixed, shares)
+            blocks += done
+            continue
         done, carried = block_rows(tables[low:high], kinds[low:high], block, low == 0, last, n_row, fixed, carried)
         blocks += done
     parts = carried

time: 27.1 us -> 26.6 us (0.982)
  waiting for transfers between devices: 6.48 us -> 5.7 us
    pallas_call x0 -> x2, Pallas kernels: none -> 1.54 us  [the longest x1 0.89 us: first_block(): pl.pallas_call(functools.partial(rest_kernel, table, block, parts, n_row)...]
    pallas_call x3 -> x2, Pallas kernels: 4.55 us -> 3.25 us  [block_rows(): pl.pallas_call(functools.partial(rows_kernel, tables, block, first, last,...]
    ppermute x3, waiting for transfers between devices: 2.45 us -> 1.99 us  [local(): came[way] = lax.ppermute(own, 'gene', list(enumerate(around(n_gene, way))))]
    ppermute x6, waiting for transfers between devices: 4.03 us -> 3.7 us  [swap_row(): lax.ppermute(value, 'row', [(me, partner(me, hop, size)) for me in range(...]
  transfers between devices with their start and end apart: 9 -> 9, of which waited for: 5 -> 4; matrix products, arithmetic and copies ran while one was open for 0% -> 0% of each run, Pallas kernels for 21% -> 23%
where the time goes in v13:
time: 26.6 us; the launch traced here: 26.5 us
  starting transfers between devices  11.1 us (42%)
  Pallas kernels  7.95 us (30%)
  waiting for transfers between devices  5.7 us (21%)
  other arithmetic  0.95 us (4%)
  between operations  0.74 us (3%)
    ppermute x3, starting transfers between devices, local(): came[way] = lax.ppermute(own, 'gene', list(enumerate(around(n_gene, way))))  6.14 us
    ppermute x6, starting transfers between devices, swap_row(): lax.ppermute(value, 'row', [(me, partner(me, hop, size)) for me in range(...  4.97 us
    ppermute x6, waiting for transfers between devices, swap_row(): lax.ppermute(value, 'row', [(me, partner(me, hop, size)) for me in range(...  3.7 us
    pallas_call x2, Pallas kernels, block_rows(): pl.pallas_call(functools.partial(rows_kernel, tables, block, first, last,...  3.25 us
    pallas_call x1, Pallas kernels, prepare(): pl.pallas_call(functools.partial(prepare_kernel, scale_k), out_shape=(VME...  2.26 us
    ppermute x3, waiting for transfers between devices, local(): came[way] = lax.ppermute(own, 'gene', list(enumerate(around(n_gene, way))))  1.99 us
    pallas_call x1, Pallas kernels, finish(): pl.pallas_call(functools.partial(finish_kernel, len(ends), len(parts)), o...  0.9 us
    convert_element_type x1, other arithmetic, local(): factor_bf = gene_factor.astype(jnp.bfloat16)  0.9 us
  transfers between devices with their start and end apart: 9, of which 4 were waited for; matrix products, arithmetic and copies ran while one was open for 0% of the time, Pallas kernels for 23%

profile of v13, /device:TPU:0, one launch (start us, length us, event | category | flops | bytes accessed | tf_op | source)
XLA Modules:
  0.0 26.5 jit_solution(13421168714659846177)
XLA Ops:
  0.6 0.9 %convert_element_type.12.own.refs_0_ = bf16[160,128]{1,0:T(8,128)(2,1)S(1)} convert(f32[160,128]{1,0:T(8,128)} %refs_7_.1) | non-fusion elementwise | flops 20480 | bytes 122880 | tf_op jit(solution)/shard_map/convert_element_type | solution.py:410
  1.5 0.5 %collective-permute-start = (bf16[160,128]{1,0:T(8,128)(2,1)S(1)}, bf16[160,128]{1,0:T(8,128)(2,1)S(1)}, u32[]{:S(2)}, u32[]{:S(2)}) collective-permute-start(bf16[160,128]{1,0:T(8,128)(2,1)S(1)} %convert_element_type.12.own.refs_0_), channel_id=1, source_target_pairs={{0,1},{1,0},{2,3},{3,2},{4,5},{5,4},{6,7},{7,6},{8,9},{9,8},{10,11... | collective-permute-start | bytes 122888 | tf_op jit(solution)/shard_map/ppermute | solution.py:330
  2.0 2.6 %collective-permute-start.2 = (bf16[160,128]{1,0:T(8,128)(2,1)S(1)}, bf16[160,128]{1,0:T(8,128)(2,1)S(1)}, u32[]{:S(2)}, u32[]{:S(2)}) collective-permute-start(bf16[160,128]{1,0:T(8,128)(2,1)S(1)} %convert_element_type.12.own.refs_0_), channel_id=1, source_target_pairs={{0,3},{1,2},{2,1},{3,0},{4,7},{5,6},{6,5},{7,4},{8,11},{9,10},{10,... | collective-permute-start | bytes 122888 | tf_op jit(solution)/shard_map/ppermute | solution.py:330
  4.6 0.1 collective-permute-start.1
  4.6 2.3 %prepare.1 = (bf16[3072,640]{1,0:T(8,128)(2,1)S(1)}, bf16[3072,128]{1,0:T(8,128)(2,1)S(1)}, bf16[128,3072]{1,0:T(8,128)(2,1)S(1)}, f32[1,640]{1,0:T(1,128)S(1)}, f32[640,128]{1,0:T(8,128)S(1)}) custom-call(bf16[3072,640]{1,0:T(8,128)(2,1)} %x_in.1, s32[3072]{0:T(1024)} %index_in.1, bf16[512,128]{1,0:T(8,128)(2,1)} %cell_in.1, f32[640]{0:T(1024)} %scale_in.1), custom_call_target="tpu_custom_call" | custom-call | flops 402653184 | bytes 7864320 | tf_op jit(solution)/shard_map/prepare/pallas_call | solution.py:74
  6.9 0.6 %early_part.1 = (f32[768,128]{1,0:T(8,128)S(1)}, f32[128,256]{1,0:T(8,128)S(1)}, bf16[128,256]{1,0:T(8,128)(2,1)S(1)}, bf16[256,128]{1,0:T(8,128)(2,1)S(1)}) custom-call(bf16[3072,640]{1,0:T(8,128)(2,1)S(1)} %get-tuple-element.29.x_ref.refs_0_, bf16[3072,128]{1,0:T(8,128)(2,1)S(1)} %get-tuple-element.30.f_ref.refs_1_, ...), custom_call_target="tpu_custom_call" | custom-call | flops 301989888 | bytes 786432 | tf_op jit(solution)/shard_map/early_part/pallas_call | solution.py:296
  7.6 0.0 collective-permute-done.2.refs_3_
  7.6 1.0 %collective-permute-done.1.refs_2_ = bf16[160,128]{1,0:T(8,128)(2,1)S(1)} collective-permute-done((bf16[160,128]{1,0:T(8,128)(2,1)S(1)}, bf16[160,128]{1,0:T(8,128)(2,1)S(1)}, u32[]{:S(2)}, u32[]{:S(2)}) %collective-permute-start.1) | collective-permute-done | bytes 40992 | tf_op jit(solution)/shard_map/ppermute | solution.py:330
  8.6 0.9 %rest_part.1 = (bf16[768,128]{1,0:T(8,128)(2,1)S(1)}, f32[128,640]{1,0:T(8,128)S(1)}, bf16[128,640]{1,0:T(8,128)(2,1)S(1)}, bf16[640,128]{1,0:T(8,128)(2,1)S(1)}) custom-call(bf16[3072,640]{1,0:T(8,128)(2,1)S(1)} %get-tuple-element.29.x_ref.refs_0_, bf16[3072,128]{1,0:T(8,128)(2,1)S(1)} %get-tuple-element.30.f_ref.refs_1_, ...), custom_call_target="tpu_custom_call" | custom-call | flops 452984832 | bytes 1179648 | tf_op jit(solution)/shard_map/rest_part/pallas_call | solution.py:311
  9.5 2.6 %collective-permute-start.3 = (bf16[768,128]{1,0:T(8,128)(2,1)S(1)}, bf16[768,128]{1,0:T(8,128)(2,1)S(1)}, u32[]{:S(2)}, u32[]{:S(2)}) collective-permute-start(bf16[768,128]{1,0:T(8,128)(2,1)S(1)} %get-tuple-element.44), channel_id=1, source_target_pairs={{0,8},{4,0},{8,12},{12,4},{1,9},{5,1},{9,13},{13,5},{2,10},{6,2},{... | collective-permute-start | bytes 589832 | tf_op jit(solution)/shard_map/ppermute | solution.py:441
  12.1 1.2 %block_rows.2 = (bf16[768,128]{1,0:T(8,128)(2,1)S(1)}, f32[128,640]{1,0:T(8,128)S(1)}) custom-call(bf16[3072,640]{1,0:T(8,128)(2,1)S(1)} %get-tuple-element.29.x_ref.refs_0_, bf16[3072,128]{1,0:T(8,128)(2,1)S(1)} %get-tuple-element.30.f_ref.refs_1_, bf16[128,3072]{1,0:T(8,128)(2,1)S(1)} %get-tuple-element.31.ft_ref.refs_2_, ...), custom_call_target="tpu_custom_call" | custom-call | flops 377487360 | bytes 983040 | tf_op jit(solution)/shard_map/block_rows/pallas_call | solution.py:195
  13.3 0.0 copy-start
  13.3 0.0 copy-start.1
  13.3 0.0 copy-start.2
  13.3 0.1 collective-permute-start.5
  13.4 2.1 %block_rows.3 = (bf16[768,128]{1,0:T(8,128)(2,1)S(1)}, f32[768,128]{1,0:T(8,128)S(1)}, f32[160,128]{1,0:T(8,128)S(1)}, bf16[160,128]{1,0:T(8,128)(2,1)S(1)}, bf1...) custom-call(bf16[3072,640]{1,0:T(8,128)(2,1)S(1)} %get-tuple-element.29.x_ref.refs_0_, ...), custom_call_target="tpu_custom_call" | custom-call | flops 754974720 | bytes 1966080 | tf_op jit(solution)/shard_map/block_rows/pallas_call | solution.py:195
  15.5 2.0 %collective-permute-done.3 = bf16[768,128]{1,0:T(8,128)(2,1)S(1)} collective-permute-done((bf16[768,128]{1,0:T(8,128)(2,1)S(1)}, bf16[768,128]{1,0:T(8,128)(2,1)S(1)}, u32[]{:S(2)}, u32[]{:S(2)}) %collective-permute-start.3) | collective-permute-done | bytes 196640 | tf_op jit(solution)/shard_map/ppermute | solution.py:441
  17.5 0.1 add_convert_fusion
  17.5 3.4 %collective-permute-start.4 = (bf16[768,128]{1,0:T(8,128)(2,1)S(1)}, bf16[768,128]{1,0:T(8,128)(2,1)S(1)}, u32[]{:S(2)}, u32[]{:S(2)}) collective-permute-start(bf16[768,128]{1,0:T(8,128)(2,1)S(1)} %add_convert_fusion), channel_id=1, source_target_pairs={{0,8},{4,0},{8,12},{12,4},{1,9},{5,1},{9,13},{13,5},{2,10},{6,2},{... | collective-permute-start | bytes 589832 | tf_op jit(solution)/shard_map/ppermute | solution.py:441
  21.0 0.9 %collective-permute-start.7 = (bf16[160,128]{1,0:T(8,128)(2,1)S(1)}, bf16[160,128]{1,0:T(8,128)(2,1)S(1)}, u32[]{:S(2)}, u32[]{:S(2)}) collective-permute-start(bf16[160,128]{1,0:T(8,128)(2,1)S(1)} %get-tuple-element.48), channel_id=1, source_target_pairs={{0,2},{1,3},{2,0},{3,1},{4,6},{5,7},{6,4},{7,5},{8,10},{9,11},{10,... | collective-permute-start | bytes 122888 | tf_op jit(solution)/shard_map/ppermute | solution.py:330
  21.9 0.9 %collective-permute-start.8 = (bf16[160,128]{1,0:T(8,128)(2,1)S(1)}, bf16[160,128]{1,0:T(8,128)(2,1)S(1)}, u32[]{:S(2)}, u32[]{:S(2)}) collective-permute-start(bf16[160,128]{1,0:T(8,128)(2,1)S(1)} %get-tuple-element.49), channel_id=1, source_target_pairs={{0,3},{1,2},{2,1},{3,0},{4,7},{5,6},{6,5},{7,4},{8,11},{9,10},{10,... | collective-permute-start | bytes 122888 | tf_op jit(solution)/shard_map/ppermute | solution.py:330
  22.8 2.3 %collective-permute-done.7.refs_5_ = bf16[160,128]{1,0:T(8,128)(2,1)S(1)} collective-permute-done((bf16[160,128]{1,0:T(8,128)(2,1)S(1)}, bf16[160,128]{1,0:T(8,128)(2,1)S(1)}, u32[]{:S(2)}, u32[]{:S(2)}) %collective-permute-start.7) | collective-permute-done | bytes 40992 | tf_op jit(solution)/shard_map/ppermute | solution.py:330
  25.2 0.4 %collective-permute-done.8.refs_6_ = bf16[160,128]{1,0:T(8,128)(2,1)S(1)} collective-permute-done((bf16[160,128]{1,0:T(8,128)(2,1)S(1)}, bf16[160,128]{1,0:T(8,128)(2,1)S(1)}, u32[]{:S(2)}, u32[]{:S(2)}) %collective-permute-start.8) | collective-permute-done | bytes 40992 | tf_op jit(solution)/shard_map/ppermute | solution.py:330
  25.6 0.9 %finish.1 = (f32[160,128]{1,0:T(8,128)}, f32[160,128]{1,0:T(8,128)}, f32[160,128]{1,0:T(8,128)}, f32[768,128]{1,0:T(8,128)}) custom-call(f32[768,128]{1,0:T(8,128)S(1)} %get-tuple-element.42.refs_0_, bf16[768,128]{1,0:T(8,128)(2,1)S(1)} %collective-permute-done.4.refs_1_, bf16[768,128]{1,0:T(8,128)(2,1)S(1)} %collective-permute-done.5.refs_2_, ...), custom_call_target="tpu_custom_call" | custom-call | flops 409600 | bytes 1753088 | tf_op jit(solution)/shard_map/finish/pallas_call | solution.py:392
  (8 shorter events, 0.0 us)
Async XLA Ops:
  1.5 5.4 %collective-permute-start = (bf16[160,128]{1,0:T(8,128)(2,1)S(1)}, bf16[160,128]{1,0:T(8,128)(2,1)S(1)}, u32[]{:S(2)}, u32[]{:S(2)}) collective-permute-start(bf16[160,128]{1,0:T(8,128)(2,1)S(1)} %convert_element_type.12.own.refs_0_), channel_id=1, source_target_pairs={{0,1},{1,0},{2,3},{3,2},{4,5},{5,4},{6,7},{7,6},{8,9},{9,8},{10,11... | collective-permute-start | bytes 122888 | tf_op jit(solution)/shard_map/ppermute | solution.py:330
  2.0 5.6 %collective-permute-start.2 = (bf16[160,128]{1,0:T(8,128)(2,1)S(1)}, bf16[160,128]{1,0:T(8,128)(2,1)S(1)}, u32[]{:S(2)}, u32[]{:S(2)}) collective-permute-start(bf16[160,128]{1,0:T(8,128)(2,1)S(1)} %convert_element_type.12.own.refs_0_), channel_id=1, source_target_pairs={{0,3},{1,2},{2,1},{3,0},{4,7},{5,6},{6,5},{7,4},{8,11},{9,10},{10,... | collective-permute-start | bytes 122888 | tf_op jit(solution)/shard_map/ppermute | solution.py:330
  4.6 4.0 %collective-permute-start.1 = (bf16[160,128]{1,0:T(8,128)(2,1)S(1)}, bf16[160,128]{1,0:T(8,128)(2,1)S(1)}, u32[]{:S(2)}, u32[]{:S(2)}) collective-permute-start(bf16[160,128]{1,0:T(8,128)(2,1)S(1)} %convert_element_type.12.own.refs_0_), channel_id=1, source_target_pairs={{0,2},{1,3},{2,0},{3,1},{4,6},{5,7},{6,4},{7,5},{8,10},{9,11},{10,... | collective-permute-start | bytes 122888 | tf_op jit(solution)/shard_map/ppermute | solution.py:330
  9.5 8.0 %collective-permute-start.3 = (bf16[768,128]{1,0:T(8,128)(2,1)S(1)}, bf16[768,128]{1,0:T(8,128)(2,1)S(1)}, u32[]{:S(2)}, u32[]{:S(2)}) collective-permute-start(bf16[768,128]{1,0:T(8,128)(2,1)S(1)} %get-tuple-element.44), channel_id=1, source_target_pairs={{0,8},{4,0},{8,12},{12,4},{1,9},{5,1},{9,13},{13,5},{2,10},{6,2},{... | collective-permute-start | bytes 589832 | tf_op jit(solution)/shard_map/ppermute | solution.py:441
  13.3 12.2 %copy-start = (f32[160,128]{1,0:T(8,128)S(1)}, f32[160,128]{1,0:T(8,128)}, u32[]{:S(2)}) copy-start(f32[160,128]{1,0:T(8,128)} %refs_7_.1) | copy-start | bytes 245764
  13.3 12.2 %copy-start.1 = (f32[160,128]{1,0:T(8,128)S(1)}, f32[160,128]{1,0:T(8,128)}, u32[]{:S(2)}) copy-start(f32[160,128]{1,0:T(8,128)} %refs_8_.1) | copy-start | bytes 245764
  13.3 12.2 %copy-start.2 = (f32[160,128]{1,0:T(8,128)S(1)}, f32[160,128]{1,0:T(8,128)}, u32[]{:S(2)}) copy-start(f32[160,128]{1,0:T(8,128)} %refs_9_.1) | copy-start | bytes 245764
  13.3 12.2 %collective-permute-start.5 = (bf16[768,128]{1,0:T(8,128)(2,1)S(1)}, bf16[768,128]{1,0:T(8,128)(2,1)S(1)}, u32[]{:S(2)}, u32[]{:S(2)}) collective-permute-start(bf16[768,128]{1,0:T(8,128)(2,1)S(1)} %get-tuple-element.45), channel_id=1, source_target_pairs={{0,4},{4,12},{8,0},{12,8},{1,5},{5,13},{9,1},{13,9},{2,6},{6,14},{... | collective-permute-start | bytes 589832 | tf_op jit(solution)/shard_map/ppermute | solution.py:441
  17.5 8.0 %collective-permute-start.4 = (bf16[768,128]{1,0:T(8,128)(2,1)S(1)}, bf16[768,128]{1,0:T(8,128)(2,1)S(1)}, u32[]{:S(2)}, u32[]{:S(2)}) collective-permute-start(bf16[768,128]{1,0:T(8,128)(2,1)S(1)} %add_convert_fusion), channel_id=1, source_target_pairs={{0,8},{4,0},{8,12},{12,4},{1,9},{5,1},{9,13},{13,5},{2,10},{6,2},{... | collective-permute-start | bytes 589832 | tf_op jit(solution)/shard_map/ppermute | solution.py:441
  21.0 1.9 %collective-permute-start.6 = (bf16[160,128]{1,0:T(8,128)(2,1)S(1)}, bf16[160,128]{1,0:T(8,128)(2,1)S(1)}, u32[]{:S(2)}, u32[]{:S(2)}) collective-permute-start(bf16[160,128]{1,0:T(8,128)(2,1)S(1)} %get-tuple-element.47), channel_id=1, source_target_pairs={{0,1},{1,0},{2,3},{3,2},{4,5},{5,4},{6,7},{7,6},{8,9},{9,8},{10,11... | collective-permute-start | bytes 122888 | tf_op jit(solution)/shard_map/ppermute | solution.py:330
  21.0 4.2 %collective-permute-start.7 = (bf16[160,128]{1,0:T(8,128)(2,1)S(1)}, bf16[160,128]{1,0:T(8,128)(2,1)S(1)}, u32[]{:S(2)}, u32[]{:S(2)}) collective-permute-start(bf16[160,128]{1,0:T(8,128)(2,1)S(1)} %get-tuple-element.48), channel_id=1, source_target_pairs={{0,2},{1,3},{2,0},{3,1},{4,6},{5,7},{6,4},{7,5},{8,10},{9,11},{10,... | collective-permute-start | bytes 122888 | tf_op jit(solution)/shard_map/ppermute | solution.py:330
  21.9 3.6 %collective-permute-start.8 = (bf16[160,128]{1,0:T(8,128)(2,1)S(1)}, bf16[160,128]{1,0:T(8,128)(2,1)S(1)}, u32[]{:S(2)}, u32[]{:S(2)}) collective-permute-start(bf16[160,128]{1,0:T(8,128)(2,1)S(1)} %get-tuple-element.49), channel_id=1, source_target_pairs={{0,3},{1,2},{2,1},{3,0},{4,7},{5,6},{6,5},{7,4},{8,11},{9,10},{10,... | collective-permute-start | bytes 122888 | tf_op jit(solution)/shard_map/ppermute | solution.py:330

commit v14 on v13

--- a/solution.py
+++ b/solution.py
@@ -89,7 +89,7 @@
             pltpu.SemaphoreType.DMA((4,)),
         ],
         compiler_params=params(),
-        cost_estimate=cost(2 * rows * cells * rank, 2 * rows * genes * 2),
+        cost_estimate=cost(8 * rows * cells * rank, 8 * rows * genes * 2),
         name="prepare",
     )(*(pltpu.with_memory_space_constraint(a, pltpu.HBM) for a in ins))
 

time: 26.6 us -> 27 us (1.015)
  waiting for transfers between devices: 5.7 us -> 6.1 us
    ppermute x3, waiting for transfers between devices: 1.99 us -> 2.67 us  [local(): came[way] = lax.ppermute(own, 'gene', list(enumerate(around(n_gene, way))))]
    ppermute x6, waiting for transfers between devices: 3.7 us -> 3.43 us  [swap_row(): lax.ppermute(value, 'row', [(me, partner(me, hop, size)) for me in range(...]
  transfers between devices with their start and end apart: 9 -> 9, of which waited for: 4 -> 5; matrix products, arithmetic and copies ran while one was open for 0% -> 0% of each run, Pallas kernels for 23% -> 23%
where the time goes in v14:
time: 27 us; the launch traced here: 26.8 us
  starting transfers between devices  11.1 us (41%)
  Pallas kernels  7.95 us (29%)
  waiting for transfers between devices  6.1 us (23%)
  other arithmetic  0.95 us (4%)
  between operations  0.73 us (3%)
    ppermute x3, starting transfers between devices, local(): came[way] = lax.ppermute(own, 'gene', list(enumerate(around(n_gene, way))))  6.14 us
    ppermute x6, starting transfers between devices, swap_row(): lax.ppermute(value, 'row', [(me, partner(me, hop, size)) for me in range(...  4.92 us
    ppermute x6, waiting for transfers between devices, swap_row(): lax.ppermute(value, 'row', [(me, partner(me, hop, size)) for me in range(...  3.43 us
    pallas_call x2, Pallas kernels, block_rows(): pl.pallas_call(functools.partial(rows_kernel, tables, block, first, last,...  3.25 us
    ppermute x3, waiting for transfers between devices, local(): came[way] = lax.ppermute(own, 'gene', list(enumerate(around(n_gene, way))))  2.67 us
    pallas_call x1, Pallas kernels, prepare(): pl.pallas_call(functools.partial(prepare_kernel, scale_k), out_shape=(VME...  2.26 us
    pallas_call x1, Pallas kernels, finish(): pl.pallas_call(functools.partial(finish_kernel, len(ends), len(parts)), o...  0.9 us
    pallas_call x1, Pallas kernels, first_block(): pl.pallas_call(functools.partial(rest_kernel, table, block, parts, n_row)...  0.9 us
  transfers between devices with their start and end apart: 9, of which 5 were waited for; matrix products, arithmetic and copies ran while one was open for 0% of the time, Pallas kernels for 23%

profile of v14, /device:TPU:0, one launch (start us, length us, event | category | flops | bytes accessed | tf_op | source)
XLA Modules:
  0.0 26.8 jit_solution(6910841267633678972)
XLA Ops:
  0.6 0.9 %convert_element_type.12.own.refs_0_ = bf16[160,128]{1,0:T(8,128)(2,1)S(1)} convert(f32[160,128]{1,0:T(8,128)} %refs_7_.1) | non-fusion elementwise | flops 20480 | bytes 122880 | tf_op jit(solution)/shard_map/convert_element_type | solution.py:410
  1.5 2.4 %collective-permute-start.2 = (bf16[160,128]{1,0:T(8,128)(2,1)S(1)}, bf16[160,128]{1,0:T(8,128)(2,1)S(1)}, u32[]{:S(2)}, u32[]{:S(2)}) collective-permute-start(bf16[160,128]{1,0:T(8,128)(2,1)S(1)} %convert_element_type.12.own.refs_0_), channel_id=1, source_target_pairs={{0,3},{1,2},{2,1},{3,0},{4,7},{5,6},{6,5},{7,4},{8,11},{9,10},{10,... | collective-permute-start | bytes 122888 | tf_op jit(solution)/shard_map/ppermute | solution.py:330
  3.9 0.6 %collective-permute-start.1 = (bf16[160,128]{1,0:T(8,128)(2,1)S(1)}, bf16[160,128]{1,0:T(8,128)(2,1)S(1)}, u32[]{:S(2)}, u32[]{:S(2)}) collective-permute-start(bf16[160,128]{1,0:T(8,128)(2,1)S(1)} %convert_element_type.12.own.refs_0_), channel_id=1, source_target_pairs={{0,2},{1,3},{2,0},{3,1},{4,6},{5,7},{6,4},{7,5},{8,10},{9,11},{10,... | collective-permute-start | bytes 122888 | tf_op jit(solution)/shard_map/ppermute | solution.py:330
  4.5 0.0 collective-permute-start
  4.6 2.3 %prepare.1 = (bf16[3072,640]{1,0:T(8,128)(2,1)S(1)}, bf16[3072,128]{1,0:T(8,128)(2,1)S(1)}, bf16[128,3072]{1,0:T(8,128)(2,1)S(1)}, f32[1,640]{1,0:T(1,128)S(1)}, f32[640,128]{1,0:T(8,128)S(1)}) custom-call(bf16[3072,640]{1,0:T(8,128)(2,1)} %x_in.1, s32[3072]{0:T(1024)} %index_in.1, bf16[512,128]{1,0:T(8,128)(2,1)} %cell_in.1, f32[640]{0:T(1024)} %scale_in.1), custom_call_target="tpu_custom_call" | custom-call | flops 1610612736 | bytes 31457280 | tf_op jit(solution)/shard_map/prepare/pallas_call | solution.py:74
  6.9 0.6 %early_part.1 = (f32[768,128]{1,0:T(8,128)S(1)}, f32[128,256]{1,0:T(8,128)S(1)}, bf16[128,256]{1,0:T(8,128)(2,1)S(1)}, bf16[256,128]{1,0:T(8,128)(2,1)S(1)}) custom-call(bf16[3072,640]{1,0:T(8,128)(2,1)S(1)} %get-tuple-element.29.x_ref.refs_0_, bf16[3072,128]{1,0:T(8,128)(2,1)S(1)} %get-tuple-element.30.f_ref.refs_1_, ...), custom_call_target="tpu_custom_call" | custom-call | flops 301989888 | bytes 786432 | tf_op jit(solution)/shard_map/early_part/pallas_call | solution.py:296
  7.5 0.5 %collective-permute-done.1.refs_2_ = bf16[160,128]{1,0:T(8,128)(2,1)S(1)} collective-permute-done((bf16[160,128]{1,0:T(8,128)(2,1)S(1)}, bf16[160,128]{1,0:T(8,128)(2,1)S(1)}, u32[]{:S(2)}, u32[]{:S(2)}) %collective-permute-start.1) | collective-permute-done | bytes 40992 | tf_op jit(solution)/shard_map/ppermute | solution.py:330
  8.1 0.9 %rest_part.1 = (bf16[768,128]{1,0:T(8,128)(2,1)S(1)}, f32[128,640]{1,0:T(8,128)S(1)}, bf16[128,640]{1,0:T(8,128)(2,1)S(1)}, bf16[640,128]{1,0:T(8,128)(2,1)S(1)}) custom-call(bf16[3072,640]{1,0:T(8,128)(2,1)S(1)} %get-tuple-element.29.x_ref.refs_0_, bf16[3072,128]{1,0:T(8,128)(2,1)S(1)} %get-tuple-element.30.f_ref.refs_1_, ...), custom_call_target="tpu_custom_call" | custom-call | flops 452984832 | bytes 1179648 | tf_op jit(solution)/shard_map/rest_part/pallas_call | solution.py:311
  9.0 2.6 %collective-permute-start.3 = (bf16[768,128]{1,0:T(8,128)(2,1)S(1)}, bf16[768,128]{1,0:T(8,128)(2,1)S(1)}, u32[]{:S(2)}, u32[]{:S(2)}) collective-permute-start(bf16[768,128]{1,0:T(8,128)(2,1)S(1)} %get-tuple-element.44), channel_id=1, source_target_pairs={{0,8},{4,0},{8,12},{12,4},{1,9},{5,1},{9,13},{13,5},{2,10},{6,2},{... | collective-permute-start | bytes 589832 | tf_op jit(solution)/shard_map/ppermute | solution.py:441
  11.6 1.2 %block_rows.2 = (bf16[768,128]{1,0:T(8,128)(2,1)S(1)}, f32[128,640]{1,0:T(8,128)S(1)}) custom-call(bf16[3072,640]{1,0:T(8,128)(2,1)S(1)} %get-tuple-element.29.x_ref.refs_0_, bf16[3072,128]{1,0:T(8,128)(2,1)S(1)} %get-tuple-element.30.f_ref.refs_1_, bf16[128,3072]{1,0:T(8,128)(2,1)S(1)} %get-tuple-element.31.ft_ref.refs_2_, ...), custom_call_target="tpu_custom_call" | custom-call | flops 377487360 | bytes 983040 | tf_op jit(solution)/shard_map/block_rows/pallas_call | solution.py:195
  12.8 0.0 copy-start
  12.8 0.0 copy-start.1
  12.8 0.0 copy-start.2
  12.8 0.1 collective-permute-start.5
  12.9 2.1 %block_rows.3 = (bf16[768,128]{1,0:T(8,128)(2,1)S(1)}, f32[768,128]{1,0:T(8,128)S(1)}, f32[160,128]{1,0:T(8,128)S(1)}, bf16[160,128]{1,0:T(8,128)(2,1)S(1)}, bf1...) custom-call(bf16[3072,640]{1,0:T(8,128)(2,1)S(1)} %get-tuple-element.29.x_ref.refs_0_, ...), custom_call_target="tpu_custom_call" | custom-call | flops 754974720 | bytes 1966080 | tf_op jit(solution)/shard_map/block_rows/pallas_call | solution.py:195
  15.0 2.0 %collective-permute-done.3 = bf16[768,128]{1,0:T(8,128)(2,1)S(1)} collective-permute-done((bf16[768,128]{1,0:T(8,128)(2,1)S(1)}, bf16[768,128]{1,0:T(8,128)(2,1)S(1)}, u32[]{:S(2)}, u32[]{:S(2)}) %collective-permute-start.3) | collective-permute-done | bytes 196640 | tf_op jit(solution)/shard_map/ppermute | solution.py:441
  16.9 0.1 add_convert_fusion
  17.0 3.4 %collective-permute-start.4 = (bf16[768,128]{1,0:T(8,128)(2,1)S(1)}, bf16[768,128]{1,0:T(8,128)(2,1)S(1)}, u32[]{:S(2)}, u32[]{:S(2)}) collective-permute-start(bf16[768,128]{1,0:T(8,128)(2,1)S(1)} %add_convert_fusion), channel_id=1, source_target_pairs={{0,8},{4,0},{8,12},{12,4},{1,9},{5,1},{9,13},{13,5},{2,10},{6,2},{... | collective-permute-start | bytes 589832 | tf_op jit(solution)/shard_map/ppermute | solution.py:441
  20.4 1.2 %collective-permute-start.7 = (bf16[160,128]{1,0:T(8,128)(2,1)S(1)}, bf16[160,128]{1,0:T(8,128)(2,1)S(1)}, u32[]{:S(2)}, u32[]{:S(2)}) collective-permute-start(bf16[160,128]{1,0:T(8,128)(2,1)S(1)} %get-tuple-element.48), channel_id=1, source_target_pairs={{0,2},{1,3},{2,0},{3,1},{4,6},{5,7},{6,4},{7,5},{8,10},{9,11},{10,... | collective-permute-start | bytes 122888 | tf_op jit(solution)/shard_map/ppermute | solution.py:330
  21.6 0.6 %collective-permute-start.8 = (bf16[160,128]{1,0:T(8,128)(2,1)S(1)}, bf16[160,128]{1,0:T(8,128)(2,1)S(1)}, u32[]{:S(2)}, u32[]{:S(2)}) collective-permute-start(bf16[160,128]{1,0:T(8,128)(2,1)S(1)} %get-tuple-element.49), channel_id=1, source_target_pairs={{0,3},{1,2},{2,1},{3,0},{4,7},{5,6},{6,5},{7,4},{8,11},{9,10},{10,... | collective-permute-start | bytes 122888 | tf_op jit(solution)/shard_map/ppermute | solution.py:330
  22.3 2.1 %collective-permute-done.7.refs_5_ = bf16[160,128]{1,0:T(8,128)(2,1)S(1)} collective-permute-done((bf16[160,128]{1,0:T(8,128)(2,1)S(1)}, bf16[160,128]{1,0:T(8,128)(2,1)S(1)}, u32[]{:S(2)}, u32[]{:S(2)}) %collective-permute-start.7) | collective-permute-done | bytes 40992 | tf_op jit(solution)/shard_map/ppermute | solution.py:330
  24.4 0.8 %collective-permute-done.8.refs_6_ = bf16[160,128]{1,0:T(8,128)(2,1)S(1)} collective-permute-done((bf16[160,128]{1,0:T(8,128)(2,1)S(1)}, bf16[160,128]{1,0:T(8,128)(2,1)S(1)}, u32[]{:S(2)}, u32[]{:S(2)}) %collective-permute-start.8) | collective-permute-done | bytes 40992 | tf_op jit(solution)/shard_map/ppermute | solution.py:330
  25.2 0.7 %collective-permute-done.4.refs_1_ = bf16[768,128]{1,0:T(8,128)(2,1)S(1)} collective-permute-done((bf16[768,128]{1,0:T(8,128)(2,1)S(1)}, bf16[768,128]{1,0:T(8,128)(2,1)S(1)}, u32[]{:S(2)}, u32[]{:S(2)}) %collective-permute-start.4) | collective-permute-done | bytes 196640 | tf_op jit(solution)/shard_map/ppermute | solution.py:441
  25.9 0.9 %finish.1 = (f32[160,128]{1,0:T(8,128)}, f32[160,128]{1,0:T(8,128)}, f32[160,128]{1,0:T(8,128)}, f32[768,128]{1,0:T(8,128)}) custom-call(f32[768,128]{1,0:T(8,128)S(1)} %get-tuple-element.42.refs_0_, bf16[768,128]{1,0:T(8,128)(2,1)S(1)} %collective-permute-done.4.refs_1_, bf16[768,128]{1,0:T(8,128)(2,1)S(1)} %collective-permute-done.5.refs_2_, ...), custom_call_target="tpu_custom_call" | custom-call | flops 409600 | bytes 1753088 | tf_op jit(solution)/shard_map/finish/pallas_call | solution.py:392
  (8 shorter events, 0.0 us)
Async XLA Ops:
  1.5 6.0 %collective-permute-start.2 = (bf16[160,128]{1,0:T(8,128)(2,1)S(1)}, bf16[160,128]{1,0:T(8,128)(2,1)S(1)}, u32[]{:S(2)}, u32[]{:S(2)}) collective-permute-start(bf16[160,128]{1,0:T(8,128)(2,1)S(1)} %convert_element_type.12.own.refs_0_), channel_id=1, source_target_pairs={{0,3},{1,2},{2,1},{3,0},{4,7},{5,6},{6,5},{7,4},{8,11},{9,10},{10,... | collective-permute-start | bytes 122888 | tf_op jit(solution)/shard_map/ppermute | solution.py:330
  3.9 4.1 %collective-permute-start.1 = (bf16[160,128]{1,0:T(8,128)(2,1)S(1)}, bf16[160,128]{1,0:T(8,128)(2,1)S(1)}, u32[]{:S(2)}, u32[]{:S(2)}) collective-permute-start(bf16[160,128]{1,0:T(8,128)(2,1)S(1)} %convert_element_type.12.own.refs_0_), channel_id=1, source_target_pairs={{0,2},{1,3},{2,0},{3,1},{4,6},{5,7},{6,4},{7,5},{8,10},{9,11},{10,... | collective-permute-start | bytes 122888 | tf_op jit(solution)/shard_map/ppermute | solution.py:330
  4.5 2.3 %collective-permute-start = (bf16[160,128]{1,0:T(8,128)(2,1)S(1)}, bf16[160,128]{1,0:T(8,128)(2,1)S(1)}, u32[]{:S(2)}, u32[]{:S(2)}) collective-permute-start(bf16[160,128]{1,0:T(8,128)(2,1)S(1)} %convert_element_type.12.own.refs_0_), channel_id=1, source_target_pairs={{0,1},{1,0},{2,3},{3,2},{4,5},{5,4},{6,7},{7,6},{8,9},{9,8},{10,11... | collective-permute-start | bytes 122888 | tf_op jit(solution)/shard_map/ppermute | solution.py:330
  9.0 8.0 %collective-permute-start.3 = (bf16[768,128]{1,0:T(8,128)(2,1)S(1)}, bf16[768,128]{1,0:T(8,128)(2,1)S(1)}, u32[]{:S(2)}, u32[]{:S(2)}) collective-permute-start(bf16[768,128]{1,0:T(8,128)(2,1)S(1)} %get-tuple-element.44), channel_id=1, source_target_pairs={{0,8},{4,0},{8,12},{12,4},{1,9},{5,1},{9,13},{13,5},{2,10},{6,2},{... | collective-permute-start | bytes 589832 | tf_op jit(solution)/shard_map/ppermute | solution.py:441
  12.8 13.1 %copy-start = (f32[160,128]{1,0:T(8,128)S(1)}, f32[160,128]{1,0:T(8,128)}, u32[]{:S(2)}) copy-start(f32[160,128]{1,0:T(8,128)} %refs_7_.1) | copy-start | bytes 245764
  12.8 13.1 %copy-start.1 = (f32[160,128]{1,0:T(8,128)S(1)}, f32[160,128]{1,0:T(8,128)}, u32[]{:S(2)}) copy-start(f32[160,128]{1,0:T(8,128)} %refs_8_.1) | copy-start | bytes 245764
  12.8 13.1 %copy-start.2 = (f32[160,128]{1,0:T(8,128)S(1)}, f32[160,128]{1,0:T(8,128)}, u32[]{:S(2)}) copy-start(f32[160,128]{1,0:T(8,128)} %refs_9_.1) | copy-start | bytes 245764
  12.8 12.4 %collective-permute-start.5 = (bf16[768,128]{1,0:T(8,128)(2,1)S(1)}, bf16[768,128]{1,0:T(8,128)(2,1)S(1)}, u32[]{:S(2)}, u32[]{:S(2)}) collective-permute-start(bf16[768,128]{1,0:T(8,128)(2,1)S(1)} %get-tuple-element.45), channel_id=1, source_target_pairs={{0,4},{4,12},{8,0},{12,8},{1,5},{5,13},{9,1},{13,9},{2,6},{6,14},{... | collective-permute-start | bytes 589832 | tf_op jit(solution)/shard_map/ppermute | solution.py:441
  17.0 8.9 %collective-permute-start.4 = (bf16[768,128]{1,0:T(8,128)(2,1)S(1)}, bf16[768,128]{1,0:T(8,128)(2,1)S(1)}, u32[]{:S(2)}, u32[]{:S(2)}) collective-permute-start(bf16[768,128]{1,0:T(8,128)(2,1)S(1)} %add_convert_fusion), channel_id=1, source_target_pairs={{0,8},{4,0},{8,12},{12,4},{1,9},{5,1},{9,13},{13,5},{2,10},{6,2},{... | collective-permute-start | bytes 589832 | tf_op jit(solution)/shard_map/ppermute | solution.py:441
  20.4 1.9 %collective-permute-start.6 = (bf16[160,128]{1,0:T(8,128)(2,1)S(1)}, bf16[160,128]{1,0:T(8,128)(2,1)S(1)}, u32[]{:S(2)}, u32[]{:S(2)}) collective-permute-start(bf16[160,128]{1,0:T(8,128)(2,1)S(1)} %get-tuple-element.47), channel_id=1, source_target_pairs={{0,1},{1,0},{2,3},{3,2},{4,5},{5,4},{6,7},{7,6},{8,9},{9,8},{10,11... | collective-permute-start | bytes 122888 | tf_op jit(solution)/shard_map/ppermute | solution.py:330
  20.4 4.0 %collective-permute-start.7 = (bf16[160,128]{1,0:T(8,128)(2,1)S(1)}, bf16[160,128]{1,0:T(8,128)(2,1)S(1)}, u32[]{:S(2)}, u32[]{:S(2)}) collective-permute-start(bf16[160,128]{1,0:T(8,128)(2,1)S(1)} %get-tuple-element.48), channel_id=1, source_target_pairs={{0,2},{1,3},{2,0},{3,1},{4,6},{5,7},{6,4},{7,5},{8,10},{9,11},{10,... | collective-permute-start | bytes 122888 | tf_op jit(solution)/shard_map/ppermute | solution.py:330
  21.6 3.5 %collective-permute-start.8 = (bf16[160,128]{1,0:T(8,128)(2,1)S(1)}, bf16[160,128]{1,0:T(8,128)(2,1)S(1)}, u32[]{:S(2)}, u32[]{:S(2)}) collective-permute-start(bf16[160,128]{1,0:T(8,128)(2,1)S(1)} %get-tuple-element.49), channel_id=1, source_target_pairs={{0,3},{1,2},{2,1},{3,0},{4,7},{5,6},{6,5},{7,4},{8,11},{9,10},{10,... | collective-permute-start | bytes 122888 | tf_op jit(solution)/shard_map/ppermute | solution.py:330

commit v15 on v14

--- a/solution.py
+++ b/solution.py
@@ -16,6 +16,7 @@
 adam_eps = 1e-08
 
 RING_MOST = 8
+LINES = ("grp", "gene")
 VMEM = pltpu.VMEM
 IN_VMEM = pl.BlockSpec(memory_space=VMEM)
 IN_ANY = pl.BlockSpec(memory_space=pl.ANY)
@@ -94,8 +95,8 @@
     )(*(pltpu.with_memory_space_constraint(a, pltpu.HBM) for a in ins))
 
 
-def pick(axis, table):
-    me = lax.axis_index(axis)
+def pick(axes, table):
+    me = lax.axis_index(axes)
     value = jnp.int32(table[0])
     for place, entry in enumerate(table[1:], 1):
         value = jnp.where(me == place, jnp.int32(entry), value)
@@ -138,7 +139,7 @@
     step = tile_of(block, 256)
     tiles = []
     for table, out in zip(tables, rows_out):
-        origin = pick("gene", table) * block if len(table) > 1 else 0
+        origin = pick(LINES, table) * block if len(table) > 1 else 0
         for at in range(0, block, step):
             start = origin + at
             if len(table) > 1:
@@ -229,7 +230,7 @@
 
 def part_of_block(table, block, here, x_ref, f_ref, ft_ref, bend_ref, wide, scaled):
     step = tile_of(block, 256)
-    origin = pick("gene", table) * block
+    origin = pick(LINES, table) * block
     tiles = [pl.ds(pl.multiple_of(origin + at, math.gcd(block, step)), step) for at in range(0, block, step)]
     bend = bend_ref[:, here]
     preds = [jnp.dot(f_ref[tile, :], wide, preferred_element_type=jnp.float32) for tile in tiles]
@@ -340,9 +341,10 @@
     return [step for pair in itertools.zip_longest(ahead, back) for step in pair if step]
 
 
-def around(size, hops):
+def around(groups, size, hops):
     ring = ring_of(size)
-    return tuple(ring[(ring.index(place) + hops) % size] for place in range(size))
+    ways = [-hops if group % 2 == 0 else hops for group in range(groups)]
+    return tuple(ring[(ring.index(place) + way) % size] for way in ways for place in range(size))
 
 
 def plus(wide, narrow):
@@ -419,7 +421,8 @@
         return (grad_cells, *finish([], [parts[0], *others], *adam))
 
     steps = steps_of(n_gene)
-    tables = [around(n_gene, way * distance) for way, distance in steps] + [tuple(range(n_gene))]
+    groups = lax.axis_size("grp")
+    tables = [around(groups, n_gene, way * distance) for way, distance in steps] + [around(groups, n_gene, 0)]
     kinds = [jnp.bfloat16] * len(steps) + [jnp.float32]
     cuts = [0, 1, 2, len(tables)] if len(steps) > 2 else [0, 1, len(tables)]
     parted = lane_parts(genes_dev, genes_dev // n_row, n_row)
@@ -438,7 +441,7 @@
     for (way, _), own in zip(steps, blocks):
         if way in came:
             own = plus(own, came[way]).astype(jnp.bfloat16)
-        came[way] = lax.ppermute(own, "gene", list(enumerate(around(n_gene, way))))
+        came[way] = lax.ppermute(own, LINES, [(at, at // n_gene * n_gene + to) for at, to in enumerate(around(groups, n_gene, way))])
     others = [swap_row(parts[hop], hop, n_row) for hop in range(1, n_row)]
     *adam_out, grad_cells = finish([blocks[-1], *came.values()], [parts[0], *others], *adam)
     return (grad_cells, *adam_out)

time: 27 us -> 28.5 us (1.056)
  the two profiles are of different devices: /device:TPU:0 before, /device:TPU:9 now
where the time goes in v15:
time: 28.5 us; the launch traced here: 28.3 us
  starting transfers between devices  14.9 us (52%)
  Pallas kernels  7.98 us (28%)
  waiting for transfers between devices  3.69 us (13%)
  other arithmetic  0.95 us (3%)
  between operations  0.75 us (3%)
    ppermute x6, starting transfers between devices, swap_row(): lax.ppermute(value, 'row', [(me, partner(me, hop, size)) for me in range(...  8.95 us
    ppermute x3, starting transfers between devices, local(): lax.ppermute(own, LINES, [(at, at // n_gene * n_gene + to) for at, to in...  5.98 us
    pallas_call x2, Pallas kernels, block_rows(): pl.pallas_call(functools.partial(rows_kernel, tables, block, first, last,...  3.28 us
    ppermute x6, waiting for transfers between devices, swap_row(): lax.ppermute(value, 'row', [(me, partner(me, hop, size)) for me in range(...  2.77 us
    pallas_call x1, Pallas kernels, prepare(): pl.pallas_call(functools.partial(prepare_kernel, scale_k), out_shape=(VME...  2.26 us
    ppermute x3, waiting for transfers between devices, local(): lax.ppermute(own, LINES, [(at, at // n_gene * n_gene + to) for at, to in...  0.92 us
    pallas_call x1, Pallas kernels, first_block(): pl.pallas_call(functools.partial(rest_kernel, table, block, parts, n_row)...  0.91 us
    pallas_call x1, Pallas kernels, finish(): pl.pallas_call(functools.partial(finish_kernel, len(ends), len(parts)), o...  0.9 us
  transfers between devices with their start and end apart: 9, of which 3 were waited for; matrix products, arithmetic and copies ran while one was open for 0% of the time, Pallas kernels for 22%

profile of v15, /device:TPU:9, one launch (start us, length us, event | category | flops | bytes accessed | tf_op | source)
XLA Modules:
  0.0 28.3 jit_solution(3714568033260046779)
XLA Ops:
  0.6 0.9 %convert_element_type.12.own.refs_0_ = bf16[160,128]{1,0:T(8,128)(2,1)S(1)} convert(f32[160,128]{1,0:T(8,128)} %refs_7_.1) | non-fusion elementwise | flops 20480 | bytes 122880 | tf_op jit(solution)/shard_map/convert_element_type | solution.py:412
  1.5 1.8 %collective-permute-start.2 = (bf16[160,128]{1,0:T(8,128)(2,1)S(1)}, bf16[160,128]{1,0:T(8,128)(2,1)S(1)}, u32[]{:S(2)}, u32[]{:S(2)}) collective-permute-start(bf16[160,128]{1,0:T(8,128)(2,1)S(1)} %convert_element_type.12.own.refs_0_), channel_id=1, source_target_pairs={{0,3},{1,2},{2,1},{3,0},{4,7},{5,6},{6,5},{7,4},{8,11},{9,10},{10,... | collective-permute-start | bytes 122888 | tf_op jit(solution)/shard_map/ppermute | solution.py:331
  3.3 0.3 collective-permute-start.1
  3.6 0.2 collective-permute-start
  3.8 2.3 %prepare.1 = (bf16[3072,640]{1,0:T(8,128)(2,1)S(1)}, bf16[3072,128]{1,0:T(8,128)(2,1)S(1)}, bf16[128,3072]{1,0:T(8,128)(2,1)S(1)}, f32[1,640]{1,0:T(1,128)S(1)}, f32[640,128]{1,0:T(8,128)S(1)}) custom-call(bf16[3072,640]{1,0:T(8,128)(2,1)} %x_in.1, s32[3072]{0:T(1024)} %index_in.1, bf16[512,128]{1,0:T(8,128)(2,1)} %cell_in.1, f32[640]{0:T(1024)} %scale_in.1), custom_call_target="tpu_custom_call" | custom-call | flops 1610612736 | bytes 31457280 | tf_op jit(solution)/shard_map/prepare/pallas_call | solution.py:75
  6.0 0.0 collective-permute-done.other.refs_1_
  6.0 0.6 %early_part.1 = (f32[768,128]{1,0:T(8,128)S(1)}, f32[128,256]{1,0:T(8,128)S(1)}, bf16[128,256]{1,0:T(8,128)(2,1)S(1)}, bf16[256,128]{1,0:T(8,128)(2,1)S(1)}) custom-call(bf16[3072,640]{1,0:T(8,128)(2,1)S(1)} %get-tuple-element.29.x_ref.refs_0_, bf16[3072,128]{1,0:T(8,128)(2,1)S(1)} %get-tuple-element.30.f_ref.refs_1_, ...), custom_call_target="tpu_custom_call" | custom-call | flops 301989888 | bytes 786432 | tf_op jit(solution)/shard_map/early_part/pallas_call | solution.py:297
  6.7 0.9 %rest_part.1 = (bf16[768,128]{1,0:T(8,128)(2,1)S(1)}, f32[128,640]{1,0:T(8,128)S(1)}, bf16[128,640]{1,0:T(8,128)(2,1)S(1)}, bf16[640,128]{1,0:T(8,128)(2,1)S(1)}) custom-call(bf16[3072,640]{1,0:T(8,128)(2,1)S(1)} %get-tuple-element.29.x_ref.refs_0_, bf16[3072,128]{1,0:T(8,128)(2,1)S(1)} %get-tuple-element.30.f_ref.refs_1_, ...), custom_call_target="tpu_custom_call" | custom-call | flops 452984832 | bytes 1179648 | tf_op jit(solution)/shard_map/rest_part/pallas_call | solution.py:312
  7.6 2.3 %collective-permute-start.3 = (bf16[768,128]{1,0:T(8,128)(2,1)S(1)}, bf16[768,128]{1,0:T(8,128)(2,1)S(1)}, u32[]{:S(2)}, u32[]{:S(2)}) collective-permute-start(bf16[768,128]{1,0:T(8,128)(2,1)S(1)} %get-tuple-element.44), channel_id=1, source_target_pairs={{0,4},{4,12},{8,0},{12,8},{16,24},{20,16},{24,28},{28,20},{1,5},{5... | collective-permute-start | bytes 589832 | tf_op jit(solution)/shard_map/ppermute | solution.py:444
  10.0 1.2 %block_rows.2 = (bf16[768,128]{1,0:T(8,128)(2,1)S(1)}, f32[128,640]{1,0:T(8,128)S(1)}) custom-call(bf16[3072,640]{1,0:T(8,128)(2,1)S(1)} %get-tuple-element.29.x_ref.refs_0_, bf16[3072,128]{1,0:T(8,128)(2,1)S(1)} %get-tuple-element.30.f_ref.refs_1_, bf16[128,3072]{1,0:T(8,128)(2,1)S(1)} %get-tuple-element.31.ft_ref.refs_2_, ...), custom_call_target="tpu_custom_call" | custom-call | flops 377487360 | bytes 983040 | tf_op jit(solution)/shard_map/block_rows/pallas_call | solution.py:196
  11.2 0.0 copy-start
  11.2 0.0 copy-start.1
  11.2 0.0 copy-start.2
  11.2 0.1 collective-permute-start.5
  11.3 2.1 %block_rows.3 = (bf16[768,128]{1,0:T(8,128)(2,1)S(1)}, f32[768,128]{1,0:T(8,128)S(1)}, f32[160,128]{1,0:T(8,128)S(1)}, bf16[160,128]{1,0:T(8,128)(2,1)S(1)}, bf1...) custom-call(bf16[3072,640]{1,0:T(8,128)(2,1)S(1)} %get-tuple-element.29.x_ref.refs_0_, ...), custom_call_target="tpu_custom_call" | custom-call | flops 754974720 | bytes 1966080 | tf_op jit(solution)/shard_map/block_rows/pallas_call | solution.py:196
  13.4 0.9 %collective-permute-done.3 = bf16[768,128]{1,0:T(8,128)(2,1)S(1)} collective-permute-done((bf16[768,128]{1,0:T(8,128)(2,1)S(1)}, bf16[768,128]{1,0:T(8,128)(2,1)S(1)}, u32[]{:S(2)}, u32[]{:S(2)}) %collective-permute-start.3) | collective-permute-done | bytes 196640 | tf_op jit(solution)/shard_map/ppermute | solution.py:444
  14.3 0.1 add_convert_fusion
  14.3 3.6 %collective-permute-start.4 = (bf16[768,128]{1,0:T(8,128)(2,1)S(1)}, bf16[768,128]{1,0:T(8,128)(2,1)S(1)}, u32[]{:S(2)}, u32[]{:S(2)}) collective-permute-start(bf16[768,128]{1,0:T(8,128)(2,1)S(1)} %add_convert_fusion), channel_id=1, source_target_pairs={{0,4},{4,12},{8,0},{12,8},{16,24},{20,16},{24,28},{28,20},{1,5},{5... | collective-permute-start | bytes 589832 | tf_op jit(solution)/shard_map/ppermute | solution.py:444
  17.9 5.1 %collective-permute-start.6 = (bf16[160,128]{1,0:T(8,128)(2,1)S(1)}, bf16[160,128]{1,0:T(8,128)(2,1)S(1)}, u32[]{:S(2)}, u32[]{:S(2)}) collective-permute-start(bf16[160,128]{1,0:T(8,128)(2,1)S(1)} %get-tuple-element.47), channel_id=1, source_target_pairs={{0,1},{1,0},{2,3},{3,2},{4,5},{5,4},{6,7},{7,6},{8,9},{9,8},{10,11... | collective-permute-start | bytes 122888 | tf_op jit(solution)/shard_map/ppermute | solution.py:331
  23.0 0.9 %collective-permute-start.7 = (bf16[160,128]{1,0:T(8,128)(2,1)S(1)}, bf16[160,128]{1,0:T(8,128)(2,1)S(1)}, u32[]{:S(2)}, u32[]{:S(2)}) collective-permute-start(bf16[160,128]{1,0:T(8,128)(2,1)S(1)} %get-tuple-element.48), channel_id=1, source_target_pairs={{0,2},{1,3},{2,0},{3,1},{4,6},{5,7},{6,4},{7,5},{8,10},{9,11},{10,... | collective-permute-start | bytes 122888 | tf_op jit(solution)/shard_map/ppermute | solution.py:331
  23.9 0.7 %collective-permute-start.8 = (bf16[160,128]{1,0:T(8,128)(2,1)S(1)}, bf16[160,128]{1,0:T(8,128)(2,1)S(1)}, u32[]{:S(2)}, u32[]{:S(2)}) collective-permute-start(bf16[160,128]{1,0:T(8,128)(2,1)S(1)} %get-tuple-element.49), channel_id=1, source_target_pairs={{0,3},{1,2},{2,1},{3,0},{4,7},{5,6},{6,5},{7,4},{8,11},{9,10},{10,... | collective-permute-start | bytes 122888 | tf_op jit(solution)/shard_map/ppermute | solution.py:331
  24.6 1.2 %collective-permute-done.7.refs_5_ = bf16[160,128]{1,0:T(8,128)(2,1)S(1)} collective-permute-done((bf16[160,128]{1,0:T(8,128)(2,1)S(1)}, bf16[160,128]{1,0:T(8,128)(2,1)S(1)}, u32[]{:S(2)}, u32[]{:S(2)}) %collective-permute-start.7) | collective-permute-done | bytes 40992 | tf_op jit(solution)/shard_map/ppermute | solution.py:331
  25.8 1.5 %collective-permute-done.8.refs_6_ = bf16[160,128]{1,0:T(8,128)(2,1)S(1)} collective-permute-done((bf16[160,128]{1,0:T(8,128)(2,1)S(1)}, bf16[160,128]{1,0:T(8,128)(2,1)S(1)}, u32[]{:S(2)}, u32[]{:S(2)}) %collective-permute-start.8) | collective-permute-done | bytes 40992 | tf_op jit(solution)/shard_map/ppermute | solution.py:331
  27.4 0.9 %finish.1 = (f32[160,128]{1,0:T(8,128)}, f32[160,128]{1,0:T(8,128)}, f32[160,128]{1,0:T(8,128)}, f32[768,128]{1,0:T(8,128)}) custom-call(f32[768,128]{1,0:T(8,128)S(1)} %get-tuple-element.42.refs_0_, bf16[768,128]{1,0:T(8,128)(2,1)S(1)} %collective-permute-done.4.refs_1_, bf16[768,128]{1,0:T(8,128)(2,1)S(1)} %collective-permute-done.5.refs_2_, ...), custom_call_target="tpu_custom_call" | custom-call | flops 409600 | bytes 1753088 | tf_op jit(solution)/shard_map/finish/pallas_call | solution.py:394
  (8 shorter events, 0.0 us)
Async XLA Ops:
  1.5 5.2 %collective-permute-start.2 = (bf16[160,128]{1,0:T(8,128)(2,1)S(1)}, bf16[160,128]{1,0:T(8,128)(2,1)S(1)}, u32[]{:S(2)}, u32[]{:S(2)}) collective-permute-start(bf16[160,128]{1,0:T(8,128)(2,1)S(1)} %convert_element_type.12.own.refs_0_), channel_id=1, source_target_pairs={{0,3},{1,2},{2,1},{3,0},{4,7},{5,6},{6,5},{7,4},{8,11},{9,10},{10,... | collective-permute-start | bytes 122888 | tf_op jit(solution)/shard_map/ppermute | solution.py:331
  3.3 3.4 %collective-permute-start.1 = (bf16[160,128]{1,0:T(8,128)(2,1)S(1)}, bf16[160,128]{1,0:T(8,128)(2,1)S(1)}, u32[]{:S(2)}, u32[]{:S(2)}) collective-permute-start(bf16[160,128]{1,0:T(8,128)(2,1)S(1)} %convert_element_type.12.own.refs_0_), channel_id=1, source_target_pairs={{0,2},{1,3},{2,0},{3,1},{4,6},{5,7},{6,4},{7,5},{8,10},{9,11},{10,... | collective-permute-start | bytes 122888 | tf_op jit(solution)/shard_map/ppermute | solution.py:331
  3.6 2.5 %collective-permute-start = (bf16[160,128]{1,0:T(8,128)(2,1)S(1)}, bf16[160,128]{1,0:T(8,128)(2,1)S(1)}, u32[]{:S(2)}, u32[]{:S(2)}) collective-permute-start(bf16[160,128]{1,0:T(8,128)(2,1)S(1)} %convert_element_type.12.own.refs_0_), channel_id=1, source_target_pairs={{0,1},{1,0},{2,3},{3,2},{4,5},{5,4},{6,7},{7,6},{8,9},{9,8},{10,11... | collective-permute-start | bytes 122888 | tf_op jit(solution)/shard_map/ppermute | solution.py:331
  7.6 6.7 %collective-permute-start.3 = (bf16[768,128]{1,0:T(8,128)(2,1)S(1)}, bf16[768,128]{1,0:T(8,128)(2,1)S(1)}, u32[]{:S(2)}, u32[]{:S(2)}) collective-permute-start(bf16[768,128]{1,0:T(8,128)(2,1)S(1)} %get-tuple-element.44), channel_id=1, source_target_pairs={{0,4},{4,12},{8,0},{12,8},{16,24},{20,16},{24,28},{28,20},{1,5},{5... | collective-permute-start | bytes 589832 | tf_op jit(solution)/shard_map/ppermute | solution.py:444
  11.2 16.2 %copy-start = (f32[160,128]{1,0:T(8,128)S(1)}, f32[160,128]{1,0:T(8,128)}, u32[]{:S(2)}) copy-start(f32[160,128]{1,0:T(8,128)} %refs_7_.1) | copy-start | bytes 245764
  11.2 16.2 %copy-start.1 = (f32[160,128]{1,0:T(8,128)S(1)}, f32[160,128]{1,0:T(8,128)}, u32[]{:S(2)}) copy-start(f32[160,128]{1,0:T(8,128)} %refs_8_.1) | copy-start | bytes 245764
  11.2 16.2 %copy-start.2 = (f32[160,128]{1,0:T(8,128)S(1)}, f32[160,128]{1,0:T(8,128)}, u32[]{:S(2)}) copy-start(f32[160,128]{1,0:T(8,128)} %refs_9_.1) | copy-start | bytes 245764
  11.2 16.2 %collective-permute-start.5 = (bf16[768,128]{1,0:T(8,128)(2,1)S(1)}, bf16[768,128]{1,0:T(8,128)(2,1)S(1)}, u32[]{:S(2)}, u32[]{:S(2)}) collective-permute-start(bf16[768,128]{1,0:T(8,128)(2,1)S(1)} %get-tuple-element.45), channel_id=1, source_target_pairs={{0,8},{4,0},{8,12},{12,4},{16,20},{20,28},{24,16},{28,24},{1,9},{5... | collective-permute-start | bytes 589832 | tf_op jit(solution)/shard_map/ppermute | solution.py:444
  14.3 13.1 %collective-permute-start.4 = (bf16[768,128]{1,0:T(8,128)(2,1)S(1)}, bf16[768,128]{1,0:T(8,128)(2,1)S(1)}, u32[]{:S(2)}, u32[]{:S(2)}) collective-permute-start(bf16[768,128]{1,0:T(8,128)(2,1)S(1)} %add_convert_fusion), channel_id=1, source_target_pairs={{0,4},{4,12},{8,0},{12,8},{16,24},{20,16},{24,28},{28,20},{1,5},{5... | collective-permute-start | bytes 589832 | tf_op jit(solution)/shard_map/ppermute | solution.py:444
  17.9 6.7 %collective-permute-start.6 = (bf16[160,128]{1,0:T(8,128)(2,1)S(1)}, bf16[160,128]{1,0:T(8,128)(2,1)S(1)}, u32[]{:S(2)}, u32[]{:S(2)}) collective-permute-start(bf16[160,128]{1,0:T(8,128)(2,1)S(1)} %get-tuple-element.47), channel_id=1, source_target_pairs={{0,1},{1,0},{2,3},{3,2},{4,5},{5,4},{6,7},{7,6},{8,9},{9,8},{10,11... | collective-permute-start | bytes 122888 | tf_op jit(solution)/shard_map/ppermute | solution.py:331
  23.0 2.9 %collective-permute-start.7 = (bf16[160,128]{1,0:T(8,128)(2,1)S(1)}, bf16[160,128]{1,0:T(8,128)(2,1)S(1)}, u32[]{:S(2)}, u32[]{:S(2)}) collective-permute-start(bf16[160,128]{1,0:T(8,128)(2,1)S(1)} %get-tuple-element.48), channel_id=1, source_target_pairs={{0,2},{1,3},{2,0},{3,1},{4,6},{5,7},{6,4},{7,5},{8,10},{9,11},{10,... | collective-permute-start | bytes 122888 | tf_op jit(solution)/shard_map/ppermute | solution.py:331
  23.9 3.5 %collective-permute-start.8 = (bf16[160,128]{1,0:T(8,128)(2,1)S(1)}, bf16[160,128]{1,0:T(8,128)(2,1)S(1)}, u32[]{:S(2)}, u32[]{:S(2)}) collective-permute-start(bf16[160,128]{1,0:T(8,128)(2,1)S(1)} %get-tuple-element.49), channel_id=1, source_target_pairs={{0,3},{1,2},{2,1},{3,0},{4,7},{5,6},{6,5},{7,4},{8,11},{9,10},{10,... | collective-permute-start | bytes 122888 | tf_op jit(solution)/shard_map/ppermute | solution.py:331

commit v16 on v14

--- a/solution.py
+++ b/solution.py
@@ -331,7 +331,7 @@
 
 
 def ring_of(size):
-    return [*range(0, size, 2), *reversed(range(1, size, 2))]
+    return [0, *range(1, size, 2), *reversed(range(2, size, 2))]
 
 
 def steps_of(size):
@@ -421,7 +421,7 @@
     steps = steps_of(n_gene)
     tables = [around(n_gene, way * distance) for way, distance in steps] + [tuple(range(n_gene))]
     kinds = [jnp.bfloat16] * len(steps) + [jnp.float32]
-    cuts = [0, 1, 2, len(tables)] if len(steps) > 2 else [0, 1, len(tables)]
+    cuts = [0, 1, len(tables)]
     parted = lane_parts(genes_dev, genes_dev // n_row, n_row)
     carried, blocks = shares, []
     for low, high in zip(cuts, cuts[1:]):

time: 27 us -> 28.8 us (1.067)
  the two profiles are of different devices: /device:TPU:0 before, /device:TPU:9 now
where the time goes in v16:
time: 28.8 us; the launch traced here: 28.6 us
  starting transfers between devices  15.9 us (55%)
  Pallas kernels  7.62 us (26%)
  waiting for transfers between devices  3.35 us (12%)
  other arithmetic  0.95 us (3%)
  between operations  0.74 us (3%)
    ppermute x6, starting transfers between devices, swap_row(): lax.ppermute(value, 'row', [(me, partner(me, hop, size)) for me in range(...  10.3 us
    ppermute x3, starting transfers between devices, local(): came[way] = lax.ppermute(own, 'gene', list(enumerate(around(n_gene, way))))  5.67 us
    pallas_call x1, Pallas kernels, block_rows(): pl.pallas_call(functools.partial(rows_kernel, tables, block, first, last,...  2.92 us
    ppermute x6, waiting for transfers between devices, swap_row(): lax.ppermute(value, 'row', [(me, partner(me, hop, size)) for me in range(...  2.65 us
    pallas_call x1, Pallas kernels, prepare(): pl.pallas_call(functools.partial(prepare_kernel, scale_k), out_shape=(VME...  2.26 us
    pallas_call x1, Pallas kernels, first_block(): pl.pallas_call(functools.partial(rest_kernel, table, block, parts, n_row)...  0.91 us
    pallas_call x1, Pallas kernels, finish(): pl.pallas_call(functools.partial(finish_kernel, len(ends), len(parts)), o...  0.9 us
    convert_element_type x1, other arithmetic, local(): factor_bf = gene_factor.astype(jnp.bfloat16)  0.9 us
  transfers between devices with their start and end apart: 9, of which 3 were waited for; matrix products, arithmetic and copies ran while one was open for 0% of the time, Pallas kernels for 20%

profile of v16, /device:TPU:9, one launch (start us, length us, event | category | flops | bytes accessed | tf_op | source)
XLA Modules:
  0.0 28.6 jit_solution(16505654163447150789)
XLA Ops:
  0.6 0.9 %convert_element_type.12.own.refs_0_ = bf16[160,128]{1,0:T(8,128)(2,1)S(1)} convert(f32[160,128]{1,0:T(8,128)} %refs_7_.1) | non-fusion elementwise | flops 20480 | bytes 122880 | tf_op jit(solution)/shard_map/convert_element_type | solution.py:410
  1.5 1.8 %collective-permute-start.2 = (bf16[160,128]{1,0:T(8,128)(2,1)S(1)}, bf16[160,128]{1,0:T(8,128)(2,1)S(1)}, u32[]{:S(2)}, u32[]{:S(2)}) collective-permute-start(bf16[160,128]{1,0:T(8,128)(2,1)S(1)} %convert_element_type.12.own.refs_0_), channel_id=1, source_target_pairs={{0,3},{1,2},{2,1},{3,0},{4,7},{5,6},{6,5},{7,4},{8,11},{9,10},{10,... | collective-permute-start | bytes 122888 | tf_op jit(solution)/shard_map/ppermute | solution.py:330
  3.3 0.3 collective-permute-start.1
  3.6 0.2 collective-permute-start
  3.8 2.3 %prepare.1 = (bf16[3072,640]{1,0:T(8,128)(2,1)S(1)}, bf16[3072,128]{1,0:T(8,128)(2,1)S(1)}, bf16[128,3072]{1,0:T(8,128)(2,1)S(1)}, f32[1,640]{1,0:T(1,128)S(1)}, f32[640,128]{1,0:T(8,128)S(1)}) custom-call(bf16[3072,640]{1,0:T(8,128)(2,1)} %x_in.1, s32[3072]{0:T(1024)} %index_in.1, bf16[512,128]{1,0:T(8,128)(2,1)} %cell_in.1, f32[640]{0:T(1024)} %scale_in.1), custom_call_target="tpu_custom_call" | custom-call | flops 1610612736 | bytes 31457280 | tf_op jit(solution)/shard_map/prepare/pallas_call | solution.py:74
  6.0 0.0 collective-permute-done.other.refs_1_
  6.0 0.6 %early_part.1 = (f32[768,128]{1,0:T(8,128)S(1)}, f32[128,256]{1,0:T(8,128)S(1)}, bf16[128,256]{1,0:T(8,128)(2,1)S(1)}, bf16[256,128]{1,0:T(8,128)(2,1)S(1)}) custom-call(bf16[3072,640]{1,0:T(8,128)(2,1)S(1)} %get-tuple-element.28.x_ref.refs_0_, bf16[3072,128]{1,0:T(8,128)(2,1)S(1)} %get-tuple-element.29.f_ref.refs_1_, ...), custom_call_target="tpu_custom_call" | custom-call | flops 301989888 | bytes 786432 | tf_op jit(solution)/shard_map/early_part/pallas_call | solution.py:296
  6.7 0.9 %rest_part.1 = (bf16[768,128]{1,0:T(8,128)(2,1)S(1)}, f32[128,640]{1,0:T(8,128)S(1)}, bf16[128,640]{1,0:T(8,128)(2,1)S(1)}, bf16[640,128]{1,0:T(8,128)(2,1)S(1)}) custom-call(bf16[3072,640]{1,0:T(8,128)(2,1)S(1)} %get-tuple-element.28.x_ref.refs_0_, bf16[3072,128]{1,0:T(8,128)(2,1)S(1)} %get-tuple-element.29.f_ref.refs_1_, ...), custom_call_target="tpu_custom_call" | custom-call | flops 452984832 | bytes 1179648 | tf_op jit(solution)/shard_map/rest_part/pallas_call | solution.py:311
  7.6 0.0 copy-start
  7.6 0.0 copy-start.1
  7.6 0.0 copy-start.2
  7.7 2.3 %collective-permute-start.3 = (bf16[768,128]{1,0:T(8,128)(2,1)S(1)}, bf16[768,128]{1,0:T(8,128)(2,1)S(1)}, u32[]{:S(2)}, u32[]{:S(2)}) collective-permute-start(bf16[768,128]{1,0:T(8,128)(2,1)S(1)} %get-tuple-element.42), channel_id=1, source_target_pairs={{0,4},{4,12},{8,0},{12,8},{1,5},{5,13},{9,1},{13,9},{2,6},{6,14},{... | collective-permute-start | bytes 589832 | tf_op jit(solution)/shard_map/ppermute | solution.py:441
  10.0 2.9 %block_rows.1 = (bf16[768,128]{1,0:T(8,128)(2,1)S(1)}, bf16[768,128]{1,0:T(8,128)(2,1)S(1)}, f32[768,128]{1,0:T(8,128)S(1)}, f32[160,128]{1,0:T(8,128)S(1)}, bf1...) custom-call(bf16[3072,640]{1,0:T(8,128)(2,1)S(1)} %get-tuple-element.28.x_ref.refs_0_, ...), custom_call_target="tpu_custom_call" | custom-call | flops 1132462080 | bytes 2949120 | tf_op jit(solution)/shard_map/block_rows/pallas_call | solution.py:195
  12.9 0.1 collective-permute-start.5
  13.0 0.7 %collective-permute-done.3 = bf16[768,128]{1,0:T(8,128)(2,1)S(1)} collective-permute-done((bf16[768,128]{1,0:T(8,128)(2,1)S(1)}, bf16[768,128]{1,0:T(8,128)(2,1)S(1)}, u32[]{:S(2)}, u32[]{:S(2)}) %collective-permute-start.3) | collective-permute-done | bytes 196640 | tf_op jit(solution)/shard_map/ppermute | solution.py:441
  13.7 0.1 add_convert_fusion
  13.8 3.3 %collective-permute-start.4 = (bf16[768,128]{1,0:T(8,128)(2,1)S(1)}, bf16[768,128]{1,0:T(8,128)(2,1)S(1)}, u32[]{:S(2)}, u32[]{:S(2)}) collective-permute-start(bf16[768,128]{1,0:T(8,128)(2,1)S(1)} %add_convert_fusion), channel_id=1, source_target_pairs={{0,4},{4,12},{8,0},{12,8},{1,5},{5,13},{9,1},{13,9},{2,6},{6,14},{... | collective-permute-start | bytes 589832 | tf_op jit(solution)/shard_map/ppermute | solution.py:441
  17.0 6.4 %collective-permute-start.6 = (bf16[160,128]{1,0:T(8,128)(2,1)S(1)}, bf16[160,128]{1,0:T(8,128)(2,1)S(1)}, u32[]{:S(2)}, u32[]{:S(2)}) collective-permute-start(bf16[160,128]{1,0:T(8,128)(2,1)S(1)} %get-tuple-element.45), channel_id=1, source_target_pairs={{0,1},{1,0},{2,3},{3,2},{4,5},{5,4},{6,7},{7,6},{8,9},{9,8},{10,11... | collective-permute-start | bytes 122888 | tf_op jit(solution)/shard_map/ppermute | solution.py:330
  23.4 0.5 %collective-permute-start.7 = (bf16[160,128]{1,0:T(8,128)(2,1)S(1)}, bf16[160,128]{1,0:T(8,128)(2,1)S(1)}, u32[]{:S(2)}, u32[]{:S(2)}) collective-permute-start(bf16[160,128]{1,0:T(8,128)(2,1)S(1)} %get-tuple-element.46), channel_id=1, source_target_pairs={{0,2},{1,3},{2,0},{3,1},{4,6},{5,7},{6,4},{7,5},{8,10},{9,11},{10,... | collective-permute-start | bytes 122888 | tf_op jit(solution)/shard_map/ppermute | solution.py:330
  23.9 1.1 %collective-permute-start.8 = (bf16[160,128]{1,0:T(8,128)(2,1)S(1)}, bf16[160,128]{1,0:T(8,128)(2,1)S(1)}, u32[]{:S(2)}, u32[]{:S(2)}) collective-permute-start(bf16[160,128]{1,0:T(8,128)(2,1)S(1)} %get-tuple-element.47), channel_id=1, source_target_pairs={{0,3},{1,2},{2,1},{3,0},{4,7},{5,6},{6,5},{7,4},{8,11},{9,10},{10,... | collective-permute-start | bytes 122888 | tf_op jit(solution)/shard_map/ppermute | solution.py:330
  25.1 1.2 %collective-permute-done.7.refs_5_ = bf16[160,128]{1,0:T(8,128)(2,1)S(1)} collective-permute-done((bf16[160,128]{1,0:T(8,128)(2,1)S(1)}, bf16[160,128]{1,0:T(8,128)(2,1)S(1)}, u32[]{:S(2)}, u32[]{:S(2)}) %collective-permute-start.7) | collective-permute-done | bytes 40992 | tf_op jit(solution)/shard_map/ppermute | solution.py:330
  26.3 1.4 %collective-permute-done.8.refs_6_ = bf16[160,128]{1,0:T(8,128)(2,1)S(1)} collective-permute-done((bf16[160,128]{1,0:T(8,128)(2,1)S(1)}, bf16[160,128]{1,0:T(8,128)(2,1)S(1)}, u32[]{:S(2)}, u32[]{:S(2)}) %collective-permute-start.8) | collective-permute-done | bytes 40992 | tf_op jit(solution)/shard_map/ppermute | solution.py:330
  27.7 0.0 collective-permute-done.4.refs_1_
  27.7 0.9 %finish.1 = (f32[160,128]{1,0:T(8,128)}, f32[160,128]{1,0:T(8,128)}, f32[160,128]{1,0:T(8,128)}, f32[768,128]{1,0:T(8,128)}) custom-call(f32[768,128]{1,0:T(8,128)S(1)} %get-tuple-element.40.refs_0_, bf16[768,128]{1,0:T(8,128)(2,1)S(1)} %collective-permute-done.4.refs_1_, bf16[768,128]{1,0:T(8,128)(2,1)S(1)} %collective-permute-done.5.refs_2_, ...), custom_call_target="tpu_custom_call" | custom-call | flops 409600 | bytes 1753088 | tf_op jit(solution)/shard_map/finish/pallas_call | solution.py:392
  (7 shorter events, 0.0 us)
Async XLA Ops:
  1.5 5.2 %collective-permute-start.2 = (bf16[160,128]{1,0:T(8,128)(2,1)S(1)}, bf16[160,128]{1,0:T(8,128)(2,1)S(1)}, u32[]{:S(2)}, u32[]{:S(2)}) collective-permute-start(bf16[160,128]{1,0:T(8,128)(2,1)S(1)} %convert_element_type.12.own.refs_0_), channel_id=1, source_target_pairs={{0,3},{1,2},{2,1},{3,0},{4,7},{5,6},{6,5},{7,4},{8,11},{9,10},{10,... | collective-permute-start | bytes 122888 | tf_op jit(solution)/shard_map/ppermute | solution.py:330
  3.3 3.4 %collective-permute-start.1 = (bf16[160,128]{1,0:T(8,128)(2,1)S(1)}, bf16[160,128]{1,0:T(8,128)(2,1)S(1)}, u32[]{:S(2)}, u32[]{:S(2)}) collective-permute-start(bf16[160,128]{1,0:T(8,128)(2,1)S(1)} %convert_element_type.12.own.refs_0_), channel_id=1, source_target_pairs={{0,2},{1,3},{2,0},{3,1},{4,6},{5,7},{6,4},{7,5},{8,10},{9,11},{10,... | collective-permute-start | bytes 122888 | tf_op jit(solution)/shard_map/ppermute | solution.py:330
  3.6 2.5 %collective-permute-start = (bf16[160,128]{1,0:T(8,128)(2,1)S(1)}, bf16[160,128]{1,0:T(8,128)(2,1)S(1)}, u32[]{:S(2)}, u32[]{:S(2)}) collective-permute-start(bf16[160,128]{1,0:T(8,128)(2,1)S(1)} %convert_element_type.12.own.refs_0_), channel_id=1, source_target_pairs={{0,1},{1,0},{2,3},{3,2},{4,5},{5,4},{6,7},{7,6},{8,9},{9,8},{10,11... | collective-permute-start | bytes 122888 | tf_op jit(solution)/shard_map/ppermute | solution.py:330
  7.6 20.1 %copy-start = (f32[160,128]{1,0:T(8,128)S(1)}, f32[160,128]{1,0:T(8,128)}, u32[]{:S(2)}) copy-start(f32[160,128]{1,0:T(8,128)} %refs_7_.1) | copy-start | bytes 245764
  7.6 20.1 %copy-start.1 = (f32[160,128]{1,0:T(8,128)S(1)}, f32[160,128]{1,0:T(8,128)}, u32[]{:S(2)}) copy-start(f32[160,128]{1,0:T(8,128)} %refs_8_.1) | copy-start | bytes 245764
  7.6 20.1 %copy-start.2 = (f32[160,128]{1,0:T(8,128)S(1)}, f32[160,128]{1,0:T(8,128)}, u32[]{:S(2)}) copy-start(f32[160,128]{1,0:T(8,128)} %refs_9_.1) | copy-start | bytes 245764
  7.7 6.0 %collective-permute-start.3 = (bf16[768,128]{1,0:T(8,128)(2,1)S(1)}, bf16[768,128]{1,0:T(8,128)(2,1)S(1)}, u32[]{:S(2)}, u32[]{:S(2)}) collective-permute-start(bf16[768,128]{1,0:T(8,128)(2,1)S(1)} %get-tuple-element.42), channel_id=1, source_target_pairs={{0,4},{4,12},{8,0},{12,8},{1,5},{5,13},{9,1},{13,9},{2,6},{6,14},{... | collective-permute-start | bytes 589832 | tf_op jit(solution)/shard_map/ppermute | solution.py:441
  12.9 14.8 %collective-permute-start.5 = (bf16[768,128]{1,0:T(8,128)(2,1)S(1)}, bf16[768,128]{1,0:T(8,128)(2,1)S(1)}, u32[]{:S(2)}, u32[]{:S(2)}) collective-permute-start(bf16[768,128]{1,0:T(8,128)(2,1)S(1)} %get-tuple-element.43), channel_id=1, source_target_pairs={{0,8},{4,0},{8,12},{12,4},{1,9},{5,1},{9,13},{13,5},{2,10},{6,2},{... | collective-permute-start | bytes 589832 | tf_op jit(solution)/shard_map/ppermute | solution.py:441
  13.8 14.0 %collective-permute-start.4 = (bf16[768,128]{1,0:T(8,128)(2,1)S(1)}, bf16[768,128]{1,0:T(8,128)(2,1)S(1)}, u32[]{:S(2)}, u32[]{:S(2)}) collective-permute-start(bf16[768,128]{1,0:T(8,128)(2,1)S(1)} %add_convert_fusion), channel_id=1, source_target_pairs={{0,4},{4,12},{8,0},{12,8},{1,5},{5,13},{9,1},{13,9},{2,6},{6,14},{... | collective-permute-start | bytes 589832 | tf_op jit(solution)/shard_map/ppermute | solution.py:441
  17.0 8.0 %collective-permute-start.6 = (bf16[160,128]{1,0:T(8,128)(2,1)S(1)}, bf16[160,128]{1,0:T(8,128)(2,1)S(1)}, u32[]{:S(2)}, u32[]{:S(2)}) collective-permute-start(bf16[160,128]{1,0:T(8,128)(2,1)S(1)} %get-tuple-element.45), channel_id=1, source_target_pairs={{0,1},{1,0},{2,3},{3,2},{4,5},{5,4},{6,7},{7,6},{8,9},{9,8},{10,11... | collective-permute-start | bytes 122888 | tf_op jit(solution)/shard_map/ppermute | solution.py:330
  23.4 2.9 %collective-permute-start.7 = (bf16[160,128]{1,0:T(8,128)(2,1)S(1)}, bf16[160,128]{1,0:T(8,128)(2,1)S(1)}, u32[]{:S(2)}, u32[]{:S(2)}) collective-permute-start(bf16[160,128]{1,0:T(8,128)(2,1)S(1)} %get-tuple-element.46), channel_id=1, source_target_pairs={{0,2},{1,3},{2,0},{3,1},{4,6},{5,7},{6,4},{7,5},{8,10},{9,11},{10,... | collective-permute-start | bytes 122888 | tf_op jit(solution)/shard_map/ppermute | solution.py:330
  23.9 3.8 %collective-permute-start.8 = (bf16[160,128]{1,0:T(8,128)(2,1)S(1)}, bf16[160,128]{1,0:T(8,128)(2,1)S(1)}, u32[]{:S(2)}, u32[]{:S(2)}) collective-permute-start(bf16[160,128]{1,0:T(8,128)(2,1)S(1)} %get-tuple-element.47), channel_id=1, source_target_pairs={{0,3},{1,2},{2,1},{3,0},{4,7},{5,6},{6,5},{7,4},{8,11},{9,10},{10,... | collective-permute-start | bytes 122888 | tf_op jit(solution)/shard_map/ppermute | solution.py:330

commit v17 on v2

v17 whole, which is shorter than its diff:
```python
import functools
import itertools
import math

import jax
import jax.numpy as jnp
from jax import lax
from jax.experimental import pallas as pl
from jax.experimental.pallas import tpu as pltpu
from jax.sharding import PartitionSpec as P

tukey_c = 4.685
beta_one = 0.9
beta_two = 0.999
learn_rate = 0.02
adam_eps = 1e-08

RING_MOST = 8
VMEM = pltpu.VMEM
IN_VMEM = pl.BlockSpec(memory_space=VMEM)
IN_ANY = pl.BlockSpec(memory_space=pl.ANY)


def tile_of(rows, most):
    best = [t for t in range(128, most + 1, 128) if rows % t == 0]
    return best[-1] if best else rows


def params():
    return pltpu.CompilerParams(vmem_limit_bytes=24 * 1024 * 1024)


def cost(flops, moved):
    return pl.CostEstimate(flops=int(flops), bytes_accessed=int(moved), transcendentals=0)


def pinned(*arrays):
    return [pltpu.with_memory_space_constraint(a, VMEM) for a in arrays]


def pick(axis, table):
    me = lax.axis_index(axis)
    value = jnp.int32(table[0])
    for place, entry in enumerate(table[1:], 1):
        value = jnp.where(me == place, jnp.int32(entry), value)
    return value


def partner(me, hop, size):
    return me ^ hop if size & (size - 1) == 0 else (me + hop) % size


def source(me, hop, size):
    return me ^ hop if size & (size - 1) == 0 else (me + size - hop) % size


def first_row(table, block):
    return pl.multiple_of(pick("gene", table) * block, block) if len(table) > 1 else 0


def gather(cells, local):
    hot = lax.broadcasted_iota(jnp.int32, (cells.shape[1], local.shape[1]), 0) == local
    hot = jnp.where(hot, 1.0, 0.0).astype(jnp.bfloat16)
    return jnp.dot(cells, hot, preferred_element_type=jnp.float32)


def predict(factors, wide):
    return jnp.dot(factors, wide, preferred_element_type=jnp.float32)


def influence(x, pred, bend):
    resid = x.astype(jnp.float32) - pred
    inside = jnp.maximum(1.0 - resid * resid * bend, 0.0)
    return (resid * (inside * inside)).astype(jnp.bfloat16)


def add_to(total, cols):
    return cols if total is None else total + cols


def prepare_kernel(scale_k, table, block, x_in, index_in, cell_in, scale_in, *refs):
    x_out, f_out, ft_out, bend_out, shrink_out, index_out, cells_out, index, cell, scale, sems = refs
    here = pl.ds(first_row(table, block), block)
    pairs = ((scale_in, scale), (cell_in, cell), (index_in, index), (x_in.at[here, :], x_out))
    loads = [pltpu.make_async_copy(src, dst, sems.at[at]) for at, (src, dst) in enumerate(pairs)]
    for load in loads:
        load.start()
    cells, rank = cell.shape
    rows = index.shape[0]
    genes = scale.shape[0]
    loads[0].wait()
    inverse = 1.0 / scale[...].reshape(1, genes)
    bend_out[...] = (inverse * inverse) * (1.0 / (tukey_c * tukey_c))
    shrink_out[...] = jnp.transpose(jnp.broadcast_to(-scale_k * (inverse * inverse), (rank, genes)))
    loads[1].wait()
    turned = jnp.transpose(cell[...].astype(jnp.float32)).astype(jnp.bfloat16)
    cells_out[...] = turned
    loads[2].wait()
    step = tile_of(rows, 512)
    for at in range(0, rows, step):
        index_out[:, at : at + step] = index[at : at + step].reshape(1, step) - lax.axis_index("row") * cells
    step = tile_of(block, 256)
    for at in range(0, block, step):
        start = first_row(table, block) + at
        if len(table) > 1:
            start = pl.multiple_of(start, math.gcd(block, step))
        picked = gather(turned, index_out[:, pl.ds(start, step)])
        ft_out[:, at : at + step] = picked.astype(jnp.bfloat16)
        f_out[at : at + step, :] = jnp.transpose(picked).astype(jnp.bfloat16)
    loads[3].wait()


def prepare(table, block, x_slab, row_index, cell_factor, gene_scale, scale_k):
    rows, genes = x_slab.shape
    cells, rank = cell_factor.shape
    ins = (x_slab, row_index, cell_factor, gene_scale)
    return pl.pallas_call(
        functools.partial(prepare_kernel, scale_k, table, block),
        out_shape=(
            VMEM((block, genes), jnp.bfloat16),
            VMEM((block, rank), jnp.bfloat16),
            VMEM((rank, block), jnp.bfloat16),
            VMEM((1, genes), jnp.float32),
            VMEM((genes, rank), jnp.float32),
            VMEM((1, rows), jnp.int32),
            VMEM((rank, cells), jnp.bfloat16),
        ),
        in_specs=[IN_ANY] * 4,
        out_specs=(IN_VMEM,) * 7,
        scratch_shapes=[
            VMEM((rows,), jnp.int32),
            VMEM((cells, rank), jnp.bfloat16),
            VMEM((genes,), jnp.float32),
            pltpu.SemaphoreType.DMA((4,)),
        ],
        compiler_params=params(),
        cost_estimate=cost(8 * block * cells * rank, 16 * block * genes),
        name="prepare",
    )(*(pltpu.with_memory_space_constraint(a, pltpu.HBM) for a in ins))


def lane_parts(genes, depth, n_row):
    if n_row != 4:
        return None
    pairs = [(2 * depth * (place // 2), 2 * depth * (place // 2 + 1)) for place in range(n_row)]
    low = [-(-begin // 128) * 128 for begin, _ in pairs]
    width = min(end // 128 * 128 - begin for begin, (_, end) in zip(low, pairs))
    if width <= 0 or any(begin not in (0, genes - width) for begin in low):
        return None
    return low, width, [width if begin == 0 else 0 for begin in low]


def lanes(table, width):
    return pl.ds(pl.multiple_of(pick("row", table), 128), width)


def over_lanes(here, x_ref, f_ref, ft_ref, bend_ref, wide, scaled):
    block = x_ref.shape[0]
    step = tile_of(block, 256)
    tiles = [pl.ds(at, step) for at in range(0, block, step)]
    bend = bend_ref[:, here]
    preds = [predict(f_ref[tile, :], wide) for tile in tiles]
    infls = [influence(x_ref[tile, here], pred, bend) for tile, pred in zip(tiles, preds)]
    rows, total = [], None
    for tile, infl in zip(tiles, infls):
        rows.append((tile, jnp.dot(infl, scaled, preferred_element_type=jnp.float32)))
        total = add_to(total, jnp.dot(ft_ref[:, tile], infl, preferred_element_type=jnp.float32))
    return rows, total


def early_kernel(parts, x_ref, f_ref, ft_ref, bend_ref, shrink_ref, own, other, *refs):
    rows_out, total_out, wide_out, scaled_out, pair = refs
    low, width, _ = parts
    depth = own.shape[0]
    odd = lax.axis_index("row") % 2
    pair[pl.ds(pl.multiple_of(odd * depth, depth), depth), :] = own[...]
    pair[pl.ds(pl.multiple_of((1 - odd) * depth, depth), depth), :] = other[...]
    inset = [begin - 2 * depth * (place // 2) for place, begin in enumerate(low)]
    whole = pair[pl.ds(pl.multiple_of(pick("row", inset), math.gcd(*inset, 128)), width), :].astype(jnp.float32)
    here = lanes(low, width)
    wide = jnp.transpose(whole).astype(jnp.bfloat16)
    scaled = (whole * shrink_ref[here, :]).astype(jnp.bfloat16)
    wide_out[...] = wide
    scaled_out[...] = scaled
    rows, total = over_lanes(here, x_ref, f_ref, ft_ref, bend_ref, wide, scaled)
    for tile, value in rows:
        rows_out[tile, :] = value
    total_out[...] = total


def rest_kernel(parts, n_row, x_ref, f_ref, ft_ref, bend_ref, shrink_ref, *refs):
    shares, refs = refs[:n_row], refs[n_row:]
    if parts:
        (rows_in, total_in, wide_in, scaled_in), refs = refs[:4], refs[4:]
    rows_out, total_out, wide_out, scaled_out, piece = refs
    me = lax.axis_index("row")
    depth = shares[0].shape[0]
    for hop in range(n_row):
        start = pl.multiple_of(source(me, hop, n_row) * depth, depth)
        piece[pl.ds(start, depth), :] = shares[hop][...]
    here = lanes(parts[2], n_row * depth - parts[1]) if parts else pl.ds(0, n_row * depth)
    whole = piece[here, :].astype(jnp.float32)
    wide = jnp.transpose(whole).astype(jnp.bfloat16)
    scaled = (whole * shrink_ref[here, :]).astype(jnp.bfloat16)
    rows, total = over_lanes(here, x_ref, f_ref, ft_ref, bend_ref, wide, scaled)
    for tile, value in rows:
        rows_out[tile, :] = (rows_in[tile, :] + value if parts else value).astype(rows_out.dtype)
    total_out[:, here] = total
    wide_out[:, here] = wide
    scaled_out[here, :] = scaled
    if parts:
        done = lanes(parts[0], parts[1])
        total_out[:, done] = total_in[...]
        wide_out[:, done] = wide_in[...]
        scaled_out[done, :] = scaled_in[...]


def first_block(kind, parts, n_row, fixed, shares):
    block, genes = fixed[0].shape
    rank = fixed[1].shape[1]
    width = parts[1] if parts else 0
    ins = pinned(*fixed)
    early = []
    if parts:
        early = pl.pallas_call(
            functools.partial(early_kernel, parts),
            out_shape=(
                VMEM((block, rank), jnp.float32),
                VMEM((rank, width), jnp.float32),
                VMEM((rank, width), jnp.bfloat16),
                VMEM((width, rank), jnp.bfloat16),
            ),
            in_specs=[IN_VMEM] * 7,
            out_specs=(IN_VMEM,) * 4,
            scratch_shapes=[VMEM((2 * (genes // n_row), rank), jnp.bfloat16)],
            compiler_params=params(),
            cost_estimate=cost(12 * block * width * rank, block * width * 4),
            name="early_part",
        )(*ins, *shares[:2])
    done, *carried = pl.pallas_call(
        functools.partial(rest_kernel, parts, n_row),
        out_shape=(
            jax.ShapeDtypeStruct((block, rank), kind),
            VMEM((rank, genes), jnp.float32),
            VMEM((rank, genes), jnp.bfloat16),
            VMEM((genes, rank), jnp.bfloat16),
        ),
        in_specs=[IN_VMEM] * (5 + n_row + len(early)),
        out_specs=(IN_VMEM,) * 4,
        scratch_shapes=[VMEM((genes, rank), jnp.bfloat16)],
        compiler_params=params(),
        cost_estimate=cost(12 * block * (genes - width) * rank, block * (genes - width) * 4),
        name="rest_part",
    )(*ins, *shares, *pinned(*early))
    return done, carried


def more_kernel(tables, block, last, n_row, x_in, index_ref, cells_ref, bend_ref, shrink_ref, *refs):
    (total_in, wide_in, scaled_in), refs = refs[:3], refs[3:]
    rows_out, refs = refs[: len(tables)], refs[len(tables) :]
    grads_out, refs = (refs[:n_row], refs[n_row:]) if last else (refs[:1], refs[1:])
    loads = []
    if tables:
        *refs, held, sems = refs
        for at, table in enumerate(tables):
            span = x_in.at[pl.ds(first_row(table, block), block), :]
            loads.append(pltpu.make_async_copy(span, held.at[at], sems.at[at]))
            loads[-1].start()
    wide, scaled, cells, bend = wide_in[...], scaled_in[...], cells_ref[...], bend_ref[...]
    total = total_in[...]
    step = tile_of(block, 256)
    tiles = [(at, low) for at in range(len(tables)) for low in range(0, block, step)]

    def factors(tile):
        at, low = tile
        start = first_row(tables[at], block) + low
        if len(tables[at]) > 1:
            start = pl.multiple_of(start, math.gcd(block, step))
        picked = gather(cells, index_ref[:, pl.ds(start, step)])
        return picked.astype(jnp.bfloat16), jnp.transpose(picked).astype(jnp.bfloat16)

    ahead, behind = None, None
    for number, (at, low) in enumerate(tiles):
        if ahead is None:
            turned, flat = factors(tiles[0])
            ahead = turned, predict(flat, wide)
        (turned, pred), ahead = ahead, None
        if number + 1 < len(tiles):
            later, flat = factors(tiles[number + 1])
            ahead = later, predict(flat, wide)
        if low == 0:
            loads[at].wait()
        now = influence(held[at, low : low + step, :], pred, bend)
        for tile in [behind] if behind else []:
            total = more_gradients(rows_out, tile, scaled, total)
        behind = at, low, turned, now
    if behind:
        total = more_gradients(rows_out, behind, scaled, total)
    if not last:
        grads_out[0][...] = total
        return
    (flipped,) = refs
    flipped[...] = jnp.transpose(total) * shrink_ref[...]
    me = lax.axis_index("row")
    depth = grads_out[0].shape[0]
    for hop in range(n_row):
        start = pl.multiple_of(partner(me, hop, n_row) * depth, depth)
        grads_out[hop][...] = flipped[pl.ds(start, depth), :].astype(grads_out[hop].dtype)


def more_gradients(rows_out, tile, scaled, total):
    at, low, turned, infl = tile
    rows = jnp.dot(infl, scaled, preferred_element_type=jnp.float32)
    rows_out[at][low : low + rows.shape[0], :] = rows.astype(rows_out[at].dtype)
    return total + jnp.dot(turned, infl, preferred_element_type=jnp.float32)


def more_blocks(tables, kinds, block, last, n_row, x_slab, shared, carried):
    genes, rank = shared[3].shape
    out = [jax.ShapeDtypeStruct((block, rank), kind) for kind in kinds]
    if last:
        out += [jax.ShapeDtypeStruct((genes // n_row, rank), jnp.bfloat16 if hop else jnp.float32) for hop in range(n_row)]
    else:
        out += [VMEM((rank, genes), jnp.float32)]
    scratch = [VMEM((genes, rank), jnp.float32)] if last else []
    if tables:
        scratch += [VMEM((len(tables), block, genes), jnp.bfloat16), pltpu.SemaphoreType.DMA((len(tables),))]
    ins = [pltpu.with_memory_space_constraint(x_slab, pltpu.HBM), *pinned(*shared, *carried)]
    work = len(tables) * block * genes
    out = pl.pallas_call(
        functools.partial(more_kernel, tables, block, last, n_row),
        out_shape=tuple(out),
        in_specs=[IN_ANY] + [IN_VMEM] * (len(ins) - 1),
        out_specs=(IN_VMEM,) * len(out),
        scratch_shapes=scratch,
        compiler_params=params(),
        cost_estimate=cost(12 * work * rank, work * 4),
        name="more_blocks",
    )(*ins)
    done, rest = list(out[: len(tables)]), list(out[len(tables) :])
    return done, rest if last else rest + list(carried[1:])


def swap_row(value, hop, size):
    return lax.ppermute(value, "row", [(me, partner(me, hop, size)) for me in range(size)])


def gather_row(own, size, before):
    shares = [own]
    for hop in range(1, size):
        fast = hop & -hop
        if size & (size - 1) or hop == fast:
            shares.append(swap_row(own, hop, size))
        else:
            held, _ = lax.optimization_barrier((shares[hop ^ fast], before))
            shares.append(swap_row(held, fast, size))
    return shares


def ring_of(size):
    return [*range(0, size, 2), *reversed(range(1, size, 2))]


def steps_of(size):
    ahead = [(1, distance) for distance in range(size // 2, 0, -1)]
    back = [(-1, distance) for distance in range((size - 1) // 2, 0, -1)]
    return [step for pair in itertools.zip_longest(ahead, back) for step in pair if step]


def around(size, hops):
    ring = ring_of(size)
    return tuple(ring[(ring.index(place) + hops) % size] for place in range(size))


def plus(wide, narrow):
    return wide.astype(jnp.float32) + narrow.astype(jnp.float32)


def finish_kernel(n_ends, n_parts, *refs):
    n_ins = n_ends + n_parts + 3
    ins, outs = refs[:n_ins], refs[n_ins : n_ins + 3 + bool(n_ends)]
    *held, sems = refs[n_ins + len(outs) :]
    ends, parts = ins[:n_ends], ins[n_ends : n_ends + n_parts]
    factor, first, second = ins[n_ends + n_parts :]
    copies = []

    def send(at, span, value):
        held[at][span, :] = value
        copies.append(pltpu.make_async_copy(held[at].at[span, :], outs[at].at[span, :], sems.at[len(copies)]))
        copies[-1].start()

    if ends:
        step = tile_of(ends[0].shape[0], 256)
        for low in range(0, ends[0].shape[0], step):
            span = pl.ds(low, step)
            rows = ends[0][span, :]
            for end in ends[1:]:
                rows = plus(rows, end[span, :])
            send(3, span, rows)
    grad = parts[0][...]
    for part in parts[1:]:
        grad = plus(grad, part[...])
    span = pl.ds(0, grad.shape[0])
    new_first = beta_one * first[...] + (1.0 - beta_one) * grad
    new_second = beta_two * second[...] + (1.0 - beta_two) * grad * grad
    send(1, span, new_first)
    send(2, span, new_second)
    first_hat = new_first / (1.0 - beta_one**10)
    second_hat = new_second / (1.0 - beta_two**10)
    send(0, span, factor[...] - learn_rate * first_hat / (jnp.sqrt(second_hat) + adam_eps))
    for copy in copies:
        copy.wait()


def finish(ends, parts, factor, first, second):
    ins = [*ends, *parts, factor, first, second]
    shapes = [factor, factor, factor] + list(ends[:1])
    n_copies = 3 + (ends[0].shape[0] // tile_of(ends[0].shape[0], 256) if ends else 0)
    return pl.pallas_call(
        functools.partial(finish_kernel, len(ends), len(parts)),
        out_shape=tuple(jax.ShapeDtypeStruct(like.shape, jnp.float32) for like in shapes),
        in_specs=[IN_VMEM] * len(ins),
        out_specs=(IN_ANY,) * len(shapes),
        scratch_shapes=[VMEM(like.shape, jnp.float32) for like in shapes] + [pltpu.SemaphoreType.DMA((n_copies,))],
        compiler_params=params(),
        cost_estimate=cost(20 * factor.size, sum(4 * a.size for a in ins)),
        name="finish",
    )(*ins)


def local(x_slab, cell_factor, row_index, gene_scale, gene_factor, first_moment, second_moment):
    rows_dev, genes_dev = x_slab.shape
    n_gene = lax.axis_size("gene")
    n_row = lax.axis_size("row")
    block = rows_dev // n_gene
    scale_k = 4.0 / math.sqrt(genes_dev * n_gene)
    factor_bf = gene_factor.astype(jnp.bfloat16)
    adam = (gene_factor, first_moment, second_moment)
    ringed = 1 < n_gene <= RING_MOST and block % 128 == 0
    steps = steps_of(n_gene) if ringed else []
    tables = [around(n_gene, way * far) for way, far in steps] + [tuple(range(n_gene))] if ringed else [(0,)]
    if not ringed:
        block = rows_dev
    *fixed, index, cells = prepare(tables[0], block, x_slab, row_index, cell_factor, gene_scale, scale_k)
    shared = (index, cells, fixed[3], fixed[4])
    shares = gather_row(factor_bf, n_row, fixed[3])
    parted = lane_parts(genes_dev, genes_dev // n_row, n_row) if ringed else None
    done, carried = first_block(jnp.bfloat16 if ringed else jnp.float32, parted, n_row, fixed, shares)

    if not ringed:
        _, parts = more_blocks([], [], block, True, n_row, x_slab, shared, carried)
        grad_cells = lax.psum_scatter(done, "gene", scatter_dimension=0, tiled=True)
        others = [swap_row(parts[hop], hop, n_row) for hop in range(1, n_row)]
        return (grad_cells, *finish([], [parts[0], *others], *adam))

    blocks = [done]
    cuts = [1, 2, len(tables)] if len(steps) > 2 else [1, len(tables)]
    for low, high in zip(cuts, cuts[1:]):
        last = high == len(tables)
        kinds = [jnp.bfloat16 if at < len(steps) else jnp.float32 for at in range(low, high)]
        done, carried = more_blocks(tables[low:high], kinds, block, last, n_row, x_slab, shared, carried)
        blocks += done
    parts = carried

    came = {}
    for (way, _), own in zip(steps, blocks):
        if way in came:
            own = plus(own, came[way]).astype(jnp.bfloat16)
        came[way] = lax.ppermute(own, "gene", list(enumerate(around(n_gene, way))))
    others = [swap_row(parts[hop], hop, n_row) for hop in range(1, n_row)]
    *adam_out, grad_cells = finish([blocks[-1], *came.values()], [parts[0], *others], *adam)
    return (grad_cells, *adam_out)


def solution(mesh):
    in_specs = (
        P(("grp", "row"), "gene"),
        P(("grp", "row"), None),
        P(("grp", "row")),
        P(("grp", "gene")),
        P(("grp", "gene", "row"), None),
        P(("grp", "gene", "row"), None),
        P(("grp", "gene", "row"), None),
    )
    out_specs = (
        P(("grp", "row", "gene"), None),
        P(("grp", "gene", "row"), None),
        P(("grp", "gene", "row"), None),
        P(("grp", "gene", "row"), None),
    )
    return jax.shard_map(local, mesh=mesh, in_specs=in_specs, out_specs=out_specs, check_vma=False)
```

time: 39.5 us -> 28.5 us (0.72)
  waiting for transfers between devices: 18.7 us -> 4.28 us
  Pallas kernels: 7.66 us -> 11.3 us
  other arithmetic: 2.47 us -> 0.95 us
  starting transfers between devices: 9.78 us -> 11 us
    all_to_all x1 -> x0, waiting for transfers between devices: 14.6 us -> none  [local(): got = lax.all_to_all(rows, 'gene', split_axis=0, concat_axis=0)]
    ppermute x0 -> x3, starting transfers between devices: none -> 6.19 us  [local(): came[way] = lax.ppermute(own, 'gene', list(enumerate(around(n_gene, way))))]
    all_to_all x1 -> x0, starting transfers between devices: 4.87 us -> none  [local(): got = lax.all_to_all(rows, 'gene', split_axis=0, concat_axis=0)]
    pallas_call x2 -> x6, Pallas kernels: 7.66 us -> 11.3 us  [the longest x2 7.44 us: more_blocks(): pl.pallas_call(functools.partial(more_kernel, tables, block, last, n_row)...]
    add x1 -> x0, other arithmetic: 0.84 us -> none  [local(): grad_cells = grad_cells + got[place].astype(jnp.float32)]
    sub x1 -> x0, other arithmetic: 0.74 us -> none  [local(): gene_factor - learn_rate * first_hat / (jnp.sqrt(second_hat) + adam_eps)]
  transfers between devices with their start and end apart: 7 -> 9, of which waited for: 4 -> 4; matrix products, arithmetic and copies ran while one was open for 2% -> 0% of each run, Pallas kernels for 6% -> 34%
where the time goes in v17:
time: 28.5 us; the launch traced here: 28.3 us
  Pallas kernels  11.3 us (40%)
  starting transfers between devices  11 us (39%)
  waiting for transfers between devices  4.28 us (15%)
  other arithmetic  0.95 us (3%)
  between operations  0.74 us (3%)
    pallas_call x2, Pallas kernels, more_blocks(): pl.pallas_call(functools.partial(more_kernel, tables, block, last, n_row)...  7.44 us
    ppermute x3, starting transfers between devices, local(): came[way] = lax.ppermute(own, 'gene', list(enumerate(around(n_gene, way))))  6.19 us
    ppermute x6, starting transfers between devices, swap_row(): lax.ppermute(value, 'row', [(me, partner(me, hop, size)) for me in range(...  4.84 us
    ppermute x6, waiting for transfers between devices, swap_row(): lax.ppermute(value, 'row', [(me, partner(me, hop, size)) for me in range(...  4.28 us
    pallas_call x1, Pallas kernels, prepare(): pl.pallas_call(functools.partial(prepare_kernel, scale_k, table, block),...  1.42 us
    pallas_call x1, Pallas kernels, finish(): pl.pallas_call(functools.partial(finish_kernel, len(ends), len(parts)), o...  0.9 us
    convert_element_type x1, other arithmetic, local(): factor_bf = gene_factor.astype(jnp.bfloat16)  0.9 us
    pallas_call x1, Pallas kernels, first_block(): pl.pallas_call(functools.partial(rest_kernel, parts, n_row), out_shape=(j...  0.85 us
  transfers between devices with their start and end apart: 9, of which 4 were waited for; matrix products, arithmetic and copies ran while one was open for 0% of the time, Pallas kernels for 34%

profile of v17, /device:TPU:0, one launch (start us, length us, event | category | flops | bytes accessed | tf_op | source)
XLA Modules:
  0.0 28.3 jit_solution(16136468841853913250)
XLA Ops:
  0.6 0.9 %convert_element_type.12.own.refs_0_ = bf16[160,128]{1,0:T(8,128)(2,1)S(1)} convert(f32[160,128]{1,0:T(8,128)} %refs_7_.1) | non-fusion elementwise | flops 20480 | bytes 122880 | tf_op jit(solution)/shard_map/convert_element_type | solution.py:437
  1.5 2.9 %collective-permute-start.1 = (bf16[160,128]{1,0:T(8,128)(2,1)S(1)}, bf16[160,128]{1,0:T(8,128)(2,1)S(1)}, u32[]{:S(2)}, u32[]{:S(2)}) collective-permute-start(bf16[160,128]{1,0:T(8,128)(2,1)S(1)} %convert_element_type.12.own.refs_0_), channel_id=1, source_target_pairs={{0,2},{1,3},{2,0},{3,1},{4,6},{5,7},{6,4},{7,5},{8,10},{9,11},{10,... | collective-permute-start | bytes 122888 | tf_op jit(solution)/shard_map/ppermute | solution.py:345
  4.5 0.0 collective-permute-start
  4.5 1.4 %prepare.1 = (bf16[768,640]{1,0:T(8,128)(2,1)S(1)}, bf16[768,128]{1,0:T(8,128)(2,1)S(1)}, bf16[128,768]{1,0:T(8,128)(2,1)S(1)}, f32[1,640]{1,0:T(1,128)S(1)}, f3...) custom-call(bf16[3072,640]{1,0:T(8,128)(2,1)} %x_in.5, s32[3072]{0:T(1024)} %index_in.1, ...), custom_call_target="tpu_custom_call" | custom-call | flops 402653184 | bytes 7864320 | tf_op jit(solution)/shard_map/prepare/pallas_call | solution.py:117
  5.9 0.5 %collective-permute-done.1.refs_2_ = bf16[160,128]{1,0:T(8,128)(2,1)S(1)} collective-permute-done((bf16[160,128]{1,0:T(8,128)(2,1)S(1)}, bf16[160,128]{1,0:T(8,128)(2,1)S(1)}, u32[]{:S(2)}, u32[]{:S(2)}) %collective-permute-start.1) | collective-permute-done | bytes 40992 | tf_op jit(solution)/shard_map/ppermute | solution.py:345
  6.4 0.0 collective-permute-start.2
  6.5 0.0 collective-permute-done.other.refs_1_
  6.5 0.6 %early_part.1 = (f32[768,128]{1,0:T(8,128)S(1)}, f32[128,256]{1,0:T(8,128)S(1)}, bf16[128,256]{1,0:T(8,128)(2,1)S(1)}, bf16[256,128]{1,0:T(8,128)(2,1)S(1)}) custom-call(bf16[768,640]{1,0:T(8,128)(2,1)S(1)} %get-tuple-element.36.x_ref, bf16[768,128]{1,0:T(8,128)(2,1)S(1)} %get-tuple-element.37.f_ref, bf16[128,768]{1,0:T(8,128)(2,1)S(1)} %get-tuple-element.38.ft_ref, ...), custom_call_target="tpu_custom_call" | custom-call | flops 301989888 | bytes 786432 | tf_op jit(solution)/shard_map/early_part/pallas_call | solution.py:225
  7.1 0.5 %collective-permute-done.2.refs_3_ = bf16[160,128]{1,0:T(8,128)(2,1)S(1)} collective-permute-done((bf16[160,128]{1,0:T(8,128)(2,1)S(1)}, bf16[160,128]{1,0:T(8,128)(2,1)S(1)}, u32[]{:S(2)}, u32[]{:S(2)}) %collective-permute-start.2) | collective-permute-done | bytes 40992 | tf_op jit(solution)/shard_map/ppermute | solution.py:345
  7.7 0.9 %rest_part.1 = (bf16[768,128]{1,0:T(8,128)(2,1)S(1)}, f32[128,640]{1,0:T(8,128)S(1)}, bf16[128,640]{1,0:T(8,128)(2,1)S(1)}, bf16[640,128]{1,0:T(8,128)(2,1)S(1)}) custom-call(bf16[768,640]{1,0:T(8,128)(2,1)S(1)} %get-tuple-element.36.x_ref, bf16[768,128]{1,0:T(8,128)(2,1)S(1)} %get-tuple-element.37.f_ref, bf16[128,768]{1,0:T(8,128)(2,1)S(1)} %get-tuple-element.38.ft_ref, ...), custom_call_target="tpu_custom_call" | custom-call | flops 452984832 | bytes 1179648 | tf_op jit(solution)/shard_map/rest_part/pallas_call | solution.py:240
  8.5 3.2 %collective-permute-start.3 = (bf16[768,128]{1,0:T(8,128)(2,1)S(1)}, bf16[768,128]{1,0:T(8,128)(2,1)S(1)}, u32[]{:S(2)}, u32[]{:S(2)}) collective-permute-start(bf16[768,128]{1,0:T(8,128)(2,1)S(1)} %get-tuple-element.50), channel_id=1, source_target_pairs={{0,8},{4,0},{8,12},{12,4},{1,9},{5,1},{9,13},{13,5},{2,10},{6,2},{... | collective-permute-start | bytes 589832 | tf_op jit(solution)/shard_map/ppermute | solution.py:469
  11.7 3.0 %more_blocks.2 = (bf16[768,128]{1,0:T(8,128)(2,1)S(1)}, f32[128,640]{1,0:T(8,128)S(1)}) custom-call(bf16[3072,640]{1,0:T(8,128)(2,1)} %x_in.5, s32[1,3072]{1,0:T(1,128)S(1)} %get-tuple-element.32.index_ref, bf16[128,512]{1,0:T(8,128)(2,1)S(1)} %get-tuple-element.33.cells_ref, f32[1,640]{1,0:T(1,128)S(1)} %get-tuple-element.34.bend_ref, ...), custom_call_target="tpu_custom_call" | custom-call | flops 754974720 | bytes 1966080 | tf_op jit(solution)/shard_map/more_blocks/pallas_call | solution.py:330
  14.7 0.0 copy-start
  14.7 0.0 copy-start.1
  14.7 0.0 copy-start.2
  14.7 0.1 collective-permute-start.5
  14.8 4.4 %more_blocks.3 = (bf16[768,128]{1,0:T(8,128)(2,1)S(1)}, f32[768,128]{1,0:T(8,128)S(1)}, f32[160,128]{1,0:T(8,128)S(1)}, bf16[160,128]{1,0:T(8,128)(2,1)S(1)}, bf...) custom-call(bf16[3072,640]{1,0:T(8,128)(2,1)} %x_in.5, s32[1,3072]{1,0:T(1,128)S(1)} %get-tuple-element.32.index_ref, ...), custom_call_target="tpu_custom_call" | custom-call | flops 1509949440 | bytes 3932160 | tf_op jit(solution)/shard_map/more_blocks/pallas_call | solution.py:330
  19.3 0.1 add_convert_fusion
  19.3 3.0 %collective-permute-start.4 = (bf16[768,128]{1,0:T(8,128)(2,1)S(1)}, bf16[768,128]{1,0:T(8,128)(2,1)S(1)}, u32[]{:S(2)}, u32[]{:S(2)}) collective-permute-start(bf16[768,128]{1,0:T(8,128)(2,1)S(1)} %add_convert_fusion), channel_id=1, source_target_pairs={{0,8},{4,0},{8,12},{12,4},{1,9},{5,1},{9,13},{13,5},{2,10},{6,2},{... | collective-permute-start | bytes 589832 | tf_op jit(solution)/shard_map/ppermute | solution.py:469
  22.3 1.5 %collective-permute-start.7 = (bf16[160,128]{1,0:T(8,128)(2,1)S(1)}, bf16[160,128]{1,0:T(8,128)(2,1)S(1)}, u32[]{:S(2)}, u32[]{:S(2)}) collective-permute-start(bf16[160,128]{1,0:T(8,128)(2,1)S(1)} %get-tuple-element.54), channel_id=1, source_target_pairs={{0,2},{1,3},{2,0},{3,1},{4,6},{5,7},{6,4},{7,5},{8,10},{9,11},{10,... | collective-permute-start | bytes 122888 | tf_op jit(solution)/shard_map/ppermute | solution.py:345
  23.8 0.4 %collective-permute-start.8 = (bf16[160,128]{1,0:T(8,128)(2,1)S(1)}, bf16[160,128]{1,0:T(8,128)(2,1)S(1)}, u32[]{:S(2)}, u32[]{:S(2)}) collective-permute-start(bf16[160,128]{1,0:T(8,128)(2,1)S(1)} %get-tuple-element.55), channel_id=1, source_target_pairs={{0,3},{1,2},{2,1},{3,0},{4,7},{5,6},{6,5},{7,4},{8,11},{9,10},{10,... | collective-permute-start | bytes 122888 | tf_op jit(solution)/shard_map/ppermute | solution.py:345
  24.2 2.1 %collective-permute-done.7.refs_5_ = bf16[160,128]{1,0:T(8,128)(2,1)S(1)} collective-permute-done((bf16[160,128]{1,0:T(8,128)(2,1)S(1)}, bf16[160,128]{1,0:T(8,128)(2,1)S(1)}, u32[]{:S(2)}, u32[]{:S(2)}) %collective-permute-start.7) | collective-permute-done | bytes 40992 | tf_op jit(solution)/shard_map/ppermute | solution.py:345
  26.3 1.0 %collective-permute-done.8.refs_6_ = bf16[160,128]{1,0:T(8,128)(2,1)S(1)} collective-permute-done((bf16[160,128]{1,0:T(8,128)(2,1)S(1)}, bf16[160,128]{1,0:T(8,128)(2,1)S(1)}, u32[]{:S(2)}, u32[]{:S(2)}) %collective-permute-start.8) | collective-permute-done | bytes 40992 | tf_op jit(solution)/shard_map/ppermute | solution.py:345
  27.4 0.9 %finish.1 = (f32[160,128]{1,0:T(8,128)}, f32[160,128]{1,0:T(8,128)}, f32[160,128]{1,0:T(8,128)}, f32[768,128]{1,0:T(8,128)}) custom-call(f32[768,128]{1,0:T(8,128)S(1)} %get-tuple-element.48.refs_0_, bf16[768,128]{1,0:T(8,128)(2,1)S(1)} %collective-permute-done.4.refs_1_, bf16[768,128]{1,0:T(8,128)(2,1)S(1)} %collective-permute-done.5.refs_2_, ...), custom_call_target="tpu_custom_call" | custom-call | flops 409600 | bytes 1753088 | tf_op jit(solution)/shard_map/finish/pallas_call | solution.py:419
  (8 shorter events, 0.0 us)
Async XLA Ops:
  1.5 4.9 %collective-permute-start.1 = (bf16[160,128]{1,0:T(8,128)(2,1)S(1)}, bf16[160,128]{1,0:T(8,128)(2,1)S(1)}, u32[]{:S(2)}, u32[]{:S(2)}) collective-permute-start(bf16[160,128]{1,0:T(8,128)(2,1)S(1)} %convert_element_type.12.own.refs_0_), channel_id=1, source_target_pairs={{0,2},{1,3},{2,0},{3,1},{4,6},{5,7},{6,4},{7,5},{8,10},{9,11},{10,... | collective-permute-start | bytes 122888 | tf_op jit(solution)/shard_map/ppermute | solution.py:345
  4.5 2.0 %collective-permute-start = (bf16[160,128]{1,0:T(8,128)(2,1)S(1)}, bf16[160,128]{1,0:T(8,128)(2,1)S(1)}, u32[]{:S(2)}, u32[]{:S(2)}) collective-permute-start(bf16[160,128]{1,0:T(8,128)(2,1)S(1)} %convert_element_type.12.own.refs_0_), channel_id=1, source_target_pairs={{0,1},{1,0},{2,3},{3,2},{4,5},{5,4},{6,7},{7,6},{8,9},{9,8},{10,11... | collective-permute-start | bytes 122888 | tf_op jit(solution)/shard_map/ppermute | solution.py:345
  6.4 1.2 %collective-permute-start.2 = (bf16[160,128]{1,0:T(8,128)(2,1)S(1)}, bf16[160,128]{1,0:T(8,128)(2,1)S(1)}, u32[]{:S(2)}, u32[]{:S(2)}) collective-permute-start(bf16[160,128]{1,0:T(8,128)(2,1)S(1)} %collective-permute-done.1.refs_2_), channel_id=1, source_target_pairs={{0,1},{1,0},{2,3},{3,2},{4,5},{5,4},{6,7},{7,6},{8,9},{9,8},{10,11... | collective-permute-start | bytes 122888 | tf_op jit(solution)/shard_map/ppermute | solution.py:345
  8.5 10.7 %collective-permute-start.3 = (bf16[768,128]{1,0:T(8,128)(2,1)S(1)}, bf16[768,128]{1,0:T(8,128)(2,1)S(1)}, u32[]{:S(2)}, u32[]{:S(2)}) collective-permute-start(bf16[768,128]{1,0:T(8,128)(2,1)S(1)} %get-tuple-element.50), channel_id=1, source_target_pairs={{0,8},{4,0},{8,12},{12,4},{1,9},{5,1},{9,13},{13,5},{2,10},{6,2},{... | collective-permute-start | bytes 589832 | tf_op jit(solution)/shard_map/ppermute | solution.py:469
  14.7 12.6 %copy-start = (f32[160,128]{1,0:T(8,128)S(1)}, f32[160,128]{1,0:T(8,128)}, u32[]{:S(2)}) copy-start(f32[160,128]{1,0:T(8,128)} %refs_7_.1) | copy-start | bytes 245764
  14.7 12.6 %copy-start.1 = (f32[160,128]{1,0:T(8,128)S(1)}, f32[160,128]{1,0:T(8,128)}, u32[]{:S(2)}) copy-start(f32[160,128]{1,0:T(8,128)} %refs_8_.1) | copy-start | bytes 245764
  14.7 12.6 %copy-start.2 = (f32[160,128]{1,0:T(8,128)S(1)}, f32[160,128]{1,0:T(8,128)}, u32[]{:S(2)}) copy-start(f32[160,128]{1,0:T(8,128)} %refs_9_.1) | copy-start | bytes 245764
  14.7 12.6 %collective-permute-start.5 = (bf16[768,128]{1,0:T(8,128)(2,1)S(1)}, bf16[768,128]{1,0:T(8,128)(2,1)S(1)}, u32[]{:S(2)}, u32[]{:S(2)}) collective-permute-start(bf16[768,128]{1,0:T(8,128)(2,1)S(1)} %get-tuple-element.51), channel_id=1, source_target_pairs={{0,4},{4,12},{8,0},{12,8},{1,5},{5,13},{9,1},{13,9},{2,6},{6,14},{... | collective-permute-start | bytes 589832 | tf_op jit(solution)/shard_map/ppermute | solution.py:469
  19.3 8.0 %collective-permute-start.4 = (bf16[768,128]{1,0:T(8,128)(2,1)S(1)}, bf16[768,128]{1,0:T(8,128)(2,1)S(1)}, u32[]{:S(2)}, u32[]{:S(2)}) collective-permute-start(bf16[768,128]{1,0:T(8,128)(2,1)S(1)} %add_convert_fusion), channel_id=1, source_target_pairs={{0,8},{4,0},{8,12},{12,4},{1,9},{5,1},{9,13},{13,5},{2,10},{6,2},{... | collective-permute-start | bytes 589832 | tf_op jit(solution)/shard_map/ppermute | solution.py:469
  22.3 1.9 %collective-permute-start.6 = (bf16[160,128]{1,0:T(8,128)(2,1)S(1)}, bf16[160,128]{1,0:T(8,128)(2,1)S(1)}, u32[]{:S(2)}, u32[]{:S(2)}) collective-permute-start(bf16[160,128]{1,0:T(8,128)(2,1)S(1)} %get-tuple-element.53), channel_id=1, source_target_pairs={{0,1},{1,0},{2,3},{3,2},{4,5},{5,4},{6,7},{7,6},{8,9},{9,8},{10,11... | collective-permute-start | bytes 122888 | tf_op jit(solution)/shard_map/ppermute | solution.py:345
  22.3 4.0 %collective-permute-start.7 = (bf16[160,128]{1,0:T(8,128)(2,1)S(1)}, bf16[160,128]{1,0:T(8,128)(2,1)S(1)}, u32[]{:S(2)}, u32[]{:S(2)}) collective-permute-start(bf16[160,128]{1,0:T(8,128)(2,1)S(1)} %get-tuple-element.54), channel_id=1, source_target_pairs={{0,2},{1,3},{2,0},{3,1},{4,6},{5,7},{6,4},{7,5},{8,10},{9,11},{10,... | collective-permute-start | bytes 122888 | tf_op jit(solution)/shard_map/ppermute | solution.py:345
  23.8 3.5 %collective-permute-start.8 = (bf16[160,128]{1,0:T(8,128)(2,1)S(1)}, bf16[160,128]{1,0:T(8,128)(2,1)S(1)}, u32[]{:S(2)}, u32[]{:S(2)}) collective-permute-start(bf16[160,128]{1,0:T(8,128)(2,1)S(1)} %get-tuple-element.55), channel_id=1, source_target_pairs={{0,3},{1,2},{2,1},{3,0},{4,7},{5,6},{6,5},{7,4},{8,11},{9,10},{10,... | collective-permute-start | bytes 122888 | tf_op jit(solution)/shard_map/ppermute | solution.py:345

commit v18 on v14

--- a/solution.py
+++ b/solution.py
@@ -135,7 +135,7 @@
         total, wide, scaled = (ref[...] for ref in carried_in)
 
     bend = bend_ref[...]
-    step = tile_of(block, 256)
+    step = tile_of(block, 512)
     tiles = []
     for table, out in zip(tables, rows_out):
         origin = pick("gene", table) * block if len(table) > 1 else 0
@@ -228,7 +228,7 @@
 
 
 def part_of_block(table, block, here, x_ref, f_ref, ft_ref, bend_ref, wide, scaled):
-    step = tile_of(block, 256)
+    step = tile_of(block, 1024)
     origin = pick("gene", table) * block
     tiles = [pl.ds(pl.multiple_of(origin + at, math.gcd(block, step)), step) for at in range(0, block, step)]
     bend = bend_ref[:, here]

time: 27 us -> 27.3 us (1.011)
  no operation moved by 1% of the time
where the time goes in v18:
time: 27.3 us; the launch traced here: 27.1 us
  starting transfers between devices  11.1 us (41%)
  Pallas kernels  8.02 us (29%)
  waiting for transfers between devices  6.34 us (23%)
  other arithmetic  0.95 us (3%)
  between operations  0.73 us (3%)
    ppermute x3, starting transfers between devices, local(): came[way] = lax.ppermute(own, 'gene', list(enumerate(around(n_gene, way))))  6.14 us
    ppermute x6, starting transfers between devices, swap_row(): lax.ppermute(value, 'row', [(me, partner(me, hop, size)) for me in range(...  4.92 us
    ppermute x6, waiting for transfers between devices, swap_row(): lax.ppermute(value, 'row', [(me, partner(me, hop, size)) for me in range(...  3.44 us
    pallas_call x2, Pallas kernels, block_rows(): pl.pallas_call(functools.partial(rows_kernel, tables, block, first, last,...  3.16 us
    ppermute x3, waiting for transfers between devices, local(): came[way] = lax.ppermute(own, 'gene', list(enumerate(around(n_gene, way))))  2.9 us
    pallas_call x1, Pallas kernels, prepare(): pl.pallas_call(functools.partial(prepare_kernel, scale_k), out_shape=(VME...  2.26 us
    pallas_call x1, Pallas kernels, first_block(): pl.pallas_call(functools.partial(rest_kernel, table, block, parts, n_row)...  0.94 us
    pallas_call x1, Pallas kernels, finish(): pl.pallas_call(functools.partial(finish_kernel, len(ends), len(parts)), o...  0.9 us
  transfers between devices with their start and end apart: 9, of which 5 were waited for; matrix products, arithmetic and copies ran while one was open for 0% of the time, Pallas kernels for 23%

profile of v18, /device:TPU:0, one launch (start us, length us, event | category | flops | bytes accessed | tf_op | source)
XLA Modules:
  0.0 27.1 jit_solution(6820801746658350819)
XLA Ops:
  0.6 0.9 %convert_element_type.12.own.refs_0_ = bf16[160,128]{1,0:T(8,128)(2,1)S(1)} convert(f32[160,128]{1,0:T(8,128)} %refs_7_.1) | non-fusion elementwise | flops 20480 | bytes 122880 | tf_op jit(solution)/shard_map/convert_element_type | solution.py:410
  1.5 2.4 %collective-permute-start.2 = (bf16[160,128]{1,0:T(8,128)(2,1)S(1)}, bf16[160,128]{1,0:T(8,128)(2,1)S(1)}, u32[]{:S(2)}, u32[]{:S(2)}) collective-permute-start(bf16[160,128]{1,0:T(8,128)(2,1)S(1)} %convert_element_type.12.own.refs_0_), channel_id=1, source_target_pairs={{0,3},{1,2},{2,1},{3,0},{4,7},{5,6},{6,5},{7,4},{8,11},{9,10},{10,... | collective-permute-start | bytes 122888 | tf_op jit(solution)/shard_map/ppermute | solution.py:330
  3.9 0.6 %collective-permute-start.1 = (bf16[160,128]{1,0:T(8,128)(2,1)S(1)}, bf16[160,128]{1,0:T(8,128)(2,1)S(1)}, u32[]{:S(2)}, u32[]{:S(2)}) collective-permute-start(bf16[160,128]{1,0:T(8,128)(2,1)S(1)} %convert_element_type.12.own.refs_0_), channel_id=1, source_target_pairs={{0,2},{1,3},{2,0},{3,1},{4,6},{5,7},{6,4},{7,5},{8,10},{9,11},{10,... | collective-permute-start | bytes 122888 | tf_op jit(solution)/shard_map/ppermute | solution.py:330
  4.5 0.0 collective-permute-start
  4.6 2.3 %prepare.1 = (bf16[3072,640]{1,0:T(8,128)(2,1)S(1)}, bf16[3072,128]{1,0:T(8,128)(2,1)S(1)}, bf16[128,3072]{1,0:T(8,128)(2,1)S(1)}, f32[1,640]{1,0:T(1,128)S(1)}, f32[640,128]{1,0:T(8,128)S(1)}) custom-call(bf16[3072,640]{1,0:T(8,128)(2,1)} %x_in.1, s32[3072]{0:T(1024)} %index_in.1, bf16[512,128]{1,0:T(8,128)(2,1)} %cell_in.1, f32[640]{0:T(1024)} %scale_in.1), custom_call_target="tpu_custom_call" | custom-call | flops 1610612736 | bytes 31457280 | tf_op jit(solution)/shard_map/prepare/pallas_call | solution.py:74
  6.9 0.8 %early_part.1 = (f32[768,128]{1,0:T(8,128)S(1)}, f32[128,256]{1,0:T(8,128)S(1)}, bf16[128,256]{1,0:T(8,128)(2,1)S(1)}, bf16[256,128]{1,0:T(8,128)(2,1)S(1)}) custom-call(bf16[3072,640]{1,0:T(8,128)(2,1)S(1)} %get-tuple-element.29.x_ref.refs_0_, bf16[3072,128]{1,0:T(8,128)(2,1)S(1)} %get-tuple-element.30.f_ref.refs_1_, ...), custom_call_target="tpu_custom_call" | custom-call | flops 301989888 | bytes 786432 | tf_op jit(solution)/shard_map/early_part/pallas_call | solution.py:296
  7.6 0.4 %collective-permute-done.1.refs_2_ = bf16[160,128]{1,0:T(8,128)(2,1)S(1)} collective-permute-done((bf16[160,128]{1,0:T(8,128)(2,1)S(1)}, bf16[160,128]{1,0:T(8,128)(2,1)S(1)}, u32[]{:S(2)}, u32[]{:S(2)}) %collective-permute-start.1) | collective-permute-done | bytes 40992 | tf_op jit(solution)/shard_map/ppermute | solution.py:330
  8.1 0.9 %rest_part.1 = (bf16[768,128]{1,0:T(8,128)(2,1)S(1)}, f32[128,640]{1,0:T(8,128)S(1)}, bf16[128,640]{1,0:T(8,128)(2,1)S(1)}, bf16[640,128]{1,0:T(8,128)(2,1)S(1)}) custom-call(bf16[3072,640]{1,0:T(8,128)(2,1)S(1)} %get-tuple-element.29.x_ref.refs_0_, bf16[3072,128]{1,0:T(8,128)(2,1)S(1)} %get-tuple-element.30.f_ref.refs_1_, ...), custom_call_target="tpu_custom_call" | custom-call | flops 452984832 | bytes 1179648 | tf_op jit(solution)/shard_map/rest_part/pallas_call | solution.py:311
  9.0 2.6 %collective-permute-start.3 = (bf16[768,128]{1,0:T(8,128)(2,1)S(1)}, bf16[768,128]{1,0:T(8,128)(2,1)S(1)}, u32[]{:S(2)}, u32[]{:S(2)}) collective-permute-start(bf16[768,128]{1,0:T(8,128)(2,1)S(1)} %get-tuple-element.44), channel_id=1, source_target_pairs={{0,8},{4,0},{8,12},{12,4},{1,9},{5,1},{9,13},{13,5},{2,10},{6,2},{... | collective-permute-start | bytes 589832 | tf_op jit(solution)/shard_map/ppermute | solution.py:441
  11.6 1.1 %block_rows.2 = (bf16[768,128]{1,0:T(8,128)(2,1)S(1)}, f32[128,640]{1,0:T(8,128)S(1)}) custom-call(bf16[3072,640]{1,0:T(8,128)(2,1)S(1)} %get-tuple-element.29.x_ref.refs_0_, bf16[3072,128]{1,0:T(8,128)(2,1)S(1)} %get-tuple-element.30.f_ref.refs_1_, bf16[128,3072]{1,0:T(8,128)(2,1)S(1)} %get-tuple-element.31.ft_ref.refs_2_, ...), custom_call_target="tpu_custom_call" | custom-call | flops 377487360 | bytes 983040 | tf_op jit(solution)/shard_map/block_rows/pallas_call | solution.py:195
  12.8 0.0 copy-start
  12.8 0.0 copy-start.1
  12.8 0.0 copy-start.2
  12.8 0.1 collective-permute-start.5
  12.9 2.0 %block_rows.3 = (bf16[768,128]{1,0:T(8,128)(2,1)S(1)}, f32[768,128]{1,0:T(8,128)S(1)}, f32[160,128]{1,0:T(8,128)S(1)}, bf16[160,128]{1,0:T(8,128)(2,1)S(1)}, bf1...) custom-call(bf16[3072,640]{1,0:T(8,128)(2,1)S(1)} %get-tuple-element.29.x_ref.refs_0_, ...), custom_call_target="tpu_custom_call" | custom-call | flops 754974720 | bytes 1966080 | tf_op jit(solution)/shard_map/block_rows/pallas_call | solution.py:195
  14.9 2.0 %collective-permute-done.3 = bf16[768,128]{1,0:T(8,128)(2,1)S(1)} collective-permute-done((bf16[768,128]{1,0:T(8,128)(2,1)S(1)}, bf16[768,128]{1,0:T(8,128)(2,1)S(1)}, u32[]{:S(2)}, u32[]{:S(2)}) %collective-permute-start.3) | collective-permute-done | bytes 196640 | tf_op jit(solution)/shard_map/ppermute | solution.py:441
  17.0 0.1 add_convert_fusion
  17.0 3.4 %collective-permute-start.4 = (bf16[768,128]{1,0:T(8,128)(2,1)S(1)}, bf16[768,128]{1,0:T(8,128)(2,1)S(1)}, u32[]{:S(2)}, u32[]{:S(2)}) collective-permute-start(bf16[768,128]{1,0:T(8,128)(2,1)S(1)} %add_convert_fusion), channel_id=1, source_target_pairs={{0,8},{4,0},{8,12},{12,4},{1,9},{5,1},{9,13},{13,5},{2,10},{6,2},{... | collective-permute-start | bytes 589832 | tf_op jit(solution)/shard_map/ppermute | solution.py:441
  20.5 1.3 %collective-permute-start.7 = (bf16[160,128]{1,0:T(8,128)(2,1)S(1)}, bf16[160,128]{1,0:T(8,128)(2,1)S(1)}, u32[]{:S(2)}, u32[]{:S(2)}) collective-permute-start(bf16[160,128]{1,0:T(8,128)(2,1)S(1)} %get-tuple-element.48), channel_id=1, source_target_pairs={{0,2},{1,3},{2,0},{3,1},{4,6},{5,7},{6,4},{7,5},{8,10},{9,11},{10,... | collective-permute-start | bytes 122888 | tf_op jit(solution)/shard_map/ppermute | solution.py:330
  21.8 0.5 %collective-permute-start.8 = (bf16[160,128]{1,0:T(8,128)(2,1)S(1)}, bf16[160,128]{1,0:T(8,128)(2,1)S(1)}, u32[]{:S(2)}, u32[]{:S(2)}) collective-permute-start(bf16[160,128]{1,0:T(8,128)(2,1)S(1)} %get-tuple-element.49), channel_id=1, source_target_pairs={{0,3},{1,2},{2,1},{3,0},{4,7},{5,6},{6,5},{7,4},{8,11},{9,10},{10,... | collective-permute-start | bytes 122888 | tf_op jit(solution)/shard_map/ppermute | solution.py:330
  22.3 2.1 %collective-permute-done.7.refs_5_ = bf16[160,128]{1,0:T(8,128)(2,1)S(1)} collective-permute-done((bf16[160,128]{1,0:T(8,128)(2,1)S(1)}, bf16[160,128]{1,0:T(8,128)(2,1)S(1)}, u32[]{:S(2)}, u32[]{:S(2)}) %collective-permute-start.7) | collective-permute-done | bytes 40992 | tf_op jit(solution)/shard_map/ppermute | solution.py:330
  24.5 0.9 %collective-permute-done.8.refs_6_ = bf16[160,128]{1,0:T(8,128)(2,1)S(1)} collective-permute-done((bf16[160,128]{1,0:T(8,128)(2,1)S(1)}, bf16[160,128]{1,0:T(8,128)(2,1)S(1)}, u32[]{:S(2)}, u32[]{:S(2)}) %collective-permute-start.8) | collective-permute-done | bytes 40992 | tf_op jit(solution)/shard_map/ppermute | solution.py:330
  25.3 0.8 %collective-permute-done.4.refs_1_ = bf16[768,128]{1,0:T(8,128)(2,1)S(1)} collective-permute-done((bf16[768,128]{1,0:T(8,128)(2,1)S(1)}, bf16[768,128]{1,0:T(8,128)(2,1)S(1)}, u32[]{:S(2)}, u32[]{:S(2)}) %collective-permute-start.4) | collective-permute-done | bytes 196640 | tf_op jit(solution)/shard_map/ppermute | solution.py:441
  26.2 0.9 %finish.1 = (f32[160,128]{1,0:T(8,128)}, f32[160,128]{1,0:T(8,128)}, f32[160,128]{1,0:T(8,128)}, f32[768,128]{1,0:T(8,128)}) custom-call(f32[768,128]{1,0:T(8,128)S(1)} %get-tuple-element.42.refs_0_, bf16[768,128]{1,0:T(8,128)(2,1)S(1)} %collective-permute-done.4.refs_1_, bf16[768,128]{1,0:T(8,128)(2,1)S(1)} %collective-permute-done.5.refs_2_, ...), custom_call_target="tpu_custom_call" | custom-call | flops 409600 | bytes 1753088 | tf_op jit(solution)/shard_map/finish/pallas_call | solution.py:392
  (8 shorter events, 0.0 us)
Async XLA Ops:
  1.5 6.1 %collective-permute-start.2 = (bf16[160,128]{1,0:T(8,128)(2,1)S(1)}, bf16[160,128]{1,0:T(8,128)(2,1)S(1)}, u32[]{:S(2)}, u32[]{:S(2)}) collective-permute-start(bf16[160,128]{1,0:T(8,128)(2,1)S(1)} %convert_element_type.12.own.refs_0_), channel_id=1, source_target_pairs={{0,3},{1,2},{2,1},{3,0},{4,7},{5,6},{6,5},{7,4},{8,11},{9,10},{10,... | collective-permute-start | bytes 122888 | tf_op jit(solution)/shard_map/ppermute | solution.py:330
  3.9 4.1 %collective-permute-start.1 = (bf16[160,128]{1,0:T(8,128)(2,1)S(1)}, bf16[160,128]{1,0:T(8,128)(2,1)S(1)}, u32[]{:S(2)}, u32[]{:S(2)}) collective-permute-start(bf16[160,128]{1,0:T(8,128)(2,1)S(1)} %convert_element_type.12.own.refs_0_), channel_id=1, source_target_pairs={{0,2},{1,3},{2,0},{3,1},{4,6},{5,7},{6,4},{7,5},{8,10},{9,11},{10,... | collective-permute-start | bytes 122888 | tf_op jit(solution)/shard_map/ppermute | solution.py:330
  4.5 2.3 %collective-permute-start = (bf16[160,128]{1,0:T(8,128)(2,1)S(1)}, bf16[160,128]{1,0:T(8,128)(2,1)S(1)}, u32[]{:S(2)}, u32[]{:S(2)}) collective-permute-start(bf16[160,128]{1,0:T(8,128)(2,1)S(1)} %convert_element_type.12.own.refs_0_), channel_id=1, source_target_pairs={{0,1},{1,0},{2,3},{3,2},{4,5},{5,4},{6,7},{7,6},{8,9},{9,8},{10,11... | collective-permute-start | bytes 122888 | tf_op jit(solution)/shard_map/ppermute | solution.py:330
  9.0 8.0 %collective-permute-start.3 = (bf16[768,128]{1,0:T(8,128)(2,1)S(1)}, bf16[768,128]{1,0:T(8,128)(2,1)S(1)}, u32[]{:S(2)}, u32[]{:S(2)}) collective-permute-start(bf16[768,128]{1,0:T(8,128)(2,1)S(1)} %get-tuple-element.44), channel_id=1, source_target_pairs={{0,8},{4,0},{8,12},{12,4},{1,9},{5,1},{9,13},{13,5},{2,10},{6,2},{... | collective-permute-start | bytes 589832 | tf_op jit(solution)/shard_map/ppermute | solution.py:441
  12.8 13.4 %copy-start = (f32[160,128]{1,0:T(8,128)S(1)}, f32[160,128]{1,0:T(8,128)}, u32[]{:S(2)}) copy-start(f32[160,128]{1,0:T(8,128)} %refs_7_.1) | copy-start | bytes 245764
  12.8 13.4 %copy-start.1 = (f32[160,128]{1,0:T(8,128)S(1)}, f32[160,128]{1,0:T(8,128)}, u32[]{:S(2)}) copy-start(f32[160,128]{1,0:T(8,128)} %refs_8_.1) | copy-start | bytes 245764
  12.8 13.4 %copy-start.2 = (f32[160,128]{1,0:T(8,128)S(1)}, f32[160,128]{1,0:T(8,128)}, u32[]{:S(2)}) copy-start(f32[160,128]{1,0:T(8,128)} %refs_9_.1) | copy-start | bytes 245764
  12.8 12.5 %collective-permute-start.5 = (bf16[768,128]{1,0:T(8,128)(2,1)S(1)}, bf16[768,128]{1,0:T(8,128)(2,1)S(1)}, u32[]{:S(2)}, u32[]{:S(2)}) collective-permute-start(bf16[768,128]{1,0:T(8,128)(2,1)S(1)} %get-tuple-element.45), channel_id=1, source_target_pairs={{0,4},{4,12},{8,0},{12,8},{1,5},{5,13},{9,1},{13,9},{2,6},{6,14},{... | collective-permute-start | bytes 589832 | tf_op jit(solution)/shard_map/ppermute | solution.py:441
  17.0 9.2 %collective-permute-start.4 = (bf16[768,128]{1,0:T(8,128)(2,1)S(1)}, bf16[768,128]{1,0:T(8,128)(2,1)S(1)}, u32[]{:S(2)}, u32[]{:S(2)}) collective-permute-start(bf16[768,128]{1,0:T(8,128)(2,1)S(1)} %add_convert_fusion), channel_id=1, source_target_pairs={{0,8},{4,0},{8,12},{12,4},{1,9},{5,1},{9,13},{13,5},{2,10},{6,2},{... | collective-permute-start | bytes 589832 | tf_op jit(solution)/shard_map/ppermute | solution.py:441
  20.5 1.9 %collective-permute-start.6 = (bf16[160,128]{1,0:T(8,128)(2,1)S(1)}, bf16[160,128]{1,0:T(8,128)(2,1)S(1)}, u32[]{:S(2)}, u32[]{:S(2)}) collective-permute-start(bf16[160,128]{1,0:T(8,128)(2,1)S(1)} %get-tuple-element.47), channel_id=1, source_target_pairs={{0,1},{1,0},{2,3},{3,2},{4,5},{5,4},{6,7},{7,6},{8,9},{9,8},{10,11... | collective-permute-start | bytes 122888 | tf_op jit(solution)/shard_map/ppermute | solution.py:330
  20.5 4.0 %collective-permute-start.7 = (bf16[160,128]{1,0:T(8,128)(2,1)S(1)}, bf16[160,128]{1,0:T(8,128)(2,1)S(1)}, u32[]{:S(2)}, u32[]{:S(2)}) collective-permute-start(bf16[160,128]{1,0:T(8,128)(2,1)S(1)} %get-tuple-element.48), channel_id=1, source_target_pairs={{0,2},{1,3},{2,0},{3,1},{4,6},{5,7},{6,4},{7,5},{8,10},{9,11},{10,... | collective-permute-start | bytes 122888 | tf_op jit(solution)/shard_map/ppermute | solution.py:330
  21.8 3.5 %collective-permute-start.8 = (bf16[160,128]{1,0:T(8,128)(2,1)S(1)}, bf16[160,128]{1,0:T(8,128)(2,1)S(1)}, u32[]{:S(2)}, u32[]{:S(2)}) collective-permute-start(bf16[160,128]{1,0:T(8,128)(2,1)S(1)} %get-tuple-element.49), channel_id=1, source_target_pairs={{0,3},{1,2},{2,1},{3,0},{4,7},{5,6},{6,5},{7,4},{8,11},{9,10},{10,... | collective-permute-start | bytes 122888 | tf_op jit(solution)/shard_map/ppermute | solution.py:330

commit v19 on v14

--- a/solution.py
+++ b/solution.py
@@ -110,13 +110,31 @@
     return me ^ hop if size & (size - 1) == 0 else (me + size - hop) % size
 
 
-def rows_kernel(tables, block, first, last, n_row, *refs):
+class Cut:
+    def __init__(self, refs):
+        self.refs = refs
+        self.dtype = refs[0].dtype
+
+    def store(self, low, value):
+        depth = self.refs[0].shape[0]
+        for at, ref in enumerate(self.refs):
+            begin, end = max(low, at * depth), min(low + value.shape[0], (at + 1) * depth)
+            if begin < end:
+                ref[begin - at * depth : end - at * depth, :] = value[begin - low : end - low, :].astype(ref.dtype)
+
+
+def grouped(refs, counts):
+    refs = list(refs)
+    return [Cut([refs.pop(0) for _ in range(count)]) for count in counts]
+
+
+def rows_kernel(tables, counts, block, first, last, n_row, *refs):
     refs = list(refs)
     take = lambda count: [refs.pop(0) for _ in range(count)]
     x_ref, f_ref, ft_ref, bend_ref, shrink_ref = take(5)
     shares = take(n_row) if first else None
     carried_in = None if first else take(3)
-    rows_out = take(len(tables))
+    rows_out = grouped(take(sum(counts)), counts)
     carried_out = None if last else take(3 if first else 1)
     parts_out = take(n_row) if last else None
     me = lax.axis_index("row")
@@ -151,7 +169,7 @@
     def gradients(tile, infl, total):
         out, at, here = tile
         cols = jnp.dot(ft_ref[:, here], infl, preferred_element_type=jnp.float32)
-        out[at : at + step, :] = jnp.dot(infl, scaled, preferred_element_type=jnp.float32).astype(out.dtype)
+        out.store(at, jnp.dot(infl, scaled, preferred_element_type=jnp.float32))
         return cols if total is None else total + cols
 
     pred = predict(tiles[0][2])
@@ -178,9 +196,10 @@
         parts_out[hop][...] = turned[pl.ds(start, depth), :].astype(parts_out[hop].dtype)
 
 
-def block_rows(tables, kinds, block, first, last, n_row, fixed, carried):
+def block_rows(tables, kinds, counts, block, first, last, n_row, fixed, carried):
     genes, rank = fixed[4].shape
-    out = [jax.ShapeDtypeStruct((block, rank), kind) for kind in kinds]
+    out = [jax.ShapeDtypeStruct((block // count, rank), kind) for kind, count in zip(kinds, counts) for _ in range(count)]
+    n_rows = len(out)
     if last:
         out += [jax.ShapeDtypeStruct((genes // n_row, rank), jnp.bfloat16 if hop else jnp.float32) for hop in range(n_row)]
     else:
@@ -193,7 +212,7 @@
     ins = pinned(*fixed) + (list(carried) if first else pinned(*carried))
     work = len(tables) * block * genes
     out = pl.pallas_call(
-        functools.partial(rows_kernel, tables, block, first, last, n_row),
+        functools.partial(rows_kernel, tables, counts, block, first, last, n_row),
         out_shape=tuple(out),
         in_specs=[IN_VMEM] * len(ins),
         out_specs=(IN_VMEM,) * len(out),
@@ -202,7 +221,7 @@
         cost_estimate=cost(6 * work * rank, work * 2),
         name="block_rows",
     )(*ins)
-    done, rest = list(out[: len(tables)]), list(out[len(tables) :])
+    done, rest = [cut.refs for cut in grouped(out[:n_rows], counts)], list(out[n_rows:])
     return done, rest if first or last else rest + list(carried[1:])
 
 
@@ -262,9 +281,10 @@
     total_out[...] = total
 
 
-def rest_kernel(table, block, parts, n_row, x_ref, f_ref, ft_ref, bend_ref, shrink_ref, *refs):
+def rest_kernel(table, count, block, parts, n_row, x_ref, f_ref, ft_ref, bend_ref, shrink_ref, *refs):
     shares, (rows_in, total_in, wide_in, scaled_in) = refs[:n_row], refs[n_row : n_row + 4]
-    rows_out, total_out, wide_out, scaled_out, piece = refs[n_row + 4 :]
+    *rows_out, total_out, wide_out, scaled_out, piece = refs[n_row + 4 :]
+    rows_out = Cut(rows_out)
     low, width, rest = parts
     me = lax.axis_index("row")
     depth = shares[0].shape[0]
@@ -278,7 +298,7 @@
     rows, total = part_of_block(table, block, here, x_ref, f_ref, ft_ref, bend_ref, wide, scaled)
     for at, value in enumerate(rows):
         span = slice(at * value.shape[0], (at + 1) * value.shape[0])
-        rows_out[span, :] = (rows_in[span, :] + value).astype(rows_out.dtype)
+        rows_out.store(span.start, rows_in[span, :] + value)
     done = lanes(low, width)
     total_out[:, here] = total
     total_out[:, done] = total_in[...]
@@ -288,7 +308,7 @@
     scaled_out[done, :] = scaled_in[...]
 
 
-def first_block(table, block, parts, n_row, fixed, shares):
+def first_block(table, count, block, parts, n_row, fixed, shares):
     genes, rank = fixed[4].shape
     depth = genes // n_row
     width = parts[1]
@@ -308,22 +328,22 @@
         cost_estimate=cost(12 * block * width * rank, block * width * 4),
         name="early_part",
     )(*ins, *shares[:2])
-    done, *carried = pl.pallas_call(
-        functools.partial(rest_kernel, table, block, parts, n_row),
+    out = pl.pallas_call(
+        functools.partial(rest_kernel, table, count, block, parts, n_row),
         out_shape=(
-            jax.ShapeDtypeStruct((block, rank), jnp.bfloat16),
+            *[jax.ShapeDtypeStruct((block // count, rank), jnp.bfloat16)] * count,
             VMEM((rank, genes), jnp.float32),
             VMEM((rank, genes), jnp.bfloat16),
             VMEM((genes, rank), jnp.bfloat16),
         ),
         in_specs=[IN_VMEM] * (9 + n_row),
-        out_specs=(IN_VMEM,) * 4,
+        out_specs=(IN_VMEM,) * (count + 3),
         scratch_shapes=[VMEM((genes, rank), jnp.bfloat16)],
         compiler_params=params(),
         cost_estimate=cost(12 * block * (genes - width) * rank, block * (genes - width) * 4),
         name="rest_part",
     )(*ins, *shares, *pinned(*early))
-    return [done], carried
+    return [list(out[:count])], list(out[count:])
 
 
 def swap_row(value, hop, size):
@@ -349,11 +369,12 @@
     return wide.astype(jnp.float32) + narrow.astype(jnp.float32)
 
 
-def finish_kernel(n_ends, n_parts, *refs):
+def finish_kernel(counts, n_parts, *refs):
+    n_ends = sum(counts)
     n_ins = n_ends + n_parts + 3
     ins, outs = refs[:n_ins], refs[n_ins : n_ins + 3 + bool(n_ends)]
     *held, sems = refs[n_ins + len(outs) :]
-    ends, parts = ins[:n_ends], ins[n_ends : n_ends + n_parts]
+    ends, parts = [cut.refs for cut in grouped(ins[:n_ends], counts)], ins[n_ends : n_ends + n_parts]
     factor, first, second = ins[n_ends + n_parts :]
     copies = []
 
@@ -363,12 +384,14 @@
         copies[-1].start()
 
     if ends:
-        step = tile_of(ends[0].shape[0], 256)
-        for low in range(0, ends[0].shape[0], step):
+        ((own,), *others) = ends
+        step = tile_of(min(end[0].shape[0] for end in ends), 256)
+        for low in range(0, own.shape[0], step):
             span = pl.ds(low, step)
-            rows = ends[0][span, :]
-            for end in ends[1:]:
-                rows = plus(rows, end[span, :])
+            rows = own[span, :]
+            for end in others:
+                at, inner = divmod(low, end[0].shape[0])
+                rows = plus(rows, end[at][pl.ds(inner, step), :])
             send(3, span, rows)
     grad = parts[0][...]
     for part in parts[1:]:
@@ -386,11 +409,11 @@
 
 
 def finish(ends, parts, factor, first, second):
-    ins = [*ends, *parts, factor, first, second]
-    shapes = [factor, factor, factor] + list(ends[:1])
-    n_copies = 3 + (ends[0].shape[0] // tile_of(ends[0].shape[0], 256) if ends else 0)
+    ins = [*itertools.chain(*ends), *parts, factor, first, second]
+    shapes = [factor, factor, factor] + ([ends[0][0]] if ends else [])
+    n_copies = 3 + (ends[0][0].shape[0] // tile_of(min(end[0].shape[0] for end in ends), 256) if ends else 0)
     return pl.pallas_call(
-        functools.partial(finish_kernel, len(ends), len(parts)),
+        functools.partial(finish_kernel, [len(end) for end in ends], len(parts)),
         out_shape=tuple(jax.ShapeDtypeStruct(like.shape, jnp.float32) for like in shapes),
         in_specs=[IN_VMEM] * len(ins),
         out_specs=(IN_ANY,) * len(shapes),
@@ -413,7 +436,7 @@
     adam = (gene_factor, first_moment, second_moment)
 
     if n_gene == 1 or n_gene > RING_MOST or block % 128:
-        (rows,), parts = block_rows([(0,)], [jnp.float32], rows_dev, True, True, n_row, fixed, shares)
+        ((rows,),), parts = block_rows([(0,)], [jnp.float32], [1], rows_dev, True, True, n_row, fixed, shares)
         grad_cells = lax.psum_scatter(rows, "gene", scatter_dimension=0, tiled=True)
         others = [swap_row(parts[hop], hop, n_row) for hop in range(1, n_row)]
         return (grad_cells, *finish([], [parts[0], *others], *adam))
@@ -421,24 +444,26 @@
     steps = steps_of(n_gene)
     tables = [around(n_gene, way * distance) for way, distance in steps] + [tuple(range(n_gene))]
     kinds = [jnp.bfloat16] * len(steps) + [jnp.float32]
+    counts = [2 if way == 1 and n_gene > 2 and block % 256 == 0 else 1 for way, _ in steps] + [1]
     cuts = [0, 1, 2, len(tables)] if len(steps) > 2 else [0, 1, len(tables)]
     parted = lane_parts(genes_dev, genes_dev // n_row, n_row)
     carried, blocks = shares, []
     for low, high in zip(cuts, cuts[1:]):
         last = high == len(tables)
         if low == 0 and parted:
-            done, carried = first_block(tables[0], block, parted, n_row, fixed, shares)
+            done, carried = first_block(tables[0], counts[0], block, parted, n_row, fixed, shares)
             blocks += done
             continue
-        done, carried = block_rows(tables[low:high], kinds[low:high], block, low == 0, last, n_row, fixed, carried)
+        done, carried = block_rows(tables[low:high], kinds[low:high], counts[low:high], block, low == 0, last, n_row, fixed, carried)
         blocks += done
     parts = carried
 
     came = {}
-    for (way, _), own in zip(steps, blocks):
+    for (way, _), halves in zip(steps, blocks):
+        targets = list(enumerate(around(n_gene, way)))
         if way in came:
-            own = plus(own, came[way]).astype(jnp.bfloat16)
-        came[way] = lax.ppermute(own, "gene", list(enumerate(around(n_gene, way))))
+            halves = [plus(own, value).astype(jnp.bfloat16) for own, value in zip(halves, came[way])]
+        came[way] = [lax.ppermute(half, "gene", targets) for half in halves]
     others = [swap_row(parts[hop], hop, n_row) for hop in range(1, n_row)]
     *adam_out, grad_cells = finish([blocks[-1], *came.values()], [parts[0], *others], *adam)
     return (grad_cells, *adam_out)

time: 27 us -> 27.6 us (1.022)
  starting transfers between devices: 11.1 us -> 13.3 us
  waiting for transfers between devices: 6.1 us -> 4.46 us
    ppermute x3 -> x5, starting transfers between devices: 6.14 us -> 7.84 us  [local(): came[way] = [lax.ppermute(half, 'gene', targets) for half in halves]]
    ppermute x3 -> x5, waiting for transfers between devices: 2.67 us -> 1.36 us  [local(): came[way] = [lax.ppermute(half, 'gene', targets) for half in halves]]
    ppermute x6, starting transfers between devices: 4.92 us -> 5.43 us  [swap_row(): lax.ppermute(value, 'row', [(me, partner(me, hop, size)) for me in range(...]
    ppermute x6, waiting for transfers between devices: 3.43 us -> 3.1 us  [swap_row(): lax.ppermute(value, 'row', [(me, partner(me, hop, size)) for me in range(...]
  transfers between devices with their start and end apart: 9 -> 11, of which waited for: 5 -> 5; matrix products, arithmetic and copies ran while one was open for 0% -> 0% of each run, Pallas kernels for 23% -> 22%
where the time goes in v19:
time: 27.6 us; the launch traced here: 27.4 us
  starting transfers between devices  13.3 us (48%)
  Pallas kernels  7.96 us (29%)
  waiting for transfers between devices  4.46 us (16%)
  other arithmetic  0.95 us (3%)
  between operations  0.74 us (3%)
    ppermute x5, starting transfers between devices, local(): came[way] = [lax.ppermute(half, 'gene', targets) for half in halves]  7.84 us
    ppermute x6, starting transfers between devices, swap_row(): lax.ppermute(value, 'row', [(me, partner(me, hop, size)) for me in range(...  5.43 us
    pallas_call x2, Pallas kernels, block_rows(): pl.pallas_call(functools.partial(rows_kernel, tables, counts, block, firs...  3.24 us
    ppermute x6, waiting for transfers between devices, swap_row(): lax.ppermute(value, 'row', [(me, partner(me, hop, size)) for me in range(...  3.1 us
    pallas_call x1, Pallas kernels, prepare(): pl.pallas_call(functools.partial(prepare_kernel, scale_k), out_shape=(VME...  2.26 us
    ppermute x5, waiting for transfers between devices, local(): came[way] = [lax.ppermute(half, 'gene', targets) for half in halves]  1.36 us
    pallas_call x1, Pallas kernels, finish(): pl.pallas_call(functools.partial(finish_kernel, [len(end) for end in ends...  0.92 us
    pallas_call x1, Pallas kernels, first_block(): pl.pallas_call(functools.partial(rest_kernel, table, count, block, parts,...  0.9 us
  transfers between devices with their start and end apart: 11, of which 5 were waited for; matrix products, arithmetic and copies ran while one was open for 0% of the time, Pallas kernels for 22%

profile of v19, /device:TPU:0, one launch (start us, length us, event | category | flops | bytes accessed | tf_op | source)
XLA Modules:
  0.0 27.4 jit_solution(2364592183751404112)
XLA Ops:
  0.6 0.9 %convert_element_type.21.own.refs_0_ = bf16[160,128]{1,0:T(8,128)(2,1)S(1)} convert(f32[160,128]{1,0:T(8,128)} %refs_8_.1) | non-fusion elementwise | flops 20480 | bytes 122880 | tf_op jit(solution)/shard_map/convert_element_type | solution.py:433
  1.5 2.4 %collective-permute-start.2 = (bf16[160,128]{1,0:T(8,128)(2,1)S(1)}, bf16[160,128]{1,0:T(8,128)(2,1)S(1)}, u32[]{:S(2)}, u32[]{:S(2)}) collective-permute-start(bf16[160,128]{1,0:T(8,128)(2,1)S(1)} %convert_element_type.21.own.refs_0_), channel_id=1, source_target_pairs={{0,3},{1,2},{2,1},{3,0},{4,7},{5,6},{6,5},{7,4},{8,11},{9,10},{10,... | collective-permute-start | bytes 122888 | tf_op jit(solution)/shard_map/ppermute | solution.py:350
  3.9 0.6 %collective-permute-start.1 = (bf16[160,128]{1,0:T(8,128)(2,1)S(1)}, bf16[160,128]{1,0:T(8,128)(2,1)S(1)}, u32[]{:S(2)}, u32[]{:S(2)}) collective-permute-start(bf16[160,128]{1,0:T(8,128)(2,1)S(1)} %convert_element_type.21.own.refs_0_), channel_id=1, source_target_pairs={{0,2},{1,3},{2,0},{3,1},{4,6},{5,7},{6,4},{7,5},{8,10},{9,11},{10,... | collective-permute-start | bytes 122888 | tf_op jit(solution)/shard_map/ppermute | solution.py:350
  4.5 0.0 collective-permute-start
  4.6 2.3 %prepare.1 = (bf16[3072,640]{1,0:T(8,128)(2,1)S(1)}, bf16[3072,128]{1,0:T(8,128)(2,1)S(1)}, bf16[128,3072]{1,0:T(8,128)(2,1)S(1)}, f32[1,640]{1,0:T(1,128)S(1)}, f32[640,128]{1,0:T(8,128)S(1)}) custom-call(bf16[3072,640]{1,0:T(8,128)(2,1)} %x_in.1, s32[3072]{0:T(1024)} %index_in.1, bf16[512,128]{1,0:T(8,128)(2,1)} %cell_in.1, f32[640]{0:T(1024)} %scale_in.1), custom_call_target="tpu_custom_call" | custom-call | flops 1610612736 | bytes 31457280 | tf_op jit(solution)/shard_map/prepare/pallas_call | solution.py:74
  6.9 0.6 %early_part.1 = (f32[768,128]{1,0:T(8,128)S(1)}, f32[128,256]{1,0:T(8,128)S(1)}, bf16[128,256]{1,0:T(8,128)(2,1)S(1)}, bf16[256,128]{1,0:T(8,128)(2,1)S(1)}) custom-call(bf16[3072,640]{1,0:T(8,128)(2,1)S(1)} %get-tuple-element.31.x_ref.refs_0_, bf16[3072,128]{1,0:T(8,128)(2,1)S(1)} %get-tuple-element.32.f_ref.refs_1_, ...), custom_call_target="tpu_custom_call" | custom-call | flops 301989888 | bytes 786432 | tf_op jit(solution)/shard_map/early_part/pallas_call | solution.py:316
  7.5 0.5 %collective-permute-done.1.refs_2_ = bf16[160,128]{1,0:T(8,128)(2,1)S(1)} collective-permute-done((bf16[160,128]{1,0:T(8,128)(2,1)S(1)}, bf16[160,128]{1,0:T(8,128)(2,1)S(1)}, u32[]{:S(2)}, u32[]{:S(2)}) %collective-permute-start.1) | collective-permute-done | bytes 40992 | tf_op jit(solution)/shard_map/ppermute | solution.py:350
  8.1 0.9 %rest_part.1 = (bf16[384,128]{1,0:T(8,128)(2,1)S(1)}, bf16[384,128]{1,0:T(8,128)(2,1)S(1)}, f32[128,640]{1,0:T(8,128)S(1)}, bf16[128,640]{1,0:T(8,128)(2,1)S(1)}, bf16[640,128]{1,0:T(8,128)(2,1)S(1)}) custom-call(bf16[3072,640]{1,0:T(8,128)(2,1)S(1)} %get-tuple-element.31.x_ref.refs_0_, bf16[3072,128]{1,0:T(8,128)(2,1)S(1)} %get-tuple-element.32.f_ref.refs_1_, ...), custom_call_target="tpu_custom_call" | custom-call | flops 452984832 | bytes 1179648 | tf_op jit(solution)/shard_map/rest_part/pallas_call | solution.py:331
  9.0 2.6 %collective-permute-start.3 = (bf16[384,128]{1,0:T(8,128)(2,1)S(1)}, bf16[384,128]{1,0:T(8,128)(2,1)S(1)}, u32[]{:S(2)}, u32[]{:S(2)}) collective-permute-start(bf16[384,128]{1,0:T(8,128)(2,1)S(1)} %get-tuple-element.46), channel_id=1, source_target_pairs={{0,8},{4,0},{8,12},{12,4},{1,9},{5,1},{9,13},{13,5},{2,10},{6,2},{... | collective-permute-start | bytes 294920 | tf_op jit(solution)/shard_map/ppermute | solution.py:466
  11.6 1.6 %collective-permute-start.5 = (bf16[384,128]{1,0:T(8,128)(2,1)S(1)}, bf16[384,128]{1,0:T(8,128)(2,1)S(1)}, u32[]{:S(2)}, u32[]{:S(2)}) collective-permute-start(bf16[384,128]{1,0:T(8,128)(2,1)S(1)} %get-tuple-element.48), channel_id=1, source_target_pairs={{0,8},{4,0},{8,12},{12,4},{1,9},{5,1},{9,13},{13,5},{2,10},{6,2},{... | collective-permute-start | bytes 294920 | tf_op jit(solution)/shard_map/ppermute | solution.py:466
  13.2 1.2 %block_rows.2 = (bf16[768,128]{1,0:T(8,128)(2,1)S(1)}, f32[128,640]{1,0:T(8,128)S(1)}) custom-call(bf16[3072,640]{1,0:T(8,128)(2,1)S(1)} %get-tuple-element.31.x_ref.refs_0_, bf16[3072,128]{1,0:T(8,128)(2,1)S(1)} %get-tuple-element.32.f_ref.refs_1_, bf16[128,3072]{1,0:T(8,128)(2,1)S(1)} %get-tuple-element.33.ft_ref.refs_2_, ...), custom_call_target="tpu_custom_call" | custom-call | flops 377487360 | bytes 983040 | tf_op jit(solution)/shard_map/block_rows/pallas_call | solution.py:214
  14.4 0.0 copy-start.1
  14.4 0.0 copy-start.2
  14.4 0.5 %collective-permute-start.7 = (bf16[768,128]{1,0:T(8,128)(2,1)S(1)}, bf16[768,128]{1,0:T(8,128)(2,1)S(1)}, u32[]{:S(2)}, u32[]{:S(2)}) collective-permute-start(bf16[768,128]{1,0:T(8,128)(2,1)S(1)} %get-tuple-element.49), channel_id=1, source_target_pairs={{0,4},{4,12},{8,0},{12,8},{1,5},{5,13},{9,1},{13,9},{2,6},{6,14},{... | collective-permute-start | bytes 589832 | tf_op jit(solution)/shard_map/ppermute | solution.py:466
  14.9 2.1 %block_rows.3 = (bf16[384,128]{1,0:T(8,128)(2,1)S(1)}, bf16[384,128]{1,0:T(8,128)(2,1)S(1)}, f32[768,128]{1,0:T(8,128)S(1)}, f32[160,128]{1,0:T(8,128)S(1)}, bf1...) custom-call(bf16[3072,640]{1,0:T(8,128)(2,1)S(1)} %get-tuple-element.31.x_ref.refs_0_, ...), custom_call_target="tpu_custom_call" | custom-call | flops 754974720 | bytes 1966080 | tf_op jit(solution)/shard_map/block_rows/pallas_call | solution.py:214
  17.0 2.5 %collective-permute-start.4 = (bf16[384,128]{1,0:T(8,128)(2,1)S(1)}, bf16[384,128]{1,0:T(8,128)(2,1)S(1)}, u32[]{:S(2)}, u32[]{:S(2)}) collective-permute-start(bf16[384,128]{1,0:T(8,128)(2,1)S(1)} %add_convert_fusion.1), channel_id=1, source_target_pairs={{0,8},{4,0},{8,12},{12,4},{1,9},{5,1},{9,13},{13,5},{2,10},{6,2},{... | collective-permute-start | bytes 294920 | tf_op jit(solution)/shard_map/ppermute | solution.py:466
  19.6 0.6 %collective-permute-start.6 = (bf16[384,128]{1,0:T(8,128)(2,1)S(1)}, bf16[384,128]{1,0:T(8,128)(2,1)S(1)}, u32[]{:S(2)}, u32[]{:S(2)}) collective-permute-start(bf16[384,128]{1,0:T(8,128)(2,1)S(1)} %add_convert_fusion), channel_id=1, source_target_pairs={{0,8},{4,0},{8,12},{12,4},{1,9},{5,1},{9,13},{13,5},{2,10},{6,2},{... | collective-permute-start | bytes 294920 | tf_op jit(solution)/shard_map/ppermute | solution.py:466
  20.2 1.4 %collective-permute-start.9 = (bf16[160,128]{1,0:T(8,128)(2,1)S(1)}, bf16[160,128]{1,0:T(8,128)(2,1)S(1)}, u32[]{:S(2)}, u32[]{:S(2)}) collective-permute-start(bf16[160,128]{1,0:T(8,128)(2,1)S(1)} %get-tuple-element.52), channel_id=1, source_target_pairs={{0,2},{1,3},{2,0},{3,1},{4,6},{5,7},{6,4},{7,5},{8,10},{9,11},{10,... | collective-permute-start | bytes 122888 | tf_op jit(solution)/shard_map/ppermute | solution.py:350
  21.6 1.0 %collective-permute-start.10 = (bf16[160,128]{1,0:T(8,128)(2,1)S(1)}, bf16[160,128]{1,0:T(8,128)(2,1)S(1)}, u32[]{:S(2)}, u32[]{:S(2)}) collective-permute-start(bf16[160,128]{1,0:T(8,128)(2,1)S(1)} %get-tuple-element.53), channel_id=1, source_target_pairs={{0,3},{1,2},{2,1},{3,0},{4,7},{5,6},{6,5},{7,4},{8,11},{9,10},{10,... | collective-permute-start | bytes 122888 | tf_op jit(solution)/shard_map/ppermute | solution.py:350
  22.6 1.6 %collective-permute-done.9.refs_6_ = bf16[160,128]{1,0:T(8,128)(2,1)S(1)} collective-permute-done((bf16[160,128]{1,0:T(8,128)(2,1)S(1)}, bf16[160,128]{1,0:T(8,128)(2,1)S(1)}, u32[]{:S(2)}, u32[]{:S(2)}) %collective-permute-start.9) | collective-permute-done | bytes 40992 | tf_op jit(solution)/shard_map/ppermute | solution.py:350
  24.2 0.9 %collective-permute-done.10.refs_7_ = bf16[160,128]{1,0:T(8,128)(2,1)S(1)} collective-permute-done((bf16[160,128]{1,0:T(8,128)(2,1)S(1)}, bf16[160,128]{1,0:T(8,128)(2,1)S(1)}, u32[]{:S(2)}, u32[]{:S(2)}) %collective-permute-start.10) | collective-permute-done | bytes 40992 | tf_op jit(solution)/shard_map/ppermute | solution.py:350
  25.1 1.0 %collective-permute-done.6.refs_2_ = bf16[384,128]{1,0:T(8,128)(2,1)S(1)} collective-permute-done((bf16[384,128]{1,0:T(8,128)(2,1)S(1)}, bf16[384,128]{1,0:T(8,128)(2,1)S(1)}, u32[]{:S(2)}, u32[]{:S(2)}) %collective-permute-start.6) | collective-permute-done | bytes 98336 | tf_op jit(solution)/shard_map/ppermute | solution.py:466
  26.2 0.3 %collective-permute-done.7.refs_3_ = bf16[768,128]{1,0:T(8,128)(2,1)S(1)} collective-permute-done((bf16[768,128]{1,0:T(8,128)(2,1)S(1)}, bf16[768,128]{1,0:T(8,128)(2,1)S(1)}, u32[]{:S(2)}, u32[]{:S(2)}) %collective-permute-start.7) | collective-permute-done | bytes 196640 | tf_op jit(solution)/shard_map/ppermute | solution.py:466
  26.5 0.9 %finish.1 = (f32[160,128]{1,0:T(8,128)}, f32[160,128]{1,0:T(8,128)}, f32[160,128]{1,0:T(8,128)}, f32[768,128]{1,0:T(8,128)}) custom-call(f32[768,128]{1,0:T(8,128)S(1)} %get-tuple-element.44.refs_0_, bf16[384,128]{1,0:T(8,128)(2,1)S(1)} %collective-permute-done.4.refs_1_, bf16[384,128]{1,0:T(8,128)(2,1)S(1)} %collective-permute-done.6.refs_2_, ...), custom_call_target="tpu_custom_call" | custom-call | flops 409600 | bytes 1753088 | tf_op jit(solution)/shard_map/finish/pallas_call | solution.py:415
  (13 shorter events, 0.1 us)
Async XLA Ops:
  1.5 6.0 %collective-permute-start.2 = (bf16[160,128]{1,0:T(8,128)(2,1)S(1)}, bf16[160,128]{1,0:T(8,128)(2,1)S(1)}, u32[]{:S(2)}, u32[]{:S(2)}) collective-permute-start(bf16[160,128]{1,0:T(8,128)(2,1)S(1)} %convert_element_type.21.own.refs_0_), channel_id=1, source_target_pairs={{0,3},{1,2},{2,1},{3,0},{4,7},{5,6},{6,5},{7,4},{8,11},{9,10},{10,... | collective-permute-start | bytes 122888 | tf_op jit(solution)/shard_map/ppermute | solution.py:350
  3.9 4.1 %collective-permute-start.1 = (bf16[160,128]{1,0:T(8,128)(2,1)S(1)}, bf16[160,128]{1,0:T(8,128)(2,1)S(1)}, u32[]{:S(2)}, u32[]{:S(2)}) collective-permute-start(bf16[160,128]{1,0:T(8,128)(2,1)S(1)} %convert_element_type.21.own.refs_0_), channel_id=1, source_target_pairs={{0,2},{1,3},{2,0},{3,1},{4,6},{5,7},{6,4},{7,5},{8,10},{9,11},{10,... | collective-permute-start | bytes 122888 | tf_op jit(solution)/shard_map/ppermute | solution.py:350
  4.5 2.3 %collective-permute-start = (bf16[160,128]{1,0:T(8,128)(2,1)S(1)}, bf16[160,128]{1,0:T(8,128)(2,1)S(1)}, u32[]{:S(2)}, u32[]{:S(2)}) collective-permute-start(bf16[160,128]{1,0:T(8,128)(2,1)S(1)} %convert_element_type.21.own.refs_0_), channel_id=1, source_target_pairs={{0,1},{1,0},{2,3},{3,2},{4,5},{5,4},{6,7},{7,6},{8,9},{9,8},{10,11... | collective-permute-start | bytes 122888 | tf_op jit(solution)/shard_map/ppermute | solution.py:350
  9.0 8.0 %collective-permute-start.3 = (bf16[384,128]{1,0:T(8,128)(2,1)S(1)}, bf16[384,128]{1,0:T(8,128)(2,1)S(1)}, u32[]{:S(2)}, u32[]{:S(2)}) collective-permute-start(bf16[384,128]{1,0:T(8,128)(2,1)S(1)} %get-tuple-element.46), channel_id=1, source_target_pairs={{0,8},{4,0},{8,12},{12,4},{1,9},{5,1},{9,13},{13,5},{2,10},{6,2},{... | collective-permute-start | bytes 294920 | tf_op jit(solution)/shard_map/ppermute | solution.py:466
  11.6 8.0 %collective-permute-start.5 = (bf16[384,128]{1,0:T(8,128)(2,1)S(1)}, bf16[384,128]{1,0:T(8,128)(2,1)S(1)}, u32[]{:S(2)}, u32[]{:S(2)}) collective-permute-start(bf16[384,128]{1,0:T(8,128)(2,1)S(1)} %get-tuple-element.48), channel_id=1, source_target_pairs={{0,8},{4,0},{8,12},{12,4},{1,9},{5,1},{9,13},{13,5},{2,10},{6,2},{... | collective-permute-start | bytes 294920 | tf_op jit(solution)/shard_map/ppermute | solution.py:466
  14.3 12.1 %copy-start = (f32[160,128]{1,0:T(8,128)S(1)}, f32[160,128]{1,0:T(8,128)}, u32[]{:S(2)}) copy-start(f32[160,128]{1,0:T(8,128)} %refs_8_.1) | copy-start | bytes 245764
  14.4 12.1 %copy-start.1 = (f32[160,128]{1,0:T(8,128)S(1)}, f32[160,128]{1,0:T(8,128)}, u32[]{:S(2)}) copy-start(f32[160,128]{1,0:T(8,128)} %refs_9_.1) | copy-start | bytes 245764
  14.4 12.1 %copy-start.2 = (f32[160,128]{1,0:T(8,128)S(1)}, f32[160,128]{1,0:T(8,128)}, u32[]{:S(2)}) copy-start(f32[160,128]{1,0:T(8,128)} %refs_10_.1) | copy-start | bytes 245764
  14.4 12.1 %collective-permute-start.7 = (bf16[768,128]{1,0:T(8,128)(2,1)S(1)}, bf16[768,128]{1,0:T(8,128)(2,1)S(1)}, u32[]{:S(2)}, u32[]{:S(2)}) collective-permute-start(bf16[768,128]{1,0:T(8,128)(2,1)S(1)} %get-tuple-element.49), channel_id=1, source_target_pairs={{0,4},{4,12},{8,0},{12,8},{1,5},{5,13},{9,1},{13,9},{2,6},{6,14},{... | collective-permute-start | bytes 589832 | tf_op jit(solution)/shard_map/ppermute | solution.py:466
  17.0 8.1 %collective-permute-start.4 = (bf16[384,128]{1,0:T(8,128)(2,1)S(1)}, bf16[384,128]{1,0:T(8,128)(2,1)S(1)}, u32[]{:S(2)}, u32[]{:S(2)}) collective-permute-start(bf16[384,128]{1,0:T(8,128)(2,1)S(1)} %add_convert_fusion.1), channel_id=1, source_target_pairs={{0,8},{4,0},{8,12},{12,4},{1,9},{5,1},{9,13},{13,5},{2,10},{6,2},{... | collective-permute-start | bytes 294920 | tf_op jit(solution)/shard_map/ppermute | solution.py:466
  19.6 6.6 %collective-permute-start.6 = (bf16[384,128]{1,0:T(8,128)(2,1)S(1)}, bf16[384,128]{1,0:T(8,128)(2,1)S(1)}, u32[]{:S(2)}, u32[]{:S(2)}) collective-permute-start(bf16[384,128]{1,0:T(8,128)(2,1)S(1)} %add_convert_fusion), channel_id=1, source_target_pairs={{0,8},{4,0},{8,12},{12,4},{1,9},{5,1},{9,13},{13,5},{2,10},{6,2},{... | collective-permute-start | bytes 294920 | tf_op jit(solution)/shard_map/ppermute | solution.py:466
  20.2 1.4 %collective-permute-start.8 = (bf16[160,128]{1,0:T(8,128)(2,1)S(1)}, bf16[160,128]{1,0:T(8,128)(2,1)S(1)}, u32[]{:S(2)}, u32[]{:S(2)}) collective-permute-start(bf16[160,128]{1,0:T(8,128)(2,1)S(1)} %get-tuple-element.51), channel_id=1, source_target_pairs={{0,1},{1,0},{2,3},{3,2},{4,5},{5,4},{6,7},{7,6},{8,9},{9,8},{10,11... | collective-permute-start | bytes 122888 | tf_op jit(solution)/shard_map/ppermute | solution.py:350
  20.2 4.0 %collective-permute-start.9 = (bf16[160,128]{1,0:T(8,128)(2,1)S(1)}, bf16[160,128]{1,0:T(8,128)(2,1)S(1)}, u32[]{:S(2)}, u32[]{:S(2)}) collective-permute-start(bf16[160,128]{1,0:T(8,128)(2,1)S(1)} %get-tuple-element.52), channel_id=1, source_target_pairs={{0,2},{1,3},{2,0},{3,1},{4,6},{5,7},{6,4},{7,5},{8,10},{9,11},{10,... | collective-permute-start | bytes 122888 | tf_op jit(solution)/shard_map/ppermute | solution.py:350
  21.6 3.5 %collective-permute-start.10 = (bf16[160,128]{1,0:T(8,128)(2,1)S(1)}, bf16[160,128]{1,0:T(8,128)(2,1)S(1)}, u32[]{:S(2)}, u32[]{:S(2)}) collective-permute-start(bf16[160,128]{1,0:T(8,128)(2,1)S(1)} %get-tuple-element.53), channel_id=1, source_target_pairs={{0,3},{1,2},{2,1},{3,0},{4,7},{5,6},{6,5},{7,4},{8,11},{9,10},{10,... | collective-permute-start | bytes 122888 | tf_op jit(solution)/shard_map/ppermute | solution.py:350

commit v20 on v14

--- a/solution.py
+++ b/solution.py
@@ -16,6 +16,7 @@
 adam_eps = 1e-08
 
 RING_MOST = 8
+LINES = ("gene", "row")
 VMEM = pltpu.VMEM
 IN_VMEM = pl.BlockSpec(memory_space=VMEM)
 IN_ANY = pl.BlockSpec(memory_space=pl.ANY)
@@ -138,7 +139,7 @@
     step = tile_of(block, 256)
     tiles = []
     for table, out in zip(tables, rows_out):
-        origin = pick("gene", table) * block if len(table) > 1 else 0
+        origin = pick(LINES, table) * block if len(table) > 1 else 0
         for at in range(0, block, step):
             start = origin + at
             if len(table) > 1:
@@ -229,7 +230,7 @@
 
 def part_of_block(table, block, here, x_ref, f_ref, ft_ref, bend_ref, wide, scaled):
     step = tile_of(block, 256)
-    origin = pick("gene", table) * block
+    origin = pick(LINES, table) * block
     tiles = [pl.ds(pl.multiple_of(origin + at, math.gcd(block, step)), step) for at in range(0, block, step)]
     bend = bend_ref[:, here]
     preds = [jnp.dot(f_ref[tile, :], wide, preferred_element_type=jnp.float32) for tile in tiles]
@@ -340,9 +341,10 @@
     return [step for pair in itertools.zip_longest(ahead, back) for step in pair if step]
 
 
-def around(size, hops):
+def around(size, rows, hops):
     ring = ring_of(size)
-    return tuple(ring[(ring.index(place) + hops) % size] for place in range(size))
+    ways = [-hops if row % 2 else hops for row in range(rows)]
+    return tuple(ring[(ring.index(place) + way) % size] for place in range(size) for way in ways)
 
 
 def plus(wide, narrow):
@@ -419,7 +421,7 @@
         return (grad_cells, *finish([], [parts[0], *others], *adam))
 
     steps = steps_of(n_gene)
-    tables = [around(n_gene, way * distance) for way, distance in steps] + [tuple(range(n_gene))]
+    tables = [around(n_gene, n_row, way * distance) for way, distance in steps] + [around(n_gene, n_row, 0)]
     kinds = [jnp.bfloat16] * len(steps) + [jnp.float32]
     cuts = [0, 1, 2, len(tables)] if len(steps) > 2 else [0, 1, len(tables)]
     parted = lane_parts(genes_dev, genes_dev // n_row, n_row)
@@ -438,7 +440,7 @@
     for (way, _), own in zip(steps, blocks):
         if way in came:
             own = plus(own, came[way]).astype(jnp.bfloat16)
-        came[way] = lax.ppermute(own, "gene", list(enumerate(around(n_gene, way))))
+        came[way] = lax.ppermute(own, LINES, [(at, to * n_row + at % n_row) for at, to in enumerate(around(n_gene, n_row, way))])
     others = [swap_row(parts[hop], hop, n_row) for hop in range(1, n_row)]
     *adam_out, grad_cells = finish([blocks[-1], *came.values()], [parts[0], *others], *adam)
     return (grad_cells, *adam_out)

time: 27 us -> 27.3 us (1.011)
  waiting for transfers between devices: 6.1 us -> 7.81 us
  starting transfers between devices: 11.1 us -> 9.62 us
    ppermute x3, starting transfers between devices: 6.14 us -> 4.69 us  [local(): lax.ppermute(own, LINES, [(at, to * n_row + at % n_row) for at, to in enu...]
    ppermute x3, waiting for transfers between devices: 2.67 us -> 4.12 us  [local(): lax.ppermute(own, LINES, [(at, to * n_row + at % n_row) for at, to in enu...]
where the time goes in v20:
time: 27.3 us; the launch traced here: 27.1 us
  starting transfers between devices  9.62 us (35%)
  Pallas kernels  7.97 us (29%)
  waiting for transfers between devices  7.81 us (29%)
  other arithmetic  0.95 us (3%)
  between operations  0.73 us (3%)
    ppermute x6, starting transfers between devices, swap_row(): lax.ppermute(value, 'row', [(me, partner(me, hop, size)) for me in range(...  4.93 us
    ppermute x3, starting transfers between devices, local(): lax.ppermute(own, LINES, [(at, to * n_row + at % n_row) for at, to in enu...  4.69 us
    ppermute x3, waiting for transfers between devices, local(): lax.ppermute(own, LINES, [(at, to * n_row + at % n_row) for at, to in enu...  4.12 us
    ppermute x6, waiting for transfers between devices, swap_row(): lax.ppermute(value, 'row', [(me, partner(me, hop, size)) for me in range(...  3.69 us
    pallas_call x2, Pallas kernels, block_rows(): pl.pallas_call(functools.partial(rows_kernel, tables, block, first, last,...  3.28 us
    pallas_call x1, Pallas kernels, prepare(): pl.pallas_call(functools.partial(prepare_kernel, scale_k), out_shape=(VME...  2.26 us
    pallas_call x1, Pallas kernels, finish(): pl.pallas_call(functools.partial(finish_kernel, len(ends), len(parts)), o...  0.9 us
    pallas_call x1, Pallas kernels, first_block(): pl.pallas_call(functools.partial(rest_kernel, table, block, parts, n_row)...  0.9 us
  transfers between devices with their start and end apart: 9, of which 5 were waited for; matrix products, arithmetic and copies ran while one was open for 0% of the time, Pallas kernels for 23%

profile of v20, /device:TPU:0, one launch (start us, length us, event | category | flops | bytes accessed | tf_op | source)
XLA Modules:
  0.0 27.1 jit_solution(1726803319859315748)
XLA Ops:
  0.6 0.9 %convert_element_type.12.own.refs_0_ = bf16[160,128]{1,0:T(8,128)(2,1)S(1)} convert(f32[160,128]{1,0:T(8,128)} %refs_7_.1) | non-fusion elementwise | flops 20480 | bytes 122880 | tf_op jit(solution)/shard_map/convert_element_type | solution.py:412
  1.5 2.4 %collective-permute-start.2 = (bf16[160,128]{1,0:T(8,128)(2,1)S(1)}, bf16[160,128]{1,0:T(8,128)(2,1)S(1)}, u32[]{:S(2)}, u32[]{:S(2)}) collective-permute-start(bf16[160,128]{1,0:T(8,128)(2,1)S(1)} %convert_element_type.12.own.refs_0_), channel_id=1, source_target_pairs={{0,3},{1,2},{2,1},{3,0},{4,7},{5,6},{6,5},{7,4},{8,11},{9,10},{10,... | collective-permute-start | bytes 122888 | tf_op jit(solution)/shard_map/ppermute | solution.py:331
  3.9 0.6 %collective-permute-start.1 = (bf16[160,128]{1,0:T(8,128)(2,1)S(1)}, bf16[160,128]{1,0:T(8,128)(2,1)S(1)}, u32[]{:S(2)}, u32[]{:S(2)}) collective-permute-start(bf16[160,128]{1,0:T(8,128)(2,1)S(1)} %convert_element_type.12.own.refs_0_), channel_id=1, source_target_pairs={{0,2},{1,3},{2,0},{3,1},{4,6},{5,7},{6,4},{7,5},{8,10},{9,11},{10,... | collective-permute-start | bytes 122888 | tf_op jit(solution)/shard_map/ppermute | solution.py:331
  4.5 0.0 collective-permute-start
  4.6 2.3 %prepare.1 = (bf16[3072,640]{1,0:T(8,128)(2,1)S(1)}, bf16[3072,128]{1,0:T(8,128)(2,1)S(1)}, bf16[128,3072]{1,0:T(8,128)(2,1)S(1)}, f32[1,640]{1,0:T(1,128)S(1)}, f32[640,128]{1,0:T(8,128)S(1)}) custom-call(bf16[3072,640]{1,0:T(8,128)(2,1)} %x_in.1, s32[3072]{0:T(1024)} %index_in.1, bf16[512,128]{1,0:T(8,128)(2,1)} %cell_in.1, f32[640]{0:T(1024)} %scale_in.1), custom_call_target="tpu_custom_call" | custom-call | flops 1610612736 | bytes 31457280 | tf_op jit(solution)/shard_map/prepare/pallas_call | solution.py:75
  6.9 0.6 %early_part.1 = (f32[768,128]{1,0:T(8,128)S(1)}, f32[128,256]{1,0:T(8,128)S(1)}, bf16[128,256]{1,0:T(8,128)(2,1)S(1)}, bf16[256,128]{1,0:T(8,128)(2,1)S(1)}) custom-call(bf16[3072,640]{1,0:T(8,128)(2,1)S(1)} %get-tuple-element.29.x_ref.refs_0_, bf16[3072,128]{1,0:T(8,128)(2,1)S(1)} %get-tuple-element.30.f_ref.refs_1_, ...), custom_call_target="tpu_custom_call" | custom-call | flops 301989888 | bytes 786432 | tf_op jit(solution)/shard_map/early_part/pallas_call | solution.py:297
  7.5 0.5 %collective-permute-done.1.refs_2_ = bf16[160,128]{1,0:T(8,128)(2,1)S(1)} collective-permute-done((bf16[160,128]{1,0:T(8,128)(2,1)S(1)}, bf16[160,128]{1,0:T(8,128)(2,1)S(1)}, u32[]{:S(2)}, u32[]{:S(2)}) %collective-permute-start.1) | collective-permute-done | bytes 40992 | tf_op jit(solution)/shard_map/ppermute | solution.py:331
  8.1 0.9 %rest_part.1 = (bf16[768,128]{1,0:T(8,128)(2,1)S(1)}, f32[128,640]{1,0:T(8,128)S(1)}, bf16[128,640]{1,0:T(8,128)(2,1)S(1)}, bf16[640,128]{1,0:T(8,128)(2,1)S(1)}) custom-call(bf16[3072,640]{1,0:T(8,128)(2,1)S(1)} %get-tuple-element.29.x_ref.refs_0_, bf16[3072,128]{1,0:T(8,128)(2,1)S(1)} %get-tuple-element.30.f_ref.refs_1_, ...), custom_call_target="tpu_custom_call" | custom-call | flops 452984832 | bytes 1179648 | tf_op jit(solution)/shard_map/rest_part/pallas_call | solution.py:312
  9.0 2.6 %collective-permute-start.3 = (bf16[768,128]{1,0:T(8,128)(2,1)S(1)}, bf16[768,128]{1,0:T(8,128)(2,1)S(1)}, u32[]{:S(2)}, u32[]{:S(2)}) collective-permute-start(bf16[768,128]{1,0:T(8,128)(2,1)S(1)} %get-tuple-element.44), channel_id=1, source_target_pairs={{0,8},{1,5},{2,10},{3,7},{4,0},{5,13},{6,2},{7,15},{8,12},{9,1},{1... | collective-permute-start | bytes 589832 | tf_op jit(solution)/shard_map/ppermute | solution.py:443
  11.6 1.2 %block_rows.2 = (bf16[768,128]{1,0:T(8,128)(2,1)S(1)}, f32[128,640]{1,0:T(8,128)S(1)}) custom-call(bf16[3072,640]{1,0:T(8,128)(2,1)S(1)} %get-tuple-element.29.x_ref.refs_0_, bf16[3072,128]{1,0:T(8,128)(2,1)S(1)} %get-tuple-element.30.f_ref.refs_1_, bf16[128,3072]{1,0:T(8,128)(2,1)S(1)} %get-tuple-element.31.ft_ref.refs_2_, ...), custom_call_target="tpu_custom_call" | custom-call | flops 377487360 | bytes 983040 | tf_op jit(solution)/shard_map/block_rows/pallas_call | solution.py:196
  12.8 0.0 copy-start
  12.8 0.0 copy-start.2
  12.8 0.1 collective-permute-start.5
  12.9 2.1 %block_rows.3 = (bf16[768,128]{1,0:T(8,128)(2,1)S(1)}, f32[768,128]{1,0:T(8,128)S(1)}, f32[160,128]{1,0:T(8,128)S(1)}, bf16[160,128]{1,0:T(8,128)(2,1)S(1)}, bf1...) custom-call(bf16[3072,640]{1,0:T(8,128)(2,1)S(1)} %get-tuple-element.29.x_ref.refs_0_, ...), custom_call_target="tpu_custom_call" | custom-call | flops 754974720 | bytes 1966080 | tf_op jit(solution)/shard_map/block_rows/pallas_call | solution.py:196
  15.0 3.3 %collective-permute-done.3 = bf16[768,128]{1,0:T(8,128)(2,1)S(1)} collective-permute-done((bf16[768,128]{1,0:T(8,128)(2,1)S(1)}, bf16[768,128]{1,0:T(8,128)(2,1)S(1)}, u32[]{:S(2)}, u32[]{:S(2)}) %collective-permute-start.3) | collective-permute-done | bytes 196640 | tf_op jit(solution)/shard_map/ppermute | solution.py:443
  18.3 0.1 add_convert_fusion
  18.3 2.0 %collective-permute-start.4 = (bf16[768,128]{1,0:T(8,128)(2,1)S(1)}, bf16[768,128]{1,0:T(8,128)(2,1)S(1)}, u32[]{:S(2)}, u32[]{:S(2)}) collective-permute-start(bf16[768,128]{1,0:T(8,128)(2,1)S(1)} %add_convert_fusion), channel_id=1, source_target_pairs={{0,8},{1,5},{2,10},{3,7},{4,0},{5,13},{6,2},{7,15},{8,12},{9,1},{1... | collective-permute-start | bytes 589832 | tf_op jit(solution)/shard_map/ppermute | solution.py:443
  20.3 0.1 collective-permute-start.6
  20.4 1.4 %collective-permute-start.7 = (bf16[160,128]{1,0:T(8,128)(2,1)S(1)}, bf16[160,128]{1,0:T(8,128)(2,1)S(1)}, u32[]{:S(2)}, u32[]{:S(2)}) collective-permute-start(bf16[160,128]{1,0:T(8,128)(2,1)S(1)} %get-tuple-element.48), channel_id=1, source_target_pairs={{0,2},{1,3},{2,0},{3,1},{4,6},{5,7},{6,4},{7,5},{8,10},{9,11},{10,... | collective-permute-start | bytes 122888 | tf_op jit(solution)/shard_map/ppermute | solution.py:331
  21.8 0.4 %collective-permute-start.8 = (bf16[160,128]{1,0:T(8,128)(2,1)S(1)}, bf16[160,128]{1,0:T(8,128)(2,1)S(1)}, u32[]{:S(2)}, u32[]{:S(2)}) collective-permute-start(bf16[160,128]{1,0:T(8,128)(2,1)S(1)} %get-tuple-element.49), channel_id=1, source_target_pairs={{0,3},{1,2},{2,1},{3,0},{4,7},{5,6},{6,5},{7,4},{8,11},{9,10},{10,... | collective-permute-start | bytes 122888 | tf_op jit(solution)/shard_map/ppermute | solution.py:331
  22.2 2.2 %collective-permute-done.7.refs_5_ = bf16[160,128]{1,0:T(8,128)(2,1)S(1)} collective-permute-done((bf16[160,128]{1,0:T(8,128)(2,1)S(1)}, bf16[160,128]{1,0:T(8,128)(2,1)S(1)}, u32[]{:S(2)}, u32[]{:S(2)}) %collective-permute-start.7) | collective-permute-done | bytes 40992 | tf_op jit(solution)/shard_map/ppermute | solution.py:331
  24.4 0.9 %collective-permute-done.8.refs_6_ = bf16[160,128]{1,0:T(8,128)(2,1)S(1)} collective-permute-done((bf16[160,128]{1,0:T(8,128)(2,1)S(1)}, bf16[160,128]{1,0:T(8,128)(2,1)S(1)}, u32[]{:S(2)}, u32[]{:S(2)}) %collective-permute-start.8) | collective-permute-done | bytes 40992 | tf_op jit(solution)/shard_map/ppermute | solution.py:331
  25.4 0.8 %collective-permute-done.5.refs_2_ = bf16[768,128]{1,0:T(8,128)(2,1)S(1)} collective-permute-done((bf16[768,128]{1,0:T(8,128)(2,1)S(1)}, bf16[768,128]{1,0:T(8,128)(2,1)S(1)}, u32[]{:S(2)}, u32[]{:S(2)}) %collective-permute-start.5) | collective-permute-done | bytes 196640 | tf_op jit(solution)/shard_map/ppermute | solution.py:443
  26.2 0.9 %finish.1 = (f32[160,128]{1,0:T(8,128)}, f32[160,128]{1,0:T(8,128)}, f32[160,128]{1,0:T(8,128)}, f32[768,128]{1,0:T(8,128)}) custom-call(f32[768,128]{1,0:T(8,128)S(1)} %get-tuple-element.42.refs_0_, bf16[768,128]{1,0:T(8,128)(2,1)S(1)} %collective-permute-done.4.refs_1_, bf16[768,128]{1,0:T(8,128)(2,1)S(1)} %collective-permute-done.5.refs_2_, ...), custom_call_target="tpu_custom_call" | custom-call | flops 409600 | bytes 1753088 | tf_op jit(solution)/shard_map/finish/pallas_call | solution.py:394
  (8 shorter events, 0.0 us)
Async XLA Ops:
  1.5 6.0 %collective-permute-start.2 = (bf16[160,128]{1,0:T(8,128)(2,1)S(1)}, bf16[160,128]{1,0:T(8,128)(2,1)S(1)}, u32[]{:S(2)}, u32[]{:S(2)}) collective-permute-start(bf16[160,128]{1,0:T(8,128)(2,1)S(1)} %convert_element_type.12.own.refs_0_), channel_id=1, source_target_pairs={{0,3},{1,2},{2,1},{3,0},{4,7},{5,6},{6,5},{7,4},{8,11},{9,10},{10,... | collective-permute-start | bytes 122888 | tf_op jit(solution)/shard_map/ppermute | solution.py:331
  3.9 4.1 %collective-permute-start.1 = (bf16[160,128]{1,0:T(8,128)(2,1)S(1)}, bf16[160,128]{1,0:T(8,128)(2,1)S(1)}, u32[]{:S(2)}, u32[]{:S(2)}) collective-permute-start(bf16[160,128]{1,0:T(8,128)(2,1)S(1)} %convert_element_type.12.own.refs_0_), channel_id=1, source_target_pairs={{0,2},{1,3},{2,0},{3,1},{4,6},{5,7},{6,4},{7,5},{8,10},{9,11},{10,... | collective-permute-start | bytes 122888 | tf_op jit(solution)/shard_map/ppermute | solution.py:331
  4.5 2.3 %collective-permute-start = (bf16[160,128]{1,0:T(8,128)(2,1)S(1)}, bf16[160,128]{1,0:T(8,128)(2,1)S(1)}, u32[]{:S(2)}, u32[]{:S(2)}) collective-permute-start(bf16[160,128]{1,0:T(8,128)(2,1)S(1)} %convert_element_type.12.own.refs_0_), channel_id=1, source_target_pairs={{0,1},{1,0},{2,3},{3,2},{4,5},{5,4},{6,7},{7,6},{8,9},{9,8},{10,11... | collective-permute-start | bytes 122888 | tf_op jit(solution)/shard_map/ppermute | solution.py:331
  9.0 9.3 %collective-permute-start.3 = (bf16[768,128]{1,0:T(8,128)(2,1)S(1)}, bf16[768,128]{1,0:T(8,128)(2,1)S(1)}, u32[]{:S(2)}, u32[]{:S(2)}) collective-permute-start(bf16[768,128]{1,0:T(8,128)(2,1)S(1)} %get-tuple-element.44), channel_id=1, source_target_pairs={{0,8},{1,5},{2,10},{3,7},{4,0},{5,13},{6,2},{7,15},{8,12},{9,1},{1... | collective-permute-start | bytes 589832 | tf_op jit(solution)/shard_map/ppermute | solution.py:443
  12.8 13.4 %copy-start = (f32[160,128]{1,0:T(8,128)S(1)}, f32[160,128]{1,0:T(8,128)}, u32[]{:S(2)}) copy-start(f32[160,128]{1,0:T(8,128)} %refs_7_.1) | copy-start | bytes 245764
  12.8 13.4 %copy-start.1 = (f32[160,128]{1,0:T(8,128)S(1)}, f32[160,128]{1,0:T(8,128)}, u32[]{:S(2)}) copy-start(f32[160,128]{1,0:T(8,128)} %refs_8_.1) | copy-start | bytes 245764
  12.8 13.4 %copy-start.2 = (f32[160,128]{1,0:T(8,128)S(1)}, f32[160,128]{1,0:T(8,128)}, u32[]{:S(2)}) copy-start(f32[160,128]{1,0:T(8,128)} %refs_9_.1) | copy-start | bytes 245764
  12.8 13.4 %collective-permute-start.5 = (bf16[768,128]{1,0:T(8,128)(2,1)S(1)}, bf16[768,128]{1,0:T(8,128)(2,1)S(1)}, u32[]{:S(2)}, u32[]{:S(2)}) collective-permute-start(bf16[768,128]{1,0:T(8,128)(2,1)S(1)} %get-tuple-element.45), channel_id=1, source_target_pairs={{0,4},{1,9},{2,6},{3,11},{4,12},{5,1},{6,14},{7,3},{8,0},{9,13},{1... | collective-permute-start | bytes 589832 | tf_op jit(solution)/shard_map/ppermute | solution.py:443
  18.3 7.8 %collective-permute-start.4 = (bf16[768,128]{1,0:T(8,128)(2,1)S(1)}, bf16[768,128]{1,0:T(8,128)(2,1)S(1)}, u32[]{:S(2)}, u32[]{:S(2)}) collective-permute-start(bf16[768,128]{1,0:T(8,128)(2,1)S(1)} %add_convert_fusion), channel_id=1, source_target_pairs={{0,8},{1,5},{2,10},{3,7},{4,0},{5,13},{6,2},{7,15},{8,12},{9,1},{1... | collective-permute-start | bytes 589832 | tf_op jit(solution)/shard_map/ppermute | solution.py:443
  20.3 1.9 %collective-permute-start.6 = (bf16[160,128]{1,0:T(8,128)(2,1)S(1)}, bf16[160,128]{1,0:T(8,128)(2,1)S(1)}, u32[]{:S(2)}, u32[]{:S(2)}) collective-permute-start(bf16[160,128]{1,0:T(8,128)(2,1)S(1)} %get-tuple-element.47), channel_id=1, source_target_pairs={{0,1},{1,0},{2,3},{3,2},{4,5},{5,4},{6,7},{7,6},{8,9},{9,8},{10,11... | collective-permute-start | bytes 122888 | tf_op jit(solution)/shard_map/ppermute | solution.py:331
  20.4 4.0 %collective-permute-start.7 = (bf16[160,128]{1,0:T(8,128)(2,1)S(1)}, bf16[160,128]{1,0:T(8,128)(2,1)S(1)}, u32[]{:S(2)}, u32[]{:S(2)}) collective-permute-start(bf16[160,128]{1,0:T(8,128)(2,1)S(1)} %get-tuple-element.48), channel_id=1, source_target_pairs={{0,2},{1,3},{2,0},{3,1},{4,6},{5,7},{6,4},{7,5},{8,10},{9,11},{10,... | collective-permute-start | bytes 122888 | tf_op jit(solution)/shard_map/ppermute | solution.py:331
  21.8 3.5 %collective-permute-start.8 = (bf16[160,128]{1,0:T(8,128)(2,1)S(1)}, bf16[160,128]{1,0:T(8,128)(2,1)S(1)}, u32[]{:S(2)}, u32[]{:S(2)}) collective-permute-start(bf16[160,128]{1,0:T(8,128)(2,1)S(1)} %get-tuple-element.49), channel_id=1, source_target_pairs={{0,3},{1,2},{2,1},{3,0},{4,7},{5,6},{6,5},{7,4},{8,11},{9,10},{10,... | collective-permute-start | bytes 122888 | tf_op jit(solution)/shard_map/ppermute | solution.py:331

commit v21 on v14

--- a/solution.py
+++ b/solution.py
@@ -206,6 +206,75 @@
     return done, rest if first or last else rest + list(carried[1:])
 
 
+def first_row(table, block):
+    return pl.multiple_of(pick("gene", table) * block, block) if len(table) > 1 else 0
+
+
+def gather(cells, local):
+    hot = lax.broadcasted_iota(jnp.int32, (cells.shape[1], local.shape[1]), 0) == local
+    hot = jnp.where(hot, 1.0, 0.0).astype(jnp.bfloat16)
+    return jnp.dot(cells, hot, preferred_element_type=jnp.float32)
+
+
+def prepare_first_kernel(scale_k, table, block, x_in, index_in, cell_in, scale_in, *refs):
+    x_out, f_out, ft_out, bend_out, shrink_out, index, flat, cell, scale, sems = refs
+    here = pl.ds(first_row(table, block), block)
+    pairs = ((scale_in, scale), (cell_in, cell), (index_in, index), (x_in.at[here, :], x_out))
+    loads = [pltpu.make_async_copy(src, dst, sems.at[at]) for at, (src, dst) in enumerate(pairs)]
+    for load in loads:
+        load.start()
+    cells, rank = cell.shape
+    rows = index.shape[0]
+    genes = scale.shape[0]
+    loads[0].wait()
+    inverse = 1.0 / scale[...].reshape(1, genes)
+    bend_out[...] = (inverse * inverse) * (1.0 / (tukey_c * tukey_c))
+    shrink_out[...] = jnp.transpose(jnp.broadcast_to(-scale_k * (inverse * inverse), (rank, genes)))
+    loads[1].wait()
+    turned = jnp.transpose(cell[...].astype(jnp.float32)).astype(jnp.bfloat16)
+    loads[2].wait()
+    step = tile_of(rows, 512)
+    for at in range(0, rows, step):
+        flat[:, at : at + step] = index[at : at + step].reshape(1, step) - lax.axis_index("row") * cells
+    step = tile_of(block, 256)
+    for at in range(0, block, step):
+        start = first_row(table, block) + at
+        if len(table) > 1:
+            start = pl.multiple_of(start, math.gcd(block, step))
+        picked = gather(turned, flat[:, pl.ds(start, step)])
+        ft_out[:, at : at + step] = picked.astype(jnp.bfloat16)
+        f_out[at : at + step, :] = jnp.transpose(picked).astype(jnp.bfloat16)
+    loads[3].wait()
+
+
+def prepare_first(table, block, x_slab, row_index, cell_factor, gene_scale, scale_k):
+    rows, genes = x_slab.shape
+    cells, rank = cell_factor.shape
+    ins = (x_slab, row_index, cell_factor, gene_scale)
+    return pl.pallas_call(
+        functools.partial(prepare_first_kernel, scale_k, table, block),
+        out_shape=(
+            VMEM((block, genes), jnp.bfloat16),
+            VMEM((block, rank), jnp.bfloat16),
+            VMEM((rank, block), jnp.bfloat16),
+            VMEM((1, genes), jnp.float32),
+            VMEM((genes, rank), jnp.float32),
+        ),
+        in_specs=[IN_ANY] * 4,
+        out_specs=(IN_VMEM,) * 5,
+        scratch_shapes=[
+            VMEM((rows,), jnp.int32),
+            VMEM((1, rows), jnp.int32),
+            VMEM((cells, rank), jnp.bfloat16),
+            VMEM((genes,), jnp.float32),
+            pltpu.SemaphoreType.DMA((4,)),
+        ],
+        compiler_params=params(),
+        cost_estimate=cost(32 * block * cells * rank, 64 * block * genes),
+        name="prepare_first",
+    )(*(pltpu.with_memory_space_constraint(a, pltpu.HBM) for a in ins))
+
+
 def lane_parts(genes, depth, n_row):
     if n_row != 4:
         return None
@@ -227,22 +296,25 @@
     return (resid * (inside * inside)).astype(jnp.bfloat16)
 
 
-def part_of_block(table, block, here, x_ref, f_ref, ft_ref, bend_ref, wide, scaled):
+def add_to(total, cols):
+    return cols if total is None else total + cols
+
+
+def over_lanes(here, x_ref, f_ref, ft_ref, bend_ref, wide, scaled):
+    block = x_ref.shape[0]
     step = tile_of(block, 256)
-    origin = pick("gene", table) * block
-    tiles = [pl.ds(pl.multiple_of(origin + at, math.gcd(block, step)), step) for at in range(0, block, step)]
+    tiles = [pl.ds(at, step) for at in range(0, block, step)]
     bend = bend_ref[:, here]
     preds = [jnp.dot(f_ref[tile, :], wide, preferred_element_type=jnp.float32) for tile in tiles]
     infls = [influence(x_ref[tile, here], pred, bend) for tile, pred in zip(tiles, preds)]
     rows, total = [], None
     for tile, infl in zip(tiles, infls):
-        cols = jnp.dot(ft_ref[:, tile], infl, preferred_element_type=jnp.float32)
-        rows.append(jnp.dot(infl, scaled, preferred_element_type=jnp.float32))
-        total = cols if total is None else total + cols
+        rows.append((tile, jnp.dot(infl, scaled, preferred_element_type=jnp.float32)))
+        total = add_to(total, jnp.dot(ft_ref[:, tile], infl, preferred_element_type=jnp.float32))
     return rows, total
 
 
-def early_kernel(table, block, parts, x_ref, f_ref, ft_ref, bend_ref, shrink_ref, own, other, *refs):
+def early_kernel(parts, x_ref, f_ref, ft_ref, bend_ref, shrink_ref, own, other, *refs):
     rows_out, total_out, wide_out, scaled_out, pair = refs
     low, width, _ = parts
     depth = own.shape[0]
@@ -256,74 +328,77 @@
     scaled = (whole * shrink_ref[here, :]).astype(jnp.bfloat16)
     wide_out[...] = wide
     scaled_out[...] = scaled
-    rows, total = part_of_block(table, block, here, x_ref, f_ref, ft_ref, bend_ref, wide, scaled)
-    for at, value in enumerate(rows):
-        rows_out[at * value.shape[0] : (at + 1) * value.shape[0], :] = value
+    rows, total = over_lanes(here, x_ref, f_ref, ft_ref, bend_ref, wide, scaled)
+    for tile, value in rows:
+        rows_out[tile, :] = value
     total_out[...] = total
 
 
-def rest_kernel(table, block, parts, n_row, x_ref, f_ref, ft_ref, bend_ref, shrink_ref, *refs):
-    shares, (rows_in, total_in, wide_in, scaled_in) = refs[:n_row], refs[n_row : n_row + 4]
-    rows_out, total_out, wide_out, scaled_out, piece = refs[n_row + 4 :]
-    low, width, rest = parts
+def rest_kernel(parts, n_row, x_ref, f_ref, ft_ref, bend_ref, shrink_ref, *refs):
+    shares, refs = refs[:n_row], refs[n_row:]
+    if parts:
+        (rows_in, total_in, wide_in, scaled_in), refs = refs[:4], refs[4:]
+    rows_out, total_out, wide_out, scaled_out, piece = refs
     me = lax.axis_index("row")
     depth = shares[0].shape[0]
     for hop in range(n_row):
         start = pl.multiple_of(source(me, hop, n_row) * depth, depth)
         piece[pl.ds(start, depth), :] = shares[hop][...]
-    here = lanes(rest, n_row * depth - width)
+    here = lanes(parts[2], n_row * depth - parts[1]) if parts else pl.ds(0, n_row * depth)
     whole = piece[here, :].astype(jnp.float32)
     wide = jnp.transpose(whole).astype(jnp.bfloat16)
     scaled = (whole * shrink_ref[here, :]).astype(jnp.bfloat16)
-    rows, total = part_of_block(table, block, here, x_ref, f_ref, ft_ref, bend_ref, wide, scaled)
-    for at, value in enumerate(rows):
-        span = slice(at * value.shape[0], (at + 1) * value.shape[0])
-        rows_out[span, :] = (rows_in[span, :] + value).astype(rows_out.dtype)
-    done = lanes(low, width)
+    rows, total = over_lanes(here, x_ref, f_ref, ft_ref, bend_ref, wide, scaled)
+    for tile, value in rows:
+        rows_out[tile, :] = (rows_in[tile, :] + value if parts else value).astype(rows_out.dtype)
     total_out[:, here] = total
-    total_out[:, done] = total_in[...]
     wide_out[:, here] = wide
-    wide_out[:, done] = wide_in[...]
     scaled_out[here, :] = scaled
-    scaled_out[done, :] = scaled_in[...]
-
-
-def first_block(table, block, parts, n_row, fixed, shares):
-    genes, rank = fixed[4].shape
-    depth = genes // n_row
-    width = parts[1]
+    if parts:
+        done = lanes(parts[0], parts[1])
+        total_out[:, done] = total_in[...]
+        wide_out[:, done] = wide_in[...]
+        scaled_out[done, :] = scaled_in[...]
+
+
+def first_block(kind, parts, n_row, fixed, shares):
+    block, genes = fixed[0].shape
+    rank = fixed[1].shape[1]
+    width = parts[1] if parts else 0
     ins = pinned(*fixed)
-    early = pl.pallas_call(
-        functools.partial(early_kernel, table, block, parts),
+    early = []
+    if parts:
+        early = pl.pallas_call(
+            functools.partial(early_kernel, parts),
+            out_shape=(
+                VMEM((block, rank), jnp.float32),
+                VMEM((rank, width), jnp.float32),
+                VMEM((rank, width), jnp.bfloat16),
+                VMEM((width, rank), jnp.bfloat16),
+            ),
+            in_specs=[IN_VMEM] * 7,
+            out_specs=(IN_VMEM,) * 4,
+            scratch_shapes=[VMEM((2 * (genes // n_row), rank), jnp.bfloat16)],
+            compiler_params=params(),
+            cost_estimate=cost(12 * block * width * rank, block * width * 4),
+            name="early_part",
+        )(*ins, *shares[:2])
+    done, *carried = pl.pallas_call(
+        functools.partial(rest_kernel, parts, n_row),
         out_shape=(
-            VMEM((block, rank), jnp.float32),
-            VMEM((rank, width), jnp.float32),
-            VMEM((rank, width), jnp.bfloat16),
-            VMEM((width, rank), jnp.bfloat16),
-        ),
-        in_specs=[IN_VMEM] * 7,
-        out_specs=(IN_VMEM,) * 4,
-        scratch_shapes=[VMEM((2 * depth, rank), jnp.bfloat16)],
-        compiler_params=params(),
-        cost_estimate=cost(12 * block * width * rank, block * width * 4),
-        name="early_part",
-    )(*ins, *shares[:2])
-    done, *carried = pl.pallas_call(
-        functools.partial(rest_kernel, table, block, parts, n_row),
-        out_shape=(
-            jax.ShapeDtypeStruct((block, rank), jnp.bfloat16),
+            jax.ShapeDtypeStruct((block, rank), kind),
             VMEM((rank, genes), jnp.float32),
             VMEM((rank, genes), jnp.bfloat16),
             VMEM((genes, rank), jnp.bfloat16),
         ),
-        in_specs=[IN_VMEM] * (9 + n_row),
+        in_specs=[IN_VMEM] * (5 + n_row + len(early)),
         out_specs=(IN_VMEM,) * 4,
         scratch_shapes=[VMEM((genes, rank), jnp.bfloat16)],
         compiler_params=params(),
         cost_estimate=cost(12 * block * (genes - width) * rank, block * (genes - width) * 4),
         name="rest_part",
     )(*ins, *shares, *pinned(*early))
-    return [done], carried
+    return done, carried
 
 
 def swap_row(value, hop, size):
@@ -409,10 +484,11 @@
     scale_k = 4.0 / math.sqrt(genes_dev * n_gene)
     factor_bf = gene_factor.astype(jnp.bfloat16)
     shares = [factor_bf] + [swap_row(factor_bf, hop, n_row) for hop in range(1, n_row)]
-    fixed = prepare(x_slab, row_index, cell_factor, gene_scale, scale_k)
     adam = (gene_factor, first_moment, second_moment)
+    values = (x_slab, row_index, cell_factor)
 
     if n_gene == 1 or n_gene > RING_MOST or block % 128:
+        fixed = prepare(*values, gene_scale, scale_k)
         (rows,), parts = block_rows([(0,)], [jnp.float32], rows_dev, True, True, n_row, fixed, shares)
         grad_cells = lax.psum_scatter(rows, "gene", scatter_dimension=0, tiled=True)
         others = [swap_row(parts[hop], hop, n_row) for hop in range(1, n_row)]
@@ -421,16 +497,16 @@
     steps = steps_of(n_gene)
     tables = [around(n_gene, way * distance) for way, distance in steps] + [tuple(range(n_gene))]
     kinds = [jnp.bfloat16] * len(steps) + [jnp.float32]
-    cuts = [0, 1, 2, len(tables)] if len(steps) > 2 else [0, 1, len(tables)]
     parted = lane_parts(genes_dev, genes_dev // n_row, n_row)
-    carried, blocks = shares, []
+    near = prepare_first(tables[0], block, *values, gene_scale, scale_k)
+    done, carried = first_block(kinds[0], parted, n_row, near, shares)
+    blocks = [done]
+    late_scale, _ = lax.optimization_barrier((gene_scale, carried[0]))
+    fixed = prepare(*values, late_scale, scale_k)
+    cuts = [1, 2, len(tables)] if len(steps) > 2 else [1, len(tables)]
     for low, high in zip(cuts, cuts[1:]):
         last = high == len(tables)
-        if low == 0 and parted:
-            done, carried = first_block(tables[0], block, parted, n_row, fixed, shares)
-            blocks += done
-            continue
-        done, carried = block_rows(tables[low:high], kinds[low:high], block, low == 0, last, n_row, fixed, carried)
+        done, carried = block_rows(tables[low:high], kinds[low:high], block, False, last, n_row, fixed, carried)
         blocks += done
     parts = carried
 

time: 27 us -> 27.7 us (1.026)
  Pallas kernels: 7.95 us -> 9.37 us
  starting transfers between devices: 11.1 us -> 10.6 us
  waiting for transfers between devices: 6.1 us -> 5.8 us
    pallas_call x2 -> x3, Pallas kernels: 1.54 us -> 2.93 us  [the longest x1 1.42 us: prepare_first(): pl.pallas_call(functools.partial(prepare_first_kernel, scale_k, table, bl...]
    ppermute x3, waiting for transfers between devices: 2.67 us -> 1.6 us  [local(): came[way] = lax.ppermute(own, 'gene', list(enumerate(around(n_gene, way))))]
    ppermute x6, waiting for transfers between devices: 3.43 us -> 4.2 us  [swap_row(): lax.ppermute(value, 'row', [(me, partner(me, hop, size)) for me in range(...]
    ppermute x3, starting transfers between devices: 6.14 us -> 5.65 us  [local(): came[way] = lax.ppermute(own, 'gene', list(enumerate(around(n_gene, way))))]
  transfers between devices with their start and end apart: 9 -> 9, of which waited for: 5 -> 4; matrix products, arithmetic and copies ran while one was open for 0% -> 0% of each run, Pallas kernels for 23% -> 28%
where the time goes in v21:
time: 27.7 us; the launch traced here: 27.5 us
  starting transfers between devices  10.6 us (38%)
  Pallas kernels  9.37 us (34%)
  waiting for transfers between devices  5.8 us (21%)
  other arithmetic  0.95 us (3%)
  between operations  0.75 us (3%)
    ppermute x3, starting transfers between devices, local(): came[way] = lax.ppermute(own, 'gene', list(enumerate(around(n_gene, way))))  5.65 us
    ppermute x6, starting transfers between devices, swap_row(): lax.ppermute(value, 'row', [(me, partner(me, hop, size)) for me in range(...  4.92 us
    ppermute x6, waiting for transfers between devices, swap_row(): lax.ppermute(value, 'row', [(me, partner(me, hop, size)) for me in range(...  4.2 us
    pallas_call x2, Pallas kernels, block_rows(): pl.pallas_call(functools.partial(rows_kernel, tables, block, first, last,...  3.28 us
    pallas_call x1, Pallas kernels, prepare(): pl.pallas_call(functools.partial(prepare_kernel, scale_k), out_shape=(VME...  2.26 us
    ppermute x3, waiting for transfers between devices, local(): came[way] = lax.ppermute(own, 'gene', list(enumerate(around(n_gene, way))))  1.6 us
    pallas_call x1, Pallas kernels, prepare_first(): pl.pallas_call(functools.partial(prepare_first_kernel, scale_k, table, bl...  1.42 us
    pallas_call x1, Pallas kernels, finish(): pl.pallas_call(functools.partial(finish_kernel, len(ends), len(parts)), o...  0.9 us
  transfers between devices with their start and end apart: 9, of which 4 were waited for; matrix products, arithmetic and copies ran while one was open for 0% of the time, Pallas kernels for 28%

profile of v21, /device:TPU:0, one launch (start us, length us, event | category | flops | bytes accessed | tf_op | source)
XLA Modules:
  0.0 27.5 jit_solution(3022095410274968584)
XLA Ops:
  0.6 0.9 %convert_element_type.12.own.refs_0_ = bf16[160,128]{1,0:T(8,128)(2,1)S(1)} convert(f32[160,128]{1,0:T(8,128)} %refs_7_.1) | non-fusion elementwise | flops 20480 | bytes 122880 | tf_op jit(solution)/shard_map/convert_element_type | solution.py:485
  1.5 2.4 %collective-permute-start.2 = (bf16[160,128]{1,0:T(8,128)(2,1)S(1)}, bf16[160,128]{1,0:T(8,128)(2,1)S(1)}, u32[]{:S(2)}, u32[]{:S(2)}) collective-permute-start(bf16[160,128]{1,0:T(8,128)(2,1)S(1)} %convert_element_type.12.own.refs_0_), channel_id=1, source_target_pairs={{0,3},{1,2},{2,1},{3,0},{4,7},{5,6},{6,5},{7,4},{8,11},{9,10},{10,... | collective-permute-start | bytes 122888 | tf_op jit(solution)/shard_map/ppermute | solution.py:405
  3.9 0.6 %collective-permute-start.1 = (bf16[160,128]{1,0:T(8,128)(2,1)S(1)}, bf16[160,128]{1,0:T(8,128)(2,1)S(1)}, u32[]{:S(2)}, u32[]{:S(2)}) collective-permute-start(bf16[160,128]{1,0:T(8,128)(2,1)S(1)} %convert_element_type.12.own.refs_0_), channel_id=1, source_target_pairs={{0,2},{1,3},{2,0},{3,1},{4,6},{5,7},{6,4},{7,5},{8,10},{9,11},{10,... | collective-permute-start | bytes 122888 | tf_op jit(solution)/shard_map/ppermute | solution.py:405
  4.5 0.0 collective-permute-start
  4.6 1.4 %prepare_first.1 = (bf16[768,640]{1,0:T(8,128)(2,1)S(1)}, bf16[768,128]{1,0:T(8,128)(2,1)S(1)}, bf16[128,768]{1,0:T(8,128)(2,1)S(1)}, f32[1,640]{1,0:T(1,128)S(1)}, f32[640,128]{1,0:T(8,128)S(1)}) custom-call(bf16[3072,640]{1,0:T(8,128)(2,1)} %x_in.3, s32[3072]{0:T(1024)} %index_in.3, bf16[512,128]{1,0:T(8,128)(2,1)} %cell_in.3, f32[640]{0:T(1024)} %scale_in.2), custom_call_target="tpu_custom_call" | custom-call | flops 1610612736 | bytes 31457280 | tf_op jit(solution)/shard_map/prepare_first/pallas_call | solution.py:254
  6.0 0.7 %early_part.1 = (f32[768,128]{1,0:T(8,128)S(1)}, f32[128,256]{1,0:T(8,128)S(1)}, bf16[128,256]{1,0:T(8,128)(2,1)S(1)}, bf16[256,128]{1,0:T(8,128)(2,1)S(1)}) custom-call(bf16[768,640]{1,0:T(8,128)(2,1)S(1)} %get-tuple-element.35.x_ref, bf16[768,128]{1,0:T(8,128)(2,1)S(1)} %get-tuple-element.36.f_ref, bf16[128,768]{1,0:T(8,128)(2,1)S(1)} %get-tuple-element.37.ft_ref, ...), custom_call_target="tpu_custom_call" | custom-call | flops 301989888 | bytes 786432 | tf_op jit(solution)/shard_map/early_part/pallas_call | solution.py:371
  6.7 1.4 %collective-permute-done.1.refs_2_ = bf16[160,128]{1,0:T(8,128)(2,1)S(1)} collective-permute-done((bf16[160,128]{1,0:T(8,128)(2,1)S(1)}, bf16[160,128]{1,0:T(8,128)(2,1)S(1)}, u32[]{:S(2)}, u32[]{:S(2)}) %collective-permute-start.1) | collective-permute-done | bytes 40992 | tf_op jit(solution)/shard_map/ppermute | solution.py:405
  8.1 0.9 %rest_part.1 = (bf16[768,128]{1,0:T(8,128)(2,1)S(1)}, f32[128,640]{1,0:T(8,128)S(1)}, bf16[128,640]{1,0:T(8,128)(2,1)S(1)}, bf16[640,128]{1,0:T(8,128)(2,1)S(1)}) custom-call(bf16[768,640]{1,0:T(8,128)(2,1)S(1)} %get-tuple-element.35.x_ref, bf16[768,128]{1,0:T(8,128)(2,1)S(1)} %get-tuple-element.36.f_ref, bf16[128,768]{1,0:T(8,128)(2,1)S(1)} %get-tuple-element.37.ft_ref, ...), custom_call_target="tpu_custom_call" | custom-call | flops 452984832 | bytes 1179648 | tf_op jit(solution)/shard_map/rest_part/pallas_call | solution.py:386
  8.9 2.6 %collective-permute-start.3 = (bf16[768,128]{1,0:T(8,128)(2,1)S(1)}, bf16[768,128]{1,0:T(8,128)(2,1)S(1)}, u32[]{:S(2)}, u32[]{:S(2)}) collective-permute-start(bf16[768,128]{1,0:T(8,128)(2,1)S(1)} %get-tuple-element.56), channel_id=1, source_target_pairs={{0,8},{4,0},{8,12},{12,4},{1,9},{5,1},{9,13},{13,5},{2,10},{6,2},{... | collective-permute-start | bytes 589832 | tf_op jit(solution)/shard_map/ppermute | solution.py:517
  11.6 2.3 %prepare.1 = (bf16[3072,640]{1,0:T(8,128)(2,1)S(1)}, bf16[3072,128]{1,0:T(8,128)(2,1)S(1)}, bf16[128,3072]{1,0:T(8,128)(2,1)S(1)}, f32[1,640]{1,0:T(1,128)S(1)}, f32[640,128]{1,0:T(8,128)S(1)}) custom-call(bf16[3072,640]{1,0:T(8,128)(2,1)} %x_in.3, s32[3072]{0:T(1024)} %index_in.3, bf16[512,128]{1,0:T(8,128)(2,1)} %cell_in.3, f32[640]{0:T(1024)} %scale_in.2), custom_call_target="tpu_custom_call" | custom-call | flops 1610612736 | bytes 31457280 | tf_op jit(solution)/shard_map/prepare/pallas_call | solution.py:74
  13.8 1.2 %block_rows.2 = (bf16[768,128]{1,0:T(8,128)(2,1)S(1)}, f32[128,640]{1,0:T(8,128)S(1)}) custom-call(bf16[3072,640]{1,0:T(8,128)(2,1)S(1)} %get-tuple-element.46.refs_0_, bf16[3072,128]{1,0:T(8,128)(2,1)S(1)} %get-tuple-element.47.refs_1_, bf16[128,3072]{1,0:T(8,128)(2,1)S(1)} %get-tuple-element.48.refs_2_, f32[1,640]{1,0:T(1,128)S(1)} %get-tuple-element.49.refs_3_, ...), custom_call_target="tpu_custom_call" | custom-call | flops 377487360 | bytes 983040 | tf_op jit(solution)/shard_map/block_rows/pallas_call | solution.py:195
  15.0 0.0 copy-start
  15.0 0.0 copy-start.1
  15.0 0.0 copy-start.2
  15.0 0.1 collective-permute-start.5
  15.1 2.1 %block_rows.3 = (bf16[768,128]{1,0:T(8,128)(2,1)S(1)}, f32[768,128]{1,0:T(8,128)S(1)}, f32[160,128]{1,0:T(8,128)S(1)}, bf16[160,128]{1,0:T(8,128)(2,1)S(1)}, bf1...) custom-call(bf16[3072,640]{1,0:T(8,128)(2,1)S(1)} %get-tuple-element.46.refs_0_, ...), custom_call_target="tpu_custom_call" | custom-call | flops 754974720 | bytes 1966080 | tf_op jit(solution)/shard_map/block_rows/pallas_call | solution.py:195
  17.2 0.1 add_convert_fusion
  17.3 3.0 %collective-permute-start.4 = (bf16[768,128]{1,0:T(8,128)(2,1)S(1)}, bf16[768,128]{1,0:T(8,128)(2,1)S(1)}, u32[]{:S(2)}, u32[]{:S(2)}) collective-permute-start(bf16[768,128]{1,0:T(8,128)(2,1)S(1)} %add_convert_fusion), channel_id=1, source_target_pairs={{0,8},{4,0},{8,12},{12,4},{1,9},{5,1},{9,13},{13,5},{2,10},{6,2},{... | collective-permute-start | bytes 589832 | tf_op jit(solution)/shard_map/ppermute | solution.py:517
  20.3 1.2 %collective-permute-start.7 = (bf16[160,128]{1,0:T(8,128)(2,1)S(1)}, bf16[160,128]{1,0:T(8,128)(2,1)S(1)}, u32[]{:S(2)}, u32[]{:S(2)}) collective-permute-start(bf16[160,128]{1,0:T(8,128)(2,1)S(1)} %get-tuple-element.60), channel_id=1, source_target_pairs={{0,2},{1,3},{2,0},{3,1},{4,6},{5,7},{6,4},{7,5},{8,10},{9,11},{10,... | collective-permute-start | bytes 122888 | tf_op jit(solution)/shard_map/ppermute | solution.py:405
  21.4 0.7 %collective-permute-start.8 = (bf16[160,128]{1,0:T(8,128)(2,1)S(1)}, bf16[160,128]{1,0:T(8,128)(2,1)S(1)}, u32[]{:S(2)}, u32[]{:S(2)}) collective-permute-start(bf16[160,128]{1,0:T(8,128)(2,1)S(1)} %get-tuple-element.61), channel_id=1, source_target_pairs={{0,3},{1,2},{2,1},{3,0},{4,7},{5,6},{6,5},{7,4},{8,11},{9,10},{10,... | collective-permute-start | bytes 122888 | tf_op jit(solution)/shard_map/ppermute | solution.py:405
  22.1 2.1 %collective-permute-done.7.refs_5_ = bf16[160,128]{1,0:T(8,128)(2,1)S(1)} collective-permute-done((bf16[160,128]{1,0:T(8,128)(2,1)S(1)}, bf16[160,128]{1,0:T(8,128)(2,1)S(1)}, u32[]{:S(2)}, u32[]{:S(2)}) %collective-permute-start.7) | collective-permute-done | bytes 40992 | tf_op jit(solution)/shard_map/ppermute | solution.py:405
  24.3 0.7 %collective-permute-done.8.refs_6_ = bf16[160,128]{1,0:T(8,128)(2,1)S(1)} collective-permute-done((bf16[160,128]{1,0:T(8,128)(2,1)S(1)}, bf16[160,128]{1,0:T(8,128)(2,1)S(1)}, u32[]{:S(2)}, u32[]{:S(2)}) %collective-permute-start.8) | collective-permute-done | bytes 40992 | tf_op jit(solution)/shard_map/ppermute | solution.py:405
  25.0 1.6 %collective-permute-done.4.refs_1_ = bf16[768,128]{1,0:T(8,128)(2,1)S(1)} collective-permute-done((bf16[768,128]{1,0:T(8,128)(2,1)S(1)}, bf16[768,128]{1,0:T(8,128)(2,1)S(1)}, u32[]{:S(2)}, u32[]{:S(2)}) %collective-permute-start.4) | collective-permute-done | bytes 196640 | tf_op jit(solution)/shard_map/ppermute | solution.py:517
  26.6 0.9 %finish.1 = (f32[160,128]{1,0:T(8,128)}, f32[160,128]{1,0:T(8,128)}, f32[160,128]{1,0:T(8,128)}, f32[768,128]{1,0:T(8,128)}) custom-call(f32[768,128]{1,0:T(8,128)S(1)} %get-tuple-element.54.refs_0_, bf16[768,128]{1,0:T(8,128)(2,1)S(1)} %collective-permute-done.4.refs_1_, bf16[768,128]{1,0:T(8,128)(2,1)S(1)} %collective-permute-done.5.refs_2_, ...), custom_call_target="tpu_custom_call" | custom-call | flops 409600 | bytes 1753088 | tf_op jit(solution)/shard_map/finish/pallas_call | solution.py:467
  (9 shorter events, 0.0 us)
Async XLA Ops:
  1.5 5.2 %collective-permute-start.2 = (bf16[160,128]{1,0:T(8,128)(2,1)S(1)}, bf16[160,128]{1,0:T(8,128)(2,1)S(1)}, u32[]{:S(2)}, u32[]{:S(2)}) collective-permute-start(bf16[160,128]{1,0:T(8,128)(2,1)S(1)} %convert_element_type.12.own.refs_0_), channel_id=1, source_target_pairs={{0,3},{1,2},{2,1},{3,0},{4,7},{5,6},{6,5},{7,4},{8,11},{9,10},{10,... | collective-permute-start | bytes 122888 | tf_op jit(solution)/shard_map/ppermute | solution.py:405
  3.9 4.1 %collective-permute-start.1 = (bf16[160,128]{1,0:T(8,128)(2,1)S(1)}, bf16[160,128]{1,0:T(8,128)(2,1)S(1)}, u32[]{:S(2)}, u32[]{:S(2)}) collective-permute-start(bf16[160,128]{1,0:T(8,128)(2,1)S(1)} %convert_element_type.12.own.refs_0_), channel_id=1, source_target_pairs={{0,2},{1,3},{2,0},{3,1},{4,6},{5,7},{6,4},{7,5},{8,10},{9,11},{10,... | collective-permute-start | bytes 122888 | tf_op jit(solution)/shard_map/ppermute | solution.py:405
  4.5 1.5 %collective-permute-start = (bf16[160,128]{1,0:T(8,128)(2,1)S(1)}, bf16[160,128]{1,0:T(8,128)(2,1)S(1)}, u32[]{:S(2)}, u32[]{:S(2)}) collective-permute-start(bf16[160,128]{1,0:T(8,128)(2,1)S(1)} %convert_element_type.12.own.refs_0_), channel_id=1, source_target_pairs={{0,1},{1,0},{2,3},{3,2},{4,5},{5,4},{6,7},{7,6},{8,9},{9,8},{10,11... | collective-permute-start | bytes 122888 | tf_op jit(solution)/shard_map/ppermute | solution.py:405
  8.9 8.3 %collective-permute-start.3 = (bf16[768,128]{1,0:T(8,128)(2,1)S(1)}, bf16[768,128]{1,0:T(8,128)(2,1)S(1)}, u32[]{:S(2)}, u32[]{:S(2)}) collective-permute-start(bf16[768,128]{1,0:T(8,128)(2,1)S(1)} %get-tuple-element.56), channel_id=1, source_target_pairs={{0,8},{4,0},{8,12},{12,4},{1,9},{5,1},{9,13},{13,5},{2,10},{6,2},{... | collective-permute-start | bytes 589832 | tf_op jit(solution)/shard_map/ppermute | solution.py:517
  15.0 11.6 %copy-start = (f32[160,128]{1,0:T(8,128)S(1)}, f32[160,128]{1,0:T(8,128)}, u32[]{:S(2)}) copy-start(f32[160,128]{1,0:T(8,128)} %refs_7_.1) | copy-start | bytes 245764
  15.0 11.5 %copy-start.1 = (f32[160,128]{1,0:T(8,128)S(1)}, f32[160,128]{1,0:T(8,128)}, u32[]{:S(2)}) copy-start(f32[160,128]{1,0:T(8,128)} %refs_8_.1) | copy-start | bytes 245764
  15.0 11.5 %copy-start.2 = (f32[160,128]{1,0:T(8,128)S(1)}, f32[160,128]{1,0:T(8,128)}, u32[]{:S(2)}) copy-start(f32[160,128]{1,0:T(8,128)} %refs_9_.1) | copy-start | bytes 245764
  15.0 9.9 %collective-permute-start.5 = (bf16[768,128]{1,0:T(8,128)(2,1)S(1)}, bf16[768,128]{1,0:T(8,128)(2,1)S(1)}, u32[]{:S(2)}, u32[]{:S(2)}) collective-permute-start(bf16[768,128]{1,0:T(8,128)(2,1)S(1)} %get-tuple-element.57), channel_id=1, source_target_pairs={{0,4},{4,12},{8,0},{12,8},{1,5},{5,13},{9,1},{13,9},{2,6},{6,14},{... | collective-permute-start | bytes 589832 | tf_op jit(solution)/shard_map/ppermute | solution.py:517
  17.3 9.3 %collective-permute-start.4 = (bf16[768,128]{1,0:T(8,128)(2,1)S(1)}, bf16[768,128]{1,0:T(8,128)(2,1)S(1)}, u32[]{:S(2)}, u32[]{:S(2)}) collective-permute-start(bf16[768,128]{1,0:T(8,128)(2,1)S(1)} %add_convert_fusion), channel_id=1, source_target_pairs={{0,8},{4,0},{8,12},{12,4},{1,9},{5,1},{9,13},{13,5},{2,10},{6,2},{... | collective-permute-start | bytes 589832 | tf_op jit(solution)/shard_map/ppermute | solution.py:517
  20.2 1.9 %collective-permute-start.6 = (bf16[160,128]{1,0:T(8,128)(2,1)S(1)}, bf16[160,128]{1,0:T(8,128)(2,1)S(1)}, u32[]{:S(2)}, u32[]{:S(2)}) collective-permute-start(bf16[160,128]{1,0:T(8,128)(2,1)S(1)} %get-tuple-element.59), channel_id=1, source_target_pairs={{0,1},{1,0},{2,3},{3,2},{4,5},{5,4},{6,7},{7,6},{8,9},{9,8},{10,11... | collective-permute-start | bytes 122888 | tf_op jit(solution)/shard_map/ppermute | solution.py:405
  20.3 4.0 %collective-permute-start.7 = (bf16[160,128]{1,0:T(8,128)(2,1)S(1)}, bf16[160,128]{1,0:T(8,128)(2,1)S(1)}, u32[]{:S(2)}, u32[]{:S(2)}) collective-permute-start(bf16[160,128]{1,0:T(8,128)(2,1)S(1)} %get-tuple-element.60), channel_id=1, source_target_pairs={{0,2},{1,3},{2,0},{3,1},{4,6},{5,7},{6,4},{7,5},{8,10},{9,11},{10,... | collective-permute-start | bytes 122888 | tf_op jit(solution)/shard_map/ppermute | solution.py:405
  21.4 3.5 %collective-permute-start.8 = (bf16[160,128]{1,0:T(8,128)(2,1)S(1)}, bf16[160,128]{1,0:T(8,128)(2,1)S(1)}, u32[]{:S(2)}, u32[]{:S(2)}) collective-permute-start(bf16[160,128]{1,0:T(8,128)(2,1)S(1)} %get-tuple-element.61), channel_id=1, source_target_pairs={{0,3},{1,2},{2,1},{3,0},{4,7},{5,6},{6,5},{7,4},{8,11},{9,10},{10,... | collective-permute-start | bytes 122888 | tf_op jit(solution)/shard_map/ppermute | solution.py:405

commit v22 on v13

--- a/solution.py
+++ b/solution.py
@@ -326,6 +326,10 @@
     return [done], carried
 
 
+def far_first(size):
+    return sorted(range(1, size), key=lambda hop: (-hop.bit_length(), hop))
+
+
 def swap_row(value, hop, size):
     return lax.ppermute(value, "row", [(me, partner(me, hop, size)) for me in range(size)])
 
@@ -415,7 +419,7 @@
     if n_gene == 1 or n_gene > RING_MOST or block % 128:
         (rows,), parts = block_rows([(0,)], [jnp.float32], rows_dev, True, True, n_row, fixed, shares)
         grad_cells = lax.psum_scatter(rows, "gene", scatter_dimension=0, tiled=True)
-        others = [swap_row(parts[hop], hop, n_row) for hop in range(1, n_row)]
+        others = [swap_row(parts[hop], hop, n_row) for hop in far_first(n_row)]
         return (grad_cells, *finish([], [parts[0], *others], *adam))
 
     steps = steps_of(n_gene)
@@ -439,7 +443,7 @@
         if way in came:
             own = plus(own, came[way]).astype(jnp.bfloat16)
         came[way] = lax.ppermute(own, "gene", list(enumerate(around(n_gene, way))))
-    others = [swap_row(parts[hop], hop, n_row) for hop in range(1, n_row)]
+    others = [swap_row(parts[hop], hop, n_row) for hop in far_first(n_row)]
     *adam_out, grad_cells = finish([blocks[-1], *came.values()], [parts[0], *others], *adam)
     return (grad_cells, *adam_out)
 

time: 26.6 us -> 26.8 us (level)
  starting transfers between devices: 11.1 us -> 11.4 us
    ppermute x6, starting transfers between devices: 4.97 us -> 5.25 us  [swap_row(): lax.ppermute(value, 'row', [(me, partner(me, hop, size)) for me in range(...]
where the time goes in v22:
time: 26.8 us; the launch traced here: 26.6 us
  starting transfers between devices  11.4 us (43%)
  Pallas kernels  7.95 us (30%)
  waiting for transfers between devices  5.58 us (21%)
  other arithmetic  0.95 us (4%)
  between operations  0.75 us (3%)
    ppermute x3, starting transfers between devices, local(): came[way] = lax.ppermute(own, 'gene', list(enumerate(around(n_gene, way))))  6.14 us
    ppermute x6, starting transfers between devices, swap_row(): lax.ppermute(value, 'row', [(me, partner(me, hop, size)) for me in range(...  5.25 us
    ppermute x6, waiting for transfers between devices, swap_row(): lax.ppermute(value, 'row', [(me, partner(me, hop, size)) for me in range(...  3.58 us
    pallas_call x2, Pallas kernels, block_rows(): pl.pallas_call(functools.partial(rows_kernel, tables, block, first, last,...  3.25 us
    pallas_call x1, Pallas kernels, prepare(): pl.pallas_call(functools.partial(prepare_kernel, scale_k), out_shape=(VME...  2.26 us
    ppermute x3, waiting for transfers between devices, local(): came[way] = lax.ppermute(own, 'gene', list(enumerate(around(n_gene, way))))  1.99 us
    pallas_call x1, Pallas kernels, finish(): pl.pallas_call(functools.partial(finish_kernel, len(ends), len(parts)), o...  0.9 us
    convert_element_type x1, other arithmetic, local(): factor_bf = gene_factor.astype(jnp.bfloat16)  0.9 us
  transfers between devices with their start and end apart: 9, of which 4 were waited for; matrix products, arithmetic and copies ran while one was open for 0% of the time, Pallas kernels for 23%

profile of v22, /device:TPU:0, one launch (start us, length us, event | category | flops | bytes accessed | tf_op | source)
XLA Modules:
  0.0 26.6 jit_solution(14856244322241416359)
XLA Ops:
  0.6 0.9 %convert_element_type.12.own.refs_0_ = bf16[160,128]{1,0:T(8,128)(2,1)S(1)} convert(f32[160,128]{1,0:T(8,128)} %refs_7_.1) | non-fusion elementwise | flops 20480 | bytes 122880 | tf_op jit(solution)/shard_map/convert_element_type | solution.py:414
  1.5 0.5 %collective-permute-start = (bf16[160,128]{1,0:T(8,128)(2,1)S(1)}, bf16[160,128]{1,0:T(8,128)(2,1)S(1)}, u32[]{:S(2)}, u32[]{:S(2)}) collective-permute-start(bf16[160,128]{1,0:T(8,128)(2,1)S(1)} %convert_element_type.12.own.refs_0_), channel_id=1, source_target_pairs={{0,1},{1,0},{2,3},{3,2},{4,5},{5,4},{6,7},{7,6},{8,9},{9,8},{10,11... | collective-permute-start | bytes 122888 | tf_op jit(solution)/shard_map/ppermute | solution.py:334
  2.0 2.6 %collective-permute-start.2 = (bf16[160,128]{1,0:T(8,128)(2,1)S(1)}, bf16[160,128]{1,0:T(8,128)(2,1)S(1)}, u32[]{:S(2)}, u32[]{:S(2)}) collective-permute-start(bf16[160,128]{1,0:T(8,128)(2,1)S(1)} %convert_element_type.12.own.refs_0_), channel_id=1, source_target_pairs={{0,3},{1,2},{2,1},{3,0},{4,7},{5,6},{6,5},{7,4},{8,11},{9,10},{10,... | collective-permute-start | bytes 122888 | tf_op jit(solution)/shard_map/ppermute | solution.py:334
  4.6 0.1 collective-permute-start.1
  4.6 2.3 %prepare.1 = (bf16[3072,640]{1,0:T(8,128)(2,1)S(1)}, bf16[3072,128]{1,0:T(8,128)(2,1)S(1)}, bf16[128,3072]{1,0:T(8,128)(2,1)S(1)}, f32[1,640]{1,0:T(1,128)S(1)}, f32[640,128]{1,0:T(8,128)S(1)}) custom-call(bf16[3072,640]{1,0:T(8,128)(2,1)} %x_in.1, s32[3072]{0:T(1024)} %index_in.1, bf16[512,128]{1,0:T(8,128)(2,1)} %cell_in.1, f32[640]{0:T(1024)} %scale_in.1), custom_call_target="tpu_custom_call" | custom-call | flops 402653184 | bytes 7864320 | tf_op jit(solution)/shard_map/prepare/pallas_call | solution.py:74
  6.9 0.6 %early_part.1 = (f32[768,128]{1,0:T(8,128)S(1)}, f32[128,256]{1,0:T(8,128)S(1)}, bf16[128,256]{1,0:T(8,128)(2,1)S(1)}, bf16[256,128]{1,0:T(8,128)(2,1)S(1)}) custom-call(bf16[3072,640]{1,0:T(8,128)(2,1)S(1)} %get-tuple-element.29.x_ref.refs_0_, bf16[3072,128]{1,0:T(8,128)(2,1)S(1)} %get-tuple-element.30.f_ref.refs_1_, ...), custom_call_target="tpu_custom_call" | custom-call | flops 301989888 | bytes 786432 | tf_op jit(solution)/shard_map/early_part/pallas_call | solution.py:296
  7.6 0.0 collective-permute-done.2.refs_3_
  7.6 1.0 %collective-permute-done.1.refs_2_ = bf16[160,128]{1,0:T(8,128)(2,1)S(1)} collective-permute-done((bf16[160,128]{1,0:T(8,128)(2,1)S(1)}, bf16[160,128]{1,0:T(8,128)(2,1)S(1)}, u32[]{:S(2)}, u32[]{:S(2)}) %collective-permute-start.1) | collective-permute-done | bytes 40992 | tf_op jit(solution)/shard_map/ppermute | solution.py:334
  8.6 0.9 %rest_part.1 = (bf16[768,128]{1,0:T(8,128)(2,1)S(1)}, f32[128,640]{1,0:T(8,128)S(1)}, bf16[128,640]{1,0:T(8,128)(2,1)S(1)}, bf16[640,128]{1,0:T(8,128)(2,1)S(1)}) custom-call(bf16[3072,640]{1,0:T(8,128)(2,1)S(1)} %get-tuple-element.29.x_ref.refs_0_, bf16[3072,128]{1,0:T(8,128)(2,1)S(1)} %get-tuple-element.30.f_ref.refs_1_, ...), custom_call_target="tpu_custom_call" | custom-call | flops 452984832 | bytes 1179648 | tf_op jit(solution)/shard_map/rest_part/pallas_call | solution.py:311
  9.5 2.6 %collective-permute-start.3 = (bf16[768,128]{1,0:T(8,128)(2,1)S(1)}, bf16[768,128]{1,0:T(8,128)(2,1)S(1)}, u32[]{:S(2)}, u32[]{:S(2)}) collective-permute-start(bf16[768,128]{1,0:T(8,128)(2,1)S(1)} %get-tuple-element.44), channel_id=1, source_target_pairs={{0,8},{4,0},{8,12},{12,4},{1,9},{5,1},{9,13},{13,5},{2,10},{6,2},{... | collective-permute-start | bytes 589832 | tf_op jit(solution)/shard_map/ppermute | solution.py:445
  12.1 1.2 %block_rows.2 = (bf16[768,128]{1,0:T(8,128)(2,1)S(1)}, f32[128,640]{1,0:T(8,128)S(1)}) custom-call(bf16[3072,640]{1,0:T(8,128)(2,1)S(1)} %get-tuple-element.29.x_ref.refs_0_, bf16[3072,128]{1,0:T(8,128)(2,1)S(1)} %get-tuple-element.30.f_ref.refs_1_, bf16[128,3072]{1,0:T(8,128)(2,1)S(1)} %get-tuple-element.31.ft_ref.refs_2_, ...), custom_call_target="tpu_custom_call" | custom-call | flops 377487360 | bytes 983040 | tf_op jit(solution)/shard_map/block_rows/pallas_call | solution.py:195
  13.3 0.0 copy-start
  13.3 0.0 copy-start.1
  13.3 0.0 copy-start.2
  13.3 0.1 collective-permute-start.5
  13.4 2.1 %block_rows.3 = (bf16[768,128]{1,0:T(8,128)(2,1)S(1)}, f32[768,128]{1,0:T(8,128)S(1)}, f32[160,128]{1,0:T(8,128)S(1)}, bf16[160,128]{1,0:T(8,128)(2,1)S(1)}, bf1...) custom-call(bf16[3072,640]{1,0:T(8,128)(2,1)S(1)} %get-tuple-element.29.x_ref.refs_0_, ...), custom_call_target="tpu_custom_call" | custom-call | flops 754974720 | bytes 1966080 | tf_op jit(solution)/shard_map/block_rows/pallas_call | solution.py:195
  15.5 2.0 %collective-permute-done.3 = bf16[768,128]{1,0:T(8,128)(2,1)S(1)} collective-permute-done((bf16[768,128]{1,0:T(8,128)(2,1)S(1)}, bf16[768,128]{1,0:T(8,128)(2,1)S(1)}, u32[]{:S(2)}, u32[]{:S(2)}) %collective-permute-start.3) | collective-permute-done | bytes 196640 | tf_op jit(solution)/shard_map/ppermute | solution.py:445
  17.5 0.1 add_convert_fusion
  17.5 3.4 %collective-permute-start.4 = (bf16[768,128]{1,0:T(8,128)(2,1)S(1)}, bf16[768,128]{1,0:T(8,128)(2,1)S(1)}, u32[]{:S(2)}, u32[]{:S(2)}) collective-permute-start(bf16[768,128]{1,0:T(8,128)(2,1)S(1)} %add_convert_fusion), channel_id=1, source_target_pairs={{0,8},{4,0},{8,12},{12,4},{1,9},{5,1},{9,13},{13,5},{2,10},{6,2},{... | collective-permute-start | bytes 589832 | tf_op jit(solution)/shard_map/ppermute | solution.py:445
  21.0 0.9 %collective-permute-start.6 = (bf16[160,128]{1,0:T(8,128)(2,1)S(1)}, bf16[160,128]{1,0:T(8,128)(2,1)S(1)}, u32[]{:S(2)}, u32[]{:S(2)}) collective-permute-start(bf16[160,128]{1,0:T(8,128)(2,1)S(1)} %get-tuple-element.47), channel_id=1, source_target_pairs={{0,2},{1,3},{2,0},{3,1},{4,6},{5,7},{6,4},{7,5},{8,10},{9,11},{10,... | collective-permute-start | bytes 122888 | tf_op jit(solution)/shard_map/ppermute | solution.py:334
  21.9 1.2 %collective-permute-start.8 = (bf16[160,128]{1,0:T(8,128)(2,1)S(1)}, bf16[160,128]{1,0:T(8,128)(2,1)S(1)}, u32[]{:S(2)}, u32[]{:S(2)}) collective-permute-start(bf16[160,128]{1,0:T(8,128)(2,1)S(1)} %get-tuple-element.49), channel_id=1, source_target_pairs={{0,1},{1,0},{2,3},{3,2},{4,5},{5,4},{6,7},{7,6},{8,9},{9,8},{10,11... | collective-permute-start | bytes 122888 | tf_op jit(solution)/shard_map/ppermute | solution.py:334
  23.1 2.0 %collective-permute-done.6.refs_4_ = bf16[160,128]{1,0:T(8,128)(2,1)S(1)} collective-permute-done((bf16[160,128]{1,0:T(8,128)(2,1)S(1)}, bf16[160,128]{1,0:T(8,128)(2,1)S(1)}, u32[]{:S(2)}, u32[]{:S(2)}) %collective-permute-start.6) | collective-permute-done | bytes 40992 | tf_op jit(solution)/shard_map/ppermute | solution.py:334
  25.2 0.5 %collective-permute-done.7.refs_5_ = bf16[160,128]{1,0:T(8,128)(2,1)S(1)} collective-permute-done((bf16[160,128]{1,0:T(8,128)(2,1)S(1)}, bf16[160,128]{1,0:T(8,128)(2,1)S(1)}, u32[]{:S(2)}, u32[]{:S(2)}) %collective-permute-start.7) | collective-permute-done | bytes 40992 | tf_op jit(solution)/shard_map/ppermute | solution.py:334
  25.7 0.9 %finish.1 = (f32[160,128]{1,0:T(8,128)}, f32[160,128]{1,0:T(8,128)}, f32[160,128]{1,0:T(8,128)}, f32[768,128]{1,0:T(8,128)}) custom-call(f32[768,128]{1,0:T(8,128)S(1)} %get-tuple-element.42.refs_0_, bf16[768,128]{1,0:T(8,128)(2,1)S(1)} %collective-permute-done.4.refs_1_, bf16[768,128]{1,0:T(8,128)(2,1)S(1)} %collective-permute-done.5.refs_2_, ...), custom_call_target="tpu_custom_call" | custom-call | flops 409600 | bytes 1753088 | tf_op jit(solution)/shard_map/finish/pallas_call | solution.py:396
  (8 shorter events, 0.0 us)
Async XLA Ops:
  1.5 5.4 %collective-permute-start = (bf16[160,128]{1,0:T(8,128)(2,1)S(1)}, bf16[160,128]{1,0:T(8,128)(2,1)S(1)}, u32[]{:S(2)}, u32[]{:S(2)}) collective-permute-start(bf16[160,128]{1,0:T(8,128)(2,1)S(1)} %convert_element_type.12.own.refs_0_), channel_id=1, source_target_pairs={{0,1},{1,0},{2,3},{3,2},{4,5},{5,4},{6,7},{7,6},{8,9},{9,8},{10,11... | collective-permute-start | bytes 122888 | tf_op jit(solution)/shard_map/ppermute | solution.py:334
  2.0 5.6 %collective-permute-start.2 = (bf16[160,128]{1,0:T(8,128)(2,1)S(1)}, bf16[160,128]{1,0:T(8,128)(2,1)S(1)}, u32[]{:S(2)}, u32[]{:S(2)}) collective-permute-start(bf16[160,128]{1,0:T(8,128)(2,1)S(1)} %convert_element_type.12.own.refs_0_), channel_id=1, source_target_pairs={{0,3},{1,2},{2,1},{3,0},{4,7},{5,6},{6,5},{7,4},{8,11},{9,10},{10,... | collective-permute-start | bytes 122888 | tf_op jit(solution)/shard_map/ppermute | solution.py:334
  4.6 4.0 %collective-permute-start.1 = (bf16[160,128]{1,0:T(8,128)(2,1)S(1)}, bf16[160,128]{1,0:T(8,128)(2,1)S(1)}, u32[]{:S(2)}, u32[]{:S(2)}) collective-permute-start(bf16[160,128]{1,0:T(8,128)(2,1)S(1)} %convert_element_type.12.own.refs_0_), channel_id=1, source_target_pairs={{0,2},{1,3},{2,0},{3,1},{4,6},{5,7},{6,4},{7,5},{8,10},{9,11},{10,... | collective-permute-start | bytes 122888 | tf_op jit(solution)/shard_map/ppermute | solution.py:334
  9.5 8.0 %collective-permute-start.3 = (bf16[768,128]{1,0:T(8,128)(2,1)S(1)}, bf16[768,128]{1,0:T(8,128)(2,1)S(1)}, u32[]{:S(2)}, u32[]{:S(2)}) collective-permute-start(bf16[768,128]{1,0:T(8,128)(2,1)S(1)} %get-tuple-element.44), channel_id=1, source_target_pairs={{0,8},{4,0},{8,12},{12,4},{1,9},{5,1},{9,13},{13,5},{2,10},{6,2},{... | collective-permute-start | bytes 589832 | tf_op jit(solution)/shard_map/ppermute | solution.py:445
  13.3 12.4 %copy-start = (f32[160,128]{1,0:T(8,128)S(1)}, f32[160,128]{1,0:T(8,128)}, u32[]{:S(2)}) copy-start(f32[160,128]{1,0:T(8,128)} %refs_7_.1) | copy-start | bytes 245764
  13.3 12.4 %copy-start.1 = (f32[160,128]{1,0:T(8,128)S(1)}, f32[160,128]{1,0:T(8,128)}, u32[]{:S(2)}) copy-start(f32[160,128]{1,0:T(8,128)} %refs_8_.1) | copy-start | bytes 245764
  13.3 12.4 %copy-start.2 = (f32[160,128]{1,0:T(8,128)S(1)}, f32[160,128]{1,0:T(8,128)}, u32[]{:S(2)}) copy-start(f32[160,128]{1,0:T(8,128)} %refs_9_.1) | copy-start | bytes 245764
  13.3 12.3 %collective-permute-start.5 = (bf16[768,128]{1,0:T(8,128)(2,1)S(1)}, bf16[768,128]{1,0:T(8,128)(2,1)S(1)}, u32[]{:S(2)}, u32[]{:S(2)}) collective-permute-start(bf16[768,128]{1,0:T(8,128)(2,1)S(1)} %get-tuple-element.45), channel_id=1, source_target_pairs={{0,4},{4,12},{8,0},{12,8},{1,5},{5,13},{9,1},{13,9},{2,6},{6,14},{... | collective-permute-start | bytes 589832 | tf_op jit(solution)/shard_map/ppermute | solution.py:445
  17.5 8.1 %collective-permute-start.4 = (bf16[768,128]{1,0:T(8,128)(2,1)S(1)}, bf16[768,128]{1,0:T(8,128)(2,1)S(1)}, u32[]{:S(2)}, u32[]{:S(2)}) collective-permute-start(bf16[768,128]{1,0:T(8,128)(2,1)S(1)} %add_convert_fusion), channel_id=1, source_target_pairs={{0,8},{4,0},{8,12},{12,4},{1,9},{5,1},{9,13},{13,5},{2,10},{6,2},{... | collective-permute-start | bytes 589832 | tf_op jit(solution)/shard_map/ppermute | solution.py:445
  21.0 4.2 %collective-permute-start.6 = (bf16[160,128]{1,0:T(8,128)(2,1)S(1)}, bf16[160,128]{1,0:T(8,128)(2,1)S(1)}, u32[]{:S(2)}, u32[]{:S(2)}) collective-permute-start(bf16[160,128]{1,0:T(8,128)(2,1)S(1)} %get-tuple-element.47), channel_id=1, source_target_pairs={{0,2},{1,3},{2,0},{3,1},{4,6},{5,7},{6,4},{7,5},{8,10},{9,11},{10,... | collective-permute-start | bytes 122888 | tf_op jit(solution)/shard_map/ppermute | solution.py:334
  21.9 3.8 %collective-permute-start.7 = (bf16[160,128]{1,0:T(8,128)(2,1)S(1)}, bf16[160,128]{1,0:T(8,128)(2,1)S(1)}, u32[]{:S(2)}, u32[]{:S(2)}) collective-permute-start(bf16[160,128]{1,0:T(8,128)(2,1)S(1)} %get-tuple-element.48), channel_id=1, source_target_pairs={{0,3},{1,2},{2,1},{3,0},{4,7},{5,6},{6,5},{7,4},{8,11},{9,10},{10,... | collective-permute-start | bytes 122888 | tf_op jit(solution)/shard_map/ppermute | solution.py:334
  21.9 3.8 %collective-permute-start.8 = (bf16[160,128]{1,0:T(8,128)(2,1)S(1)}, bf16[160,128]{1,0:T(8,128)(2,1)S(1)}, u32[]{:S(2)}, u32[]{:S(2)}) collective-permute-start(bf16[160,128]{1,0:T(8,128)(2,1)S(1)} %get-tuple-element.49), channel_id=1, source_target_pairs={{0,1},{1,0},{2,3},{3,2},{4,5},{5,4},{6,7},{7,6},{8,9},{9,8},{10,11... | collective-permute-start | bytes 122888 | tf_op jit(solution)/shard_map/ppermute | solution.py:334

commit v23 on v20

--- a/solution.py
+++ b/solution.py
@@ -90,7 +90,7 @@
             pltpu.SemaphoreType.DMA((4,)),
         ],
         compiler_params=params(),
-        cost_estimate=cost(8 * rows * cells * rank, 8 * rows * genes * 2),
+        cost_estimate=cost(2 * rows * cells * rank, 2 * rows * genes * 2),
         name="prepare",
     )(*(pltpu.with_memory_space_constraint(a, pltpu.HBM) for a in ins))
 
@@ -342,9 +342,8 @@
 
 
 def around(size, rows, hops):
-    ring = ring_of(size)
-    ways = [-hops if row % 2 else hops for row in range(rows)]
-    return tuple(ring[(ring.index(place) + way) % size] for place in range(size) for way in ways)
+    rings = [list(range(size)) if row % 2 else ring_of(size) for row in range(rows)]
+    return tuple(ring[(ring.index(place) + hops) % size] for place in range(size) for ring in rings)
 
 
 def plus(wide, narrow):

time: 27.3 us -> 27 us (0.989)
  starting transfers between devices: 9.62 us -> 8.25 us
  waiting for transfers between devices: 7.81 us -> 8.94 us
    ppermute x3, starting transfers between devices: 4.69 us -> 3.29 us  [local(): lax.ppermute(own, LINES, [(at, to * n_row + at % n_row) for at, to in enu...]
    ppermute x3, waiting for transfers between devices: 4.12 us -> 5.32 us  [local(): lax.ppermute(own, LINES, [(at, to * n_row + at % n_row) for at, to in enu...]
where the time goes in v23:
time: 27 us; the launch traced here: 26.9 us
  waiting for transfers between devices  8.94 us (33%)
  starting transfers between devices  8.25 us (31%)
  Pallas kernels  7.97 us (30%)
  other arithmetic  0.95 us (4%)
  between operations  0.73 us (3%)
    ppermute x3, waiting for transfers between devices, local(): lax.ppermute(own, LINES, [(at, to * n_row + at % n_row) for at, to in enu...  5.32 us
    ppermute x6, starting transfers between devices, swap_row(): lax.ppermute(value, 'row', [(me, partner(me, hop, size)) for me in range(...  4.97 us
    ppermute x6, waiting for transfers between devices, swap_row(): lax.ppermute(value, 'row', [(me, partner(me, hop, size)) for me in range(...  3.63 us
    ppermute x3, starting transfers between devices, local(): lax.ppermute(own, LINES, [(at, to * n_row + at % n_row) for at, to in enu...  3.29 us
    pallas_call x2, Pallas kernels, block_rows(): pl.pallas_call(functools.partial(rows_kernel, tables, block, first, last,...  3.28 us
    pallas_call x1, Pallas kernels, prepare(): pl.pallas_call(functools.partial(prepare_kernel, scale_k), out_shape=(VME...  2.26 us
    pallas_call x1, Pallas kernels, finish(): pl.pallas_call(functools.partial(finish_kernel, len(ends), len(parts)), o...  0.9 us
    convert_element_type x1, other arithmetic, local(): factor_bf = gene_factor.astype(jnp.bfloat16)  0.9 us
  transfers between devices with their start and end apart: 9, of which 5 were waited for; matrix products, arithmetic and copies ran while one was open for 0% of the time, Pallas kernels for 23%

profile of v23, /device:TPU:0, one launch (start us, length us, event | category | flops | bytes accessed | tf_op | source)
XLA Modules:
  0.0 26.9 jit_solution(2636251592770578178)
XLA Ops:
  0.6 0.9 %convert_element_type.12.own.refs_0_ = bf16[160,128]{1,0:T(8,128)(2,1)S(1)} convert(f32[160,128]{1,0:T(8,128)} %refs_7_.1) | non-fusion elementwise | flops 20480 | bytes 122880 | tf_op jit(solution)/shard_map/convert_element_type | solution.py:411
  1.5 0.5 %collective-permute-start = (bf16[160,128]{1,0:T(8,128)(2,1)S(1)}, bf16[160,128]{1,0:T(8,128)(2,1)S(1)}, u32[]{:S(2)}, u32[]{:S(2)}) collective-permute-start(bf16[160,128]{1,0:T(8,128)(2,1)S(1)} %convert_element_type.12.own.refs_0_), channel_id=1, source_target_pairs={{0,1},{1,0},{2,3},{3,2},{4,5},{5,4},{6,7},{7,6},{8,9},{9,8},{10,11... | collective-permute-start | bytes 122888 | tf_op jit(solution)/shard_map/ppermute | solution.py:331
  2.0 2.6 %collective-permute-start.2 = (bf16[160,128]{1,0:T(8,128)(2,1)S(1)}, bf16[160,128]{1,0:T(8,128)(2,1)S(1)}, u32[]{:S(2)}, u32[]{:S(2)}) collective-permute-start(bf16[160,128]{1,0:T(8,128)(2,1)S(1)} %convert_element_type.12.own.refs_0_), channel_id=1, source_target_pairs={{0,3},{1,2},{2,1},{3,0},{4,7},{5,6},{6,5},{7,4},{8,11},{9,10},{10,... | collective-permute-start | bytes 122888 | tf_op jit(solution)/shard_map/ppermute | solution.py:331
  4.6 0.1 collective-permute-start.1
  4.6 2.3 %prepare.1 = (bf16[3072,640]{1,0:T(8,128)(2,1)S(1)}, bf16[3072,128]{1,0:T(8,128)(2,1)S(1)}, bf16[128,3072]{1,0:T(8,128)(2,1)S(1)}, f32[1,640]{1,0:T(1,128)S(1)}, f32[640,128]{1,0:T(8,128)S(1)}) custom-call(bf16[3072,640]{1,0:T(8,128)(2,1)} %x_in.1, s32[3072]{0:T(1024)} %index_in.1, bf16[512,128]{1,0:T(8,128)(2,1)} %cell_in.1, f32[640]{0:T(1024)} %scale_in.1), custom_call_target="tpu_custom_call" | custom-call | flops 402653184 | bytes 7864320 | tf_op jit(solution)/shard_map/prepare/pallas_call | solution.py:75
  6.9 0.6 %early_part.1 = (f32[768,128]{1,0:T(8,128)S(1)}, f32[128,256]{1,0:T(8,128)S(1)}, bf16[128,256]{1,0:T(8,128)(2,1)S(1)}, bf16[256,128]{1,0:T(8,128)(2,1)S(1)}) custom-call(bf16[3072,640]{1,0:T(8,128)(2,1)S(1)} %get-tuple-element.29.x_ref.refs_0_, bf16[3072,128]{1,0:T(8,128)(2,1)S(1)} %get-tuple-element.30.f_ref.refs_1_, ...), custom_call_target="tpu_custom_call" | custom-call | flops 301989888 | bytes 786432 | tf_op jit(solution)/shard_map/early_part/pallas_call | solution.py:297
  7.6 1.0 %collective-permute-done.1.refs_2_ = bf16[160,128]{1,0:T(8,128)(2,1)S(1)} collective-permute-done((bf16[160,128]{1,0:T(8,128)(2,1)S(1)}, bf16[160,128]{1,0:T(8,128)(2,1)S(1)}, u32[]{:S(2)}, u32[]{:S(2)}) %collective-permute-start.1) | collective-permute-done | bytes 40992 | tf_op jit(solution)/shard_map/ppermute | solution.py:331
  8.6 0.9 %rest_part.1 = (bf16[768,128]{1,0:T(8,128)(2,1)S(1)}, f32[128,640]{1,0:T(8,128)S(1)}, bf16[128,640]{1,0:T(8,128)(2,1)S(1)}, bf16[640,128]{1,0:T(8,128)(2,1)S(1)}) custom-call(bf16[3072,640]{1,0:T(8,128)(2,1)S(1)} %get-tuple-element.29.x_ref.refs_0_, bf16[3072,128]{1,0:T(8,128)(2,1)S(1)} %get-tuple-element.30.f_ref.refs_1_, ...), custom_call_target="tpu_custom_call" | custom-call | flops 452984832 | bytes 1179648 | tf_op jit(solution)/shard_map/rest_part/pallas_call | solution.py:312
  9.5 2.6 %collective-permute-start.3 = (bf16[768,128]{1,0:T(8,128)(2,1)S(1)}, bf16[768,128]{1,0:T(8,128)(2,1)S(1)}, u32[]{:S(2)}, u32[]{:S(2)}) collective-permute-start(bf16[768,128]{1,0:T(8,128)(2,1)S(1)} %get-tuple-element.44), channel_id=1, source_target_pairs={{0,8},{1,5},{2,10},{3,7},{4,0},{5,9},{6,2},{7,11},{8,12},{9,13},{1... | collective-permute-start | bytes 589832 | tf_op jit(solution)/shard_map/ppermute | solution.py:442
  12.1 1.2 %block_rows.2 = (bf16[768,128]{1,0:T(8,128)(2,1)S(1)}, f32[128,640]{1,0:T(8,128)S(1)}) custom-call(bf16[3072,640]{1,0:T(8,128)(2,1)S(1)} %get-tuple-element.29.x_ref.refs_0_, bf16[3072,128]{1,0:T(8,128)(2,1)S(1)} %get-tuple-element.30.f_ref.refs_1_, bf16[128,3072]{1,0:T(8,128)(2,1)S(1)} %get-tuple-element.31.ft_ref.refs_2_, ...), custom_call_target="tpu_custom_call" | custom-call | flops 377487360 | bytes 983040 | tf_op jit(solution)/shard_map/block_rows/pallas_call | solution.py:196
  13.3 0.0 copy-start
  13.3 0.0 copy-start.1
  13.3 0.0 copy-start.2
  13.3 0.1 collective-permute-start.5
  13.4 2.1 %block_rows.3 = (bf16[768,128]{1,0:T(8,128)(2,1)S(1)}, f32[768,128]{1,0:T(8,128)S(1)}, f32[160,128]{1,0:T(8,128)S(1)}, bf16[160,128]{1,0:T(8,128)(2,1)S(1)}, bf1...) custom-call(bf16[3072,640]{1,0:T(8,128)(2,1)S(1)} %get-tuple-element.29.x_ref.refs_0_, ...), custom_call_target="tpu_custom_call" | custom-call | flops 754974720 | bytes 1966080 | tf_op jit(solution)/shard_map/block_rows/pallas_call | solution.py:196
  15.5 4.3 %collective-permute-done.3 = bf16[768,128]{1,0:T(8,128)(2,1)S(1)} collective-permute-done((bf16[768,128]{1,0:T(8,128)(2,1)S(1)}, bf16[768,128]{1,0:T(8,128)(2,1)S(1)}, u32[]{:S(2)}, u32[]{:S(2)}) %collective-permute-start.3) | collective-permute-done | bytes 196640 | tf_op jit(solution)/shard_map/ppermute | solution.py:442
  19.8 0.1 add_convert_fusion
  19.9 0.6 %collective-permute-start.4 = (bf16[768,128]{1,0:T(8,128)(2,1)S(1)}, bf16[768,128]{1,0:T(8,128)(2,1)S(1)}, u32[]{:S(2)}, u32[]{:S(2)}) collective-permute-start(bf16[768,128]{1,0:T(8,128)(2,1)S(1)} %add_convert_fusion), channel_id=1, source_target_pairs={{0,8},{1,5},{2,10},{3,7},{4,0},{5,9},{6,2},{7,11},{8,12},{9,13},{1... | collective-permute-start | bytes 589832 | tf_op jit(solution)/shard_map/ppermute | solution.py:442
  20.5 0.4 %collective-permute-start.7 = (bf16[160,128]{1,0:T(8,128)(2,1)S(1)}, bf16[160,128]{1,0:T(8,128)(2,1)S(1)}, u32[]{:S(2)}, u32[]{:S(2)}) collective-permute-start(bf16[160,128]{1,0:T(8,128)(2,1)S(1)} %get-tuple-element.48), channel_id=1, source_target_pairs={{0,2},{1,3},{2,0},{3,1},{4,6},{5,7},{6,4},{7,5},{8,10},{9,11},{10,... | collective-permute-start | bytes 122888 | tf_op jit(solution)/shard_map/ppermute | solution.py:331
  20.8 1.5 %collective-permute-start.8 = (bf16[160,128]{1,0:T(8,128)(2,1)S(1)}, bf16[160,128]{1,0:T(8,128)(2,1)S(1)}, u32[]{:S(2)}, u32[]{:S(2)}) collective-permute-start(bf16[160,128]{1,0:T(8,128)(2,1)S(1)} %get-tuple-element.49), channel_id=1, source_target_pairs={{0,3},{1,2},{2,1},{3,0},{4,7},{5,6},{6,5},{7,4},{8,11},{9,10},{10,... | collective-permute-start | bytes 122888 | tf_op jit(solution)/shard_map/ppermute | solution.py:331
  22.3 2.5 %collective-permute-done.7.refs_5_ = bf16[160,128]{1,0:T(8,128)(2,1)S(1)} collective-permute-done((bf16[160,128]{1,0:T(8,128)(2,1)S(1)}, bf16[160,128]{1,0:T(8,128)(2,1)S(1)}, u32[]{:S(2)}, u32[]{:S(2)}) %collective-permute-start.7) | collective-permute-done | bytes 40992 | tf_op jit(solution)/shard_map/ppermute | solution.py:331
  24.8 0.1 collective-permute-done.8.refs_6_
  24.9 1.0 %collective-permute-done.4.refs_1_ = bf16[768,128]{1,0:T(8,128)(2,1)S(1)} collective-permute-done((bf16[768,128]{1,0:T(8,128)(2,1)S(1)}, bf16[768,128]{1,0:T(8,128)(2,1)S(1)}, u32[]{:S(2)}, u32[]{:S(2)}) %collective-permute-start.4) | collective-permute-done | bytes 196640 | tf_op jit(solution)/shard_map/ppermute | solution.py:442
  26.0 0.9 %finish.1 = (f32[160,128]{1,0:T(8,128)}, f32[160,128]{1,0:T(8,128)}, f32[160,128]{1,0:T(8,128)}, f32[768,128]{1,0:T(8,128)}) custom-call(f32[768,128]{1,0:T(8,128)S(1)} %get-tuple-element.42.refs_0_, bf16[768,128]{1,0:T(8,128)(2,1)S(1)} %collective-permute-done.4.refs_1_, bf16[768,128]{1,0:T(8,128)(2,1)S(1)} %collective-permute-done.5.refs_2_, ...), custom_call_target="tpu_custom_call" | custom-call | flops 409600 | bytes 1753088 | tf_op jit(solution)/shard_map/finish/pallas_call | solution.py:393
  (8 shorter events, 0.0 us)
Async XLA Ops:
  1.5 5.4 %collective-permute-start = (bf16[160,128]{1,0:T(8,128)(2,1)S(1)}, bf16[160,128]{1,0:T(8,128)(2,1)S(1)}, u32[]{:S(2)}, u32[]{:S(2)}) collective-permute-start(bf16[160,128]{1,0:T(8,128)(2,1)S(1)} %convert_element_type.12.own.refs_0_), channel_id=1, source_target_pairs={{0,1},{1,0},{2,3},{3,2},{4,5},{5,4},{6,7},{7,6},{8,9},{9,8},{10,11... | collective-permute-start | bytes 122888 | tf_op jit(solution)/shard_map/ppermute | solution.py:331
  2.0 5.6 %collective-permute-start.2 = (bf16[160,128]{1,0:T(8,128)(2,1)S(1)}, bf16[160,128]{1,0:T(8,128)(2,1)S(1)}, u32[]{:S(2)}, u32[]{:S(2)}) collective-permute-start(bf16[160,128]{1,0:T(8,128)(2,1)S(1)} %convert_element_type.12.own.refs_0_), channel_id=1, source_target_pairs={{0,3},{1,2},{2,1},{3,0},{4,7},{5,6},{6,5},{7,4},{8,11},{9,10},{10,... | collective-permute-start | bytes 122888 | tf_op jit(solution)/shard_map/ppermute | solution.py:331
  4.6 4.0 %collective-permute-start.1 = (bf16[160,128]{1,0:T(8,128)(2,1)S(1)}, bf16[160,128]{1,0:T(8,128)(2,1)S(1)}, u32[]{:S(2)}, u32[]{:S(2)}) collective-permute-start(bf16[160,128]{1,0:T(8,128)(2,1)S(1)} %convert_element_type.12.own.refs_0_), channel_id=1, source_target_pairs={{0,2},{1,3},{2,0},{3,1},{4,6},{5,7},{6,4},{7,5},{8,10},{9,11},{10,... | collective-permute-start | bytes 122888 | tf_op jit(solution)/shard_map/ppermute | solution.py:331
  9.5 10.3 %collective-permute-start.3 = (bf16[768,128]{1,0:T(8,128)(2,1)S(1)}, bf16[768,128]{1,0:T(8,128)(2,1)S(1)}, u32[]{:S(2)}, u32[]{:S(2)}) collective-permute-start(bf16[768,128]{1,0:T(8,128)(2,1)S(1)} %get-tuple-element.44), channel_id=1, source_target_pairs={{0,8},{1,5},{2,10},{3,7},{4,0},{5,9},{6,2},{7,11},{8,12},{9,13},{1... | collective-permute-start | bytes 589832 | tf_op jit(solution)/shard_map/ppermute | solution.py:442
  13.3 12.6 %copy-start = (f32[160,128]{1,0:T(8,128)S(1)}, f32[160,128]{1,0:T(8,128)}, u32[]{:S(2)}) copy-start(f32[160,128]{1,0:T(8,128)} %refs_7_.1) | copy-start | bytes 245764
  13.3 12.6 %copy-start.1 = (f32[160,128]{1,0:T(8,128)S(1)}, f32[160,128]{1,0:T(8,128)}, u32[]{:S(2)}) copy-start(f32[160,128]{1,0:T(8,128)} %refs_8_.1) | copy-start | bytes 245764
  13.3 12.6 %copy-start.2 = (f32[160,128]{1,0:T(8,128)S(1)}, f32[160,128]{1,0:T(8,128)}, u32[]{:S(2)}) copy-start(f32[160,128]{1,0:T(8,128)} %refs_9_.1) | copy-start | bytes 245764
  13.3 11.6 %collective-permute-start.5 = (bf16[768,128]{1,0:T(8,128)(2,1)S(1)}, bf16[768,128]{1,0:T(8,128)(2,1)S(1)}, u32[]{:S(2)}, u32[]{:S(2)}) collective-permute-start(bf16[768,128]{1,0:T(8,128)(2,1)S(1)} %get-tuple-element.45), channel_id=1, source_target_pairs={{0,4},{1,13},{2,6},{3,15},{4,12},{5,1},{6,14},{7,3},{8,0},{9,5},{1... | collective-permute-start | bytes 589832 | tf_op jit(solution)/shard_map/ppermute | solution.py:442
  19.9 6.1 %collective-permute-start.4 = (bf16[768,128]{1,0:T(8,128)(2,1)S(1)}, bf16[768,128]{1,0:T(8,128)(2,1)S(1)}, u32[]{:S(2)}, u32[]{:S(2)}) collective-permute-start(bf16[768,128]{1,0:T(8,128)(2,1)S(1)} %add_convert_fusion), channel_id=1, source_target_pairs={{0,8},{1,5},{2,10},{3,7},{4,0},{5,9},{6,2},{7,11},{8,12},{9,13},{1... | collective-permute-start | bytes 589832 | tf_op jit(solution)/shard_map/ppermute | solution.py:442
  20.5 1.9 %collective-permute-start.6 = (bf16[160,128]{1,0:T(8,128)(2,1)S(1)}, bf16[160,128]{1,0:T(8,128)(2,1)S(1)}, u32[]{:S(2)}, u32[]{:S(2)}) collective-permute-start(bf16[160,128]{1,0:T(8,128)(2,1)S(1)} %get-tuple-element.47), channel_id=1, source_target_pairs={{0,1},{1,0},{2,3},{3,2},{4,5},{5,4},{6,7},{7,6},{8,9},{9,8},{10,11... | collective-permute-start | bytes 122888 | tf_op jit(solution)/shard_map/ppermute | solution.py:331
  20.5 4.4 %collective-permute-start.7 = (bf16[160,128]{1,0:T(8,128)(2,1)S(1)}, bf16[160,128]{1,0:T(8,128)(2,1)S(1)}, u32[]{:S(2)}, u32[]{:S(2)}) collective-permute-start(bf16[160,128]{1,0:T(8,128)(2,1)S(1)} %get-tuple-element.48), channel_id=1, source_target_pairs={{0,2},{1,3},{2,0},{3,1},{4,6},{5,7},{6,4},{7,5},{8,10},{9,11},{10,... | collective-permute-start | bytes 122888 | tf_op jit(solution)/shard_map/ppermute | solution.py:331
  20.8 4.1 %collective-permute-start.8 = (bf16[160,128]{1,0:T(8,128)(2,1)S(1)}, bf16[160,128]{1,0:T(8,128)(2,1)S(1)}, u32[]{:S(2)}, u32[]{:S(2)}) collective-permute-start(bf16[160,128]{1,0:T(8,128)(2,1)S(1)} %get-tuple-element.49), channel_id=1, source_target_pairs={{0,3},{1,2},{2,1},{3,0},{4,7},{5,6},{6,5},{7,4},{8,11},{9,10},{10,... | collective-permute-start | bytes 122888 | tf_op jit(solution)/shard_map/ppermute | solution.py:331

commit v24 on v13

--- a/solution.py
+++ b/solution.py
@@ -135,7 +135,7 @@
         total, wide, scaled = (ref[...] for ref in carried_in)
 
     bend = bend_ref[...]
-    step = tile_of(block, 256)
+    step = tile_of(block, 512)
     tiles = []
     for table, out in zip(tables, rows_out):
         origin = pick("gene", table) * block if len(table) > 1 else 0
@@ -363,7 +363,7 @@
         copies[-1].start()
 
     if ends:
-        step = tile_of(ends[0].shape[0], 256)
+        step = tile_of(ends[0].shape[0], 512)
         for low in range(0, ends[0].shape[0], step):
             span = pl.ds(low, step)
             rows = ends[0][span, :]
@@ -388,7 +388,7 @@
 def finish(ends, parts, factor, first, second):
     ins = [*ends, *parts, factor, first, second]
     shapes = [factor, factor, factor] + list(ends[:1])
-    n_copies = 3 + (ends[0].shape[0] // tile_of(ends[0].shape[0], 256) if ends else 0)
+    n_copies = 3 + (ends[0].shape[0] // tile_of(ends[0].shape[0], 512) if ends else 0)
     return pl.pallas_call(
         functools.partial(finish_kernel, len(ends), len(parts)),
         out_shape=tuple(jax.ShapeDtypeStruct(like.shape, jnp.float32) for like in shapes),

time: 26.6 us -> 26.6 us (level)
  no operation moved by 1% of the time
where the time goes in v24:
time: 26.6 us; the launch traced here: 26.5 us
  starting transfers between devices  11.1 us (42%)
  Pallas kernels  7.86 us (30%)
  waiting for transfers between devices  5.79 us (22%)
  other arithmetic  0.95 us (4%)
  between operations  0.74 us (3%)
    ppermute x3, starting transfers between devices, local(): came[way] = lax.ppermute(own, 'gene', list(enumerate(around(n_gene, way))))  6.14 us
    ppermute x6, starting transfers between devices, swap_row(): lax.ppermute(value, 'row', [(me, partner(me, hop, size)) for me in range(...  4.97 us
    ppermute x6, waiting for transfers between devices, swap_row(): lax.ppermute(value, 'row', [(me, partner(me, hop, size)) for me in range(...  3.7 us
    pallas_call x2, Pallas kernels, block_rows(): pl.pallas_call(functools.partial(rows_kernel, tables, block, first, last,...  3.16 us
    pallas_call x1, Pallas kernels, prepare(): pl.pallas_call(functools.partial(prepare_kernel, scale_k), out_shape=(VME...  2.26 us
    ppermute x3, waiting for transfers between devices, local(): came[way] = lax.ppermute(own, 'gene', list(enumerate(around(n_gene, way))))  2.09 us
    pallas_call x1, Pallas kernels, finish(): pl.pallas_call(functools.partial(finish_kernel, len(ends), len(parts)), o...  0.9 us
    convert_element_type x1, other arithmetic, local(): factor_bf = gene_factor.astype(jnp.bfloat16)  0.9 us
  transfers between devices with their start and end apart: 9, of which 4 were waited for; matrix products, arithmetic and copies ran while one was open for 0% of the time, Pallas kernels for 23%

profile of v24, /device:TPU:0, one launch (start us, length us, event | category | flops | bytes accessed | tf_op | source)
XLA Modules:
  0.0 26.5 jit_solution(2555846467874831640)
XLA Ops:
  0.6 0.9 %convert_element_type.12.own.refs_0_ = bf16[160,128]{1,0:T(8,128)(2,1)S(1)} convert(f32[160,128]{1,0:T(8,128)} %refs_7_.1) | non-fusion elementwise | flops 20480 | bytes 122880 | tf_op jit(solution)/shard_map/convert_element_type | solution.py:410
  1.5 0.5 %collective-permute-start = (bf16[160,128]{1,0:T(8,128)(2,1)S(1)}, bf16[160,128]{1,0:T(8,128)(2,1)S(1)}, u32[]{:S(2)}, u32[]{:S(2)}) collective-permute-start(bf16[160,128]{1,0:T(8,128)(2,1)S(1)} %convert_element_type.12.own.refs_0_), channel_id=1, source_target_pairs={{0,1},{1,0},{2,3},{3,2},{4,5},{5,4},{6,7},{7,6},{8,9},{9,8},{10,11... | collective-permute-start | bytes 122888 | tf_op jit(solution)/shard_map/ppermute | solution.py:330
  2.0 2.6 %collective-permute-start.2 = (bf16[160,128]{1,0:T(8,128)(2,1)S(1)}, bf16[160,128]{1,0:T(8,128)(2,1)S(1)}, u32[]{:S(2)}, u32[]{:S(2)}) collective-permute-start(bf16[160,128]{1,0:T(8,128)(2,1)S(1)} %convert_element_type.12.own.refs_0_), channel_id=1, source_target_pairs={{0,3},{1,2},{2,1},{3,0},{4,7},{5,6},{6,5},{7,4},{8,11},{9,10},{10,... | collective-permute-start | bytes 122888 | tf_op jit(solution)/shard_map/ppermute | solution.py:330
  4.6 0.1 collective-permute-start.1
  4.6 2.3 %prepare.1 = (bf16[3072,640]{1,0:T(8,128)(2,1)S(1)}, bf16[3072,128]{1,0:T(8,128)(2,1)S(1)}, bf16[128,3072]{1,0:T(8,128)(2,1)S(1)}, f32[1,640]{1,0:T(1,128)S(1)}, f32[640,128]{1,0:T(8,128)S(1)}) custom-call(bf16[3072,640]{1,0:T(8,128)(2,1)} %x_in.1, s32[3072]{0:T(1024)} %index_in.1, bf16[512,128]{1,0:T(8,128)(2,1)} %cell_in.1, f32[640]{0:T(1024)} %scale_in.1), custom_call_target="tpu_custom_call" | custom-call | flops 402653184 | bytes 7864320 | tf_op jit(solution)/shard_map/prepare/pallas_call | solution.py:74
  6.9 0.0 collective-permute-done.other.refs_1_
  6.9 0.6 %early_part.1 = (f32[768,128]{1,0:T(8,128)S(1)}, f32[128,256]{1,0:T(8,128)S(1)}, bf16[128,256]{1,0:T(8,128)(2,1)S(1)}, bf16[256,128]{1,0:T(8,128)(2,1)S(1)}) custom-call(bf16[3072,640]{1,0:T(8,128)(2,1)S(1)} %get-tuple-element.29.x_ref.refs_0_, bf16[3072,128]{1,0:T(8,128)(2,1)S(1)} %get-tuple-element.30.f_ref.refs_1_, ...), custom_call_target="tpu_custom_call" | custom-call | flops 301989888 | bytes 786432 | tf_op jit(solution)/shard_map/early_part/pallas_call | solution.py:296
  7.6 1.0 %collective-permute-done.1.refs_2_ = bf16[160,128]{1,0:T(8,128)(2,1)S(1)} collective-permute-done((bf16[160,128]{1,0:T(8,128)(2,1)S(1)}, bf16[160,128]{1,0:T(8,128)(2,1)S(1)}, u32[]{:S(2)}, u32[]{:S(2)}) %collective-permute-start.1) | collective-permute-done | bytes 40992 | tf_op jit(solution)/shard_map/ppermute | solution.py:330
  8.6 0.9 %rest_part.1 = (bf16[768,128]{1,0:T(8,128)(2,1)S(1)}, f32[128,640]{1,0:T(8,128)S(1)}, bf16[128,640]{1,0:T(8,128)(2,1)S(1)}, bf16[640,128]{1,0:T(8,128)(2,1)S(1)}) custom-call(bf16[3072,640]{1,0:T(8,128)(2,1)S(1)} %get-tuple-element.29.x_ref.refs_0_, bf16[3072,128]{1,0:T(8,128)(2,1)S(1)} %get-tuple-element.30.f_ref.refs_1_, ...), custom_call_target="tpu_custom_call" | custom-call | flops 452984832 | bytes 1179648 | tf_op jit(solution)/shard_map/rest_part/pallas_call | solution.py:311
  9.5 2.6 %collective-permute-start.3 = (bf16[768,128]{1,0:T(8,128)(2,1)S(1)}, bf16[768,128]{1,0:T(8,128)(2,1)S(1)}, u32[]{:S(2)}, u32[]{:S(2)}) collective-permute-start(bf16[768,128]{1,0:T(8,128)(2,1)S(1)} %get-tuple-element.44), channel_id=1, source_target_pairs={{0,8},{4,0},{8,12},{12,4},{1,9},{5,1},{9,13},{13,5},{2,10},{6,2},{... | collective-permute-start | bytes 589832 | tf_op jit(solution)/shard_map/ppermute | solution.py:441
  12.1 1.1 %block_rows.2 = (bf16[768,128]{1,0:T(8,128)(2,1)S(1)}, f32[128,640]{1,0:T(8,128)S(1)}) custom-call(bf16[3072,640]{1,0:T(8,128)(2,1)S(1)} %get-tuple-element.29.x_ref.refs_0_, bf16[3072,128]{1,0:T(8,128)(2,1)S(1)} %get-tuple-element.30.f_ref.refs_1_, bf16[128,3072]{1,0:T(8,128)(2,1)S(1)} %get-tuple-element.31.ft_ref.refs_2_, ...), custom_call_target="tpu_custom_call" | custom-call | flops 377487360 | bytes 983040 | tf_op jit(solution)/shard_map/block_rows/pallas_call | solution.py:195
  13.3 0.0 copy-start
  13.3 0.0 copy-start.1
  13.3 0.0 copy-start.2
  13.3 0.1 collective-permute-start.5
  13.4 2.0 %block_rows.3 = (bf16[768,128]{1,0:T(8,128)(2,1)S(1)}, f32[768,128]{1,0:T(8,128)S(1)}, f32[160,128]{1,0:T(8,128)S(1)}, bf16[160,128]{1,0:T(8,128)(2,1)S(1)}, bf1...) custom-call(bf16[3072,640]{1,0:T(8,128)(2,1)S(1)} %get-tuple-element.29.x_ref.refs_0_, ...), custom_call_target="tpu_custom_call" | custom-call | flops 754974720 | bytes 1966080 | tf_op jit(solution)/shard_map/block_rows/pallas_call | solution.py:195
  15.4 2.1 %collective-permute-done.3 = bf16[768,128]{1,0:T(8,128)(2,1)S(1)} collective-permute-done((bf16[768,128]{1,0:T(8,128)(2,1)S(1)}, bf16[768,128]{1,0:T(8,128)(2,1)S(1)}, u32[]{:S(2)}, u32[]{:S(2)}) %collective-permute-start.3) | collective-permute-done | bytes 196640 | tf_op jit(solution)/shard_map/ppermute | solution.py:441
  17.5 0.1 add_convert_fusion
  17.5 3.4 %collective-permute-start.4 = (bf16[768,128]{1,0:T(8,128)(2,1)S(1)}, bf16[768,128]{1,0:T(8,128)(2,1)S(1)}, u32[]{:S(2)}, u32[]{:S(2)}) collective-permute-start(bf16[768,128]{1,0:T(8,128)(2,1)S(1)} %add_convert_fusion), channel_id=1, source_target_pairs={{0,8},{4,0},{8,12},{12,4},{1,9},{5,1},{9,13},{13,5},{2,10},{6,2},{... | collective-permute-start | bytes 589832 | tf_op jit(solution)/shard_map/ppermute | solution.py:441
  21.0 0.9 %collective-permute-start.7 = (bf16[160,128]{1,0:T(8,128)(2,1)S(1)}, bf16[160,128]{1,0:T(8,128)(2,1)S(1)}, u32[]{:S(2)}, u32[]{:S(2)}) collective-permute-start(bf16[160,128]{1,0:T(8,128)(2,1)S(1)} %get-tuple-element.48), channel_id=1, source_target_pairs={{0,2},{1,3},{2,0},{3,1},{4,6},{5,7},{6,4},{7,5},{8,10},{9,11},{10,... | collective-permute-start | bytes 122888 | tf_op jit(solution)/shard_map/ppermute | solution.py:330
  21.9 0.9 %collective-permute-start.8 = (bf16[160,128]{1,0:T(8,128)(2,1)S(1)}, bf16[160,128]{1,0:T(8,128)(2,1)S(1)}, u32[]{:S(2)}, u32[]{:S(2)}) collective-permute-start(bf16[160,128]{1,0:T(8,128)(2,1)S(1)} %get-tuple-element.49), channel_id=1, source_target_pairs={{0,3},{1,2},{2,1},{3,0},{4,7},{5,6},{6,5},{7,4},{8,11},{9,10},{10,... | collective-permute-start | bytes 122888 | tf_op jit(solution)/shard_map/ppermute | solution.py:330
  22.8 2.3 %collective-permute-done.7.refs_5_ = bf16[160,128]{1,0:T(8,128)(2,1)S(1)} collective-permute-done((bf16[160,128]{1,0:T(8,128)(2,1)S(1)}, bf16[160,128]{1,0:T(8,128)(2,1)S(1)}, u32[]{:S(2)}, u32[]{:S(2)}) %collective-permute-start.7) | collective-permute-done | bytes 40992 | tf_op jit(solution)/shard_map/ppermute | solution.py:330
  25.1 0.4 %collective-permute-done.8.refs_6_ = bf16[160,128]{1,0:T(8,128)(2,1)S(1)} collective-permute-done((bf16[160,128]{1,0:T(8,128)(2,1)S(1)}, bf16[160,128]{1,0:T(8,128)(2,1)S(1)}, u32[]{:S(2)}, u32[]{:S(2)}) %collective-permute-start.8) | collective-permute-done | bytes 40992 | tf_op jit(solution)/shard_map/ppermute | solution.py:330
  25.6 0.9 %finish.1 = (f32[160,128]{1,0:T(8,128)}, f32[160,128]{1,0:T(8,128)}, f32[160,128]{1,0:T(8,128)}, f32[768,128]{1,0:T(8,128)}) custom-call(f32[768,128]{1,0:T(8,128)S(1)} %get-tuple-element.42.refs_0_, bf16[768,128]{1,0:T(8,128)(2,1)S(1)} %collective-permute-done.4.refs_1_, bf16[768,128]{1,0:T(8,128)(2,1)S(1)} %collective-permute-done.5.refs_2_, ...), custom_call_target="tpu_custom_call" | custom-call | flops 409600 | bytes 1753088 | tf_op jit(solution)/shard_map/finish/pallas_call | solution.py:392
  (8 shorter events, 0.0 us)
Async XLA Ops:
  1.5 5.4 %collective-permute-start = (bf16[160,128]{1,0:T(8,128)(2,1)S(1)}, bf16[160,128]{1,0:T(8,128)(2,1)S(1)}, u32[]{:S(2)}, u32[]{:S(2)}) collective-permute-start(bf16[160,128]{1,0:T(8,128)(2,1)S(1)} %convert_element_type.12.own.refs_0_), channel_id=1, source_target_pairs={{0,1},{1,0},{2,3},{3,2},{4,5},{5,4},{6,7},{7,6},{8,9},{9,8},{10,11... | collective-permute-start | bytes 122888 | tf_op jit(solution)/shard_map/ppermute | solution.py:330
  2.0 5.6 %collective-permute-start.2 = (bf16[160,128]{1,0:T(8,128)(2,1)S(1)}, bf16[160,128]{1,0:T(8,128)(2,1)S(1)}, u32[]{:S(2)}, u32[]{:S(2)}) collective-permute-start(bf16[160,128]{1,0:T(8,128)(2,1)S(1)} %convert_element_type.12.own.refs_0_), channel_id=1, source_target_pairs={{0,3},{1,2},{2,1},{3,0},{4,7},{5,6},{6,5},{7,4},{8,11},{9,10},{10,... | collective-permute-start | bytes 122888 | tf_op jit(solution)/shard_map/ppermute | solution.py:330
  4.6 4.0 %collective-permute-start.1 = (bf16[160,128]{1,0:T(8,128)(2,1)S(1)}, bf16[160,128]{1,0:T(8,128)(2,1)S(1)}, u32[]{:S(2)}, u32[]{:S(2)}) collective-permute-start(bf16[160,128]{1,0:T(8,128)(2,1)S(1)} %convert_element_type.12.own.refs_0_), channel_id=1, source_target_pairs={{0,2},{1,3},{2,0},{3,1},{4,6},{5,7},{6,4},{7,5},{8,10},{9,11},{10,... | collective-permute-start | bytes 122888 | tf_op jit(solution)/shard_map/ppermute | solution.py:330
  9.5 8.0 %collective-permute-start.3 = (bf16[768,128]{1,0:T(8,128)(2,1)S(1)}, bf16[768,128]{1,0:T(8,128)(2,1)S(1)}, u32[]{:S(2)}, u32[]{:S(2)}) collective-permute-start(bf16[768,128]{1,0:T(8,128)(2,1)S(1)} %get-tuple-element.44), channel_id=1, source_target_pairs={{0,8},{4,0},{8,12},{12,4},{1,9},{5,1},{9,13},{13,5},{2,10},{6,2},{... | collective-permute-start | bytes 589832 | tf_op jit(solution)/shard_map/ppermute | solution.py:441
  13.3 12.3 %copy-start = (f32[160,128]{1,0:T(8,128)S(1)}, f32[160,128]{1,0:T(8,128)}, u32[]{:S(2)}) copy-start(f32[160,128]{1,0:T(8,128)} %refs_7_.1) | copy-start | bytes 245764
  13.3 12.3 %copy-start.1 = (f32[160,128]{1,0:T(8,128)S(1)}, f32[160,128]{1,0:T(8,128)}, u32[]{:S(2)}) copy-start(f32[160,128]{1,0:T(8,128)} %refs_8_.1) | copy-start | bytes 245764
  13.3 12.3 %copy-start.2 = (f32[160,128]{1,0:T(8,128)S(1)}, f32[160,128]{1,0:T(8,128)}, u32[]{:S(2)}) copy-start(f32[160,128]{1,0:T(8,128)} %refs_9_.1) | copy-start | bytes 245764
  13.3 12.2 %collective-permute-start.5 = (bf16[768,128]{1,0:T(8,128)(2,1)S(1)}, bf16[768,128]{1,0:T(8,128)(2,1)S(1)}, u32[]{:S(2)}, u32[]{:S(2)}) collective-permute-start(bf16[768,128]{1,0:T(8,128)(2,1)S(1)} %get-tuple-element.45), channel_id=1, source_target_pairs={{0,4},{4,12},{8,0},{12,8},{1,5},{5,13},{9,1},{13,9},{2,6},{6,14},{... | collective-permute-start | bytes 589832 | tf_op jit(solution)/shard_map/ppermute | solution.py:441
  17.5 8.0 %collective-permute-start.4 = (bf16[768,128]{1,0:T(8,128)(2,1)S(1)}, bf16[768,128]{1,0:T(8,128)(2,1)S(1)}, u32[]{:S(2)}, u32[]{:S(2)}) collective-permute-start(bf16[768,128]{1,0:T(8,128)(2,1)S(1)} %add_convert_fusion), channel_id=1, source_target_pairs={{0,8},{4,0},{8,12},{12,4},{1,9},{5,1},{9,13},{13,5},{2,10},{6,2},{... | collective-permute-start | bytes 589832 | tf_op jit(solution)/shard_map/ppermute | solution.py:441
  21.0 1.9 %collective-permute-start.6 = (bf16[160,128]{1,0:T(8,128)(2,1)S(1)}, bf16[160,128]{1,0:T(8,128)(2,1)S(1)}, u32[]{:S(2)}, u32[]{:S(2)}) collective-permute-start(bf16[160,128]{1,0:T(8,128)(2,1)S(1)} %get-tuple-element.47), channel_id=1, source_target_pairs={{0,1},{1,0},{2,3},{3,2},{4,5},{5,4},{6,7},{7,6},{8,9},{9,8},{10,11... | collective-permute-start | bytes 122888 | tf_op jit(solution)/shard_map/ppermute | solution.py:330
  21.0 4.2 %collective-permute-start.7 = (bf16[160,128]{1,0:T(8,128)(2,1)S(1)}, bf16[160,128]{1,0:T(8,128)(2,1)S(1)}, u32[]{:S(2)}, u32[]{:S(2)}) collective-permute-start(bf16[160,128]{1,0:T(8,128)(2,1)S(1)} %get-tuple-element.48), channel_id=1, source_target_pairs={{0,2},{1,3},{2,0},{3,1},{4,6},{5,7},{6,4},{7,5},{8,10},{9,11},{10,... | collective-permute-start | bytes 122888 | tf_op jit(solution)/shard_map/ppermute | solution.py:330
  21.9 3.6 %collective-permute-start.8 = (bf16[160,128]{1,0:T(8,128)(2,1)S(1)}, bf16[160,128]{1,0:T(8,128)(2,1)S(1)}, u32[]{:S(2)}, u32[]{:S(2)}) collective-permute-start(bf16[160,128]{1,0:T(8,128)(2,1)S(1)} %get-tuple-element.49), channel_id=1, source_target_pairs={{0,3},{1,2},{2,1},{3,0},{4,7},{5,6},{6,5},{7,4},{8,11},{9,10},{10,... | collective-permute-start | bytes 122888 | tf_op jit(solution)/shard_map/ppermute | solution.py:330

commit v25 on v24

--- a/solution.py
+++ b/solution.py
@@ -232,13 +232,21 @@
     origin = pick("gene", table) * block
     tiles = [pl.ds(pl.multiple_of(origin + at, math.gcd(block, step)), step) for at in range(0, block, step)]
     bend = bend_ref[:, here]
-    preds = [jnp.dot(f_ref[tile, :], wide, preferred_element_type=jnp.float32) for tile in tiles]
-    infls = [influence(x_ref[tile, here], pred, bend) for tile, pred in zip(tiles, preds)]
+    predict = lambda tile: jnp.dot(f_ref[tile, :], wide, preferred_element_type=jnp.float32)
     rows, total = [], None
-    for tile, infl in zip(tiles, infls):
-        cols = jnp.dot(ft_ref[:, tile], infl, preferred_element_type=jnp.float32)
-        rows.append(jnp.dot(infl, scaled, preferred_element_type=jnp.float32))
-        total = cols if total is None else total + cols
+    pred, behind = predict(tiles[0]), None
+    for at, tile in enumerate([*tiles, None]):
+        now = None
+        if tile is not None:
+            later = predict(tiles[at + 1]) if at + 1 < len(tiles) else None
+            now = tile, influence(x_ref[tile, here], pred, bend)
+            pred = later
+        if behind is not None:
+            last, infl = behind
+            cols = jnp.dot(ft_ref[:, last], infl, preferred_element_type=jnp.float32)
+            rows.append(jnp.dot(infl, scaled, preferred_element_type=jnp.float32))
+            total = cols if total is None else total + cols
+        behind = now
     return rows, total
 
 

time: 26.6 us -> 26.6 us (level)
  no operation moved by 1% of the time
where the time goes in v25:
time: 26.6 us; the launch traced here: 26.5 us
  starting transfers between devices  11.1 us (42%)
  Pallas kernels  7.86 us (30%)
  waiting for transfers between devices  5.79 us (22%)
  other arithmetic  0.95 us (4%)
  between operations  0.74 us (3%)
    ppermute x3, starting transfers between devices, local(): came[way] = lax.ppermute(own, 'gene', list(enumerate(around(n_gene, way))))  6.14 us
    ppermute x6, starting transfers between devices, swap_row(): lax.ppermute(value, 'row', [(me, partner(me, hop, size)) for me in range(...  4.97 us
    ppermute x6, waiting for transfers between devices, swap_row(): lax.ppermute(value, 'row', [(me, partner(me, hop, size)) for me in range(...  3.7 us
    pallas_call x2, Pallas kernels, block_rows(): pl.pallas_call(functools.partial(rows_kernel, tables, block, first, last,...  3.16 us
    pallas_call x1, Pallas kernels, prepare(): pl.pallas_call(functools.partial(prepare_kernel, scale_k), out_shape=(VME...  2.26 us
    ppermute x3, waiting for transfers between devices, local(): came[way] = lax.ppermute(own, 'gene', list(enumerate(around(n_gene, way))))  2.09 us
    pallas_call x1, Pallas kernels, finish(): pl.pallas_call(functools.partial(finish_kernel, len(ends), len(parts)), o...  0.9 us
    convert_element_type x1, other arithmetic, local(): factor_bf = gene_factor.astype(jnp.bfloat16)  0.9 us
  transfers between devices with their start and end apart: 9, of which 4 were waited for; matrix products, arithmetic and copies ran while one was open for 0% of the time, Pallas kernels for 23%

profile of v25, /device:TPU:0, one launch (start us, length us, event | category | flops | bytes accessed | tf_op | source)
XLA Modules:
  0.0 26.5 jit_solution(10514250907767994312)
XLA Ops:
  0.6 0.9 %convert_element_type.12.own.refs_0_ = bf16[160,128]{1,0:T(8,128)(2,1)S(1)} convert(f32[160,128]{1,0:T(8,128)} %refs_7_.1) | non-fusion elementwise | flops 20480 | bytes 122880 | tf_op jit(solution)/shard_map/convert_element_type | solution.py:418
  1.5 0.5 %collective-permute-start = (bf16[160,128]{1,0:T(8,128)(2,1)S(1)}, bf16[160,128]{1,0:T(8,128)(2,1)S(1)}, u32[]{:S(2)}, u32[]{:S(2)}) collective-permute-start(bf16[160,128]{1,0:T(8,128)(2,1)S(1)} %convert_element_type.12.own.refs_0_), channel_id=1, source_target_pairs={{0,1},{1,0},{2,3},{3,2},{4,5},{5,4},{6,7},{7,6},{8,9},{9,8},{10,11... | collective-permute-start | bytes 122888 | tf_op jit(solution)/shard_map/ppermute | solution.py:338
  2.0 2.6 %collective-permute-start.2 = (bf16[160,128]{1,0:T(8,128)(2,1)S(1)}, bf16[160,128]{1,0:T(8,128)(2,1)S(1)}, u32[]{:S(2)}, u32[]{:S(2)}) collective-permute-start(bf16[160,128]{1,0:T(8,128)(2,1)S(1)} %convert_element_type.12.own.refs_0_), channel_id=1, source_target_pairs={{0,3},{1,2},{2,1},{3,0},{4,7},{5,6},{6,5},{7,4},{8,11},{9,10},{10,... | collective-permute-start | bytes 122888 | tf_op jit(solution)/shard_map/ppermute | solution.py:338
  4.6 0.1 collective-permute-start.1
  4.6 2.3 %prepare.1 = (bf16[3072,640]{1,0:T(8,128)(2,1)S(1)}, bf16[3072,128]{1,0:T(8,128)(2,1)S(1)}, bf16[128,3072]{1,0:T(8,128)(2,1)S(1)}, f32[1,640]{1,0:T(1,128)S(1)}, f32[640,128]{1,0:T(8,128)S(1)}) custom-call(bf16[3072,640]{1,0:T(8,128)(2,1)} %x_in.1, s32[3072]{0:T(1024)} %index_in.1, bf16[512,128]{1,0:T(8,128)(2,1)} %cell_in.1, f32[640]{0:T(1024)} %scale_in.1), custom_call_target="tpu_custom_call" | custom-call | flops 402653184 | bytes 7864320 | tf_op jit(solution)/shard_map/prepare/pallas_call | solution.py:74
  6.9 0.0 collective-permute-done.other.refs_1_
  6.9 0.6 %early_part.1 = (f32[768,128]{1,0:T(8,128)S(1)}, f32[128,256]{1,0:T(8,128)S(1)}, bf16[128,256]{1,0:T(8,128)(2,1)S(1)}, bf16[256,128]{1,0:T(8,128)(2,1)S(1)}) custom-call(bf16[3072,640]{1,0:T(8,128)(2,1)S(1)} %get-tuple-element.29.x_ref.refs_0_, bf16[3072,128]{1,0:T(8,128)(2,1)S(1)} %get-tuple-element.30.f_ref.refs_1_, ...), custom_call_target="tpu_custom_call" | custom-call | flops 301989888 | bytes 786432 | tf_op jit(solution)/shard_map/early_part/pallas_call | solution.py:304
  7.6 1.0 %collective-permute-done.1.refs_2_ = bf16[160,128]{1,0:T(8,128)(2,1)S(1)} collective-permute-done((bf16[160,128]{1,0:T(8,128)(2,1)S(1)}, bf16[160,128]{1,0:T(8,128)(2,1)S(1)}, u32[]{:S(2)}, u32[]{:S(2)}) %collective-permute-start.1) | collective-permute-done | bytes 40992 | tf_op jit(solution)/shard_map/ppermute | solution.py:338
  8.6 0.9 %rest_part.1 = (bf16[768,128]{1,0:T(8,128)(2,1)S(1)}, f32[128,640]{1,0:T(8,128)S(1)}, bf16[128,640]{1,0:T(8,128)(2,1)S(1)}, bf16[640,128]{1,0:T(8,128)(2,1)S(1)}) custom-call(bf16[3072,640]{1,0:T(8,128)(2,1)S(1)} %get-tuple-element.29.x_ref.refs_0_, bf16[3072,128]{1,0:T(8,128)(2,1)S(1)} %get-tuple-element.30.f_ref.refs_1_, ...), custom_call_target="tpu_custom_call" | custom-call | flops 452984832 | bytes 1179648 | tf_op jit(solution)/shard_map/rest_part/pallas_call | solution.py:319
  9.5 2.6 %collective-permute-start.3 = (bf16[768,128]{1,0:T(8,128)(2,1)S(1)}, bf16[768,128]{1,0:T(8,128)(2,1)S(1)}, u32[]{:S(2)}, u32[]{:S(2)}) collective-permute-start(bf16[768,128]{1,0:T(8,128)(2,1)S(1)} %get-tuple-element.44), channel_id=1, source_target_pairs={{0,8},{4,0},{8,12},{12,4},{1,9},{5,1},{9,13},{13,5},{2,10},{6,2},{... | collective-permute-start | bytes 589832 | tf_op jit(solution)/shard_map/ppermute | solution.py:449
  12.1 1.1 %block_rows.2 = (bf16[768,128]{1,0:T(8,128)(2,1)S(1)}, f32[128,640]{1,0:T(8,128)S(1)}) custom-call(bf16[3072,640]{1,0:T(8,128)(2,1)S(1)} %get-tuple-element.29.x_ref.refs_0_, bf16[3072,128]{1,0:T(8,128)(2,1)S(1)} %get-tuple-element.30.f_ref.refs_1_, bf16[128,3072]{1,0:T(8,128)(2,1)S(1)} %get-tuple-element.31.ft_ref.refs_2_, ...), custom_call_target="tpu_custom_call" | custom-call | flops 377487360 | bytes 983040 | tf_op jit(solution)/shard_map/block_rows/pallas_call | solution.py:195
  13.3 0.0 copy-start
  13.3 0.0 copy-start.1
  13.3 0.0 copy-start.2
  13.3 0.1 collective-permute-start.5
  13.4 2.0 %block_rows.3 = (bf16[768,128]{1,0:T(8,128)(2,1)S(1)}, f32[768,128]{1,0:T(8,128)S(1)}, f32[160,128]{1,0:T(8,128)S(1)}, bf16[160,128]{1,0:T(8,128)(2,1)S(1)}, bf1...) custom-call(bf16[3072,640]{1,0:T(8,128)(2,1)S(1)} %get-tuple-element.29.x_ref.refs_0_, ...), custom_call_target="tpu_custom_call" | custom-call | flops 754974720 | bytes 1966080 | tf_op jit(solution)/shard_map/block_rows/pallas_call | solution.py:195
  15.4 2.1 %collective-permute-done.3 = bf16[768,128]{1,0:T(8,128)(2,1)S(1)} collective-permute-done((bf16[768,128]{1,0:T(8,128)(2,1)S(1)}, bf16[768,128]{1,0:T(8,128)(2,1)S(1)}, u32[]{:S(2)}, u32[]{:S(2)}) %collective-permute-start.3) | collective-permute-done | bytes 196640 | tf_op jit(solution)/shard_map/ppermute | solution.py:449
  17.5 0.1 add_convert_fusion
  17.5 3.4 %collective-permute-start.4 = (bf16[768,128]{1,0:T(8,128)(2,1)S(1)}, bf16[768,128]{1,0:T(8,128)(2,1)S(1)}, u32[]{:S(2)}, u32[]{:S(2)}) collective-permute-start(bf16[768,128]{1,0:T(8,128)(2,1)S(1)} %add_convert_fusion), channel_id=1, source_target_pairs={{0,8},{4,0},{8,12},{12,4},{1,9},{5,1},{9,13},{13,5},{2,10},{6,2},{... | collective-permute-start | bytes 589832 | tf_op jit(solution)/shard_map/ppermute | solution.py:449
  21.0 0.9 %collective-permute-start.7 = (bf16[160,128]{1,0:T(8,128)(2,1)S(1)}, bf16[160,128]{1,0:T(8,128)(2,1)S(1)}, u32[]{:S(2)}, u32[]{:S(2)}) collective-permute-start(bf16[160,128]{1,0:T(8,128)(2,1)S(1)} %get-tuple-element.48), channel_id=1, source_target_pairs={{0,2},{1,3},{2,0},{3,1},{4,6},{5,7},{6,4},{7,5},{8,10},{9,11},{10,... | collective-permute-start | bytes 122888 | tf_op jit(solution)/shard_map/ppermute | solution.py:338
  21.9 0.9 %collective-permute-start.8 = (bf16[160,128]{1,0:T(8,128)(2,1)S(1)}, bf16[160,128]{1,0:T(8,128)(2,1)S(1)}, u32[]{:S(2)}, u32[]{:S(2)}) collective-permute-start(bf16[160,128]{1,0:T(8,128)(2,1)S(1)} %get-tuple-element.49), channel_id=1, source_target_pairs={{0,3},{1,2},{2,1},{3,0},{4,7},{5,6},{6,5},{7,4},{8,11},{9,10},{10,... | collective-permute-start | bytes 122888 | tf_op jit(solution)/shard_map/ppermute | solution.py:338
  22.8 2.3 %collective-permute-done.7.refs_5_ = bf16[160,128]{1,0:T(8,128)(2,1)S(1)} collective-permute-done((bf16[160,128]{1,0:T(8,128)(2,1)S(1)}, bf16[160,128]{1,0:T(8,128)(2,1)S(1)}, u32[]{:S(2)}, u32[]{:S(2)}) %collective-permute-start.7) | collective-permute-done | bytes 40992 | tf_op jit(solution)/shard_map/ppermute | solution.py:338
  25.1 0.4 %collective-permute-done.8.refs_6_ = bf16[160,128]{1,0:T(8,128)(2,1)S(1)} collective-permute-done((bf16[160,128]{1,0:T(8,128)(2,1)S(1)}, bf16[160,128]{1,0:T(8,128)(2,1)S(1)}, u32[]{:S(2)}, u32[]{:S(2)}) %collective-permute-start.8) | collective-permute-done | bytes 40992 | tf_op jit(solution)/shard_map/ppermute | solution.py:338
  25.6 0.9 %finish.1 = (f32[160,128]{1,0:T(8,128)}, f32[160,128]{1,0:T(8,128)}, f32[160,128]{1,0:T(8,128)}, f32[768,128]{1,0:T(8,128)}) custom-call(f32[768,128]{1,0:T(8,128)S(1)} %get-tuple-element.42.refs_0_, bf16[768,128]{1,0:T(8,128)(2,1)S(1)} %collective-permute-done.4.refs_1_, bf16[768,128]{1,0:T(8,128)(2,1)S(1)} %collective-permute-done.5.refs_2_, ...), custom_call_target="tpu_custom_call" | custom-call | flops 409600 | bytes 1753088 | tf_op jit(solution)/shard_map/finish/pallas_call | solution.py:400
  (8 shorter events, 0.0 us)
Async XLA Ops:
  1.5 5.4 %collective-permute-start = (bf16[160,128]{1,0:T(8,128)(2,1)S(1)}, bf16[160,128]{1,0:T(8,128)(2,1)S(1)}, u32[]{:S(2)}, u32[]{:S(2)}) collective-permute-start(bf16[160,128]{1,0:T(8,128)(2,1)S(1)} %convert_element_type.12.own.refs_0_), channel_id=1, source_target_pairs={{0,1},{1,0},{2,3},{3,2},{4,5},{5,4},{6,7},{7,6},{8,9},{9,8},{10,11... | collective-permute-start | bytes 122888 | tf_op jit(solution)/shard_map/ppermute | solution.py:338
  2.0 5.6 %collective-permute-start.2 = (bf16[160,128]{1,0:T(8,128)(2,1)S(1)}, bf16[160,128]{1,0:T(8,128)(2,1)S(1)}, u32[]{:S(2)}, u32[]{:S(2)}) collective-permute-start(bf16[160,128]{1,0:T(8,128)(2,1)S(1)} %convert_element_type.12.own.refs_0_), channel_id=1, source_target_pairs={{0,3},{1,2},{2,1},{3,0},{4,7},{5,6},{6,5},{7,4},{8,11},{9,10},{10,... | collective-permute-start | bytes 122888 | tf_op jit(solution)/shard_map/ppermute | solution.py:338
  4.6 4.0 %collective-permute-start.1 = (bf16[160,128]{1,0:T(8,128)(2,1)S(1)}, bf16[160,128]{1,0:T(8,128)(2,1)S(1)}, u32[]{:S(2)}, u32[]{:S(2)}) collective-permute-start(bf16[160,128]{1,0:T(8,128)(2,1)S(1)} %convert_element_type.12.own.refs_0_), channel_id=1, source_target_pairs={{0,2},{1,3},{2,0},{3,1},{4,6},{5,7},{6,4},{7,5},{8,10},{9,11},{10,... | collective-permute-start | bytes 122888 | tf_op jit(solution)/shard_map/ppermute | solution.py:338
  9.5 8.0 %collective-permute-start.3 = (bf16[768,128]{1,0:T(8,128)(2,1)S(1)}, bf16[768,128]{1,0:T(8,128)(2,1)S(1)}, u32[]{:S(2)}, u32[]{:S(2)}) collective-permute-start(bf16[768,128]{1,0:T(8,128)(2,1)S(1)} %get-tuple-element.44), channel_id=1, source_target_pairs={{0,8},{4,0},{8,12},{12,4},{1,9},{5,1},{9,13},{13,5},{2,10},{6,2},{... | collective-permute-start | bytes 589832 | tf_op jit(solution)/shard_map/ppermute | solution.py:449
  13.3 12.3 %copy-start = (f32[160,128]{1,0:T(8,128)S(1)}, f32[160,128]{1,0:T(8,128)}, u32[]{:S(2)}) copy-start(f32[160,128]{1,0:T(8,128)} %refs_7_.1) | copy-start | bytes 245764
  13.3 12.3 %copy-start.1 = (f32[160,128]{1,0:T(8,128)S(1)}, f32[160,128]{1,0:T(8,128)}, u32[]{:S(2)}) copy-start(f32[160,128]{1,0:T(8,128)} %refs_8_.1) | copy-start | bytes 245764
  13.3 12.3 %copy-start.2 = (f32[160,128]{1,0:T(8,128)S(1)}, f32[160,128]{1,0:T(8,128)}, u32[]{:S(2)}) copy-start(f32[160,128]{1,0:T(8,128)} %refs_9_.1) | copy-start | bytes 245764
  13.3 12.2 %collective-permute-start.5 = (bf16[768,128]{1,0:T(8,128)(2,1)S(1)}, bf16[768,128]{1,0:T(8,128)(2,1)S(1)}, u32[]{:S(2)}, u32[]{:S(2)}) collective-permute-start(bf16[768,128]{1,0:T(8,128)(2,1)S(1)} %get-tuple-element.45), channel_id=1, source_target_pairs={{0,4},{4,12},{8,0},{12,8},{1,5},{5,13},{9,1},{13,9},{2,6},{6,14},{... | collective-permute-start | bytes 589832 | tf_op jit(solution)/shard_map/ppermute | solution.py:449
  17.5 8.0 %collective-permute-start.4 = (bf16[768,128]{1,0:T(8,128)(2,1)S(1)}, bf16[768,128]{1,0:T(8,128)(2,1)S(1)}, u32[]{:S(2)}, u32[]{:S(2)}) collective-permute-start(bf16[768,128]{1,0:T(8,128)(2,1)S(1)} %add_convert_fusion), channel_id=1, source_target_pairs={{0,8},{4,0},{8,12},{12,4},{1,9},{5,1},{9,13},{13,5},{2,10},{6,2},{... | collective-permute-start | bytes 589832 | tf_op jit(solution)/shard_map/ppermute | solution.py:449
  21.0 1.9 %collective-permute-start.6 = (bf16[160,128]{1,0:T(8,128)(2,1)S(1)}, bf16[160,128]{1,0:T(8,128)(2,1)S(1)}, u32[]{:S(2)}, u32[]{:S(2)}) collective-permute-start(bf16[160,128]{1,0:T(8,128)(2,1)S(1)} %get-tuple-element.47), channel_id=1, source_target_pairs={{0,1},{1,0},{2,3},{3,2},{4,5},{5,4},{6,7},{7,6},{8,9},{9,8},{10,11... | collective-permute-start | bytes 122888 | tf_op jit(solution)/shard_map/ppermute | solution.py:338
  21.0 4.2 %collective-permute-start.7 = (bf16[160,128]{1,0:T(8,128)(2,1)S(1)}, bf16[160,128]{1,0:T(8,128)(2,1)S(1)}, u32[]{:S(2)}, u32[]{:S(2)}) collective-permute-start(bf16[160,128]{1,0:T(8,128)(2,1)S(1)} %get-tuple-element.48), channel_id=1, source_target_pairs={{0,2},{1,3},{2,0},{3,1},{4,6},{5,7},{6,4},{7,5},{8,10},{9,11},{10,... | collective-permute-start | bytes 122888 | tf_op jit(solution)/shard_map/ppermute | solution.py:338
  21.9 3.6 %collective-permute-start.8 = (bf16[160,128]{1,0:T(8,128)(2,1)S(1)}, bf16[160,128]{1,0:T(8,128)(2,1)S(1)}, u32[]{:S(2)}, u32[]{:S(2)}) collective-permute-start(bf16[160,128]{1,0:T(8,128)(2,1)S(1)} %get-tuple-element.49), channel_id=1, source_target_pairs={{0,3},{1,2},{2,1},{3,0},{4,7},{5,6},{6,5},{7,4},{8,11},{9,10},{10,... | collective-permute-start | bytes 122888 | tf_op jit(solution)/shard_map/ppermute | solution.py:338

commit v26 on v25

--- a/solution.py
+++ b/solution.py
@@ -56,7 +56,7 @@
     table = jnp.transpose(cell[...].astype(jnp.float32)).astype(jnp.bfloat16)
     base = lax.axis_index("row") * cells
     loads[2].wait()
-    step = tile_of(rows, 512)
+    step = tile_of(rows, 256)
     for at in range(0, rows, step):
         local = index[at : at + step].reshape(1, step) - base
         hot = lax.broadcasted_iota(jnp.int32, (cells, step), 0) == local

time: 26.6 us -> 26.6 us (level)
  no operation moved by 1% of the time
where the time goes in v26:
time: 26.6 us; the launch traced here: 26.5 us
  starting transfers between devices  11.1 us (42%)
  Pallas kernels  7.86 us (30%)
  waiting for transfers between devices  5.79 us (22%)
  other arithmetic  0.95 us (4%)
  between operations  0.74 us (3%)
    ppermute x3, starting transfers between devices, local(): came[way] = lax.ppermute(own, 'gene', list(enumerate(around(n_gene, way))))  6.14 us
    ppermute x6, starting transfers between devices, swap_row(): lax.ppermute(value, 'row', [(me, partner(me, hop, size)) for me in range(...  4.97 us
    ppermute x6, waiting for transfers between devices, swap_row(): lax.ppermute(value, 'row', [(me, partner(me, hop, size)) for me in range(...  3.7 us
    pallas_call x2, Pallas kernels, block_rows(): pl.pallas_call(functools.partial(rows_kernel, tables, block, first, last,...  3.16 us
    pallas_call x1, Pallas kernels, prepare(): pl.pallas_call(functools.partial(prepare_kernel, scale_k), out_shape=(VME...  2.26 us
    ppermute x3, waiting for transfers between devices, local(): came[way] = lax.ppermute(own, 'gene', list(enumerate(around(n_gene, way))))  2.09 us
    pallas_call x1, Pallas kernels, finish(): pl.pallas_call(functools.partial(finish_kernel, len(ends), len(parts)), o...  0.9 us
    convert_element_type x1, other arithmetic, local(): factor_bf = gene_factor.astype(jnp.bfloat16)  0.9 us
  transfers between devices with their start and end apart: 9, of which 4 were waited for; matrix products, arithmetic and copies ran while one was open for 0% of the time, Pallas kernels for 23%

profile of v26, /device:TPU:0, one launch (start us, length us, event | category | flops | bytes accessed | tf_op | source)
XLA Modules:
  0.0 26.5 jit_solution(7617167582558958703)
XLA Ops:
  0.6 0.9 %convert_element_type.12.own.refs_0_ = bf16[160,128]{1,0:T(8,128)(2,1)S(1)} convert(f32[160,128]{1,0:T(8,128)} %refs_7_.1) | non-fusion elementwise | flops 20480 | bytes 122880 | tf_op jit(solution)/shard_map/convert_element_type | solution.py:418
  1.5 0.5 %collective-permute-start = (bf16[160,128]{1,0:T(8,128)(2,1)S(1)}, bf16[160,128]{1,0:T(8,128)(2,1)S(1)}, u32[]{:S(2)}, u32[]{:S(2)}) collective-permute-start(bf16[160,128]{1,0:T(8,128)(2,1)S(1)} %convert_element_type.12.own.refs_0_), channel_id=1, source_target_pairs={{0,1},{1,0},{2,3},{3,2},{4,5},{5,4},{6,7},{7,6},{8,9},{9,8},{10,11... | collective-permute-start | bytes 122888 | tf_op jit(solution)/shard_map/ppermute | solution.py:338
  2.0 2.6 %collective-permute-start.2 = (bf16[160,128]{1,0:T(8,128)(2,1)S(1)}, bf16[160,128]{1,0:T(8,128)(2,1)S(1)}, u32[]{:S(2)}, u32[]{:S(2)}) collective-permute-start(bf16[160,128]{1,0:T(8,128)(2,1)S(1)} %convert_element_type.12.own.refs_0_), channel_id=1, source_target_pairs={{0,3},{1,2},{2,1},{3,0},{4,7},{5,6},{6,5},{7,4},{8,11},{9,10},{10,... | collective-permute-start | bytes 122888 | tf_op jit(solution)/shard_map/ppermute | solution.py:338
  4.6 0.1 collective-permute-start.1
  4.6 2.3 %prepare.1 = (bf16[3072,640]{1,0:T(8,128)(2,1)S(1)}, bf16[3072,128]{1,0:T(8,128)(2,1)S(1)}, bf16[128,3072]{1,0:T(8,128)(2,1)S(1)}, f32[1,640]{1,0:T(1,128)S(1)}, f32[640,128]{1,0:T(8,128)S(1)}) custom-call(bf16[3072,640]{1,0:T(8,128)(2,1)} %x_in.1, s32[3072]{0:T(1024)} %index_in.1, bf16[512,128]{1,0:T(8,128)(2,1)} %cell_in.1, f32[640]{0:T(1024)} %scale_in.1), custom_call_target="tpu_custom_call" | custom-call | flops 402653184 | bytes 7864320 | tf_op jit(solution)/shard_map/prepare/pallas_call | solution.py:74
  6.9 0.0 collective-permute-done.other.refs_1_
  6.9 0.6 %early_part.1 = (f32[768,128]{1,0:T(8,128)S(1)}, f32[128,256]{1,0:T(8,128)S(1)}, bf16[128,256]{1,0:T(8,128)(2,1)S(1)}, bf16[256,128]{1,0:T(8,128)(2,1)S(1)}) custom-call(bf16[3072,640]{1,0:T(8,128)(2,1)S(1)} %get-tuple-element.29.x_ref.refs_0_, bf16[3072,128]{1,0:T(8,128)(2,1)S(1)} %get-tuple-element.30.f_ref.refs_1_, ...), custom_call_target="tpu_custom_call" | custom-call | flops 301989888 | bytes 786432 | tf_op jit(solution)/shard_map/early_part/pallas_call | solution.py:304
  7.6 1.0 %collective-permute-done.1.refs_2_ = bf16[160,128]{1,0:T(8,128)(2,1)S(1)} collective-permute-done((bf16[160,128]{1,0:T(8,128)(2,1)S(1)}, bf16[160,128]{1,0:T(8,128)(2,1)S(1)}, u32[]{:S(2)}, u32[]{:S(2)}) %collective-permute-start.1) | collective-permute-done | bytes 40992 | tf_op jit(solution)/shard_map/ppermute | solution.py:338
  8.6 0.9 %rest_part.1 = (bf16[768,128]{1,0:T(8,128)(2,1)S(1)}, f32[128,640]{1,0:T(8,128)S(1)}, bf16[128,640]{1,0:T(8,128)(2,1)S(1)}, bf16[640,128]{1,0:T(8,128)(2,1)S(1)}) custom-call(bf16[3072,640]{1,0:T(8,128)(2,1)S(1)} %get-tuple-element.29.x_ref.refs_0_, bf16[3072,128]{1,0:T(8,128)(2,1)S(1)} %get-tuple-element.30.f_ref.refs_1_, ...), custom_call_target="tpu_custom_call" | custom-call | flops 452984832 | bytes 1179648 | tf_op jit(solution)/shard_map/rest_part/pallas_call | solution.py:319
  9.5 2.6 %collective-permute-start.3 = (bf16[768,128]{1,0:T(8,128)(2,1)S(1)}, bf16[768,128]{1,0:T(8,128)(2,1)S(1)}, u32[]{:S(2)}, u32[]{:S(2)}) collective-permute-start(bf16[768,128]{1,0:T(8,128)(2,1)S(1)} %get-tuple-element.44), channel_id=1, source_target_pairs={{0,8},{4,0},{8,12},{12,4},{1,9},{5,1},{9,13},{13,5},{2,10},{6,2},{... | collective-permute-start | bytes 589832 | tf_op jit(solution)/shard_map/ppermute | solution.py:449
  12.1 1.1 %block_rows.2 = (bf16[768,128]{1,0:T(8,128)(2,1)S(1)}, f32[128,640]{1,0:T(8,128)S(1)}) custom-call(bf16[3072,640]{1,0:T(8,128)(2,1)S(1)} %get-tuple-element.29.x_ref.refs_0_, bf16[3072,128]{1,0:T(8,128)(2,1)S(1)} %get-tuple-element.30.f_ref.refs_1_, bf16[128,3072]{1,0:T(8,128)(2,1)S(1)} %get-tuple-element.31.ft_ref.refs_2_, ...), custom_call_target="tpu_custom_call" | custom-call | flops 377487360 | bytes 983040 | tf_op jit(solution)/shard_map/block_rows/pallas_call | solution.py:195
  13.3 0.0 copy-start
  13.3 0.0 copy-start.1
  13.3 0.0 copy-start.2
  13.3 0.1 collective-permute-start.5
  13.4 2.0 %block_rows.3 = (bf16[768,128]{1,0:T(8,128)(2,1)S(1)}, f32[768,128]{1,0:T(8,128)S(1)}, f32[160,128]{1,0:T(8,128)S(1)}, bf16[160,128]{1,0:T(8,128)(2,1)S(1)}, bf1...) custom-call(bf16[3072,640]{1,0:T(8,128)(2,1)S(1)} %get-tuple-element.29.x_ref.refs_0_, ...), custom_call_target="tpu_custom_call" | custom-call | flops 754974720 | bytes 1966080 | tf_op jit(solution)/shard_map/block_rows/pallas_call | solution.py:195
  15.4 2.1 %collective-permute-done.3 = bf16[768,128]{1,0:T(8,128)(2,1)S(1)} collective-permute-done((bf16[768,128]{1,0:T(8,128)(2,1)S(1)}, bf16[768,128]{1,0:T(8,128)(2,1)S(1)}, u32[]{:S(2)}, u32[]{:S(2)}) %collective-permute-start.3) | collective-permute-done | bytes 196640 | tf_op jit(solution)/shard_map/ppermute | solution.py:449
  17.5 0.1 add_convert_fusion
  17.5 3.4 %collective-permute-start.4 = (bf16[768,128]{1,0:T(8,128)(2,1)S(1)}, bf16[768,128]{1,0:T(8,128)(2,1)S(1)}, u32[]{:S(2)}, u32[]{:S(2)}) collective-permute-start(bf16[768,128]{1,0:T(8,128)(2,1)S(1)} %add_convert_fusion), channel_id=1, source_target_pairs={{0,8},{4,0},{8,12},{12,4},{1,9},{5,1},{9,13},{13,5},{2,10},{6,2},{... | collective-permute-start | bytes 589832 | tf_op jit(solution)/shard_map/ppermute | solution.py:449
  21.0 0.9 %collective-permute-start.7 = (bf16[160,128]{1,0:T(8,128)(2,1)S(1)}, bf16[160,128]{1,0:T(8,128)(2,1)S(1)}, u32[]{:S(2)}, u32[]{:S(2)}) collective-permute-start(bf16[160,128]{1,0:T(8,128)(2,1)S(1)} %get-tuple-element.48), channel_id=1, source_target_pairs={{0,2},{1,3},{2,0},{3,1},{4,6},{5,7},{6,4},{7,5},{8,10},{9,11},{10,... | collective-permute-start | bytes 122888 | tf_op jit(solution)/shard_map/ppermute | solution.py:338
  21.9 0.9 %collective-permute-start.8 = (bf16[160,128]{1,0:T(8,128)(2,1)S(1)}, bf16[160,128]{1,0:T(8,128)(2,1)S(1)}, u32[]{:S(2)}, u32[]{:S(2)}) collective-permute-start(bf16[160,128]{1,0:T(8,128)(2,1)S(1)} %get-tuple-element.49), channel_id=1, source_target_pairs={{0,3},{1,2},{2,1},{3,0},{4,7},{5,6},{6,5},{7,4},{8,11},{9,10},{10,... | collective-permute-start | bytes 122888 | tf_op jit(solution)/shard_map/ppermute | solution.py:338
  22.8 2.3 %collective-permute-done.7.refs_5_ = bf16[160,128]{1,0:T(8,128)(2,1)S(1)} collective-permute-done((bf16[160,128]{1,0:T(8,128)(2,1)S(1)}, bf16[160,128]{1,0:T(8,128)(2,1)S(1)}, u32[]{:S(2)}, u32[]{:S(2)}) %collective-permute-start.7) | collective-permute-done | bytes 40992 | tf_op jit(solution)/shard_map/ppermute | solution.py:338
  25.1 0.4 %collective-permute-done.8.refs_6_ = bf16[160,128]{1,0:T(8,128)(2,1)S(1)} collective-permute-done((bf16[160,128]{1,0:T(8,128)(2,1)S(1)}, bf16[160,128]{1,0:T(8,128)(2,1)S(1)}, u32[]{:S(2)}, u32[]{:S(2)}) %collective-permute-start.8) | collective-permute-done | bytes 40992 | tf_op jit(solution)/shard_map/ppermute | solution.py:338
  25.6 0.9 %finish.1 = (f32[160,128]{1,0:T(8,128)}, f32[160,128]{1,0:T(8,128)}, f32[160,128]{1,0:T(8,128)}, f32[768,128]{1,0:T(8,128)}) custom-call(f32[768,128]{1,0:T(8,128)S(1)} %get-tuple-element.42.refs_0_, bf16[768,128]{1,0:T(8,128)(2,1)S(1)} %collective-permute-done.4.refs_1_, bf16[768,128]{1,0:T(8,128)(2,1)S(1)} %collective-permute-done.5.refs_2_, ...), custom_call_target="tpu_custom_call" | custom-call | flops 409600 | bytes 1753088 | tf_op jit(solution)/shard_map/finish/pallas_call | solution.py:400
  (8 shorter events, 0.0 us)
Async XLA Ops:
  1.5 5.4 %collective-permute-start = (bf16[160,128]{1,0:T(8,128)(2,1)S(1)}, bf16[160,128]{1,0:T(8,128)(2,1)S(1)}, u32[]{:S(2)}, u32[]{:S(2)}) collective-permute-start(bf16[160,128]{1,0:T(8,128)(2,1)S(1)} %convert_element_type.12.own.refs_0_), channel_id=1, source_target_pairs={{0,1},{1,0},{2,3},{3,2},{4,5},{5,4},{6,7},{7,6},{8,9},{9,8},{10,11... | collective-permute-start | bytes 122888 | tf_op jit(solution)/shard_map/ppermute | solution.py:338
  2.0 5.6 %collective-permute-start.2 = (bf16[160,128]{1,0:T(8,128)(2,1)S(1)}, bf16[160,128]{1,0:T(8,128)(2,1)S(1)}, u32[]{:S(2)}, u32[]{:S(2)}) collective-permute-start(bf16[160,128]{1,0:T(8,128)(2,1)S(1)} %convert_element_type.12.own.refs_0_), channel_id=1, source_target_pairs={{0,3},{1,2},{2,1},{3,0},{4,7},{5,6},{6,5},{7,4},{8,11},{9,10},{10,... | collective-permute-start | bytes 122888 | tf_op jit(solution)/shard_map/ppermute | solution.py:338
  4.6 4.0 %collective-permute-start.1 = (bf16[160,128]{1,0:T(8,128)(2,1)S(1)}, bf16[160,128]{1,0:T(8,128)(2,1)S(1)}, u32[]{:S(2)}, u32[]{:S(2)}) collective-permute-start(bf16[160,128]{1,0:T(8,128)(2,1)S(1)} %convert_element_type.12.own.refs_0_), channel_id=1, source_target_pairs={{0,2},{1,3},{2,0},{3,1},{4,6},{5,7},{6,4},{7,5},{8,10},{9,11},{10,... | collective-permute-start | bytes 122888 | tf_op jit(solution)/shard_map/ppermute | solution.py:338
  9.5 8.0 %collective-permute-start.3 = (bf16[768,128]{1,0:T(8,128)(2,1)S(1)}, bf16[768,128]{1,0:T(8,128)(2,1)S(1)}, u32[]{:S(2)}, u32[]{:S(2)}) collective-permute-start(bf16[768,128]{1,0:T(8,128)(2,1)S(1)} %get-tuple-element.44), channel_id=1, source_target_pairs={{0,8},{4,0},{8,12},{12,4},{1,9},{5,1},{9,13},{13,5},{2,10},{6,2},{... | collective-permute-start | bytes 589832 | tf_op jit(solution)/shard_map/ppermute | solution.py:449
  13.3 12.3 %copy-start = (f32[160,128]{1,0:T(8,128)S(1)}, f32[160,128]{1,0:T(8,128)}, u32[]{:S(2)}) copy-start(f32[160,128]{1,0:T(8,128)} %refs_7_.1) | copy-start | bytes 245764
  13.3 12.3 %copy-start.1 = (f32[160,128]{1,0:T(8,128)S(1)}, f32[160,128]{1,0:T(8,128)}, u32[]{:S(2)}) copy-start(f32[160,128]{1,0:T(8,128)} %refs_8_.1) | copy-start | bytes 245764
  13.3 12.3 %copy-start.2 = (f32[160,128]{1,0:T(8,128)S(1)}, f32[160,128]{1,0:T(8,128)}, u32[]{:S(2)}) copy-start(f32[160,128]{1,0:T(8,128)} %refs_9_.1) | copy-start | bytes 245764
  13.3 12.2 %collective-permute-start.5 = (bf16[768,128]{1,0:T(8,128)(2,1)S(1)}, bf16[768,128]{1,0:T(8,128)(2,1)S(1)}, u32[]{:S(2)}, u32[]{:S(2)}) collective-permute-start(bf16[768,128]{1,0:T(8,128)(2,1)S(1)} %get-tuple-element.45), channel_id=1, source_target_pairs={{0,4},{4,12},{8,0},{12,8},{1,5},{5,13},{9,1},{13,9},{2,6},{6,14},{... | collective-permute-start | bytes 589832 | tf_op jit(solution)/shard_map/ppermute | solution.py:449
  17.5 8.0 %collective-permute-start.4 = (bf16[768,128]{1,0:T(8,128)(2,1)S(1)}, bf16[768,128]{1,0:T(8,128)(2,1)S(1)}, u32[]{:S(2)}, u32[]{:S(2)}) collective-permute-start(bf16[768,128]{1,0:T(8,128)(2,1)S(1)} %add_convert_fusion), channel_id=1, source_target_pairs={{0,8},{4,0},{8,12},{12,4},{1,9},{5,1},{9,13},{13,5},{2,10},{6,2},{... | collective-permute-start | bytes 589832 | tf_op jit(solution)/shard_map/ppermute | solution.py:449
  21.0 1.9 %collective-permute-start.6 = (bf16[160,128]{1,0:T(8,128)(2,1)S(1)}, bf16[160,128]{1,0:T(8,128)(2,1)S(1)}, u32[]{:S(2)}, u32[]{:S(2)}) collective-permute-start(bf16[160,128]{1,0:T(8,128)(2,1)S(1)} %get-tuple-element.47), channel_id=1, source_target_pairs={{0,1},{1,0},{2,3},{3,2},{4,5},{5,4},{6,7},{7,6},{8,9},{9,8},{10,11... | collective-permute-start | bytes 122888 | tf_op jit(solution)/shard_map/ppermute | solution.py:338
  21.0 4.2 %collective-permute-start.7 = (bf16[160,128]{1,0:T(8,128)(2,1)S(1)}, bf16[160,128]{1,0:T(8,128)(2,1)S(1)}, u32[]{:S(2)}, u32[]{:S(2)}) collective-permute-start(bf16[160,128]{1,0:T(8,128)(2,1)S(1)} %get-tuple-element.48), channel_id=1, source_target_pairs={{0,2},{1,3},{2,0},{3,1},{4,6},{5,7},{6,4},{7,5},{8,10},{9,11},{10,... | collective-permute-start | bytes 122888 | tf_op jit(solution)/shard_map/ppermute | solution.py:338
  21.9 3.6 %collective-permute-start.8 = (bf16[160,128]{1,0:T(8,128)(2,1)S(1)}, bf16[160,128]{1,0:T(8,128)(2,1)S(1)}, u32[]{:S(2)}, u32[]{:S(2)}) collective-permute-start(bf16[160,128]{1,0:T(8,128)(2,1)S(1)} %get-tuple-element.49), channel_id=1, source_target_pairs={{0,3},{1,2},{2,1},{3,0},{4,7},{5,6},{6,5},{7,4},{8,11},{9,10},{10,... | collective-permute-start | bytes 122888 | tf_op jit(solution)/shard_map/ppermute | solution.py:338

commit v27 on v26

--- a/solution.py
+++ b/solution.py
@@ -423,7 +423,7 @@
     if n_gene == 1 or n_gene > RING_MOST or block % 128:
         (rows,), parts = block_rows([(0,)], [jnp.float32], rows_dev, True, True, n_row, fixed, shares)
         grad_cells = lax.psum_scatter(rows, "gene", scatter_dimension=0, tiled=True)
-        others = [swap_row(parts[hop], hop, n_row) for hop in range(1, n_row)]
+        others = [swap_row(parts[hop], hop, n_row) for hop in reversed(range(1, n_row))]
         return (grad_cells, *finish([], [parts[0], *others], *adam))
 
     steps = steps_of(n_gene)
@@ -447,7 +447,7 @@
         if way in came:
             own = plus(own, came[way]).astype(jnp.bfloat16)
         came[way] = lax.ppermute(own, "gene", list(enumerate(around(n_gene, way))))
-    others = [swap_row(parts[hop], hop, n_row) for hop in range(1, n_row)]
+    others = [swap_row(parts[hop], hop, n_row) for hop in reversed(range(1, n_row))]
     *adam_out, grad_cells = finish([blocks[-1], *came.values()], [parts[0], *others], *adam)
     return (grad_cells, *adam_out)
 

time: 26.6 us -> 26.5 us (level)
  no operation moved by 1% of the time
where the time goes in v27:
time: 26.5 us; the launch traced here: 26.3 us
  starting transfers between devices  11.1 us (42%)
  Pallas kernels  7.86 us (30%)
  waiting for transfers between devices  5.67 us (21%)
  other arithmetic  0.95 us (4%)
  between operations  0.75 us (3%)
    ppermute x3, starting transfers between devices, local(): came[way] = lax.ppermute(own, 'gene', list(enumerate(around(n_gene, way))))  6.14 us
    ppermute x6, starting transfers between devices, swap_row(): lax.ppermute(value, 'row', [(me, partner(me, hop, size)) for me in range(...  4.97 us
    ppermute x6, waiting for transfers between devices, swap_row(): lax.ppermute(value, 'row', [(me, partner(me, hop, size)) for me in range(...  3.58 us
    pallas_call x2, Pallas kernels, block_rows(): pl.pallas_call(functools.partial(rows_kernel, tables, block, first, last,...  3.16 us
    pallas_call x1, Pallas kernels, prepare(): pl.pallas_call(functools.partial(prepare_kernel, scale_k), out_shape=(VME...  2.26 us
    ppermute x3, waiting for transfers between devices, local(): came[way] = lax.ppermute(own, 'gene', list(enumerate(around(n_gene, way))))  2.09 us
    pallas_call x1, Pallas kernels, finish(): pl.pallas_call(functools.partial(finish_kernel, len(ends), len(parts)), o...  0.9 us
    convert_element_type x1, other arithmetic, local(): factor_bf = gene_factor.astype(jnp.bfloat16)  0.9 us
  transfers between devices with their start and end apart: 9, of which 4 were waited for; matrix products, arithmetic and copies ran while one was open for 0% of the time, Pallas kernels for 23%

profile of v27, /device:TPU:0, one launch (start us, length us, event | category | flops | bytes accessed | tf_op | source)
XLA Modules:
  0.0 26.3 jit_solution(226939844322576824)
XLA Ops:
  0.6 0.9 %convert_element_type.12.own.refs_0_ = bf16[160,128]{1,0:T(8,128)(2,1)S(1)} convert(f32[160,128]{1,0:T(8,128)} %refs_7_.1) | non-fusion elementwise | flops 20480 | bytes 122880 | tf_op jit(solution)/shard_map/convert_element_type | solution.py:418
  1.5 0.5 %collective-permute-start = (bf16[160,128]{1,0:T(8,128)(2,1)S(1)}, bf16[160,128]{1,0:T(8,128)(2,1)S(1)}, u32[]{:S(2)}, u32[]{:S(2)}) collective-permute-start(bf16[160,128]{1,0:T(8,128)(2,1)S(1)} %convert_element_type.12.own.refs_0_), channel_id=1, source_target_pairs={{0,1},{1,0},{2,3},{3,2},{4,5},{5,4},{6,7},{7,6},{8,9},{9,8},{10,11... | collective-permute-start | bytes 122888 | tf_op jit(solution)/shard_map/ppermute | solution.py:338
  2.0 2.6 %collective-permute-start.2 = (bf16[160,128]{1,0:T(8,128)(2,1)S(1)}, bf16[160,128]{1,0:T(8,128)(2,1)S(1)}, u32[]{:S(2)}, u32[]{:S(2)}) collective-permute-start(bf16[160,128]{1,0:T(8,128)(2,1)S(1)} %convert_element_type.12.own.refs_0_), channel_id=1, source_target_pairs={{0,3},{1,2},{2,1},{3,0},{4,7},{5,6},{6,5},{7,4},{8,11},{9,10},{10,... | collective-permute-start | bytes 122888 | tf_op jit(solution)/shard_map/ppermute | solution.py:338
  4.6 0.1 collective-permute-start.1
  4.6 2.3 %prepare.1 = (bf16[3072,640]{1,0:T(8,128)(2,1)S(1)}, bf16[3072,128]{1,0:T(8,128)(2,1)S(1)}, bf16[128,3072]{1,0:T(8,128)(2,1)S(1)}, f32[1,640]{1,0:T(1,128)S(1)}, f32[640,128]{1,0:T(8,128)S(1)}) custom-call(bf16[3072,640]{1,0:T(8,128)(2,1)} %x_in.1, s32[3072]{0:T(1024)} %index_in.1, bf16[512,128]{1,0:T(8,128)(2,1)} %cell_in.1, f32[640]{0:T(1024)} %scale_in.1), custom_call_target="tpu_custom_call" | custom-call | flops 402653184 | bytes 7864320 | tf_op jit(solution)/shard_map/prepare/pallas_call | solution.py:74
  6.9 0.6 %early_part.1 = (f32[768,128]{1,0:T(8,128)S(1)}, f32[128,256]{1,0:T(8,128)S(1)}, bf16[128,256]{1,0:T(8,128)(2,1)S(1)}, bf16[256,128]{1,0:T(8,128)(2,1)S(1)}) custom-call(bf16[3072,640]{1,0:T(8,128)(2,1)S(1)} %get-tuple-element.29.x_ref.refs_0_, bf16[3072,128]{1,0:T(8,128)(2,1)S(1)} %get-tuple-element.30.f_ref.refs_1_, ...), custom_call_target="tpu_custom_call" | custom-call | flops 301989888 | bytes 786432 | tf_op jit(solution)/shard_map/early_part/pallas_call | solution.py:304
  7.6 0.0 collective-permute-done.2.refs_3_
  7.6 1.0 %collective-permute-done.1.refs_2_ = bf16[160,128]{1,0:T(8,128)(2,1)S(1)} collective-permute-done((bf16[160,128]{1,0:T(8,128)(2,1)S(1)}, bf16[160,128]{1,0:T(8,128)(2,1)S(1)}, u32[]{:S(2)}, u32[]{:S(2)}) %collective-permute-start.1) | collective-permute-done | bytes 40992 | tf_op jit(solution)/shard_map/ppermute | solution.py:338
  8.6 0.9 %rest_part.1 = (bf16[768,128]{1,0:T(8,128)(2,1)S(1)}, f32[128,640]{1,0:T(8,128)S(1)}, bf16[128,640]{1,0:T(8,128)(2,1)S(1)}, bf16[640,128]{1,0:T(8,128)(2,1)S(1)}) custom-call(bf16[3072,640]{1,0:T(8,128)(2,1)S(1)} %get-tuple-element.29.x_ref.refs_0_, bf16[3072,128]{1,0:T(8,128)(2,1)S(1)} %get-tuple-element.30.f_ref.refs_1_, ...), custom_call_target="tpu_custom_call" | custom-call | flops 452984832 | bytes 1179648 | tf_op jit(solution)/shard_map/rest_part/pallas_call | solution.py:319
  9.5 2.6 %collective-permute-start.3 = (bf16[768,128]{1,0:T(8,128)(2,1)S(1)}, bf16[768,128]{1,0:T(8,128)(2,1)S(1)}, u32[]{:S(2)}, u32[]{:S(2)}) collective-permute-start(bf16[768,128]{1,0:T(8,128)(2,1)S(1)} %get-tuple-element.44), channel_id=1, source_target_pairs={{0,8},{4,0},{8,12},{12,4},{1,9},{5,1},{9,13},{13,5},{2,10},{6,2},{... | collective-permute-start | bytes 589832 | tf_op jit(solution)/shard_map/ppermute | solution.py:449
  12.1 1.1 %block_rows.2 = (bf16[768,128]{1,0:T(8,128)(2,1)S(1)}, f32[128,640]{1,0:T(8,128)S(1)}) custom-call(bf16[3072,640]{1,0:T(8,128)(2,1)S(1)} %get-tuple-element.29.x_ref.refs_0_, bf16[3072,128]{1,0:T(8,128)(2,1)S(1)} %get-tuple-element.30.f_ref.refs_1_, bf16[128,3072]{1,0:T(8,128)(2,1)S(1)} %get-tuple-element.31.ft_ref.refs_2_, ...), custom_call_target="tpu_custom_call" | custom-call | flops 377487360 | bytes 983040 | tf_op jit(solution)/shard_map/block_rows/pallas_call | solution.py:195
  13.3 0.0 copy-start
  13.3 0.0 copy-start.1
  13.3 0.0 copy-start.2
  13.3 0.1 collective-permute-start.5
  13.4 2.0 %block_rows.3 = (bf16[768,128]{1,0:T(8,128)(2,1)S(1)}, f32[768,128]{1,0:T(8,128)S(1)}, f32[160,128]{1,0:T(8,128)S(1)}, bf16[160,128]{1,0:T(8,128)(2,1)S(1)}, bf1...) custom-call(bf16[3072,640]{1,0:T(8,128)(2,1)S(1)} %get-tuple-element.29.x_ref.refs_0_, ...), custom_call_target="tpu_custom_call" | custom-call | flops 754974720 | bytes 1966080 | tf_op jit(solution)/shard_map/block_rows/pallas_call | solution.py:195
  15.4 2.1 %collective-permute-done.3 = bf16[768,128]{1,0:T(8,128)(2,1)S(1)} collective-permute-done((bf16[768,128]{1,0:T(8,128)(2,1)S(1)}, bf16[768,128]{1,0:T(8,128)(2,1)S(1)}, u32[]{:S(2)}, u32[]{:S(2)}) %collective-permute-start.3) | collective-permute-done | bytes 196640 | tf_op jit(solution)/shard_map/ppermute | solution.py:449
  17.5 0.1 add_convert_fusion
  17.5 3.4 %collective-permute-start.4 = (bf16[768,128]{1,0:T(8,128)(2,1)S(1)}, bf16[768,128]{1,0:T(8,128)(2,1)S(1)}, u32[]{:S(2)}, u32[]{:S(2)}) collective-permute-start(bf16[768,128]{1,0:T(8,128)(2,1)S(1)} %add_convert_fusion), channel_id=1, source_target_pairs={{0,8},{4,0},{8,12},{12,4},{1,9},{5,1},{9,13},{13,5},{2,10},{6,2},{... | collective-permute-start | bytes 589832 | tf_op jit(solution)/shard_map/ppermute | solution.py:449
  21.0 1.0 %collective-permute-start.7 = (bf16[160,128]{1,0:T(8,128)(2,1)S(1)}, bf16[160,128]{1,0:T(8,128)(2,1)S(1)}, u32[]{:S(2)}, u32[]{:S(2)}) collective-permute-start(bf16[160,128]{1,0:T(8,128)(2,1)S(1)} %get-tuple-element.48), channel_id=1, source_target_pairs={{0,2},{1,3},{2,0},{3,1},{4,6},{5,7},{6,4},{7,5},{8,10},{9,11},{10,... | collective-permute-start | bytes 122888 | tf_op jit(solution)/shard_map/ppermute | solution.py:338
  22.0 0.9 %collective-permute-start.8 = (bf16[160,128]{1,0:T(8,128)(2,1)S(1)}, bf16[160,128]{1,0:T(8,128)(2,1)S(1)}, u32[]{:S(2)}, u32[]{:S(2)}) collective-permute-start(bf16[160,128]{1,0:T(8,128)(2,1)S(1)} %get-tuple-element.49), channel_id=1, source_target_pairs={{0,1},{1,0},{2,3},{3,2},{4,5},{5,4},{6,7},{7,6},{8,9},{9,8},{10,11... | collective-permute-start | bytes 122888 | tf_op jit(solution)/shard_map/ppermute | solution.py:338
  22.8 1.6 %collective-permute-done.6.refs_4_ = bf16[160,128]{1,0:T(8,128)(2,1)S(1)} collective-permute-done((bf16[160,128]{1,0:T(8,128)(2,1)S(1)}, bf16[160,128]{1,0:T(8,128)(2,1)S(1)}, u32[]{:S(2)}, u32[]{:S(2)}) %collective-permute-start.6) | collective-permute-done | bytes 40992 | tf_op jit(solution)/shard_map/ppermute | solution.py:338
  24.4 1.0 %collective-permute-done.7.refs_5_ = bf16[160,128]{1,0:T(8,128)(2,1)S(1)} collective-permute-done((bf16[160,128]{1,0:T(8,128)(2,1)S(1)}, bf16[160,128]{1,0:T(8,128)(2,1)S(1)}, u32[]{:S(2)}, u32[]{:S(2)}) %collective-permute-start.7) | collective-permute-done | bytes 40992 | tf_op jit(solution)/shard_map/ppermute | solution.py:338
  25.4 0.9 %finish.1 = (f32[160,128]{1,0:T(8,128)}, f32[160,128]{1,0:T(8,128)}, f32[160,128]{1,0:T(8,128)}, f32[768,128]{1,0:T(8,128)}) custom-call(f32[768,128]{1,0:T(8,128)S(1)} %get-tuple-element.42.refs_0_, bf16[768,128]{1,0:T(8,128)(2,1)S(1)} %collective-permute-done.4.refs_1_, bf16[768,128]{1,0:T(8,128)(2,1)S(1)} %collective-permute-done.5.refs_2_, ...), custom_call_target="tpu_custom_call" | custom-call | flops 409600 | bytes 1753088 | tf_op jit(solution)/shard_map/finish/pallas_call | solution.py:400
  (8 shorter events, 0.0 us)
Async XLA Ops:
  1.5 5.4 %collective-permute-start = (bf16[160,128]{1,0:T(8,128)(2,1)S(1)}, bf16[160,128]{1,0:T(8,128)(2,1)S(1)}, u32[]{:S(2)}, u32[]{:S(2)}) collective-permute-start(bf16[160,128]{1,0:T(8,128)(2,1)S(1)} %convert_element_type.12.own.refs_0_), channel_id=1, source_target_pairs={{0,1},{1,0},{2,3},{3,2},{4,5},{5,4},{6,7},{7,6},{8,9},{9,8},{10,11... | collective-permute-start | bytes 122888 | tf_op jit(solution)/shard_map/ppermute | solution.py:338
  2.0 5.6 %collective-permute-start.2 = (bf16[160,128]{1,0:T(8,128)(2,1)S(1)}, bf16[160,128]{1,0:T(8,128)(2,1)S(1)}, u32[]{:S(2)}, u32[]{:S(2)}) collective-permute-start(bf16[160,128]{1,0:T(8,128)(2,1)S(1)} %convert_element_type.12.own.refs_0_), channel_id=1, source_target_pairs={{0,3},{1,2},{2,1},{3,0},{4,7},{5,6},{6,5},{7,4},{8,11},{9,10},{10,... | collective-permute-start | bytes 122888 | tf_op jit(solution)/shard_map/ppermute | solution.py:338
  4.6 4.0 %collective-permute-start.1 = (bf16[160,128]{1,0:T(8,128)(2,1)S(1)}, bf16[160,128]{1,0:T(8,128)(2,1)S(1)}, u32[]{:S(2)}, u32[]{:S(2)}) collective-permute-start(bf16[160,128]{1,0:T(8,128)(2,1)S(1)} %convert_element_type.12.own.refs_0_), channel_id=1, source_target_pairs={{0,2},{1,3},{2,0},{3,1},{4,6},{5,7},{6,4},{7,5},{8,10},{9,11},{10,... | collective-permute-start | bytes 122888 | tf_op jit(solution)/shard_map/ppermute | solution.py:338
  9.5 8.0 %collective-permute-start.3 = (bf16[768,128]{1,0:T(8,128)(2,1)S(1)}, bf16[768,128]{1,0:T(8,128)(2,1)S(1)}, u32[]{:S(2)}, u32[]{:S(2)}) collective-permute-start(bf16[768,128]{1,0:T(8,128)(2,1)S(1)} %get-tuple-element.44), channel_id=1, source_target_pairs={{0,8},{4,0},{8,12},{12,4},{1,9},{5,1},{9,13},{13,5},{2,10},{6,2},{... | collective-permute-start | bytes 589832 | tf_op jit(solution)/shard_map/ppermute | solution.py:449
  13.3 12.1 %copy-start = (f32[160,128]{1,0:T(8,128)S(1)}, f32[160,128]{1,0:T(8,128)}, u32[]{:S(2)}) copy-start(f32[160,128]{1,0:T(8,128)} %refs_7_.1) | copy-start | bytes 245764
  13.3 12.1 %copy-start.1 = (f32[160,128]{1,0:T(8,128)S(1)}, f32[160,128]{1,0:T(8,128)}, u32[]{:S(2)}) copy-start(f32[160,128]{1,0:T(8,128)} %refs_8_.1) | copy-start | bytes 245764
  13.3 12.1 %copy-start.2 = (f32[160,128]{1,0:T(8,128)S(1)}, f32[160,128]{1,0:T(8,128)}, u32[]{:S(2)}) copy-start(f32[160,128]{1,0:T(8,128)} %refs_9_.1) | copy-start | bytes 245764
  13.3 12.1 %collective-permute-start.5 = (bf16[768,128]{1,0:T(8,128)(2,1)S(1)}, bf16[768,128]{1,0:T(8,128)(2,1)S(1)}, u32[]{:S(2)}, u32[]{:S(2)}) collective-permute-start(bf16[768,128]{1,0:T(8,128)(2,1)S(1)} %get-tuple-element.45), channel_id=1, source_target_pairs={{0,4},{4,12},{8,0},{12,8},{1,5},{5,13},{9,1},{13,9},{2,6},{6,14},{... | collective-permute-start | bytes 589832 | tf_op jit(solution)/shard_map/ppermute | solution.py:449
  17.5 7.9 %collective-permute-start.4 = (bf16[768,128]{1,0:T(8,128)(2,1)S(1)}, bf16[768,128]{1,0:T(8,128)(2,1)S(1)}, u32[]{:S(2)}, u32[]{:S(2)}) collective-permute-start(bf16[768,128]{1,0:T(8,128)(2,1)S(1)} %add_convert_fusion), channel_id=1, source_target_pairs={{0,8},{4,0},{8,12},{12,4},{1,9},{5,1},{9,13},{13,5},{2,10},{6,2},{... | collective-permute-start | bytes 589832 | tf_op jit(solution)/shard_map/ppermute | solution.py:449
  21.0 3.4 %collective-permute-start.6 = (bf16[160,128]{1,0:T(8,128)(2,1)S(1)}, bf16[160,128]{1,0:T(8,128)(2,1)S(1)}, u32[]{:S(2)}, u32[]{:S(2)}) collective-permute-start(bf16[160,128]{1,0:T(8,128)(2,1)S(1)} %get-tuple-element.47), channel_id=1, source_target_pairs={{0,3},{1,2},{2,1},{3,0},{4,7},{5,6},{6,5},{7,4},{8,11},{9,10},{10,... | collective-permute-start | bytes 122888 | tf_op jit(solution)/shard_map/ppermute | solution.py:338
  21.0 4.4 %collective-permute-start.7 = (bf16[160,128]{1,0:T(8,128)(2,1)S(1)}, bf16[160,128]{1,0:T(8,128)(2,1)S(1)}, u32[]{:S(2)}, u32[]{:S(2)}) collective-permute-start(bf16[160,128]{1,0:T(8,128)(2,1)S(1)} %get-tuple-element.48), channel_id=1, source_target_pairs={{0,2},{1,3},{2,0},{3,1},{4,6},{5,7},{6,4},{7,5},{8,10},{9,11},{10,... | collective-permute-start | bytes 122888 | tf_op jit(solution)/shard_map/ppermute | solution.py:338
  22.0 3.4 %collective-permute-start.8 = (bf16[160,128]{1,0:T(8,128)(2,1)S(1)}, bf16[160,128]{1,0:T(8,128)(2,1)S(1)}, u32[]{:S(2)}, u32[]{:S(2)}) collective-permute-start(bf16[160,128]{1,0:T(8,128)(2,1)S(1)} %get-tuple-element.49), channel_id=1, source_target_pairs={{0,1},{1,0},{2,3},{3,2},{4,5},{5,4},{6,7},{7,6},{8,9},{9,8},{10,11... | collective-permute-start | bytes 122888 | tf_op jit(solution)/shard_map/ppermute | solution.py:338
